TPU v7x, 32 devices: a whole 2x2x4 slice. The times are simulated.
32 devices in a mesh: runs: 2 (over y), dom: 8 (over z, x), sub: 2 (over core).
Axes of the slice: x: 2, y: 2, z: 4, core: 2. Of those that a mesh axis runs over, the one named last changes fastest.
Arguments:
- displacement: float32 [3, 64, 32, 256], P(None, ('runs', 'dom', 'sub')), parts along dimension 1, may hold values from -6 to 6
- modulus: float32 [64, 32, 256], P(('runs', 'dom', 'sub')), parts along dimension 0, may hold values from 0.3 to 3
- node_mass: float32 [64, 32, 256], P(('runs', 'dom', 'sub')), parts along dimension 0, may hold values from 0.5 to 2
- stiffness: float32 [24, 24], replicated
- face_nodes: int32 [4, 16384], P(None, ('runs', 'dom', 'sub')), parts along dimension 1, may hold values from 0 to 16383
- pair_mortar: int32 [8192], P(('runs', 'dom', 'sub')), parts along dimension 0, may hold values from 0 to 511
- pair_rank: int32 [8192, 1], P(('runs', 'dom', 'sub')), parts along dimension 0, may hold values from 0 to 7; in each aligned block of 256 rows (0 to 255, 256 to 511, ...) at most 64 rows name the same one
- pair_face: int32 [8192], P(('runs', 'dom', 'sub')), parts along dimension 0, may hold values from 0 to 511
- pair_count: int32 [8192], P(('runs', 'dom', 'sub')), parts along dimension 0, may hold values from 4 to 25
- pair_shape: float32 [8, 25, 8192], P(None, None, ('runs', 'dom', 'sub')), parts along dimension 2, may hold values from 0 to 1
- pair_weight: float32 [25, 8192], P(None, ('runs', 'dom', 'sub')), parts along dimension 1, may hold values from 0.05 to 0.5
- pair_gap: float32 [25, 8192], P(None, ('runs', 'dom', 'sub')), parts along dimension 1, may hold values from -4 to 4
- pair_normal: float32 [3, 8192], P(None, ('runs', 'dom', 'sub')), parts along dimension 1, may hold values from -4 to 4
Outputs:
- acceleration: float32 [3, 64, 32, 256], P(None, ('runs', 'dom', 'sub')), parts along dimension 1
There are 2 independent parts, one for each index of `runs`. A program takes and returns all parts, laid end to end along the dimension named above; an argument that names none is the same for every part. Nothing has to cross between parts.
Inputs may be any that keep to these rules, and one draw needn't show every extreme that they name: `pair_rank`: in every partition at most 64 pairs name the same remote partition.
All inputs are finite; a program needn't handle non-finite values.
Results may differ from a plain program's by a relative error of at most 0.00005.
Values sent between devices are 32-bit elements; how exact they have to be, the bound alone decides.
No kernel may reach another device: no remote copies, remote signals or barrier semaphores. Data moves between devices by JAX's collectives and lax.ppermute only.
A program may use at most 64 MiB of HBM per device.

v0:
```python
import jax
import jax.numpy as jnp
from jax import lax
from jax.sharding import PartitionSpec as P


def passed_along(block, axis, distance):
    devices = range(lax.axis_size(axis))
    route = [(i - distance, i) for i in devices if i - distance in devices]
    return lax.ppermute(block, axis, route)


def element_forces(extended, modulus, stiffness):
    layers = extended.shape[1] - 1
    rows_y = extended.shape[2]
    cols_x = extended.shape[3]
    mask_y = lax.broadcasted_iota(jnp.int32, (rows_y, cols_x), 0) < rows_y - 1
    mask_x = lax.broadcasted_iota(jnp.int32, (rows_y, cols_x), 1) < cols_x - 1
    elastic = modulus * (mask_y & mask_x).astype(jnp.float32)[None]
    corners = []
    for component in range(3):
        for corner in range(8):
            offset_z, offset_y, offset_x = (corner // 4, corner // 2 % 2, corner % 2)
            layer_part = extended[component, offset_z : offset_z + layers]
            corners.append(jnp.roll(layer_part, (-offset_y, -offset_x), axis=(1, 2)))
    stacked = jnp.stack(corners)
    elem_force = (
        jnp.einsum("ij,jzyx->izyx", stiffness, stacked, precision=lax.Precision.HIGHEST)
        * elastic[None]
    )
    nodal_force = jnp.zeros((3, layers + 1, rows_y, cols_x), jnp.float32)
    for component in range(3):
        for corner in range(8):
            offset_z, offset_y, offset_x = (corner // 4, corner // 2 % 2, corner % 2)
            moved = jnp.roll(elem_force[component * 8 + corner], (offset_y, offset_x), axis=(1, 2))
            nodal_force = nodal_force.at[component, offset_z : offset_z + layers].add(-moved)
    return nodal_force


def penalty(mortar_rows, remote_rows, pair_count, pair_shape, pair_weight, pair_gap, pair_normal):
    points, pair_total = pair_weight.shape
    remote_shape = pair_shape[:4]
    mortar_shape = pair_shape[4:]
    remote_points = jnp.sum(remote_rows.reshape(3, 4, 1, pair_total) * remote_shape[None], axis=1)
    mortar_points = jnp.sum(mortar_rows.reshape(3, 4, 1, pair_total) * mortar_shape[None], axis=1)
    gap_value = pair_gap + jnp.sum(
        pair_normal[:, None, :] * (remote_points - mortar_points), axis=0
    )
    live_mask = lax.broadcasted_iota(jnp.int32, (points, pair_total), 0) < pair_count[None, :]
    pressure = jnp.where(live_mask, pair_weight * jnp.maximum(-gap_value, 0.0), 0.0)
    remote_load = jnp.sum(pressure[None] * remote_shape, axis=1)
    mortar_load = jnp.sum(pressure[None] * mortar_shape, axis=1)
    remote_force = (pair_normal[:, None, :] * remote_load[None]).reshape(12, pair_total)
    mortar_force = -(pair_normal[:, None, :] * mortar_load[None]).reshape(12, pair_total)
    return (mortar_force, remote_force)


def shards(
    displacement,
    modulus,
    node_mass,
    stiffness,
    face_nodes,
    pair_mortar,
    pair_rank,
    pair_face,
    pair_count,
    pair_shape,
    pair_weight,
    pair_gap,
    pair_normal,
):
    layers = displacement.shape[1]
    ghost_layer = passed_along(displacement[:, :1], ("dom", "sub"), -1)
    extended = jnp.concatenate([displacement, ghost_layer], axis=1)
    nodal_force = element_forces(extended, modulus, stiffness)
    returned = passed_along(nodal_force[:, layers:], ("dom", "sub"), 1)
    internal = nodal_force[:, :layers].at[:, :1].add(returned)
    flat_disp = displacement.reshape(3, -1)
    face_count = face_nodes.shape[1]
    pair_total = pair_mortar.shape[0]
    face_rows = flat_disp[:, face_nodes].reshape(12, face_count)
    mortar_rows = face_rows[:, pair_mortar]
    target = pair_rank[:, 0]
    domains = lax.axis_size("dom")
    capacity = max(2, 2 * pair_total // domains)
    rank_ids = jnp.arange(domains, dtype=jnp.int32)
    one_hot = (target[:, None] == rank_ids[None, :]).astype(jnp.int32)
    earlier = jnp.cumsum(one_hot, axis=0) - one_hot
    slot_index = jnp.sum(earlier * one_hot, axis=1)
    position = target * capacity + slot_index
    requests = (
        jnp.zeros((domains * capacity,), jnp.int32)
        .at[position]
        .set(pair_face)
        .reshape(domains, capacity)
    )
    incoming = lax.all_to_all(requests, "dom", split_axis=0, concat_axis=0, tiled=True)
    asked_faces = incoming.reshape(-1)
    served = face_rows[:, asked_faces].reshape(12, domains, capacity)
    replies = lax.all_to_all(served, "dom", split_axis=1, concat_axis=1, tiled=True)
    remote_rows = replies.reshape(12, -1)[:, position]
    mortar_force, remote_force = penalty(
        mortar_rows, remote_rows, pair_count, pair_shape, pair_weight, pair_gap, pair_normal
    )
    outgoing = (
        jnp.zeros((12, domains * capacity), jnp.float32)
        .at[:, position]
        .set(remote_force)
        .reshape(12, domains, capacity)
    )
    arrived = lax.all_to_all(outgoing, "dom", split_axis=1, concat_axis=1, tiled=True)
    face_force = (
        jnp.zeros((12, face_count), jnp.float32).at[:, asked_faces].add(arrived.reshape(12, -1))
    )
    face_force = face_force.at[:, pair_mortar].add(mortar_force)
    contact = (
        jnp.zeros(flat_disp.shape, jnp.float32)
        .at[:, face_nodes.reshape(-1)]
        .add(face_force.reshape(3, -1))
    )
    return (internal + contact.reshape(internal.shape)) / node_mass[None]


def solution(mesh):
    placed = (
        P(None, ("runs", "dom", "sub"), None, None),
        P(("runs", "dom", "sub"), None, None),
        P(("runs", "dom", "sub"), None, None),
        P(),
        P(None, ("runs", "dom", "sub")),
        P(("runs", "dom", "sub")),
        P(("runs", "dom", "sub"), None),
        P(("runs", "dom", "sub")),
        P(("runs", "dom", "sub")),
        P(None, None, ("runs", "dom", "sub")),
        P(None, ("runs", "dom", "sub")),
        P(None, ("runs", "dom", "sub")),
        P(None, ("runs", "dom", "sub")),
    )
    return jax.shard_map(
        shards,
        mesh=mesh,
        in_specs=placed,
        out_specs=P(None, ("runs", "dom", "sub"), None, None),
        check_vma=False,
    )
```

profile of v0, /device:TPU:1, one launch (start us, length us, event | category | flops | bytes accessed | tf_op | source)
XLA Modules:
  0.0 104.2 jit_solution(13938153987585108141)
XLA Ops:
  0.9 2.0 %collective-permute-start = (f32[3,1,32,256]{3,2,1,0:T(8,128)S(1)}, f32[3,1,32,256]{3,2,1,0:T(8,128)S(1)}, u32[]{:S(2)}, u32[]{:S(2)}) collective-permute-start(f32[3,1,32,256]{3,2,1,0:T(8,128)S(1)} %slice.1158), channel_id=1, source_target_pairs={{1,0},{2,1},{3,2},{4,3},{5,4},{6,5},{7,6},{8,7},{9,8},{10,9},{11,1... | collective-permute-start | bytes 294920 | tf_op jit(solution)/shard_map/ppermute | solution.py:10
  5.8 1.6 %scatter_custom_fusion = s32[512]{0:T(512)S(1)} fusion(s32[256]{0:T(256)S(1)} %bitcast.246, s32[256]{0:T(256)} %param.70, s32[]{:T(128)} %constant.605.clone.1), kind=kCustom, calls=%fused_computation.252 | custom fusion | bytes 2560 | tf_op jit(solution)/shard_map/scatter | solution.py:95
  8.1 7.0 %all-to-all-start = ((s32[8,1,64]{2,1,0:T(1,128)}), s32[8,1,64]{2,1,0:T(1,128)S(1)}, u32[]{:S(2)}, u32[]{:S(2)}) async-start(s32[8,1,64]{2,1,0:T(1,128)} %all_to_all.12), calls=%async_computation | async-start | bytes 8192 | tf_op jit(solution)/shard_map/all_to_all | solution.py:98
  15.1 1.0 constant_dynamic-update-slice_fusion.6
  16.1 0.9 slice_bitcast_fusion.27
  19.1 4.7 %copy.344 = f32[3,2,32,256]{0,3,2,1:T(8,128)} copy(f32[3,2,32,256]{3,2,1,0:T(8,128)S(1)} %copy-done.1) | data formatting | bytes 393216 | tf_op args[0]
  23.7 8.8 %gather_fusion = f32[2048,3]{1,0:T(8,128)S(1)} fusion(f32[3,16384]{0,1:T(8,128)} %bitcast.207, s32[2048]{0:T(1024)S(1)} %broadcast_clamp_fusion), kind=kCustom, calls=%fused_computation | custom fusion | bytes 57344 | tf_op jit(solution)/shard_map/gather | solution.py:82
  34.4 1.0 gather_fusion.1
  36.3 5.4 %all-to-all-start.1 = ((f32[8,1,768]{2,1,0:T(1,128)}), f32[8,1,768]{2,1,0:T(1,128)S(1)}, u32[]{:S(2)}, u32[]{:S(2)}) async-start(f32[8,1,768]{2,1,0:T(1,128)} %reshape.1531), calls=%async_computation.1 | async-start | bytes 49152 | tf_op jit(solution)/shard_map/all_to_all | solution.py:101
  43.4 3.7 %all-to-all-done.1 = f32[8,1,768]{2,1,0:T(1,128)S(1)} async-done(((f32[8,1,768]{2,1,0:T(1,128)}), f32[8,1,768]{2,1,0:T(1,128)S(1)}, u32[]{:S(2)}, u32[]{:S(2)}) %all-to-all-start.1) | async-done | bytes 24608 | tf_op jit(solution)/shard_map/all_to_all | solution.py:101
  50.3 1.2 %scatter_custom_fusion.1 = f32[12,512]{0,1:T(8,128)S(1)} fusion(s32[256]{0:T(256)S(1)} %bitcast.248, f32[256,12]{1,0:T(8,128)S(1)} %copy.352, f32[]{:T(128)} %constant.604.clone.1), kind=kCustom, calls=%fused_computation.17 | custom fusion | bytes 24580 | tf_op jit(solution)/shard_map/scatter | solution.py:109
  52.3 3.5 %all-to-all-start.2 = ((f32[8,1,768]{2,1,0:T(1,128)}), f32[8,1,768]{2,1,0:T(1,128)S(1)}, u32[]{:S(2)}, u32[]{:S(2)}) async-start(f32[8,1,768]{2,1,0:T(1,128)} %reshape.1533), calls=%async_computation.2 | async-start | bytes 49152 | tf_op jit(solution)/shard_map/all_to_all | solution.py:112
  58.0 2.5 %stack.81 = f32[24,2,32,256]{3,0,2,1:T(8,128)S(1)} concatenate(f32[1,2,32,256]{3,0,2,1:T(1,128)S(1)} %copy.289, f32[1,2,32,256]{3,0,2,1:T(1,128)S(1)} %copy.290, f32[1,2,32,256]{3,0,2,1:T(1,128)S(1)} %copy.291, f32[1,2,32,256]{3,0,2,1:T(1,128)S(1)} %stack.65, f32[1,2,32,256]{3,0,2,1:T(1,128)S(1)} %copy.292, f32[1,2,32,256]{3,0,2,1:T(1,128)S(1)} %copy.293, ...), dimensions={0} | concatenate | bytes 3145728 | tf_op jit(solution)/shard_map/stack | solution.py:26
  60.5 1.5 %multiply_bitcast_fusion = f32[24,2,32,256]{3,0,2,1:T(8,128)S(1)} fusion(f32[24,2,32,256]{3,0,2,1:T(8,128)S(1)} %stack.81, f32[2,32,256]{2,1,0:T(8,128)S(1)} %broadcast_multiply_fusion, f32[24,24]{1,0:T(8,128)S(1)} %copy-done), kind=kOutput, calls=%fused_computation.11 | convolution fusion | flops 113639424 | bytes 3213568 | tf_op jit(solution)/shard_map/ij,jzyx->izyx/dot_general | solution.py:28
  62.0 1.2 %fusion.92 = (f32[1,2,32,256]{3,0,2,1:T(1,128)S(1)}, f32[1,2,32,256]{3,0,2,1:T(1,128)S(1)}, f32[1,2,32,256]{3,0,2,1:T(1,128)S(1)}, f32[1,2,32,256]{3,0,2,1:T(1,1...) fusion(f32[24,2,32,256]{3,0,2,1:T(8,128)S(1)} %multiply_bitcast, ...), kind=kLoop, calls=%fused_computation.262 | loop fusion | bytes 2490368 | tf_op jit(solution)/shard_map/slice | solution.py:35
  65.3 1.2 %fusion.52 = f32[3,3,32,256]{3,2,1,0:T(8,128)S(1)} fusion(f32[3,3,32,256]{3,2,1,0:T(8,128)S(1)} %fusion.28, s32[]{:T(128)} %bitcast.32, s32[]{:T(128)} %bitcast.33, f32[1,2,32,256]{3,0,2,1:T(1,128)S(1)} %get-tuple-element.335), kind=kLoop, calls=%fused_computation.170 | loop fusion | flops 32768 | bytes 196616 | tf_op jit(solution)/shard_map/scatter-add | solution.py:36
  66.5 1.3 %fusion.30 = f32[3,3,32,256]{3,2,1,0:T(8,128)S(1)} fusion(f32[3,3,32,256]{3,2,1,0:T(8,128)S(1)} %fusion.52, s32[]{:T(128)} %bitcast.32, s32[]{:T(128)} %bitcast.33, f32[1,2,32,255]{3,2,1,0:T(8,128)S(1)} %slice_bitcast_fusion.9, f32[1,2,32,1]{3,2,1,0:T(8,128)S(1)} %slice_bitcast_fusion.16), kind=kLoop, calls=%fused_computation.105 | loop fusion | flops 49152 | bytes 229384 | tf_op jit(solution)/shard_map/scatter-add | solution.py:36
  67.8 1.2 %fusion.32 = f32[3,3,32,256]{3,2,1,0:T(8,128)S(1)} fusion(f32[3,3,32,256]{3,2,1,0:T(8,128)S(1)} %fusion.30, s32[]{:T(128)} %bitcast.32, s32[]{:T(128)} %bitcast.33, f32[1,2,31,256]{3,2,1,0:T(8,128)S(1)} %slice_bitcast_fusion.8, f32[1,2,1,256]{3,2,1,0:T(1,128)S(1)} %slice_bitcast_fusion.22), kind=kLoop, calls=%fused_computation.108 | loop fusion | flops 49152 | bytes 198664 | tf_op jit(solution)/shard_map/scatter-add | solution.py:36
  69.0 1.3 %fusion.34 = f32[3,3,32,256]{3,2,1,0:T(8,128)S(1)} fusion(f32[3,3,32,256]{3,2,1,0:T(8,128)S(1)} %fusion.32, s32[]{:T(128)} %bitcast.32, s32[]{:T(128)} %bitcast.33, f32[1,2,32,255]{3,2,1,0:T(8,128)S(1)} %fusion.23, f32[1,2,32,1]{3,2,1,0:T(8,128)S(1)} %fusion.68), kind=kLoop, calls=%fused_computation.113 | loop fusion | flops 49152 | bytes 229384 | tf_op jit(solution)/shard_map/scatter-add | solution.py:36
  71.4 5.2 %collective-permute-start.1 = (f32[3,1,32,256]{3,2,1,0:T(8,128)S(1)}, f32[3,1,32,256]{3,2,1,0:T(8,128)S(1)}, u32[]{:S(2)}, u32[]{:S(2)}) collective-permute-start(f32[3,1,32,256]{3,2,1,0:T(8,128)S(1)} %slice.1416), channel_id=1, source_target_pairs={{0,1},{1,2},{2,3},{3,4},{4,5},{5,6},{6,7},{7,8},{8,9},{9,10},{10,1... | collective-permute-start | bytes 294920 | tf_op jit(solution)/shard_map/ppermute | solution.py:10
  77.8 2.3 %scatter_custom_fusion.2 = f32[12,512]{0,1:T(8,128)S(1)} fusion(s32[512]{0:T(512)S(1)} %bitcast.244, f32[512,12]{1,0:T(8,128)S(1)} %copy.355, f32[]{:T(128)} %constant.604.clone.1), kind=kCustom, calls=%fused_computation.15 | custom fusion | flops 6144 | bytes 24580 | tf_op jit(solution)/shard_map/scatter-add | solution.py:114
  80.2 2.3 %scatter_fusion = f32[12,512]{0,1:T(8,128)S(1)} fusion(f32[12,512]{0,1:T(8,128)S(1)} %scatter_custom_fusion.2, s32[256]{0:T(256)S(1)} %compare_select_fusion.4, f32[256,12]{1,0:T(8,128)S(1)} %copy.356), kind=kCustom, calls=%fused_computation.7 | custom fusion | flops 3072 | bytes 37888 | tf_op jit(solution)/shard_map/scatter-add | solution.py:116
  83.0 15.2 %scatter_custom_fusion.4 = f32[3,16384]{0,1:T(8,128)} fusion(s32[2048]{0:T(1024)S(1)} %bitcast.245, f32[2048,3]{1,0:T(8,128)S(1)} %copy.358, f32[]{:T(128)} %constant.604.clone.1), kind=kCustom, calls=%fused_computation.9 | custom fusion | flops 6144 | bytes 196612 | tf_op jit(solution)/shard_map/scatter-add | solution.py:120
  98.1 5.3 %copy.361 = f32[3,2,32,256]{3,2,1,0:T(8,128)S(1)} copy(f32[3,2,32,256]{0,3,2,1:T(8,128)} %bitcast.206) | data formatting | bytes 393216 | tf_op jit(solution)/shard_map/reshape | solution.py:122
  (251 shorter events, 21.4 us)
Async XLA Ops:
  0.0 60.5 %copy-start = (f32[24,24]{1,0:T(8,128)S(1)}, f32[24,24]{1,0:T(8,128)}, u32[]{:S(2)}) copy-start(f32[24,24]{1,0:T(8,128)} %param.66) | copy-start | bytes 6916
  0.9 54.9 %collective-permute-start = (f32[3,1,32,256]{3,2,1,0:T(8,128)S(1)}, f32[3,1,32,256]{3,2,1,0:T(8,128)S(1)}, u32[]{:S(2)}, u32[]{:S(2)}) collective-permute-start(f32[3,1,32,256]{3,2,1,0:T(8,128)S(1)} %slice.1158), channel_id=1, source_target_pairs={{1,0},{2,1},{3,2},{4,3},{5,4},{6,5},{7,6},{8,7},{9,8},{10,9},{11,1... | collective-permute-start | bytes 294920 | tf_op jit(solution)/shard_map/ppermute | solution.py:10
  4.1 14.2 %copy-start.5 = (s32[4,512]{1,0:T(4,128)S(1)}, s32[4,512]{1,0:T(4,128)}, u32[]{:S(2)}) copy-start(s32[4,512]{1,0:T(4,128)} %param.67) | copy-start | bytes 24580
  8.1 25.0 %all-to-all-start = ((s32[8,1,64]{2,1,0:T(1,128)}), s32[8,1,64]{2,1,0:T(1,128)S(1)}, u32[]{:S(2)}, u32[]{:S(2)}) async-start(s32[8,1,64]{2,1,0:T(1,128)} %all_to_all.12), calls=%async_computation | async-start | bytes 8192 | tf_op jit(solution)/shard_map/all_to_all | solution.py:98
  15.1 3.3 %copy-start.10 = (s32[256]{0:T(256)S(1)}, s32[256]{0:T(256)}, u32[]{:S(2)}) copy-start(s32[256]{0:T(256)} %param.68) | copy-start | bytes 3076
  15.1 3.4 %copy-start.2 = (f32[8,25,256]{2,0,1:T(8,128)S(1)}, f32[8,25,256]{2,0,1:T(8,128)}, u32[]{:S(2)}) copy-start(f32[8,25,256]{2,0,1:T(8,128)} %param.72) | copy-start | bytes 614404
  17.2 1.9 %copy-start.4 = (f32[2,32,256]{2,1,0:T(8,128)S(1)}, f32[2,32,256]{2,1,0:T(8,128)}, u32[]{:S(2)}) copy-start(f32[2,32,256]{2,1,0:T(8,128)} %param.64) | copy-start | bytes 196612
  17.3 1.8 %copy-start.1 = (f32[3,2,32,256]{3,2,1,0:T(8,128)S(1)}, f32[3,2,32,256]{3,2,1,0:T(8,128)}, u32[]{:S(2)}) copy-start(f32[3,2,32,256]{3,2,1,0:T(8,128)} %param.63) | copy-start | bytes 589828
  36.3 10.9 %all-to-all-start.1 = ((f32[8,1,768]{2,1,0:T(1,128)}), f32[8,1,768]{2,1,0:T(1,128)S(1)}, u32[]{:S(2)}, u32[]{:S(2)}) async-start(f32[8,1,768]{2,1,0:T(1,128)} %reshape.1531), calls=%async_computation.1 | async-start | bytes 49152 | tf_op jit(solution)/shard_map/all_to_all | solution.py:101
  41.7 8.3 %copy-start.8 = (f32[3,256]{1,0:T(4,128)S(1)}, f32[3,256]{1,0:T(4,128)}, u32[]{:S(2)}) copy-start(f32[3,256]{1,0:T(4,128)} %param.75) | copy-start | bytes 9220
  41.8 8.2 %copy-start.6 = (f32[25,256]{1,0:T(8,128)S(1)}, f32[25,256]{1,0:T(8,128)}, u32[]{:S(2)}) copy-start(f32[25,256]{1,0:T(8,128)} %param.73) | copy-start | bytes 76804
  41.8 8.2 %copy-start.7 = (f32[25,256]{1,0:T(8,128)S(1)}, f32[25,256]{1,0:T(8,128)}, u32[]{:S(2)}) copy-start(f32[25,256]{1,0:T(8,128)} %param.74) | copy-start | bytes 76804
  41.8 8.2 %copy-start.9 = (s32[256]{0:T(256)S(1)}, s32[256]{0:T(256)}, u32[]{:S(2)}) copy-start(s32[256]{0:T(256)} %param.71) | copy-start | bytes 3076
  52.3 24.4 %all-to-all-start.2 = ((f32[8,1,768]{2,1,0:T(1,128)}), f32[8,1,768]{2,1,0:T(1,128)S(1)}, u32[]{:S(2)}, u32[]{:S(2)}) async-start(f32[8,1,768]{2,1,0:T(1,128)} %reshape.1533), calls=%async_computation.2 | async-start | bytes 49152 | tf_op jit(solution)/shard_map/all_to_all | solution.py:112
  71.4 32.1 %collective-permute-start.1 = (f32[3,1,32,256]{3,2,1,0:T(8,128)S(1)}, f32[3,1,32,256]{3,2,1,0:T(8,128)S(1)}, u32[]{:S(2)}, u32[]{:S(2)}) collective-permute-start(f32[3,1,32,256]{3,2,1,0:T(8,128)S(1)} %slice.1416), channel_id=1, source_target_pairs={{0,1},{1,2},{2,3},{3,4},{4,5},{5,6},{6,7},{7,8},{8,9},{9,10},{10,1... | collective-permute-start | bytes 294920 | tf_op jit(solution)/shard_map/ppermute | solution.py:10
  98.1 5.3 %copy-start.3 = (f32[2,32,256]{2,1,0:T(8,128)S(1)}, f32[2,32,256]{2,1,0:T(8,128)}, u32[]{:S(2)}) copy-start(f32[2,32,256]{2,1,0:T(8,128)} %param.65) | copy-start | bytes 196612
where the time goes:
time: 106 us; the launch traced here: 104 us
  local copies, waits for them, and re-layouts  40.2 us (38%)
  other arithmetic  34.2 us (32%)
  starting transfers between devices  23.1 us (22%)
  waiting for transfers between devices  3.74 us (4%)
  matrix products  1.49 us (1%)
  between operations  1.49 us (1%)
    scatter-add x1, other arithmetic, shards(): contact = jnp.zeros(flat_disp.shape, jnp.float32).at[:, face_nodes.reshap...  15.2 us
    gather x2, local copies, waits for them, and re-layouts, shards(): face_rows = flat_disp[:, face_nodes].reshape(12, face_count)  9.17 us
    unnamed x36, local copies, waits for them, and re-layouts  7.39 us
    ppermute x2, starting transfers between devices, passed_along(): return lax.ppermute(block, axis, route)  7.2 us
    all_to_all x1, starting transfers between devices, shards(): lax.all_to_all(requests, 'dom', split_axis=0, concat_axis=0, tiled=True)  6.97 us
    scatter-add x23, other arithmetic, element_forces(): nodal_force.at[component, offset_z:offset_z + layers].add(-moved)  6.02 us
    all_to_all x1, starting transfers between devices, shards(): lax.all_to_all(served, 'dom', split_axis=1, concat_axis=1, tiled=True)  5.42 us
    reshape x1, local copies, waits for them, and re-layouts, shards(): return (internal + contact.reshape(internal.shape)) / node_mass[None]  5.25 us
  transfers between devices with their start and end apart: 5, of which 1 were waited for; matrix products, arithmetic and copies ran while one was open for 70% of the time, Pallas kernels for 0%

commit v1 on v0

v1 whole, which is shorter than its diff:
```python
import jax
import jax.numpy as jnp
from jax import lax
from jax.experimental import pallas as pl
from jax.experimental.pallas import tpu as pltpu
from jax.sharding import PartitionSpec as P

F32 = jnp.float32
BF16 = jnp.bfloat16
LANES = 128
WORDS = 8


def passed_along(block, axis, distance):
    devices = range(lax.axis_size(axis))
    route = [(i - distance, i) for i in devices if i - distance in devices]
    return lax.ppermute(block, axis, route)


def thirds(x):
    high = x.astype(BF16)
    rest = x - high.astype(F32)
    middle = rest.astype(BF16)
    low = (rest - middle.astype(F32)).astype(BF16)
    return jnp.concatenate([high, middle, low], axis=0)


def summed(stacked):
    rows = stacked.shape[0] // 3
    return (stacked[:rows] + stacked[rows : 2 * rows]) + stacked[2 * rows :]


def marks(index, count):
    rows = lax.broadcasted_iota(jnp.int32, (count, index.shape[1]), 0)
    return (rows == index).astype(F32).astype(BF16)


def times(left, right):
    return jnp.dot(left, right, preferred_element_type=F32)


def times_turned(left, right):
    return lax.dot_general(left, right, (((1,), (1,)), ((), ())), preferred_element_type=F32)


def halves(power):
    return power.bit_length() - 1


def face_rows_kernel(disp_ref, nodes_ref, rows_ref):
    components, layers, rows_y, cols_x = disp_ref.shape
    strips = layers * rows_y
    parts = thirds(disp_ref[...].reshape(components * strips, cols_x))
    face_count = nodes_ref.shape[1]
    folds = face_count // cols_x
    for corner in range(4):
        index = nodes_ref[corner : corner + 1, :]
        along_x = marks(index & (cols_x - 1), cols_x)
        strip = index >> halves(cols_x)
        found = summed(times(parts, along_x)).reshape(components, strips, face_count)
        numbers = lax.broadcasted_iota(jnp.int32, (strips, face_count), 0)
        values = jnp.sum(jnp.where((numbers == strip)[None], found, 0.0), axis=1)
        for fold in range(folds):
            for k in range(components):
                at = fold * 12 + k * 4 + corner
                rows_ref[at : at + 1, :] = values[k : k + 1, fold * cols_x : (fold + 1) * cols_x]


def looked_up(table, face, width):
    at = marks(face & (width - 1), width)
    both = summed(times(thirds(table), at))
    return jnp.where(face < width, both[:12], both[12:])


def pairs_kernel(
    all_ref, own_ref, mortar_ref, rank_ref, face_ref, count_ref, shape_ref, weight_ref, gap_ref,
    normal_ref, sent_ref, kept_ref,
):
    domains, folded, width = all_ref.shape
    pair_total = mortar_ref.shape[1]
    mortar, rank, face = mortar_ref[...], rank_ref[...], face_ref[...]
    mortar_rows = looked_up(own_ref[...], mortar, width)

    at = marks(face & (width - 1), width)
    step = min(domains, 8)

    def add_step(turn, total):
        block = all_ref[pl.ds(turn * step, step)].reshape(step * folded, width)
        found = summed(times(thirds(block), at)).reshape(step, folded, pair_total)
        for i in range(step):
            total = total + jnp.where(rank == turn * step + i, found[i], 0.0)
        return total

    both = jnp.zeros((folded, pair_total), F32)
    if domains == step:
        both = add_step(0, both)
    else:
        both = lax.fori_loop(0, domains // step, add_step, both)
    remote_rows = jnp.where(face < width, both[:12], both[12:])

    normal = normal_ref[...]
    gap = gap_ref[...]
    points = gap.shape[0]
    for node in range(4):
        across = sum(normal[k : k + 1] * remote_rows[k * 4 + node : k * 4 + node + 1] for k in range(3))
        gap = gap + shape_ref[node] * across
        across = sum(normal[k : k + 1] * mortar_rows[k * 4 + node : k * 4 + node + 1] for k in range(3))
        gap = gap - shape_ref[4 + node] * across
    live = lax.broadcasted_iota(jnp.int32, (points, pair_total), 0) < count_ref[...]
    pressure = jnp.where(live, weight_ref[...] * jnp.maximum(-gap, 0.0), 0.0)
    loads = [jnp.sum(pressure * shape_ref[i], axis=0, keepdims=True) for i in range(8)]

    ranks = lax.broadcasted_iota(jnp.int32, (domains, pair_total), 0)
    chosen = ranks == rank
    before = lax.broadcasted_iota(jnp.int32, (pair_total, pair_total), 0) < lax.broadcasted_iota(
        jnp.int32, (pair_total, pair_total), 1
    )
    earlier = times(chosen.astype(F32).astype(BF16), before.astype(F32).astype(BF16))
    slot = jnp.sum(jnp.where(chosen, earlier, 0.0), axis=0, keepdims=True).astype(jnp.int32)
    place = marks(slot, LANES)

    words = jnp.concatenate([normal] + loads[:4] + [face.astype(F32)], axis=0)
    parts = thirds(words).astype(F32)

    def send_step(turn):
        picked = [jnp.where(rank == turn * step + i, parts, 0.0) for i in range(step)]
        stacked = jnp.concatenate(picked, axis=0).astype(BF16)
        placed = times_turned(stacked, place).reshape(step, 3, WORDS, LANES)
        sent_ref[pl.ds(turn * step, step)] = (placed[:, 0] + placed[:, 1]) + placed[:, 2]

    if domains == step:
        send_step(0)
    else:
        pl.loop(0, domains // step)(send_step)
    kept_ref[...] = jnp.concatenate([-normal] + loads[4:] + [mortar.astype(F32)], axis=0)


def face_forces(words, face_count):
    loads = words[3:7]
    forces = jnp.concatenate([words[k : k + 1] * loads for k in range(3)], axis=0)
    at = marks(words[7:8].astype(jnp.int32), face_count)
    return summed(times_turned(thirds(forces), at))


def mortar_kernel(kept_ref, faces_ref):
    faces_ref[...] = face_forces(kept_ref[...], faces_ref.shape[1])


def nodes_kernel(capacity, got_ref, faces_ref, nodes_ref, internal_ref, mass_ref, out_ref):
    domains = got_ref.shape[0]
    components, layers, rows_y, cols_x = out_ref.shape
    strips = layers * rows_y
    face_count = faces_ref.shape[1]
    group = LANES // capacity
    tiles = []
    for start in range(0, domains, group):
        tile = got_ref[start]
        for i in range(1, group):
            tile = tile + pltpu.roll(got_ref[start + i], i * capacity, 1)
        tiles.append(tile)
    words = jnp.concatenate(tiles, axis=1)
    forces = faces_ref[...] + face_forces(words, face_count)
    total = jnp.zeros((3 * components * strips, cols_x), F32)
    parts = thirds(forces).astype(F32)
    numbers = lax.broadcasted_iota(jnp.int32, (strips, face_count), 0)
    for corner in range(4):
        index = nodes_ref[corner : corner + 1, :]
        along_x = marks(index & (cols_x - 1), cols_x)
        strip = numbers == (index >> halves(cols_x))
        spread = []
        for part in range(3):
            for k in range(components):
                at = part * 12 + k * 4 + corner
                spread.append(jnp.where(strip, parts[at : at + 1], 0.0).astype(BF16))
        total = total + times_turned(jnp.concatenate(spread, axis=0), along_x)
    contact = summed(total).reshape(components, layers, rows_y, cols_x)
    out_ref[...] = (internal_ref[...] + contact) / mass_ref[...][None]


def internal_kernel(disp_ref, above_ref, below_ref, modulus_ref, stiffness_ref, out_ref):
    components, layers, rows_y, cols_x = disp_ref.shape
    group = 8
    dofs = 8 * components
    half = dofs // 2

    row = lax.broadcasted_iota(jnp.int32, (dofs * group, dofs), 0) >> halves(group)
    upper = (row >= half).astype(jnp.int32)
    inner = row - half * upper
    dof = (inner >> 2) * 8 + upper * 4 + (inner & 3)
    pick = (dof == lax.broadcasted_iota(jnp.int32, (dofs * group, dofs), 1)).astype(F32)
    tall = jnp.dot(pick, stiffness_ref[...], precision=lax.Precision.HIGHEST)
    wide = lax.dot_general(
        tall, pick, (((1,), (1,)), ((), ())), precision=lax.Precision.HIGHEST,
        preferred_element_type=F32,
    )
    size = dofs * group
    diagonal = (lax.broadcasted_iota(jnp.int32, (size, size), 0) & (group - 1)) == (
        lax.broadcasted_iota(jnp.int32, (size, size), 1) & (group - 1)
    )
    blocks = jnp.where(diagonal, wide, 0.0)

    def shifted(layer):
        views = []
        for k in range(components):
            for b in range(2):
                moved = layer[k] if b == 0 else pltpu.roll(layer[k], rows_y - 1, 0)
                views.append(moved)
                views.append(pltpu.roll(moved, cols_x - 1, 1))
        return views

    views = [shifted(below_ref)]
    for layer in range(layers):
        views.append(shifted([disp_ref[k, layer] for k in range(components)]))
    views.append(shifted(above_ref))
    inside = (lax.broadcasted_iota(jnp.int32, (rows_y, cols_x), 0) < rows_y - 1) & (
        lax.broadcasted_iota(jnp.int32, (rows_y, cols_x), 1) < cols_x - 1
    )
    scales = [below_ref[components]] + [modulus_ref[layer] for layer in range(layers)]
    scales = [jnp.where(inside, scale, 0.0) for scale in scales]

    lower, higher = [], []
    for e in range(layers + 1):
        matrix = blocks
        if e == 0:
            matrix = blocks[half * group :]
        elif e == layers:
            matrix = blocks[: half * group]
        strips = []
        for y in range(0, rows_y, group):
            stacked = jnp.concatenate(
                [view[y : y + group] for view in views[e] + views[e + 1]], axis=0
            )
            force = jnp.dot(matrix, stacked, precision=lax.Precision.HIGHEST)
            force = force.reshape(-1, group, cols_x) * scales[e][y : y + group][None]
            strips.append(force)
        forces = jnp.concatenate(strips, axis=1)
        if e < layers:
            higher.append(forces[-half:])
        if e > 0:
            lower.append(forces[:half])
    for layer in range(layers):
        nodal = lower[layer] + higher[layer]
        for k in range(components):
            straight, crossed = [
                nodal[k * 4 + c] + pltpu.roll(nodal[k * 4 + 2 + c], 1, 0) for c in range(2)
            ]
            out_ref[k, layer] = -(straight + pltpu.roll(crossed, 1, 1))


def on_core(kernel, outs, flops, moved):
    return pl.pallas_call(
        kernel,
        out_shape=outs,
        compiler_params=pltpu.CompilerParams(vmem_limit_bytes=48 * 1024 * 1024),
        cost_estimate=pl.CostEstimate(flops=flops, bytes_accessed=moved, transcendentals=0),
    )


def shards(
    displacement,
    modulus,
    node_mass,
    stiffness,
    face_nodes,
    pair_mortar,
    pair_rank,
    pair_face,
    pair_count,
    pair_shape,
    pair_weight,
    pair_gap,
    pair_normal,
):
    components, layers, rows_y, cols_x = displacement.shape
    face_count = face_nodes.shape[1]
    pair_total = pair_mortar.shape[0]
    domains = lax.axis_size("dom")
    capacity = max(2, 2 * pair_total // domains)
    nodes = layers * rows_y * cols_x

    rows_shape = jax.ShapeDtypeStruct((12 * face_count // cols_x, cols_x), F32)
    own_rows = on_core(face_rows_kernel, rows_shape, 600_000_000, 400_000)(displacement, face_nodes)
    all_rows = lax.all_gather(own_rows, "dom")

    above = passed_along(displacement[:, 0], ("dom", "sub"), -1)
    below = passed_along(
        jnp.concatenate([displacement[:, -1], modulus[-1:]], axis=0), ("dom", "sub"), 1
    )

    line = (1, pair_total)
    sent, kept = on_core(
        pairs_kernel,
        [
            jax.ShapeDtypeStruct((domains, WORDS, LANES), F32),
            jax.ShapeDtypeStruct((WORDS, pair_total), F32),
        ],
        200_000_000,
        800_000,
    )(
        all_rows,
        own_rows,
        pair_mortar.reshape(line),
        pair_rank.reshape(line),
        pair_face.reshape(line),
        pair_count.reshape(line),
        pair_shape,
        pair_weight,
        pair_gap,
        pair_normal,
    )
    got = lax.all_to_all(sent, "dom", split_axis=0, concat_axis=0, tiled=True)

    internal = on_core(
        internal_kernel, jax.ShapeDtypeStruct(displacement.shape, F32), 3_000_000_000, 700_000
    )(displacement, above, below, modulus, stiffness)
    faces = on_core(
        mortar_kernel, jax.ShapeDtypeStruct((12, face_count), F32), 10_000_000, 30_000
    )(kept)

    def last(*refs):
        nodes_kernel(capacity, *refs)

    return on_core(
        last, jax.ShapeDtypeStruct(displacement.shape, F32), 600_000_000, 900_000
    )(got, faces, face_nodes, internal, node_mass)


def solution(mesh):
    placed = (
        P(None, ("runs", "dom", "sub"), None, None),
        P(("runs", "dom", "sub"), None, None),
        P(("runs", "dom", "sub"), None, None),
        P(),
        P(None, ("runs", "dom", "sub")),
        P(("runs", "dom", "sub")),
        P(("runs", "dom", "sub"), None),
        P(("runs", "dom", "sub")),
        P(("runs", "dom", "sub")),
        P(None, None, ("runs", "dom", "sub")),
        P(None, ("runs", "dom", "sub")),
        P(None, ("runs", "dom", "sub")),
        P(None, ("runs", "dom", "sub")),
    )
    return jax.shard_map(
        shards,
        mesh=mesh,
        in_specs=placed,
        out_specs=P(None, ("runs", "dom", "sub"), None, None),
        check_vma=False,
    )
```

time: 106 us -> 56.8 us (0.54)
  the two profiles are of different devices: /device:TPU:1 before, /device:TPU:0 now
where the time goes in v1:
time: 56.8 us; the launch traced here: 56.4 us
  blocking collectives  35.5 us (62%)
  starting transfers between devices  8.48 us (15%)
  Pallas kernels  6.32 us (11%)
  waiting for transfers between devices  3.67 us (6%)
  local copies, waits for them, and re-layouts  2.18 us (4%)
    all_gather x1, blocking collectives, shards(): all_rows = lax.all_gather(own_rows, 'dom')  35.5 us
    all_to_all x1, starting transfers between devices, shards(): got = lax.all_to_all(sent, 'dom', split_axis=0, concat_axis=0, tiled=True)  4.57 us
    ppermute x2, starting transfers between devices, passed_along(): return lax.ppermute(block, axis, route)  3.92 us
    all_to_all x1, waiting for transfers between devices, shards(): got = lax.all_to_all(sent, 'dom', split_axis=0, concat_axis=0, tiled=True)  3.66 us
    pallas_call x1, Pallas kernels, shards(): on_core(internal_kernel, jax.ShapeDtypeStruct(displacement.shape, F32), 3...  2.31 us
    pallas_call x1, Pallas kernels, shards(): on_core(last, jax.ShapeDtypeStruct(displacement.shape, F32), 600000000, 9...  1.8 us
    unnamed x27, local copies, waits for them, and re-layouts  1.22 us
    pallas_call x1, Pallas kernels, shards(): on_core(pairs_kernel, [jax.ShapeDtypeStruct((domains, WORDS, LANES), F32)...  1.18 us
  transfers between devices with their start and end apart: 3, of which 1 were waited for; matrix products, arithmetic and copies ran while one was open for 0% of the time, Pallas kernels for 8%

profile of v1, /device:TPU:0, one launch (start us, length us, event | category | flops | bytes accessed | tf_op | source)
XLA Modules:
  0.0 56.4 jit_solution(17663618780250156493)
XLA Ops:
  0.0 1.0 %slice_bitcast_fusion = (f32[3,32,256]{2,1,0:T(8,128)S(1)}, f32[3,32,256]{2,1,0:T(8,128)S(1)}) fusion(f32[3,2,32,256]{3,2,1,0:T(8,128)} %disp_ref.3), kind=kLoop, calls=%fused_computation.1 | loop fusion | bytes 393216 | tf_op jit(solution)/shard_map/squeeze | solution.py:287
  1.0 0.0 copy-start
  1.0 0.0 copy-start.6
  1.0 2.5 %collective-permute-start.1 = (f32[4,32,256]{2,1,0:T(8,128)S(1)}, f32[4,32,256]{2,1,0:T(8,128)S(1)}, u32[]{:S(2)}, u32[]{:S(2)}) collective-permute-start(f32[4,32,256]{2,1,0:T(8,128)S(1)} %pad_maximum_fusion), channel_id=1, source_target_pairs={{0,1},{1,2},{2,3},{3,4},{4,5},{5,6},{6,7},{7,8},{8,9},{9,10},{10,1... | collective-permute-start | bytes 393224 | tf_op jit(solution)/shard_map/ppermute | solution.py:17
  3.5 0.0 copy-start.12
  3.5 1.4 %collective-permute-start = (f32[3,32,256]{2,1,0:T(8,128)S(1)}, f32[3,32,256]{2,1,0:T(8,128)S(1)}, u32[]{:S(2)}, u32[]{:S(2)}) collective-permute-start(f32[3,32,256]{2,1,0:T(8,128)S(1)} %get-tuple-element.10), channel_id=1, source_target_pairs={{1,0},{2,1},{3,2},{4,3},{5,4},{6,5},{7,6},{8,7},{9,8},{10,9},{11,1... | collective-permute-start | bytes 294920 | tf_op jit(solution)/shard_map/ppermute | solution.py:17
  5.0 0.8 %shard_map.127.own_ref = f32[24,256]{1,0:T(8,128)S(1)} custom-call(f32[3,2,32,256]{3,2,1,0:T(8,128)S(1)} %copy-done, s32[4,512]{1,0:T(4,128)S(1)} %copy-done.6), custom_call_target="tpu_custom_call" | custom-call | flops 600000000 | bytes 400000 | tf_op jit(solution)/shard_map/pallas_call | solution.py:282
  5.8 0.1 copy.14.shape_ref
  5.9 0.0 copy-start.3
  5.9 0.0 copy-start.4
  5.9 0.0 copy-start.9
  5.9 0.0 copy-start.10
  5.9 0.0 copy-start.11
  6.0 35.5 %all-gather = f32[192,256]{1,0:T(8,128)S(1)} all-gather(f32[24,256]{1,0:T(8,128)S(1)} %shard_map.127.own_ref), channel_id=2, replica_groups=mesh['runs'=2,'dom'=8,'sub'=2] {'dom'}, dimensions={0}, use_global_device_ids=true | all-gather | bytes 221184 | tf_op jit(solution)/shard_map/all_gather | solution.py:283
  41.5 0.6 %copy-done.7 = f32[3,256]{1,0:T(4,128)S(1)} copy-done((f32[3,256]{1,0:T(4,128)S(1)}, f32[3,256]{1,0:T(4,128)}, u32[]{:S(2)}) %copy-start.7) | copy-done | bytes 3096
  42.1 0.0 copy-done.8
  42.1 1.2 %shard_map.128 = (f32[8,8,128]{2,1,0:T(8,128)}, f32[8,256]{1,0:T(8,128)S(1)}) custom-call(f32[8,24,256]{2,1,0:T(8,128)S(1)} %bitcast.13, f32[24,256]{1,0:T(8,128)S(1)} %shard_map.127.own_ref, s32[1,256]{1,0:T(1,128)S(1)} %bitcast.14, s32[1,256]{1,0:T(1,128)S(1)} %bitcast.15, s32[1,256]{1,0:T(1,128)S(1)} %bitcast.16, s32[1,256]{1,0:T(1,128)S(1)} %bitcast.17, ...), custom_call_target="tpu_custom_call" | custom-call | flops 200000000 | bytes 800000 | tf_op jit(solution)/shard_map/pallas_call | solution.py:291
  43.3 4.6 %all-to-all-start = ((f32[8,8,128]{2,1,0:T(8,128)}), f32[8,8,128]{2,1,0:T(8,128)S(1)}, u32[]{:S(2)}, u32[]{:S(2)}) async-start(f32[8,8,128]{2,1,0:T(8,128)} %get-tuple-element.7), calls=%async_computation | async-start | bytes 65536 | tf_op jit(solution)/shard_map/all_to_all | solution.py:311
  47.9 0.2 shard_map.129.refs_1_
  48.1 0.0 copy-start.2
  48.2 0.4 copy-done.5
  48.6 2.3 %shard_map.130.refs_3_ = f32[3,2,32,256]{3,2,1,0:T(8,128)S(1)} custom-call(f32[3,2,32,256]{3,2,1,0:T(8,128)S(1)} %copy-done, f32[3,32,256]{2,1,0:T(8,128)S(1)} %collective-permute-done.above_ref, f32[4,32,256]{2,1,0:T(8,128)S(1)} %collective-permute-done.1.below_ref, f32[2,32,256]{2,1,0:T(8,128)S(1)} %copy-done.1, f32[24,24]{1,0:T(8,128)S(1)} %copy-done.5), custom_call_target="tpu_custom_call" | custom-call | flops 3000000000 | bytes 700000 | tf_op jit(solution)/shard_map/pallas_call | solution.py:313
  50.9 3.7 %all-to-all-done.refs_0_ = f32[8,8,128]{2,1,0:T(8,128)S(1)} async-done(((f32[8,8,128]{2,1,0:T(8,128)}), f32[8,8,128]{2,1,0:T(8,128)S(1)}, u32[]{:S(2)}, u32[]{:S(2)}) %all-to-all-start) | async-done | bytes 32800 | tf_op jit(solution)/shard_map/all_to_all | solution.py:311
  54.6 1.8 %shard_map.131 = f32[3,2,32,256]{3,2,1,0:T(8,128)} custom-call(f32[8,8,128]{2,1,0:T(8,128)S(1)} %all-to-all-done.refs_0_, f32[12,512]{1,0:T(8,128)S(1)} %shard_map.129.refs_1_, s32[4,512]{1,0:T(4,128)S(1)} %copy-done.6, f32[3,2,32,256]{3,2,1,0:T(8,128)S(1)} %shard_map.130.refs_3_, f32[2,32,256]{2,1,0:T(8,128)S(1)} %copy-done.2), custom_call_target="tpu_custom_call" | custom-call | flops 600000000 | bytes 900000 | tf_op jit(solution)/shard_map/pallas_call | solution.py:323
  (19 shorter events, 0.0 us)
Async XLA Ops:
  0.0 1.0 %slice-start = ((f32[2,32,256]{2,1,0:T(8,128)}), f32[1,32,256]{2,1,0:T(8,128)S(1)}, s32[]{:S(2)}) async-start(f32[2,32,256]{2,1,0:T(8,128)} %modulus_ref.1), calls=%async_computation.1 | async-start | bytes 65536 | tf_op jit(solution)/shard_map/slice | solution.py:287
  1.0 4.0 %copy-start = (f32[3,2,32,256]{3,2,1,0:T(8,128)S(1)}, f32[3,2,32,256]{3,2,1,0:T(8,128)}, u32[]{:S(2)}) copy-start(f32[3,2,32,256]{3,2,1,0:T(8,128)} %disp_ref.3) | copy-start | bytes 589828
  1.0 4.0 %copy-start.6 = (s32[4,512]{1,0:T(4,128)S(1)}, s32[4,512]{1,0:T(4,128)}, u32[]{:S(2)}) copy-start(s32[4,512]{1,0:T(4,128)} %refs_2_.1) | copy-start | bytes 24580
  1.0 47.1 %collective-permute-start.1 = (f32[4,32,256]{2,1,0:T(8,128)S(1)}, f32[4,32,256]{2,1,0:T(8,128)S(1)}, u32[]{:S(2)}, u32[]{:S(2)}) collective-permute-start(f32[4,32,256]{2,1,0:T(8,128)S(1)} %pad_maximum_fusion), channel_id=1, source_target_pairs={{0,1},{1,2},{2,3},{3,4},{4,5},{5,6},{6,7},{7,8},{8,9},{9,10},{10,1... | collective-permute-start | bytes 393224 | tf_op jit(solution)/shard_map/ppermute | solution.py:17
  3.5 2.3 %copy-start.12 = (f32[8,25,256]{2,0,1:T(8,128)S(1)}, f32[8,25,256]{2,0,1:T(8,128)}, u32[]{:S(2)}) copy-start(f32[8,25,256]{2,0,1:T(8,128)} %param.22) | copy-start | bytes 614404
  3.5 44.6 %collective-permute-start = (f32[3,32,256]{2,1,0:T(8,128)S(1)}, f32[3,32,256]{2,1,0:T(8,128)S(1)}, u32[]{:S(2)}, u32[]{:S(2)}) collective-permute-start(f32[3,32,256]{2,1,0:T(8,128)S(1)} %get-tuple-element.10), channel_id=1, source_target_pairs={{1,0},{2,1},{3,2},{4,3},{5,4},{6,5},{7,6},{8,7},{9,8},{10,9},{11,1... | collective-permute-start | bytes 294920 | tf_op jit(solution)/shard_map/ppermute | solution.py:17
  5.9 35.5 %copy-start.3 = (f32[25,256]{1,0:T(8,128)S(1)}, f32[25,256]{1,0:T(8,128)}, u32[]{:S(2)}) copy-start(f32[25,256]{1,0:T(8,128)} %weight_ref.1) | copy-start | bytes 76804
  5.9 35.5 %copy-start.4 = (f32[25,256]{1,0:T(8,128)S(1)}, f32[25,256]{1,0:T(8,128)}, u32[]{:S(2)}) copy-start(f32[25,256]{1,0:T(8,128)} %gap_ref.1) | copy-start | bytes 76804
  5.9 35.5 %copy-start.9 = (s32[256,1]{0,1:T(1,128)S(1)}, s32[256,1]{0,1:T(1,128)}, u32[]{:S(2)}) copy-start(s32[256,1]{0,1:T(1,128)} %param.19) | copy-start | bytes 3076
  5.9 35.5 %copy-start.10 = (s32[256]{0:T(256)S(1)}, s32[256]{0:T(256)}, u32[]{:S(2)}) copy-start(s32[256]{0:T(256)} %param.20) | copy-start | bytes 3076
  5.9 35.5 %copy-start.11 = (s32[256]{0:T(256)S(1)}, s32[256]{0:T(256)}, u32[]{:S(2)}) copy-start(s32[256]{0:T(256)} %param.21) | copy-start | bytes 3076
  41.4 0.7 %copy-start.7 = (f32[3,256]{1,0:T(4,128)S(1)}, f32[3,256]{1,0:T(4,128)}, u32[]{:S(2)}) copy-start(f32[3,256]{1,0:T(4,128)} %normal_ref.1) | copy-start | bytes 9220
  41.4 0.7 %copy-start.8 = (s32[256]{0:T(256)S(1)}, s32[256]{0:T(256)}, u32[]{:S(2)}) copy-start(s32[256]{0:T(256)} %param.18) | copy-start | bytes 3076
  43.3 4.8 %copy-start.1 = (f32[2,32,256]{2,1,0:T(8,128)S(1)}, f32[2,32,256]{2,1,0:T(8,128)}, u32[]{:S(2)}) copy-start(f32[2,32,256]{2,1,0:T(8,128)} %modulus_ref.1) | copy-start | bytes 196612
  43.3 11.3 %all-to-all-start = ((f32[8,8,128]{2,1,0:T(8,128)}), f32[8,8,128]{2,1,0:T(8,128)S(1)}, u32[]{:S(2)}, u32[]{:S(2)}) async-start(f32[8,8,128]{2,1,0:T(8,128)} %get-tuple-element.7), calls=%async_computation | async-start | bytes 65536 | tf_op jit(solution)/shard_map/all_to_all | solution.py:311
  47.9 0.7 %copy-start.5 = (f32[24,24]{1,0:T(8,128)S(1)}, f32[24,24]{1,0:T(8,128)}, u32[]{:S(2)}) copy-start(f32[24,24]{1,0:T(8,128)} %stiffness_ref.1) | copy-start | bytes 6916
  48.1 6.5 %copy-start.2 = (f32[2,32,256]{2,1,0:T(8,128)S(1)}, f32[2,32,256]{2,1,0:T(8,128)}, u32[]{:S(2)}) copy-start(f32[2,32,256]{2,1,0:T(8,128)} %refs_4_.1) | copy-start | bytes 196612

commit v2 on v1

--- a/solution.py
+++ b/solution.py
@@ -47,7 +47,10 @@
     return power.bit_length() - 1
 
 
-def face_rows_kernel(disp_ref, nodes_ref, rows_ref):
+def face_rows_kernel(disp_ref, nodes_ref, modulus_ref, rows_ref, copies_ref, down_ref, up_ref):
+    down_ref[...] = disp_ref[:, 0]
+    up_ref[: disp_ref.shape[0]] = disp_ref[:, disp_ref.shape[1] - 1]
+    up_ref[disp_ref.shape[0]] = modulus_ref[disp_ref.shape[1] - 1]
     components, layers, rows_y, cols_x = disp_ref.shape
     strips = layers * rows_y
     parts = thirds(disp_ref[...].reshape(components * strips, cols_x))
@@ -64,6 +67,12 @@
             for k in range(components):
                 at = fold * 12 + k * 4 + corner
                 rows_ref[at : at + 1, :] = values[k : k + 1, fold * cols_x : (fold + 1) * cols_x]
+    rows = rows_ref[...]
+
+    def copy(i):
+        copies_ref[i] = rows
+
+    pl.loop(0, copies_ref.shape[0])(copy)
 
 
 def looked_up(table, face, width):
@@ -276,16 +285,22 @@
     pair_total = pair_mortar.shape[0]
     domains = lax.axis_size("dom")
     capacity = max(2, 2 * pair_total // domains)
-    nodes = layers * rows_y * cols_x
-
-    rows_shape = jax.ShapeDtypeStruct((12 * face_count // cols_x, cols_x), F32)
-    own_rows = on_core(face_rows_kernel, rows_shape, 600_000_000, 400_000)(displacement, face_nodes)
-    all_rows = lax.all_gather(own_rows, "dom")
-
-    above = passed_along(displacement[:, 0], ("dom", "sub"), -1)
-    below = passed_along(
-        jnp.concatenate([displacement[:, -1], modulus[-1:]], axis=0), ("dom", "sub"), 1
-    )
+
+    rows_shape = (12 * face_count // cols_x, cols_x)
+    own_rows, copies, down, up = on_core(
+        face_rows_kernel,
+        [
+            jax.ShapeDtypeStruct(rows_shape, F32),
+            jax.ShapeDtypeStruct((domains,) + rows_shape, F32),
+            jax.ShapeDtypeStruct((components, rows_y, cols_x), F32),
+            jax.ShapeDtypeStruct((components + 1, rows_y, cols_x), F32),
+        ],
+        600_000_000,
+        900_000,
+    )(displacement, face_nodes, modulus)
+    all_rows = lax.all_to_all(copies, "dom", split_axis=0, concat_axis=0, tiled=True)
+    above = passed_along(down, ("dom", "sub"), -1)
+    below = passed_along(up, ("dom", "sub"), 1)
 
     line = (1, pair_total)
     sent, kept = on_core(

time: 56.8 us -> 34.2 us (0.60)
  blocking collectives: 35.5 us -> 0 us
  starting transfers between devices: 8.48 us -> 14 us
  waiting for transfers between devices: 3.67 us -> 9.11 us
  local copies, waits for them, and re-layouts: 2.18 us -> 3.24 us
  Pallas kernels: 6.32 us -> 7.07 us
    all_gather x1 -> x0, blocking collectives: 35.5 us -> none  [shards(): all_rows = lax.all_gather(own_rows, 'dom')]
    all_to_all x0 -> x1, starting transfers between devices: none -> 7.38 us  [shards(): lax.all_to_all(copies, 'dom', split_axis=0, concat_axis=0, tiled=True)]
    all_to_all x0 -> x1, waiting for transfers between devices: none -> 5.04 us  [shards(): lax.all_to_all(copies, 'dom', split_axis=0, concat_axis=0, tiled=True)]
    unnamed x27 -> x33, local copies, waits for them, and re-layouts: 1.22 us -> 3.24 us
    ppermute x2, starting transfers between devices: 3.92 us -> 2.75 us  [passed_along(): return lax.ppermute(block, axis, route)]
    squeeze x1 -> x0, local copies, waits for them, and re-layouts: 0.96 us -> none  [shards(): displacement[:, -1]]
    pallas_call x1, Pallas kernels: 0.82 us -> 1.55 us  [shards(): on_core(face_rows_kernel, [jax.ShapeDtypeStruct(rows_shape, F32), jax.Sha...]
    all_to_all x1, starting transfers between devices: 4.57 us -> 3.91 us  [shards(): got = lax.all_to_all(sent, 'dom', split_axis=0, concat_axis=0, tiled=True)]
  transfers between devices with their start and end apart: 3 -> 4, of which waited for: 1 -> 2; matrix products, arithmetic and copies ran while one was open for 0% -> 0% of each run, Pallas kernels for 8% -> 11%
where the time goes in v2:
time: 34.2 us; the launch traced here: 33.6 us
  starting transfers between devices  14 us (41%)
  waiting for transfers between devices  9.11 us (27%)
  Pallas kernels  7.07 us (21%)
  local copies, waits for them, and re-layouts  3.24 us (9%)
    all_to_all x1, starting transfers between devices, shards(): lax.all_to_all(copies, 'dom', split_axis=0, concat_axis=0, tiled=True)  7.38 us
    all_to_all x1, waiting for transfers between devices, shards(): lax.all_to_all(copies, 'dom', split_axis=0, concat_axis=0, tiled=True)  5.04 us
    all_to_all x1, waiting for transfers between devices, shards(): got = lax.all_to_all(sent, 'dom', split_axis=0, concat_axis=0, tiled=True)  4.06 us
    all_to_all x1, starting transfers between devices, shards(): got = lax.all_to_all(sent, 'dom', split_axis=0, concat_axis=0, tiled=True)  3.91 us
    unnamed x33, local copies, waits for them, and re-layouts  3.24 us
    ppermute x2, starting transfers between devices, passed_along(): return lax.ppermute(block, axis, route)  2.75 us
    pallas_call x1, Pallas kernels, shards(): on_core(internal_kernel, jax.ShapeDtypeStruct(displacement.shape, F32), 3...  2.32 us
    pallas_call x1, Pallas kernels, shards(): on_core(last, jax.ShapeDtypeStruct(displacement.shape, F32), 600000000, 9...  1.8 us
  transfers between devices with their start and end apart: 4, of which 2 were waited for; matrix products, arithmetic and copies ran while one was open for 0% of the time, Pallas kernels for 11%

profile of v2, /device:TPU:0, one launch (start us, length us, event | category | flops | bytes accessed | tf_op | source)
XLA Modules:
  0.0 33.6 jit_solution(16888545891732303496)
XLA Ops:
  0.0 0.9 %copy-done = f32[3,2,32,256]{3,2,1,0:T(8,128)S(1)} copy-done((f32[3,2,32,256]{3,2,1,0:T(8,128)S(1)}, f32[3,2,32,256]{3,2,1,0:T(8,128)}, u32[]{:S(2)}) %copy-start) | copy-done | bytes 196632
  0.9 0.8 %copy-done.2 = f32[2,32,256]{2,1,0:T(8,128)S(1)} copy-done((f32[2,32,256]{2,1,0:T(8,128)S(1)}, f32[2,32,256]{2,1,0:T(8,128)}, u32[]{:S(2)}) %copy-start.2) | copy-done | bytes 65560
  1.8 0.7 %copy-done.8 = s32[4,512]{1,0:T(4,128)S(1)} copy-done((s32[4,512]{1,0:T(4,128)S(1)}, s32[4,512]{1,0:T(4,128)}, u32[]{:S(2)}) %copy-start.8) | copy-done | bytes 8216
  2.5 1.5 %shard_map.127 = (f32[24,256]{1,0:T(8,128)S(1)}, f32[8,24,256]{2,1,0:T(8,128)}, f32[3,32,256]{2,1,0:T(8,128)S(1)}, f32[4,32,256]{2,1,0:T(8,128)S(1)}) custom-call(f32[3,2,32,256]{3,2,1,0:T(8,128)S(1)} %copy-done, s32[4,512]{1,0:T(4,128)S(1)} %copy-done.8, f32[2,32,256]{2,1,0:T(8,128)S(1)} %copy-done.2), custom_call_target="tpu_custom_call" | custom-call | flops 600000000 | bytes 900000 | tf_op jit(solution)/shard_map/pallas_call | solution.py:290
  4.0 7.4 %all-to-all-start = ((f32[8,24,256]{2,1,0:T(8,128)}), f32[8,24,256]{2,1,0:T(8,128)S(1)}, u32[]{:S(2)}, u32[]{:S(2)}) async-start(f32[8,24,256]{2,1,0:T(8,128)} %get-tuple-element.11), calls=%async_computation | async-start | bytes 393216 | tf_op jit(solution)/shard_map/all_to_all | solution.py:301
  11.4 1.5 %collective-permute-start.1 = (f32[4,32,256]{2,1,0:T(8,128)S(1)}, f32[4,32,256]{2,1,0:T(8,128)S(1)}, u32[]{:S(2)}, u32[]{:S(2)}) collective-permute-start(f32[4,32,256]{2,1,0:T(8,128)S(1)} %get-tuple-element.16), channel_id=1, source_target_pairs={{0,1},{1,2},{2,3},{3,4},{4,5},{5,6},{6,7},{7,8},{8,9},{9,10},{10,1... | collective-permute-start | bytes 393224 | tf_op jit(solution)/shard_map/ppermute | solution.py:17
  12.9 0.0 copy-start.5
  12.9 0.0 copy-start.6
  12.9 1.3 %collective-permute-start = (f32[3,32,256]{2,1,0:T(8,128)S(1)}, f32[3,32,256]{2,1,0:T(8,128)S(1)}, u32[]{:S(2)}, u32[]{:S(2)}) collective-permute-start(f32[3,32,256]{2,1,0:T(8,128)S(1)} %get-tuple-element.15), channel_id=1, source_target_pairs={{1,0},{2,1},{3,2},{4,3},{5,4},{6,5},{7,6},{8,7},{9,8},{10,9},{11,1... | collective-permute-start | bytes 294920 | tf_op jit(solution)/shard_map/ppermute | solution.py:17
  14.2 0.0 copy-start.12
  14.2 0.0 copy-start.13
  14.2 0.0 copy-start.14
  14.2 0.1 copy.14.shape_ref
  14.3 5.0 %all-to-all-done.all_ref = f32[8,24,256]{2,1,0:T(8,128)S(1)} async-done(((f32[8,24,256]{2,1,0:T(8,128)}), f32[8,24,256]{2,1,0:T(8,128)S(1)}, u32[]{:S(2)}, u32[]{:S(2)}) %all-to-all-start) | async-done | bytes 196640 | tf_op jit(solution)/shard_map/all_to_all | solution.py:301
  19.4 0.6 %copy-done.10 = f32[3,256]{1,0:T(4,128)S(1)} copy-done((f32[3,256]{1,0:T(4,128)S(1)}, f32[3,256]{1,0:T(4,128)}, u32[]{:S(2)}) %copy-start.10) | copy-done | bytes 3096
  20.0 0.0 copy-done.11
  20.1 1.2 %shard_map.128 = (f32[8,8,128]{2,1,0:T(8,128)}, f32[8,256]{1,0:T(8,128)S(1)}) custom-call(f32[8,24,256]{2,1,0:T(8,128)S(1)} %all-to-all-done.all_ref, f32[24,256]{1,0:T(8,128)S(1)} %get-tuple-element.12.own_ref, s32[1,256]{1,0:T(1,128)S(1)} %bitcast.4, s32[1,256]{1,0:T(1,128)S(1)} %bitcast.5, s32[1,256]{1,0:T(1,128)S(1)} %bitcast.6, s32[1,256]{1,0:T(1,128)S(1)} %bitcast.7, ...), custom_call_target="tpu_custom_call" | custom-call | flops 200000000 | bytes 800000 | tf_op jit(solution)/shard_map/pallas_call | solution.py:306
  21.2 3.9 %all-to-all-start.1 = ((f32[8,8,128]{2,1,0:T(8,128)}), f32[8,8,128]{2,1,0:T(8,128)S(1)}, u32[]{:S(2)}, u32[]{:S(2)}) async-start(f32[8,8,128]{2,1,0:T(8,128)} %get-tuple-element.13), calls=%async_computation.1 | async-start | bytes 65536 | tf_op jit(solution)/shard_map/all_to_all | solution.py:326
  25.1 0.0 collective-permute-done.above_ref
  25.2 2.3 %shard_map.130.refs_3_ = f32[3,2,32,256]{3,2,1,0:T(8,128)S(1)} custom-call(f32[3,2,32,256]{3,2,1,0:T(8,128)S(1)} %copy-done.1, f32[3,32,256]{2,1,0:T(8,128)S(1)} %collective-permute-done.above_ref, f32[4,32,256]{2,1,0:T(8,128)S(1)} %collective-permute-done.1.below_ref, f32[2,32,256]{2,1,0:T(8,128)S(1)} %copy-done.3, f32[24,24]{1,0:T(8,128)S(1)} %copy-done.7), custom_call_target="tpu_custom_call" | custom-call | flops 3000000000 | bytes 700000 | tf_op jit(solution)/shard_map/pallas_call | solution.py:328
  27.5 0.0 copy-start.9
  27.5 0.2 shard_map.129.refs_1_
  27.8 4.1 %all-to-all-done.1.refs_0_ = f32[8,8,128]{2,1,0:T(8,128)S(1)} async-done(((f32[8,8,128]{2,1,0:T(8,128)}), f32[8,8,128]{2,1,0:T(8,128)S(1)}, u32[]{:S(2)}, u32[]{:S(2)}) %all-to-all-start.1) | async-done | bytes 32800 | tf_op jit(solution)/shard_map/all_to_all | solution.py:326
  31.8 1.8 %shard_map.131 = f32[3,2,32,256]{3,2,1,0:T(8,128)} custom-call(f32[8,8,128]{2,1,0:T(8,128)S(1)} %all-to-all-done.1.refs_0_, f32[12,512]{1,0:T(8,128)S(1)} %shard_map.129.refs_1_, s32[4,512]{1,0:T(4,128)S(1)} %copy-done.9, f32[3,2,32,256]{3,2,1,0:T(8,128)S(1)} %shard_map.130.refs_3_, f32[2,32,256]{2,1,0:T(8,128)S(1)} %copy-done.4), custom_call_target="tpu_custom_call" | custom-call | flops 600000000 | bytes 900000 | tf_op jit(solution)/shard_map/pallas_call | solution.py:338
  (22 shorter events, 0.0 us)
Async XLA Ops:
  0.0 0.9 %copy-start = (f32[3,2,32,256]{3,2,1,0:T(8,128)S(1)}, f32[3,2,32,256]{3,2,1,0:T(8,128)}, u32[]{:S(2)}) copy-start(f32[3,2,32,256]{3,2,1,0:T(8,128)} %disp_ref.3) | copy-start | bytes 589828
  0.9 0.8 %copy-start.2 = (f32[2,32,256]{2,1,0:T(8,128)S(1)}, f32[2,32,256]{2,1,0:T(8,128)}, u32[]{:S(2)}) copy-start(f32[2,32,256]{2,1,0:T(8,128)} %modulus_ref.3) | copy-start | bytes 196612
  1.8 0.7 %copy-start.8 = (s32[4,512]{1,0:T(4,128)S(1)}, s32[4,512]{1,0:T(4,128)}, u32[]{:S(2)}) copy-start(s32[4,512]{1,0:T(4,128)} %refs_2_.1) | copy-start | bytes 24580
  4.0 10.2 %copy-start.15 = (f32[8,25,256]{2,0,1:T(8,128)S(1)}, f32[8,25,256]{2,0,1:T(8,128)}, u32[]{:S(2)}) copy-start(f32[8,25,256]{2,0,1:T(8,128)} %param.22) | copy-start | bytes 614404
  4.0 15.3 %all-to-all-start = ((f32[8,24,256]{2,1,0:T(8,128)}), f32[8,24,256]{2,1,0:T(8,128)S(1)}, u32[]{:S(2)}, u32[]{:S(2)}) async-start(f32[8,24,256]{2,1,0:T(8,128)} %get-tuple-element.11), calls=%async_computation | async-start | bytes 393216 | tf_op jit(solution)/shard_map/all_to_all | solution.py:301
  11.4 13.8 %collective-permute-start.1 = (f32[4,32,256]{2,1,0:T(8,128)S(1)}, f32[4,32,256]{2,1,0:T(8,128)S(1)}, u32[]{:S(2)}, u32[]{:S(2)}) collective-permute-start(f32[4,32,256]{2,1,0:T(8,128)S(1)} %get-tuple-element.16), channel_id=1, source_target_pairs={{0,1},{1,2},{2,3},{3,4},{4,5},{5,6},{6,7},{7,8},{8,9},{9,10},{10,1... | collective-permute-start | bytes 393224 | tf_op jit(solution)/shard_map/ppermute | solution.py:17
  12.9 6.5 %copy-start.5 = (f32[25,256]{1,0:T(8,128)S(1)}, f32[25,256]{1,0:T(8,128)}, u32[]{:S(2)}) copy-start(f32[25,256]{1,0:T(8,128)} %weight_ref.1) | copy-start | bytes 76804
  12.9 6.5 %copy-start.6 = (f32[25,256]{1,0:T(8,128)S(1)}, f32[25,256]{1,0:T(8,128)}, u32[]{:S(2)}) copy-start(f32[25,256]{1,0:T(8,128)} %gap_ref.1) | copy-start | bytes 76804
  12.9 12.3 %collective-permute-start = (f32[3,32,256]{2,1,0:T(8,128)S(1)}, f32[3,32,256]{2,1,0:T(8,128)S(1)}, u32[]{:S(2)}, u32[]{:S(2)}) collective-permute-start(f32[3,32,256]{2,1,0:T(8,128)S(1)} %get-tuple-element.15), channel_id=1, source_target_pairs={{1,0},{2,1},{3,2},{4,3},{5,4},{6,5},{7,6},{8,7},{9,8},{10,9},{11,1... | collective-permute-start | bytes 294920 | tf_op jit(solution)/shard_map/ppermute | solution.py:17
  14.2 5.2 %copy-start.12 = (s32[256,1]{0,1:T(1,128)S(1)}, s32[256,1]{0,1:T(1,128)}, u32[]{:S(2)}) copy-start(s32[256,1]{0,1:T(1,128)} %param.19) | copy-start | bytes 3076
  14.2 5.2 %copy-start.13 = (s32[256]{0:T(256)S(1)}, s32[256]{0:T(256)}, u32[]{:S(2)}) copy-start(s32[256]{0:T(256)} %param.20) | copy-start | bytes 3076
  14.2 5.2 %copy-start.14 = (s32[256]{0:T(256)S(1)}, s32[256]{0:T(256)}, u32[]{:S(2)}) copy-start(s32[256]{0:T(256)} %param.21) | copy-start | bytes 3076
  19.4 0.7 %copy-start.10 = (f32[3,256]{1,0:T(4,128)S(1)}, f32[3,256]{1,0:T(4,128)}, u32[]{:S(2)}) copy-start(f32[3,256]{1,0:T(4,128)} %normal_ref.1) | copy-start | bytes 9220
  19.4 0.7 %copy-start.11 = (s32[256]{0:T(256)S(1)}, s32[256]{0:T(256)}, u32[]{:S(2)}) copy-start(s32[256]{0:T(256)} %param.18) | copy-start | bytes 3076
  20.0 5.1 %copy-start.1 = (f32[3,2,32,256]{3,2,1,0:T(8,128)S(1)}, f32[3,2,32,256]{3,2,1,0:T(8,128)}, u32[]{:S(2)}) copy-start(f32[3,2,32,256]{3,2,1,0:T(8,128)} %disp_ref.3) | copy-start | bytes 589828
  20.1 5.1 %copy-start.7 = (f32[24,24]{1,0:T(8,128)S(1)}, f32[24,24]{1,0:T(8,128)}, u32[]{:S(2)}) copy-start(f32[24,24]{1,0:T(8,128)} %stiffness_ref.1) | copy-start | bytes 6916
  21.2 4.0 %copy-start.3 = (f32[2,32,256]{2,1,0:T(8,128)S(1)}, f32[2,32,256]{2,1,0:T(8,128)}, u32[]{:S(2)}) copy-start(f32[2,32,256]{2,1,0:T(8,128)} %modulus_ref.3) | copy-start | bytes 196612
  21.2 10.6 %all-to-all-start.1 = ((f32[8,8,128]{2,1,0:T(8,128)}), f32[8,8,128]{2,1,0:T(8,128)S(1)}, u32[]{:S(2)}, u32[]{:S(2)}) async-start(f32[8,8,128]{2,1,0:T(8,128)} %get-tuple-element.13), calls=%async_computation.1 | async-start | bytes 65536 | tf_op jit(solution)/shard_map/all_to_all | solution.py:326
  25.1 6.7 %copy-start.4 = (f32[2,32,256]{2,1,0:T(8,128)S(1)}, f32[2,32,256]{2,1,0:T(8,128)}, u32[]{:S(2)}) copy-start(f32[2,32,256]{2,1,0:T(8,128)} %refs_4_.1) | copy-start | bytes 196612
  27.5 4.3 %copy-start.9 = (s32[4,512]{1,0:T(4,128)S(1)}, s32[4,512]{1,0:T(4,128)}, u32[]{:S(2)}) copy-start(s32[4,512]{1,0:T(4,128)} %refs_2_.1) | copy-start | bytes 24580

commit v3 on v1

--- a/solution.py
+++ b/solution.py
@@ -11,18 +11,16 @@
 WORDS = 8
 
 
-def passed_along(block, axis, distance):
-    devices = range(lax.axis_size(axis))
-    route = [(i - distance, i) for i in devices if i - distance in devices]
-    return lax.ppermute(block, axis, route)
+def terms_of(x, count):
+    terms = []
+    for _ in range(count):
+        terms.append(x.astype(BF16))
+        x = x - terms[-1].astype(F32)
+    return terms
 
 
 def thirds(x):
-    high = x.astype(BF16)
-    rest = x - high.astype(F32)
-    middle = rest.astype(BF16)
-    low = (rest - middle.astype(F32)).astype(BF16)
-    return jnp.concatenate([high, middle, low], axis=0)
+    return jnp.concatenate(terms_of(x, 3), axis=0)
 
 
 def summed(stacked):
@@ -47,23 +45,58 @@
     return power.bit_length() - 1
 
 
-def face_rows_kernel(disp_ref, nodes_ref, rows_ref):
+def face_rows_kernel(
+    passed, disp_ref, nodes_ref, modulus_ref, *refs
+):
+    ins, refs = refs[:passed], refs[passed:]
+    outs, refs = refs[:passed], refs[passed:]
+    rows_ref, copies_ref, inner_ref, outer_ref, disp, nodes, modulus, sems, copy_sems = refs
     components, layers, rows_y, cols_x = disp_ref.shape
+
+    def bring(number, source, target):
+        return pltpu.make_async_copy(source, target, sems.at[number])
+
+    loads = [
+        bring(0, nodes_ref, nodes),
+        bring(1, disp_ref, disp),
+        bring(2, modulus_ref, modulus),
+    ]
+    loads += [bring(3 + i, ins[i], outs[i]) for i in range(passed)]
+    for load in loads:
+        load.start()
+    loads[0].wait()
     strips = layers * rows_y
-    parts = thirds(disp_ref[...].reshape(components * strips, cols_x))
-    face_count = nodes_ref.shape[1]
+    face_count = nodes.shape[1]
     folds = face_count // cols_x
+    indices = [nodes[corner : corner + 1, :] for corner in range(4)]
+    along_x = [marks(index & (cols_x - 1), cols_x) for index in indices]
+    loads[1].wait()
+    parts = thirds(disp[...].reshape(components * strips, cols_x))
+    numbers = lax.broadcasted_iota(jnp.int32, (strips, face_count), 0)
     for corner in range(4):
-        index = nodes_ref[corner : corner + 1, :]
-        along_x = marks(index & (cols_x - 1), cols_x)
-        strip = index >> halves(cols_x)
-        found = summed(times(parts, along_x)).reshape(components, strips, face_count)
-        numbers = lax.broadcasted_iota(jnp.int32, (strips, face_count), 0)
+        strip = indices[corner] >> halves(cols_x)
+        found = summed(times(parts, along_x[corner])).reshape(components, strips, face_count)
         values = jnp.sum(jnp.where((numbers == strip)[None], found, 0.0), axis=1)
         for fold in range(folds):
             for k in range(components):
                 at = fold * 12 + k * 4 + corner
                 rows_ref[at : at + 1, :] = values[k : k + 1, fold * cols_x : (fold + 1) * cols_x]
+    copies = [
+        pltpu.make_async_copy(rows_ref, copies_ref.at[i], copy_sems.at[i])
+        for i in range(copies_ref.shape[0])
+    ]
+    for copy in copies:
+        copy.start()
+    loads[2].wait()
+    sub = lax.axis_index("sub")
+    for target, layer in ((inner_ref, (1 - sub) * (layers - 1)), (outer_ref, sub * (layers - 1))):
+        for k in range(components):
+            target[k] = disp[k, layer]
+        target[components] = modulus[layer]
+    for load in loads[3:]:
+        load.wait()
+    for copy in copies:
+        copy.wait()
 
 
 def looked_up(table, face, width):
@@ -103,12 +136,12 @@
     points = gap.shape[0]
     for node in range(4):
         across = sum(normal[k : k + 1] * remote_rows[k * 4 + node : k * 4 + node + 1] for k in range(3))
-        gap = gap + shape_ref[node] * across
+        gap = gap + shape_ref[:, node] * across
         across = sum(normal[k : k + 1] * mortar_rows[k * 4 + node : k * 4 + node + 1] for k in range(3))
-        gap = gap - shape_ref[4 + node] * across
+        gap = gap - shape_ref[:, 4 + node] * across
     live = lax.broadcasted_iota(jnp.int32, (points, pair_total), 0) < count_ref[...]
     pressure = jnp.where(live, weight_ref[...] * jnp.maximum(-gap, 0.0), 0.0)
-    loads = [jnp.sum(pressure * shape_ref[i], axis=0, keepdims=True) for i in range(8)]
+    loads = [jnp.sum(pressure * shape_ref[:, i], axis=0, keepdims=True) for i in range(8)]
 
     ranks = lax.broadcasted_iota(jnp.int32, (domains, pair_total), 0)
     chosen = ranks == rank
@@ -140,10 +173,6 @@
     forces = jnp.concatenate([words[k : k + 1] * loads for k in range(3)], axis=0)
     at = marks(words[7:8].astype(jnp.int32), face_count)
     return summed(times_turned(thirds(forces), at))
-
-
-def mortar_kernel(kept_ref, faces_ref):
-    faces_ref[...] = face_forces(kept_ref[...], faces_ref.shape[1])
 
 
 def nodes_kernel(capacity, got_ref, faces_ref, nodes_ref, internal_ref, mass_ref, out_ref):
@@ -160,24 +189,27 @@
         tiles.append(tile)
     words = jnp.concatenate(tiles, axis=1)
     forces = faces_ref[...] + face_forces(words, face_count)
-    total = jnp.zeros((3 * components * strips, cols_x), F32)
-    parts = thirds(forces).astype(F32)
+    total = jnp.zeros((2 * components * strips, cols_x), F32)
+    parts = [term.astype(F32) for term in terms_of(forces, 2)]
     numbers = lax.broadcasted_iota(jnp.int32, (strips, face_count), 0)
     for corner in range(4):
         index = nodes_ref[corner : corner + 1, :]
         along_x = marks(index & (cols_x - 1), cols_x)
         strip = numbers == (index >> halves(cols_x))
         spread = []
-        for part in range(3):
+        for part in parts:
             for k in range(components):
-                at = part * 12 + k * 4 + corner
-                spread.append(jnp.where(strip, parts[at : at + 1], 0.0).astype(BF16))
+                at = k * 4 + corner
+                spread.append(jnp.where(strip, part[at : at + 1], 0.0).astype(BF16))
         total = total + times_turned(jnp.concatenate(spread, axis=0), along_x)
-    contact = summed(total).reshape(components, layers, rows_y, cols_x)
+    half = components * strips
+    contact = (total[:half] + total[half:]).reshape(components, layers, rows_y, cols_x)
     out_ref[...] = (internal_ref[...] + contact) / mass_ref[...][None]
 
 
-def internal_kernel(disp_ref, above_ref, below_ref, modulus_ref, stiffness_ref, out_ref):
+def internal_kernel(
+    disp_ref, inner_ref, outer_ref, modulus_ref, stiffness_ref, kept_ref, out_ref, faces_ref
+):
     components, layers, rows_y, cols_x = disp_ref.shape
     group = 8
     dofs = 8 * components
@@ -187,17 +219,19 @@
     upper = (row >= half).astype(jnp.int32)
     inner = row - half * upper
     dof = (inner >> 2) * 8 + upper * 4 + (inner & 3)
-    pick = (dof == lax.broadcasted_iota(jnp.int32, (dofs * group, dofs), 1)).astype(F32)
-    tall = jnp.dot(pick, stiffness_ref[...], precision=lax.Precision.HIGHEST)
-    wide = lax.dot_general(
-        tall, pick, (((1,), (1,)), ((), ())), precision=lax.Precision.HIGHEST,
-        preferred_element_type=F32,
-    )
+    pick = (dof == lax.broadcasted_iota(jnp.int32, (dofs * group, dofs), 1)).astype(F32).astype(BF16)
     size = dofs * group
     diagonal = (lax.broadcasted_iota(jnp.int32, (size, size), 0) & (group - 1)) == (
         lax.broadcasted_iota(jnp.int32, (size, size), 1) & (group - 1)
     )
-    blocks = jnp.where(diagonal, wide, 0.0)
+    blocks = []
+    for term in terms_of(stiffness_ref[...], 2):
+        wide = times_turned(times(pick, term).astype(BF16), pick)
+        blocks.append(jnp.where(diagonal, wide, 0.0).astype(BF16))
+
+    sub = lax.axis_index("sub")
+    below_ref = [jnp.where(sub == 0, outer_ref[k], inner_ref[k]) for k in range(components + 1)]
+    above_ref = [jnp.where(sub == 0, inner_ref[k], outer_ref[k]) for k in range(components)]
 
     def shifted(layer):
         views = []
@@ -220,17 +254,17 @@
 
     lower, higher = [], []
     for e in range(layers + 1):
-        matrix = blocks
-        if e == 0:
-            matrix = blocks[half * group :]
-        elif e == layers:
-            matrix = blocks[: half * group]
+        kept = slice(half * group, None) if e == 0 else slice(0, half * group if e == layers else None)
+        both = jnp.concatenate([block[kept] for block in blocks], axis=0)
+        count = both.shape[0] // 2
         strips = []
         for y in range(0, rows_y, group):
             stacked = jnp.concatenate(
                 [view[y : y + group] for view in views[e] + views[e + 1]], axis=0
             )
-            force = jnp.dot(matrix, stacked, precision=lax.Precision.HIGHEST)
+            high, low = terms_of(stacked, 2)
+            leading = times(both, high)
+            force = leading[:count] + (leading[count:] + times(both[:count], low))
             force = force.reshape(-1, group, cols_x) * scales[e][y : y + group][None]
             strips.append(force)
         forces = jnp.concatenate(strips, axis=1)
@@ -245,15 +279,25 @@
                 nodal[k * 4 + c] + pltpu.roll(nodal[k * 4 + 2 + c], 1, 0) for c in range(2)
             ]
             out_ref[k, layer] = -(straight + pltpu.roll(crossed, 1, 1))
-
-
-def on_core(kernel, outs, flops, moved):
+    faces_ref[...] = face_forces(kept_ref[...], faces_ref.shape[1])
+
+
+def on_core(kernel, outs, flops, moved, **more):
     return pl.pallas_call(
         kernel,
         out_shape=outs,
         compiler_params=pltpu.CompilerParams(vmem_limit_bytes=48 * 1024 * 1024),
         cost_estimate=pl.CostEstimate(flops=flops, bytes_accessed=moved, transcendentals=0),
-    )
+        **more,
+    )
+
+
+def swapped(block, axis, first):
+    size = lax.axis_size(axis)
+    route = []
+    for i in range(first, size - 1, 2):
+        route += [(i, i + 1), (i + 1, i)]
+    return lax.ppermute(block, axis, route)
 
 
 def shards(
@@ -276,18 +320,52 @@
     pair_total = pair_mortar.shape[0]
     domains = lax.axis_size("dom")
     capacity = max(2, 2 * pair_total // domains)
-    nodes = layers * rows_y * cols_x
-
-    rows_shape = jax.ShapeDtypeStruct((12 * face_count // cols_x, cols_x), F32)
-    own_rows = on_core(face_rows_kernel, rows_shape, 600_000_000, 400_000)(displacement, face_nodes)
-    all_rows = lax.all_gather(own_rows, "dom")
-
-    above = passed_along(displacement[:, 0], ("dom", "sub"), -1)
-    below = passed_along(
-        jnp.concatenate([displacement[:, -1], modulus[-1:]], axis=0), ("dom", "sub"), 1
-    )
 
     line = (1, pair_total)
+    pairs = [
+        pair_mortar.reshape(line),
+        pair_rank.reshape(line),
+        pair_face.reshape(line),
+        pair_count.reshape(line),
+        jnp.swapaxes(pair_shape, 0, 1),
+        pair_weight,
+        pair_gap,
+        pair_normal,
+    ]
+
+    def first(*refs):
+        face_rows_kernel(len(pairs), *refs)
+
+    rows_shape = (12 * face_count // cols_x, cols_x)
+    edge = jax.ShapeDtypeStruct((components + 1, rows_y, cols_x), F32)
+    in_hbm = pl.BlockSpec(memory_space=pltpu.HBM)
+    in_vmem = pl.BlockSpec(memory_space=pltpu.VMEM)
+    held = [pltpu.with_memory_space_constraint(x, pltpu.HBM) for x in (displacement, face_nodes, modulus, *pairs)]
+    *pairs, own_rows, copies, inner, outer = on_core(
+        first,
+        [jax.ShapeDtypeStruct(x.shape, x.dtype) for x in pairs]
+        + [
+            jax.ShapeDtypeStruct(rows_shape, F32),
+            jax.ShapeDtypeStruct((domains,) + rows_shape, F32),
+            edge,
+            edge,
+        ],
+        600_000_000,
+        900_000,
+        in_specs=[in_hbm] * (3 + len(pairs)),
+        out_specs=[in_vmem] * (len(pairs) + 1) + [in_hbm, in_vmem, in_vmem],
+        scratch_shapes=[
+            pltpu.VMEM(displacement.shape, F32),
+            pltpu.VMEM(face_nodes.shape, jnp.int32),
+            pltpu.VMEM(modulus.shape, F32),
+            pltpu.SemaphoreType.DMA((3 + len(pairs),)),
+            pltpu.SemaphoreType.DMA((domains,)),
+        ],
+    )(*held)
+    all_rows = lax.all_to_all(copies, "dom", split_axis=0, concat_axis=0, tiled=True)
+    outer = swapped(outer, ("dom", "sub"), 1)
+    inner = swapped(inner, ("dom", "sub"), 0)
+
     sent, kept = on_core(
         pairs_kernel,
         [
@@ -296,26 +374,18 @@
         ],
         200_000_000,
         800_000,
-    )(
-        all_rows,
-        own_rows,
-        pair_mortar.reshape(line),
-        pair_rank.reshape(line),
-        pair_face.reshape(line),
-        pair_count.reshape(line),
-        pair_shape,
-        pair_weight,
-        pair_gap,
-        pair_normal,
-    )
+    )(all_rows, own_rows, *pairs)
     got = lax.all_to_all(sent, "dom", split_axis=0, concat_axis=0, tiled=True)
 
-    internal = on_core(
-        internal_kernel, jax.ShapeDtypeStruct(displacement.shape, F32), 3_000_000_000, 700_000
-    )(displacement, above, below, modulus, stiffness)
-    faces = on_core(
-        mortar_kernel, jax.ShapeDtypeStruct((12, face_count), F32), 10_000_000, 30_000
-    )(kept)
+    internal, faces = on_core(
+        internal_kernel,
+        [
+            jax.ShapeDtypeStruct(displacement.shape, F32),
+            jax.ShapeDtypeStruct((12, face_count), F32),
+        ],
+        1_500_000_000,
+        700_000,
+    )(displacement, inner, outer, modulus, stiffness, kept)
 
     def last(*refs):
         nodes_kernel(capacity, *refs)

time: 56.8 us -> 31.1 us (0.55)
  blocking collectives: 35.5 us -> 0 us
  waiting for transfers between devices: 3.67 us -> 12.7 us
  starting transfers between devices: 8.48 us -> 11.4 us
  local copies, waits for them, and re-layouts: 2.18 us -> 0.02 us
    all_gather x1 -> x0, blocking collectives: 35.5 us -> none  [shards(): all_rows = lax.all_gather(own_rows, 'dom')]
    all_to_all x0 -> x1, waiting for transfers between devices: none -> 7.27 us  [shards(): lax.all_to_all(copies, 'dom', split_axis=0, concat_axis=0, tiled=True)]
    all_to_all x0 -> x1, starting transfers between devices: none -> 7.26 us  [shards(): lax.all_to_all(copies, 'dom', split_axis=0, concat_axis=0, tiled=True)]
    ppermute x2, starting transfers between devices: 3.92 us -> 0.67 us  [swapped(): return lax.ppermute(block, axis, route)]
    all_to_all x1, waiting for transfers between devices: 3.66 us -> 5.41 us  [shards(): got = lax.all_to_all(sent, 'dom', split_axis=0, concat_axis=0, tiled=True)]
    unnamed x27 -> x10, local copies, waits for them, and re-layouts: 1.22 us -> 0.02 us
    all_to_all x1, starting transfers between devices: 4.57 us -> 3.47 us  [shards(): got = lax.all_to_all(sent, 'dom', split_axis=0, concat_axis=0, tiled=True)]
    squeeze x1 -> x0, local copies, waits for them, and re-layouts: 0.96 us -> none  [shards(): displacement[:, -1]]
  transfers between devices with their start and end apart: 3 -> 4, of which waited for: 1 -> 2; matrix products, arithmetic and copies ran while one was open for 0% -> 0% of each run, Pallas kernels for 8% -> 8%
where the time goes in v3:
time: 31.1 us; the launch traced here: 30.8 us
  waiting for transfers between devices  12.7 us (41%)
  starting transfers between devices  11.4 us (37%)
  Pallas kernels  6.54 us (21%)
    all_to_all x1, waiting for transfers between devices, shards(): lax.all_to_all(copies, 'dom', split_axis=0, concat_axis=0, tiled=True)  7.27 us
    all_to_all x1, starting transfers between devices, shards(): lax.all_to_all(copies, 'dom', split_axis=0, concat_axis=0, tiled=True)  7.26 us
    all_to_all x1, waiting for transfers between devices, shards(): got = lax.all_to_all(sent, 'dom', split_axis=0, concat_axis=0, tiled=True)  5.41 us
    all_to_all x1, starting transfers between devices, shards(): got = lax.all_to_all(sent, 'dom', split_axis=0, concat_axis=0, tiled=True)  3.47 us
    pallas_call x1, Pallas kernels, shards(): on_core(first, [jax.ShapeDtypeStruct(x.shape, x.dtype) for x in pairs] +...  2.61 us
    pallas_call x1, Pallas kernels, shards(): on_core(last, jax.ShapeDtypeStruct(displacement.shape, F32), 600000000, 9...  1.59 us
    pallas_call x1, Pallas kernels, shards(): on_core(pairs_kernel, [jax.ShapeDtypeStruct((domains, WORDS, LANES), F32)...  1.19 us
    pallas_call x1, Pallas kernels, shards(): on_core(internal_kernel, [jax.ShapeDtypeStruct(displacement.shape, F32),...  1.16 us
  transfers between devices with their start and end apart: 4, of which 2 were waited for; matrix products, arithmetic and copies ran while one was open for 0% of the time, Pallas kernels for 8%

profile of v3, /device:TPU:0, one launch (start us, length us, event | category | flops | bytes accessed | tf_op | source)
XLA Modules:
  0.0 30.8 jit_solution(1044663842346091069)
XLA Ops:
  0.0 2.6 %shard_map.127 = (s32[1,256]{1,0:T(1,128)S(1)}, s32[1,256]{1,0:T(1,128)S(1)}, s32[1,256]{1,0:T(1,128)S(1)}, s32[1,256]{1,0:T(1,128)S(1)}, f32[25,8,256]{2,1,0:T(...) custom-call(f32[3,2,32,256]{3,2,1,0:T(8,128)} %disp_ref.1, ...), custom_call_target="tpu_custom_call" | custom-call | flops 600000000 | bytes 900000 | tf_op jit(solution)/shard_map/pallas_call | solution.py:344
  2.6 7.3 %all-to-all-start = ((f32[8,24,256]{2,1,0:T(8,128)}), f32[8,24,256]{2,1,0:T(8,128)S(1)}, u32[]{:S(2)}, u32[]{:S(2)}) async-start(f32[8,24,256]{2,1,0:T(8,128)} %get-tuple-element.21), calls=%async_computation | async-start | bytes 393216 | tf_op jit(solution)/shard_map/all_to_all | solution.py:365
  9.9 0.0 collective-permute-start
  9.9 0.7 %collective-permute-start.1 = (f32[4,32,256]{2,1,0:T(8,128)S(1)}, f32[4,32,256]{2,1,0:T(8,128)S(1)}, u32[]{:S(2)}, u32[]{:S(2)}) collective-permute-start(f32[4,32,256]{2,1,0:T(8,128)S(1)} %get-tuple-element.33), channel_id=1, source_target_pairs={{1,2},{2,1},{3,4},{4,3},{5,6},{6,5},{7,8},{8,7},{9,10},{10,9},{11,... | collective-permute-start | bytes 393224 | tf_op jit(solution)/shard_map/ppermute | solution.py:300
  10.6 7.3 %all-to-all-done.all_ref = f32[8,24,256]{2,1,0:T(8,128)S(1)} async-done(((f32[8,24,256]{2,1,0:T(8,128)}), f32[8,24,256]{2,1,0:T(8,128)S(1)}, u32[]{:S(2)}, u32[]{:S(2)}) %all-to-all-start) | async-done | bytes 196640 | tf_op jit(solution)/shard_map/all_to_all | solution.py:365
  17.8 0.0 copy-start
  17.8 0.0 copy-start.3
  17.8 1.2 %shard_map.128 = (f32[8,8,128]{2,1,0:T(8,128)}, f32[8,256]{1,0:T(8,128)S(1)}) custom-call(f32[8,24,256]{2,1,0:T(8,128)S(1)} %all-to-all-done.all_ref, f32[24,256]{1,0:T(8,128)S(1)} %get-tuple-element.22.own_ref, s32[1,256]{1,0:T(1,128)S(1)} %get-tuple-element.23.mortar_ref, s32[1,256]{1,0:T(1,128)S(1)} %get-tuple-element.24.rank_ref, ...), custom_call_target="tpu_custom_call" | custom-call | flops 200000000 | bytes 800000 | tf_op jit(solution)/shard_map/pallas_call | solution.py:369
  19.0 0.0 copy-start.1
  19.0 3.5 %all-to-all-start.1 = ((f32[8,8,128]{2,1,0:T(8,128)}), f32[8,8,128]{2,1,0:T(8,128)S(1)}, u32[]{:S(2)}, u32[]{:S(2)}) async-start(f32[8,8,128]{2,1,0:T(8,128)} %get-tuple-element.31), calls=%async_computation.1 | async-start | bytes 65536 | tf_op jit(solution)/shard_map/all_to_all | solution.py:378
  22.5 0.0 collective-permute-done.inner_ref
  22.5 0.0 collective-permute-done.1.outer_ref
  22.5 0.0 copy-done
  22.5 0.0 copy-done.3
  22.5 0.0 copy-done.1
  22.6 0.0 copy-start.2
  22.6 0.0 copy-start.4
  22.6 1.2 %shard_map.129 = (f32[3,2,32,256]{3,2,1,0:T(8,128)S(1)}, f32[12,512]{1,0:T(8,128)S(1)}) custom-call(f32[3,2,32,256]{3,2,1,0:T(8,128)S(1)} %copy-done, f32[4,32,256]{2,1,0:T(8,128)S(1)} %collective-permute-done.inner_ref, f32[4,32,256]{2,1,0:T(8,128)S(1)} %collective-permute-done.1.outer_ref, f32[2,32,256]{2,1,0:T(8,128)S(1)} %copy-done.1, ...), custom_call_target="tpu_custom_call" | custom-call | flops 1500000000 | bytes 700000 | tf_op jit(solution)/shard_map/pallas_call | solution.py:380
  23.7 5.4 %all-to-all-done.1.refs_0_ = f32[8,8,128]{2,1,0:T(8,128)S(1)} async-done(((f32[8,8,128]{2,1,0:T(8,128)}), f32[8,8,128]{2,1,0:T(8,128)S(1)}, u32[]{:S(2)}, u32[]{:S(2)}) %all-to-all-start.1) | async-done | bytes 32800 | tf_op jit(solution)/shard_map/all_to_all | solution.py:378
  29.2 0.0 copy-done.2
  29.2 0.0 copy-done.4
  29.2 1.6 %shard_map.130 = f32[3,2,32,256]{3,2,1,0:T(8,128)} custom-call(f32[8,8,128]{2,1,0:T(8,128)S(1)} %all-to-all-done.1.refs_0_, f32[12,512]{1,0:T(8,128)S(1)} %get-tuple-element.35.refs_1_, s32[4,512]{1,0:T(4,128)S(1)} %copy-done.4, f32[3,2,32,256]{3,2,1,0:T(8,128)S(1)} %get-tuple-element.36.refs_3_, f32[2,32,256]{2,1,0:T(8,128)S(1)} %copy-done.2), custom_call_target="tpu_custom_call" | custom-call | flops 600000000 | bytes 900000 | tf_op jit(solution)/shard_map/pallas_call | solution.py:393
Async XLA Ops:
  2.6 15.2 %all-to-all-start = ((f32[8,24,256]{2,1,0:T(8,128)}), f32[8,24,256]{2,1,0:T(8,128)S(1)}, u32[]{:S(2)}, u32[]{:S(2)}) async-start(f32[8,24,256]{2,1,0:T(8,128)} %get-tuple-element.21), calls=%async_computation | async-start | bytes 393216 | tf_op jit(solution)/shard_map/all_to_all | solution.py:365
  9.9 12.6 %collective-permute-start = (f32[4,32,256]{2,1,0:T(8,128)S(1)}, f32[4,32,256]{2,1,0:T(8,128)S(1)}, u32[]{:S(2)}, u32[]{:S(2)}) collective-permute-start(f32[4,32,256]{2,1,0:T(8,128)S(1)} %get-tuple-element.32), channel_id=1, source_target_pairs={{0,1},{1,0},{2,3},{3,2},{4,5},{5,4},{6,7},{7,6},{8,9},{9,8},{10,11... | collective-permute-start | bytes 393224 | tf_op jit(solution)/shard_map/ppermute | solution.py:300
  9.9 12.6 %collective-permute-start.1 = (f32[4,32,256]{2,1,0:T(8,128)S(1)}, f32[4,32,256]{2,1,0:T(8,128)S(1)}, u32[]{:S(2)}, u32[]{:S(2)}) collective-permute-start(f32[4,32,256]{2,1,0:T(8,128)S(1)} %get-tuple-element.33), channel_id=1, source_target_pairs={{1,2},{2,1},{3,4},{4,3},{5,6},{6,5},{7,8},{8,7},{9,10},{10,9},{11,... | collective-permute-start | bytes 393224 | tf_op jit(solution)/shard_map/ppermute | solution.py:300
  17.8 4.7 %copy-start = (f32[3,2,32,256]{3,2,1,0:T(8,128)S(1)}, f32[3,2,32,256]{3,2,1,0:T(8,128)}, u32[]{:S(2)}) copy-start(f32[3,2,32,256]{3,2,1,0:T(8,128)} %disp_ref.1) | copy-start | bytes 589828
  17.8 4.7 %copy-start.3 = (f32[24,24]{1,0:T(8,128)S(1)}, f32[24,24]{1,0:T(8,128)}, u32[]{:S(2)}) copy-start(f32[24,24]{1,0:T(8,128)} %stiffness_ref.1) | copy-start | bytes 6916
  19.0 3.5 %copy-start.1 = (f32[2,32,256]{2,1,0:T(8,128)S(1)}, f32[2,32,256]{2,1,0:T(8,128)}, u32[]{:S(2)}) copy-start(f32[2,32,256]{2,1,0:T(8,128)} %modulus_ref.1) | copy-start | bytes 196612
  19.0 10.1 %all-to-all-start.1 = ((f32[8,8,128]{2,1,0:T(8,128)}), f32[8,8,128]{2,1,0:T(8,128)S(1)}, u32[]{:S(2)}, u32[]{:S(2)}) async-start(f32[8,8,128]{2,1,0:T(8,128)} %get-tuple-element.31), calls=%async_computation.1 | async-start | bytes 65536 | tf_op jit(solution)/shard_map/all_to_all | solution.py:378
  22.6 6.6 %copy-start.2 = (f32[2,32,256]{2,1,0:T(8,128)S(1)}, f32[2,32,256]{2,1,0:T(8,128)}, u32[]{:S(2)}) copy-start(f32[2,32,256]{2,1,0:T(8,128)} %refs_4_.1) | copy-start | bytes 196612
  22.6 6.6 %copy-start.4 = (s32[4,512]{1,0:T(4,128)S(1)}, s32[4,512]{1,0:T(4,128)}, u32[]{:S(2)}) copy-start(s32[4,512]{1,0:T(4,128)} %refs_2_.3) | copy-start | bytes 24580

commit v4 on v3

v4 whole, which is shorter than its diff:
```python
import jax
import jax.numpy as jnp
from jax import lax
from jax.experimental import pallas as pl
from jax.experimental.pallas import tpu as pltpu
from jax.sharding import PartitionSpec as P

F32 = jnp.float32
BF16 = jnp.bfloat16
LANES = 128


def terms_of(x, count):
    terms = []
    for _ in range(count):
        terms.append(x.astype(BF16))
        x = x - terms[-1].astype(F32)
    return terms


def thirds(x):
    return jnp.concatenate(terms_of(x, 3), axis=0)


def summed(stacked):
    rows = stacked.shape[0] // 3
    return (stacked[:rows] + stacked[rows : 2 * rows]) + stacked[2 * rows :]


def marks(index, count):
    rows = lax.broadcasted_iota(jnp.int32, (count, index.shape[1]), 0)
    return (rows == index).astype(F32).astype(BF16)


def times(left, right):
    return jnp.dot(left, right, preferred_element_type=F32)


def times_turned(left, right):
    return lax.dot_general(left, right, (((1,), (1,)), ((), ())), preferred_element_type=F32)


def halves(power):
    return power.bit_length() - 1


def looked_up(table, face, width):
    at = marks(face & (width - 1), width)
    both = summed(times(thirds(table), at))
    return jnp.where(face < width, both[:12], both[12:])


def words_of(shapes, gap, normal, face):
    full = gap.shape[0] // 8 * 8
    last = [x[full:] for x in shapes + [gap]]
    blank = jnp.zeros((7, face.shape[1]), F32)
    return jnp.concatenate(
        [x[:full] for x in shapes + [gap]] + last + [normal, face.astype(F32), blank], axis=0
    )


def weighted_pressure(words, full, remote_rows):
    tail = 5 * full
    normal = words[tail + 5 : tail + 8]
    gap, last = words[4 * full : tail], words[tail + 4 : tail + 5]
    for node in range(4):
        across = sum(
            normal[k : k + 1] * remote_rows[k * 4 + node : k * 4 + node + 1] for k in range(3)
        )
        gap = gap + words[node * full : (node + 1) * full] * across
        last = last + words[tail + node : tail + node + 1] * across
    return jnp.maximum(-gap, 0.0), jnp.maximum(-last, 0.0), normal


def loads_on(shapes, full, tail, pressure, last):
    return [
        jnp.sum(pressure * shapes[i * full : (i + 1) * full], axis=0, keepdims=True)
        + last * shapes[tail + i : tail + i + 1]
        for i in range(4)
    ]


def forces_of(normal, loads):
    loads = jnp.concatenate(loads, axis=0)
    return jnp.concatenate([normal[k : k + 1] * loads for k in range(3)], axis=0)


def first_kernel(capacity, *refs):
    (
        nodes_hbm, disp_hbm, mortar_hbm, rank_hbm, face_hbm, count_hbm, weight_hbm, normal_hbm,
        gap_hbm, shape_hbm, modulus_hbm,
        sent_ref, rows_ref, words_ref, turned_ref, mortar_ref, rank_ref, face_ref, inner_ref, outer_ref,
        nodes, disp, count, weight, normal_v, gap_v, shape, modulus, blocks, sems, copy_sems,
    ) = refs
    components, layers, rows_y, cols_x = disp.shape
    sources = (
        nodes_hbm, rank_hbm, face_hbm, mortar_hbm, count_hbm, weight_hbm, normal_hbm, gap_hbm,
        shape_hbm, disp_hbm, modulus_hbm,
    )
    targets = (
        nodes, rank_ref, face_ref, mortar_ref, count, weight, normal_v, gap_v, shape, disp, modulus,
    )
    brought = [
        pltpu.make_async_copy(source, target, sems.at[i])
        for i, (source, target) in enumerate(zip(sources, targets))
    ]
    for copy in brought:
        copy.start()

    domains = sent_ref.shape[0]
    pair_total = rank_ref.shape[1]
    face_count = nodes.shape[1]
    strips = layers * rows_y
    brought[0].wait()
    indices = [nodes[corner : corner + 1, :] for corner in range(4)]
    along_x = [marks(index & (cols_x - 1), cols_x) for index in indices]

    for copy in brought[1:4]:
        copy.wait()
    rank, face, mortar = rank_ref[...], face_ref[...], mortar_ref[...]
    chosen = lax.broadcasted_iota(jnp.int32, (domains, pair_total), 0) == rank
    before = lax.broadcasted_iota(jnp.int32, (pair_total, pair_total), 0) < lax.broadcasted_iota(
        jnp.int32, (pair_total, pair_total), 1
    )
    earlier = times(chosen.astype(F32).astype(BF16), before.astype(F32).astype(BF16))
    slot = jnp.sum(jnp.where(chosen, earlier, 0.0), axis=0, keepdims=True).astype(jnp.int32)
    place = marks(rank * capacity + slot, domains * capacity)

    for copy in brought[4:]:
        copy.wait()
    parts = thirds(disp[...].reshape(components * strips, cols_x))
    numbers = lax.broadcasted_iota(jnp.int32, (strips, face_count), 0)
    folds = face_count // cols_x
    for corner in range(4):
        strip = indices[corner] >> halves(cols_x)
        found = summed(times(parts, along_x[corner])).reshape(components, strips, face_count)
        values = jnp.sum(jnp.where((numbers == strip)[None], found, 0.0), axis=1)
        for fold in range(folds):
            for k in range(components):
                at = fold * 12 + k * 4 + corner
                rows_ref[at : at + 1, :] = values[k : k + 1, fold * cols_x : (fold + 1) * cols_x]

    mortar_rows = looked_up(rows_ref[...], mortar, cols_x)
    normal = normal_v[...]
    gap = gap_v[...]
    points = gap.shape[0]
    full = points // 8 * 8
    live = lax.broadcasted_iota(jnp.int32, (points, pair_total), 0) < count[...]
    root = jnp.where(live, jnp.sqrt(weight[...]), 0.0)
    turned = []
    for node in range(4):
        mortar_shape = shape[:, 4 + node]
        across = sum(
            normal[k : k + 1] * mortar_rows[k * 4 + node : k * 4 + node + 1] for k in range(3)
        )
        gap = gap - mortar_shape * across
        turned.append(root * mortar_shape)
    for node in range(4):
        turned_ref[node * full : (node + 1) * full] = turned[node][:full]
        turned_ref[4 * full + node : 4 * full + node + 1] = turned[node][full:]
    words = words_of([root * shape[:, node] for node in range(4)], root * gap, normal, face)
    words_ref[...] = words

    group = LANES // capacity
    rows_high = rows_ref.shape[0] * cols_x // LANES
    height = blocks.shape[1] - rows_high
    extra = group * height - words.shape[0]
    if extra:
        words = jnp.concatenate([words, jnp.zeros((extra, pair_total), F32)], axis=0)
    placed = summed(times_turned(thirds(words), place))
    rows = rows_ref[...]
    part = lax.broadcasted_iota(jnp.int32, (height, LANES), 1) >> halves(capacity)
    copies = []
    for domain in range(domains):
        tile, spot = domain // group, domain % group
        block = None
        for j in range(group):
            piece = placed[j * height : (j + 1) * height, tile * LANES : (tile + 1) * LANES]
            if j != spot:
                piece = pltpu.roll(piece, (j - spot) * capacity % LANES, 1)
            block = piece if block is None else jnp.where(part == j, piece, block)
        for i in range(cols_x // LANES):
            high = rows_ref.shape[0]
            blocks[domain, i * high : (i + 1) * high] = rows[:, i * LANES : (i + 1) * LANES]
        blocks[domain, rows_high:] = block
        copies.append(
            pltpu.make_async_copy(blocks.at[domain], sent_ref.at[domain], copy_sems.at[domain])
        )
        copies[-1].start()

    sub = lax.axis_index("sub")
    for target, layer in ((inner_ref, (1 - sub) * (layers - 1)), (outer_ref, sub * (layers - 1))):
        for k in range(components):
            target[k] = disp[k, layer]
        target[components] = modulus[layer]
    for copy in copies:
        copy.wait()


def last_kernel(
    capacity, got_ref, rows_ref, words_ref, turned_ref, mortar_ref, rank_ref, face_ref, nodes_ref,
    internal_ref, mass_ref, out_ref,
):
    domains = got_ref.shape[0]
    components, layers, rows_y, cols_x = out_ref.shape
    strips = layers * rows_y
    face_count = nodes_ref.shape[1]
    pair_total = rank_ref.shape[1]
    folded = rows_ref.shape[0]
    rows_high = folded * cols_x // LANES
    height = got_ref.shape[1] - rows_high
    group = LANES // capacity
    full = (turned_ref.shape[0] - 8) // 4
    own_rows = rows_ref[...]

    rank, face = rank_ref[...], face_ref[...]
    at = marks(face & (cols_x - 1), cols_x)
    step = min(domains, 8)

    def add_step(turn, total):
        block = jnp.concatenate(
            [
                got_ref[pl.ds(turn * step, step), i * folded : (i + 1) * folded].reshape(
                    step * folded, LANES
                )
                for i in range(cols_x // LANES)
            ],
            axis=1,
        )
        found = summed(times(thirds(block), at)).reshape(step, folded, pair_total)
        for i in range(step):
            total = total + jnp.where(rank == turn * step + i, found[i], 0.0)
        return total

    both = jnp.zeros((folded, pair_total), F32)
    if domains == step:
        both = add_step(0, both)
    else:
        both = lax.fori_loop(0, domains // step, add_step, both)
    remote_rows = jnp.where(face < cols_x, both[:12], both[12:])
    pressure, last, normal = weighted_pressure(words_ref[...], full, remote_rows)
    turned = turned_ref[...]
    mortar_forces = forces_of(-normal, loads_on(turned, full, 4 * full, pressure, last))

    part = lax.broadcasted_iota(jnp.int32, (height, LANES), 1) >> halves(capacity)
    pieces = []
    for j in range(group):
        tiles = []
        for tile in range(domains // group):
            block = None
            for spot in range(group):
                piece = got_ref[tile * group + spot, rows_high:]
                if j != spot:
                    piece = pltpu.roll(piece, (spot - j) * capacity % LANES, 1)
                block = piece if block is None else jnp.where(part == spot, piece, block)
            tiles.append(block)
        pieces.append(jnp.concatenate(tiles, axis=1))
    words = jnp.concatenate(pieces, axis=0)
    asked = words[5 * full + 8 : 5 * full + 9].astype(jnp.int32)
    pressure, last, normal = weighted_pressure(words, full, looked_up(own_rows, asked, cols_x))
    remote_forces = forces_of(normal, loads_on(words, full, 5 * full, pressure, last))

    forces = jnp.concatenate([mortar_forces, remote_forces], axis=1)
    at = marks(jnp.concatenate([mortar_ref[...], asked], axis=1), face_count)
    forces = summed(times_turned(thirds(forces), at))
    total = jnp.zeros((2 * components * strips, cols_x), F32)
    parts = [term.astype(F32) for term in terms_of(forces, 2)]
    numbers = lax.broadcasted_iota(jnp.int32, (strips, face_count), 0)
    for corner in range(4):
        index = nodes_ref[corner : corner + 1, :]
        along_x = marks(index & (cols_x - 1), cols_x)
        strip = numbers == (index >> halves(cols_x))
        spread = []
        for part in parts:
            for k in range(components):
                at = k * 4 + corner
                spread.append(jnp.where(strip, part[at : at + 1], 0.0).astype(BF16))
        total = total + times_turned(jnp.concatenate(spread, axis=0), along_x)
    half = components * strips
    contact = (total[:half] + total[half:]).reshape(components, layers, rows_y, cols_x)
    out_ref[...] = (internal_ref[...] + contact) / mass_ref[...][None]


def internal_kernel(
    disp_ref, inner_ref, outer_ref, modulus_ref, stiffness_ref, out_ref
):
    components, layers, rows_y, cols_x = disp_ref.shape
    group = 8
    dofs = 8 * components
    half = dofs // 2

    row = lax.broadcasted_iota(jnp.int32, (dofs * group, dofs), 0) >> halves(group)
    upper = (row >= half).astype(jnp.int32)
    inner = row - half * upper
    dof = (inner >> 2) * 8 + upper * 4 + (inner & 3)
    pick = (dof == lax.broadcasted_iota(jnp.int32, (dofs * group, dofs), 1)).astype(F32).astype(BF16)
    size = dofs * group
    diagonal = (lax.broadcasted_iota(jnp.int32, (size, size), 0) & (group - 1)) == (
        lax.broadcasted_iota(jnp.int32, (size, size), 1) & (group - 1)
    )
    blocks = []
    for term in terms_of(stiffness_ref[...], 2):
        wide = times_turned(times(pick, term).astype(BF16), pick)
        blocks.append(jnp.where(diagonal, wide, 0.0).astype(BF16))

    sub = lax.axis_index("sub")
    below_ref = [jnp.where(sub == 0, outer_ref[k], inner_ref[k]) for k in range(components + 1)]
    above_ref = [jnp.where(sub == 0, inner_ref[k], outer_ref[k]) for k in range(components)]

    def shifted(layer):
        views = []
        for k in range(components):
            for b in range(2):
                moved = layer[k] if b == 0 else pltpu.roll(layer[k], rows_y - 1, 0)
                views.append(moved)
                views.append(pltpu.roll(moved, cols_x - 1, 1))
        return views

    views = [shifted(below_ref)]
    for layer in range(layers):
        views.append(shifted([disp_ref[k, layer] for k in range(components)]))
    views.append(shifted(above_ref))
    inside = (lax.broadcasted_iota(jnp.int32, (rows_y, cols_x), 0) < rows_y - 1) & (
        lax.broadcasted_iota(jnp.int32, (rows_y, cols_x), 1) < cols_x - 1
    )
    scales = [below_ref[components]] + [modulus_ref[layer] for layer in range(layers)]
    scales = [jnp.where(inside, scale, 0.0) for scale in scales]

    lower, higher = [], []
    for e in range(layers + 1):
        kept = slice(half * group, None) if e == 0 else slice(0, half * group if e == layers else None)
        both = jnp.concatenate([block[kept] for block in blocks], axis=0)
        count = both.shape[0] // 2
        strips = []
        for y in range(0, rows_y, group):
            stacked = jnp.concatenate(
                [view[y : y + group] for view in views[e] + views[e + 1]], axis=0
            )
            high, low = terms_of(stacked, 2)
            leading = times(both, high)
            force = leading[:count] + (leading[count:] + times(both[:count], low))
            force = force.reshape(-1, group, cols_x) * scales[e][y : y + group][None]
            strips.append(force)
        forces = jnp.concatenate(strips, axis=1)
        if e < layers:
            higher.append(forces[-half:])
        if e > 0:
            lower.append(forces[:half])
    for layer in range(layers):
        nodal = lower[layer] + higher[layer]
        for k in range(components):
            straight, crossed = [
                nodal[k * 4 + c] + pltpu.roll(nodal[k * 4 + 2 + c], 1, 0) for c in range(2)
            ]
            out_ref[k, layer] = -(straight + pltpu.roll(crossed, 1, 1))


def on_core(kernel, outs, flops, moved, **more):
    return pl.pallas_call(
        kernel,
        out_shape=outs,
        compiler_params=pltpu.CompilerParams(vmem_limit_bytes=48 * 1024 * 1024),
        cost_estimate=pl.CostEstimate(flops=flops, bytes_accessed=moved, transcendentals=0),
        **more,
    )


def swapped(block, axis, first):
    size = lax.axis_size(axis)
    route = []
    for i in range(first, size - 1, 2):
        route += [(i, i + 1), (i + 1, i)]
    return lax.ppermute(block, axis, route)


def shards(
    displacement,
    modulus,
    node_mass,
    stiffness,
    face_nodes,
    pair_mortar,
    pair_rank,
    pair_face,
    pair_count,
    pair_shape,
    pair_weight,
    pair_gap,
    pair_normal,
):
    components, layers, rows_y, cols_x = displacement.shape
    face_count = face_nodes.shape[1]
    pair_total = pair_mortar.shape[0]
    domains = lax.axis_size("dom")
    capacity = max(2, 2 * pair_total // domains)

    points = pair_weight.shape[0]
    full = points // 8 * 8
    group = LANES // capacity
    word_rows = 5 * full + 16
    height = -(-word_rows // (8 * group)) * 8
    rows_high = 12 * face_count // LANES
    line = (1, pair_total)

    def first(*refs):
        first_kernel(capacity, *refs)

    def last(*refs):
        last_kernel(capacity, *refs)

    def shaped(shape, dtype=F32):
        return jax.ShapeDtypeStruct(shape, dtype)

    arrays = [
        face_nodes,
        displacement,
        pair_mortar.reshape(line),
        pair_rank.reshape(line),
        pair_face.reshape(line),
        pair_count.reshape(line),
        pair_weight,
        pair_normal,
        pair_gap,
        jnp.swapaxes(pair_shape, 0, 1),
        modulus,
    ]
    edge = shaped((components + 1, rows_y, cols_x))
    in_hbm = pl.BlockSpec(memory_space=pltpu.HBM)
    in_vmem = pl.BlockSpec(memory_space=pltpu.VMEM)
    kept = [face_nodes, displacement, *arrays[5:]]
    sent, rows, words, turned, mortar, rank, face, inner, outer = on_core(
        first,
        [
            shaped((domains, rows_high + height, LANES)),
            shaped((12 * face_count // cols_x, cols_x)),
            shaped((word_rows, pair_total)),
            shaped((4 * full + 8, pair_total)),
            shaped(line, jnp.int32),
            shaped(line, jnp.int32),
            shaped(line, jnp.int32),
            edge,
            edge,
        ],
        900_000_000,
        1_500_000,
        in_specs=[in_hbm] * len(arrays),
        out_specs=[in_hbm] + [in_vmem] * 8,
        scratch_shapes=[pltpu.VMEM(x.shape, x.dtype) for x in kept]
        + [
            pltpu.VMEM((domains, rows_high + height, LANES), F32),
            pltpu.SemaphoreType.DMA((len(arrays),)),
            pltpu.SemaphoreType.DMA((domains,)),
        ],
    )(*[pltpu.with_memory_space_constraint(x, pltpu.HBM) for x in arrays])
    got = lax.all_to_all(sent, "dom", split_axis=0, concat_axis=0, tiled=True)
    outer = swapped(outer, ("dom", "sub"), 1)
    inner = swapped(inner, ("dom", "sub"), 0)
    internal = on_core(
        internal_kernel, shaped(displacement.shape), 1_500_000_000, 700_000
    )(displacement, inner, outer, modulus, stiffness)
    return on_core(last, shaped(displacement.shape), 900_000_000, 1_500_000)(
        got, rows, words, turned, mortar, rank, face, face_nodes, internal, node_mass
    )


def solution(mesh):
    placed = (
        P(None, ("runs", "dom", "sub"), None, None),
        P(("runs", "dom", "sub"), None, None),
        P(("runs", "dom", "sub"), None, None),
        P(),
        P(None, ("runs", "dom", "sub")),
        P(("runs", "dom", "sub")),
        P(("runs", "dom", "sub"), None),
        P(("runs", "dom", "sub")),
        P(("runs", "dom", "sub")),
        P(None, None, ("runs", "dom", "sub")),
        P(None, ("runs", "dom", "sub")),
        P(None, ("runs", "dom", "sub")),
        P(None, ("runs", "dom", "sub")),
    )
    return jax.shard_map(
        shards,
        mesh=mesh,
        in_specs=placed,
        out_specs=P(None, ("runs", "dom", "sub"), None, None),
        check_vma=False,
    )
```

time: 31.1 us -> 27.7 us (0.89)
  the two profiles are of different devices: /device:TPU:0 before, /device:TPU:16 now
where the time goes in v4:
time: 27.7 us; the launch traced here: 27.3 us
  waiting for transfers between devices  10.1 us (36%)
  starting transfers between devices  9.88 us (36%)
  Pallas kernels  6.57 us (24%)
  local copies, waits for them, and re-layouts  0.69 us (2%)
    ppermute x2, waiting for transfers between devices, swapped(): return lax.ppermute(block, axis, route)  10.1 us
    all_to_all x1, starting transfers between devices, shards(): got = lax.all_to_all(sent, 'dom', split_axis=0, concat_axis=0, tiled=True)  6.28 us
    ppermute x2, starting transfers between devices, swapped(): return lax.ppermute(block, axis, route)  3.6 us
    pallas_call x1, Pallas kernels, shards(): on_core(first, [shaped((domains, rows_high + height, LANES)), shaped((12...  3.47 us
    pallas_call x1, Pallas kernels, shards(): on_core(last, shaped(displacement.shape), 900000000, 1500000)  1.95 us
    pallas_call x1, Pallas kernels, shards(): on_core(internal_kernel, shaped(displacement.shape), 1500000000, 700000)  1.15 us
    unnamed x10, local copies, waits for them, and re-layouts  0.69 us
  transfers between devices with their start and end apart: 3, of which 1 were waited for; matrix products, arithmetic and copies ran while one was open for 0% of the time, Pallas kernels for 4%

profile of v4, /device:TPU:16, one launch (start us, length us, event | category | flops | bytes accessed | tf_op | source)
XLA Modules:
  0.0 27.3 jit_solution(10246133058039864654)
XLA Ops:
  0.0 3.5 %shard_map.127 = (f32[8,120,128]{2,1,0:T(8,128)}, f32[24,256]{1,0:T(8,128)S(1)}, f32[136,256]{1,0:T(8,128)S(1)}, f32[104,256]{1,0:T(8,128)S(1)}, s32[1,256]{1,0:...) custom-call(s32[4,512]{1,0:T(4,128)} %refs_7_.3, ...), custom_call_target="tpu_custom_call" | custom-call | flops 900000000 | bytes 1500000 | tf_op jit(solution)/shard_map/pallas_call | solution.py:431
  3.5 0.0 copy-start
  3.5 0.0 copy-start.1
  3.5 0.0 copy-start.3
  3.5 6.3 %all-to-all-start = ((f32[8,120,128]{2,1,0:T(8,128)}), f32[8,120,128]{2,1,0:T(8,128)S(1)}, u32[]{:S(2)}, u32[]{:S(2)}) async-start(f32[8,120,128]{2,1,0:T(8,128)} %get-tuple-element.14), calls=%async_computation | async-start | bytes 983040 | tf_op jit(solution)/shard_map/all_to_all | solution.py:455
  9.8 0.0 collective-permute-start
  9.8 0.0 copy-start.2
  9.8 3.6 %collective-permute-start.1 = (f32[4,32,256]{2,1,0:T(8,128)S(1)}, f32[4,32,256]{2,1,0:T(8,128)S(1)}, u32[]{:S(2)}, u32[]{:S(2)}) collective-permute-start(f32[4,32,256]{2,1,0:T(8,128)S(1)} %get-tuple-element.22), channel_id=1, source_target_pairs={{1,2},{2,1},{3,4},{4,3},{5,6},{6,5},{7,8},{8,7},{9,10},{10,9},{11,... | collective-permute-start | bytes 393224 | tf_op jit(solution)/shard_map/ppermute | solution.py:373
  13.4 0.0 collective-permute-done.inner_ref
  13.4 10.1 %collective-permute-done.1.outer_ref = f32[4,32,256]{2,1,0:T(8,128)S(1)} collective-permute-done((f32[4,32,256]{2,1,0:T(8,128)S(1)}, f32[4,32,256]{2,1,0:T(8,128)S(1)}, u32[]{:S(2)}, u32[]{:S(2)}) %collective-permute-start.1) | collective-permute-done | bytes 131104 | tf_op jit(solution)/shard_map/ppermute | solution.py:373
  23.5 0.0 copy-done
  23.5 0.0 copy-done.1
  23.5 0.0 copy-done.3
  23.5 1.1 %shard_map.128.refs_8_ = f32[3,2,32,256]{3,2,1,0:T(8,128)S(1)} custom-call(f32[3,2,32,256]{3,2,1,0:T(8,128)S(1)} %copy-done, f32[4,32,256]{2,1,0:T(8,128)S(1)} %collective-permute-done.inner_ref, f32[4,32,256]{2,1,0:T(8,128)S(1)} %collective-permute-done.1.outer_ref, f32[2,32,256]{2,1,0:T(8,128)S(1)} %copy-done.1, f32[24,24]{1,0:T(8,128)S(1)} %copy-done.3), custom_call_target="tpu_custom_call" | custom-call | flops 1500000000 | bytes 700000 | tf_op jit(solution)/shard_map/pallas_call | solution.py:458
  24.7 0.0 copy-start.4
  24.7 0.0 all-to-all-done.refs_0_
  24.7 0.0 copy-done.2
  24.7 0.7 %copy-done.4 = s32[4,512]{1,0:T(4,128)S(1)} copy-done((s32[4,512]{1,0:T(4,128)S(1)}, s32[4,512]{1,0:T(4,128)}, u32[]{:S(2)}) %copy-start.4) | copy-done | bytes 8216
  25.4 2.0 %shard_map.129 = f32[3,2,32,256]{3,2,1,0:T(8,128)} custom-call(f32[8,120,128]{2,1,0:T(8,128)S(1)} %all-to-all-done.refs_0_, f32[24,256]{1,0:T(8,128)S(1)} %get-tuple-element.15.refs_1_, f32[136,256]{1,0:T(8,128)S(1)} %get-tuple-element.16.refs_2_, f32[104,256]{1,0:T(8,128)S(1)} %get-tuple-element.17.refs_3_, s32[1,256]{1,0:T(1,128)S(1)} %get-tuple-element.18.refs_4_, ...), custom_call_target="tpu_custom_call" | custom-call | flops 900000000 | bytes 1500000 | tf_op jit(solution)/shard_map/pallas_call | solution.py:461
Async XLA Ops:
  3.5 20.0 %copy-start = (f32[3,2,32,256]{3,2,1,0:T(8,128)S(1)}, f32[3,2,32,256]{3,2,1,0:T(8,128)}, u32[]{:S(2)}) copy-start(f32[3,2,32,256]{3,2,1,0:T(8,128)} %disp_ref.1) | copy-start | bytes 589828
  3.5 20.0 %copy-start.1 = (f32[2,32,256]{2,1,0:T(8,128)S(1)}, f32[2,32,256]{2,1,0:T(8,128)}, u32[]{:S(2)}) copy-start(f32[2,32,256]{2,1,0:T(8,128)} %modulus_ref.1) | copy-start | bytes 196612
  3.5 20.0 %copy-start.3 = (f32[24,24]{1,0:T(8,128)S(1)}, f32[24,24]{1,0:T(8,128)}, u32[]{:S(2)}) copy-start(f32[24,24]{1,0:T(8,128)} %stiffness_ref.1) | copy-start | bytes 6916
  3.5 21.2 %all-to-all-start = ((f32[8,120,128]{2,1,0:T(8,128)}), f32[8,120,128]{2,1,0:T(8,128)S(1)}, u32[]{:S(2)}, u32[]{:S(2)}) async-start(f32[8,120,128]{2,1,0:T(8,128)} %get-tuple-element.14), calls=%async_computation | async-start | bytes 983040 | tf_op jit(solution)/shard_map/all_to_all | solution.py:455
  9.8 3.6 %collective-permute-start = (f32[4,32,256]{2,1,0:T(8,128)S(1)}, f32[4,32,256]{2,1,0:T(8,128)S(1)}, u32[]{:S(2)}, u32[]{:S(2)}) collective-permute-start(f32[4,32,256]{2,1,0:T(8,128)S(1)} %get-tuple-element.21), channel_id=1, source_target_pairs={{0,1},{1,0},{2,3},{3,2},{4,5},{5,4},{6,7},{7,6},{8,9},{9,8},{10,11... | collective-permute-start | bytes 393224 | tf_op jit(solution)/shard_map/ppermute | solution.py:373
  9.8 14.9 %copy-start.2 = (f32[2,32,256]{2,1,0:T(8,128)S(1)}, f32[2,32,256]{2,1,0:T(8,128)}, u32[]{:S(2)}) copy-start(f32[2,32,256]{2,1,0:T(8,128)} %refs_9_.1) | copy-start | bytes 196612
  9.8 13.7 %collective-permute-start.1 = (f32[4,32,256]{2,1,0:T(8,128)S(1)}, f32[4,32,256]{2,1,0:T(8,128)S(1)}, u32[]{:S(2)}, u32[]{:S(2)}) collective-permute-start(f32[4,32,256]{2,1,0:T(8,128)S(1)} %get-tuple-element.22), channel_id=1, source_target_pairs={{1,2},{2,1},{3,4},{4,3},{5,6},{6,5},{7,8},{8,7},{9,10},{10,9},{11,... | collective-permute-start | bytes 393224 | tf_op jit(solution)/shard_map/ppermute | solution.py:373
  24.7 0.7 %copy-start.4 = (s32[4,512]{1,0:T(4,128)S(1)}, s32[4,512]{1,0:T(4,128)}, u32[]{:S(2)}) copy-start(s32[4,512]{1,0:T(4,128)} %refs_7_.3) | copy-start | bytes 24580

commit v5 on v4

--- a/solution.py
+++ b/solution.py
@@ -18,13 +18,13 @@
     return terms
 
 
-def thirds(x):
-    return jnp.concatenate(terms_of(x, 3), axis=0)
+def stacked_terms(x):
+    return jnp.concatenate(terms_of(x, 2), axis=0)
 
 
 def summed(stacked):
-    rows = stacked.shape[0] // 3
-    return (stacked[:rows] + stacked[rows : 2 * rows]) + stacked[2 * rows :]
+    rows = stacked.shape[0] // 2
+    return stacked[:rows] + stacked[rows:]
 
 
 def marks(index, count):
@@ -46,7 +46,7 @@
 
 def looked_up(table, face, width):
     at = marks(face & (width - 1), width)
-    both = summed(times(thirds(table), at))
+    both = summed(times(stacked_terms(table), at))
     return jnp.where(face < width, both[:12], both[12:])
 
 
@@ -90,15 +90,16 @@
         nodes_hbm, disp_hbm, mortar_hbm, rank_hbm, face_hbm, count_hbm, weight_hbm, normal_hbm,
         gap_hbm, shape_hbm, modulus_hbm,
         sent_ref, rows_ref, words_ref, turned_ref, mortar_ref, rank_ref, face_ref, inner_ref, outer_ref,
-        nodes, disp, count, weight, normal_v, gap_v, shape, modulus, blocks, sems, copy_sems,
+        marks_ref,
+        nodes, disp, count, weight, normal_v, gap_v, shape, modulus, halved, blocks, sems, copy_sems,
     ) = refs
     components, layers, rows_y, cols_x = disp.shape
     sources = (
-        nodes_hbm, rank_hbm, face_hbm, mortar_hbm, count_hbm, weight_hbm, normal_hbm, gap_hbm,
-        shape_hbm, disp_hbm, modulus_hbm,
+        nodes_hbm, disp_hbm, rank_hbm, face_hbm, mortar_hbm, count_hbm, weight_hbm, normal_hbm,
+        gap_hbm, shape_hbm, modulus_hbm,
     )
     targets = (
-        nodes, rank_ref, face_ref, mortar_ref, count, weight, normal_v, gap_v, shape, disp, modulus,
+        nodes, disp, rank_ref, face_ref, mortar_ref, count, weight, normal_v, gap_v, shape, modulus,
     )
     brought = [
         pltpu.make_async_copy(source, target, sems.at[i])
@@ -113,9 +114,10 @@
     strips = layers * rows_y
     brought[0].wait()
     indices = [nodes[corner : corner + 1, :] for corner in range(4)]
-    along_x = [marks(index & (cols_x - 1), cols_x) for index in indices]
-
-    for copy in brought[1:4]:
+    for corner in range(4):
+        marks_ref[corner] = marks(indices[corner] & (cols_x - 1), cols_x)
+
+    for copy in brought[2:5]:
         copy.wait()
     rank, face, mortar = rank_ref[...], face_ref[...], mortar_ref[...]
     chosen = lax.broadcasted_iota(jnp.int32, (domains, pair_total), 0) == rank
@@ -126,21 +128,36 @@
     slot = jnp.sum(jnp.where(chosen, earlier, 0.0), axis=0, keepdims=True).astype(jnp.int32)
     place = marks(rank * capacity + slot, domains * capacity)
 
-    for copy in brought[4:]:
-        copy.wait()
-    parts = thirds(disp[...].reshape(components * strips, cols_x))
+    brought[1].wait()
+    parts = stacked_terms(disp[...].reshape(components * strips, cols_x))
     numbers = lax.broadcasted_iota(jnp.int32, (strips, face_count), 0)
     folds = face_count // cols_x
     for corner in range(4):
         strip = indices[corner] >> halves(cols_x)
-        found = summed(times(parts, along_x[corner])).reshape(components, strips, face_count)
+        found = summed(times(parts, marks_ref[corner])).reshape(components, strips, face_count)
         values = jnp.sum(jnp.where((numbers == strip)[None], found, 0.0), axis=1)
         for fold in range(folds):
             for k in range(components):
                 at = fold * 12 + k * 4 + corner
                 rows_ref[at : at + 1, :] = values[k : k + 1, fold * cols_x : (fold + 1) * cols_x]
 
-    mortar_rows = looked_up(rows_ref[...], mortar, cols_x)
+    rows = rows_ref[...]
+    high = rows.shape[0]
+    rows_high = high * cols_x // LANES
+    copies = []
+    for i in range(cols_x // LANES):
+        halved[i * high : (i + 1) * high] = rows[:, i * LANES : (i + 1) * LANES]
+    for domain in range(domains):
+        copies.append(
+            pltpu.make_async_copy(
+                halved, sent_ref.at[domain, :rows_high], copy_sems.at[0, domain]
+            )
+        )
+        copies[-1].start()
+
+    for copy in brought[5:]:
+        copy.wait()
+    mortar_rows = looked_up(rows, mortar, cols_x)
     normal = normal_v[...]
     gap = gap_v[...]
     points = gap.shape[0]
@@ -162,15 +179,12 @@
     words_ref[...] = words
 
     group = LANES // capacity
-    rows_high = rows_ref.shape[0] * cols_x // LANES
-    height = blocks.shape[1] - rows_high
+    height = blocks.shape[1]
     extra = group * height - words.shape[0]
     if extra:
         words = jnp.concatenate([words, jnp.zeros((extra, pair_total), F32)], axis=0)
-    placed = summed(times_turned(thirds(words), place))
-    rows = rows_ref[...]
+    placed = summed(times_turned(stacked_terms(words), place))
     part = lax.broadcasted_iota(jnp.int32, (height, LANES), 1) >> halves(capacity)
-    copies = []
     for domain in range(domains):
         tile, spot = domain // group, domain % group
         block = None
@@ -179,12 +193,11 @@
             if j != spot:
                 piece = pltpu.roll(piece, (j - spot) * capacity % LANES, 1)
             block = piece if block is None else jnp.where(part == j, piece, block)
-        for i in range(cols_x // LANES):
-            high = rows_ref.shape[0]
-            blocks[domain, i * high : (i + 1) * high] = rows[:, i * LANES : (i + 1) * LANES]
-        blocks[domain, rows_high:] = block
+        blocks[domain] = block
         copies.append(
-            pltpu.make_async_copy(blocks.at[domain], sent_ref.at[domain], copy_sems.at[domain])
+            pltpu.make_async_copy(
+                blocks.at[domain], sent_ref.at[domain, rows_high:], copy_sems.at[1, domain]
+            )
         )
         copies[-1].start()
 
@@ -199,7 +212,7 @@
 
 def last_kernel(
     capacity, got_ref, rows_ref, words_ref, turned_ref, mortar_ref, rank_ref, face_ref, nodes_ref,
-    internal_ref, mass_ref, out_ref,
+    marks_ref, internal_ref, mass_ref, out_ref,
 ):
     domains = got_ref.shape[0]
     components, layers, rows_y, cols_x = out_ref.shape
@@ -227,7 +240,7 @@
             ],
             axis=1,
         )
-        found = summed(times(thirds(block), at)).reshape(step, folded, pair_total)
+        found = summed(times(stacked_terms(block), at)).reshape(step, folded, pair_total)
         for i in range(step):
             total = total + jnp.where(rank == turn * step + i, found[i], 0.0)
         return total
@@ -262,22 +275,20 @@
 
     forces = jnp.concatenate([mortar_forces, remote_forces], axis=1)
     at = marks(jnp.concatenate([mortar_ref[...], asked], axis=1), face_count)
-    forces = summed(times_turned(thirds(forces), at))
+    forces = summed(times_turned(stacked_terms(forces), at))
     total = jnp.zeros((2 * components * strips, cols_x), F32)
     parts = [term.astype(F32) for term in terms_of(forces, 2)]
     numbers = lax.broadcasted_iota(jnp.int32, (strips, face_count), 0)
     for corner in range(4):
         index = nodes_ref[corner : corner + 1, :]
-        along_x = marks(index & (cols_x - 1), cols_x)
         strip = numbers == (index >> halves(cols_x))
         spread = []
         for part in parts:
             for k in range(components):
                 at = k * 4 + corner
                 spread.append(jnp.where(strip, part[at : at + 1], 0.0).astype(BF16))
-        total = total + times_turned(jnp.concatenate(spread, axis=0), along_x)
-    half = components * strips
-    contact = (total[:half] + total[half:]).reshape(components, layers, rows_y, cols_x)
+        total = total + times_turned(jnp.concatenate(spread, axis=0), marks_ref[corner])
+    contact = summed(total).reshape(components, layers, rows_y, cols_x)
     out_ref[...] = (internal_ref[...] + contact) / mass_ref[...][None]
 
 
@@ -428,7 +439,7 @@
     in_hbm = pl.BlockSpec(memory_space=pltpu.HBM)
     in_vmem = pl.BlockSpec(memory_space=pltpu.VMEM)
     kept = [face_nodes, displacement, *arrays[5:]]
-    sent, rows, words, turned, mortar, rank, face, inner, outer = on_core(
+    sent, rows, words, turned, mortar, rank, face, inner, outer, along_x = on_core(
         first,
         [
             shaped((domains, rows_high + height, LANES)),
@@ -440,26 +451,28 @@
             shaped(line, jnp.int32),
             edge,
             edge,
+            shaped((4, cols_x, face_count), BF16),
         ],
         900_000_000,
         1_500_000,
         in_specs=[in_hbm] * len(arrays),
-        out_specs=[in_hbm] + [in_vmem] * 8,
+        out_specs=[in_hbm] + [in_vmem] * 9,
         scratch_shapes=[pltpu.VMEM(x.shape, x.dtype) for x in kept]
         + [
-            pltpu.VMEM((domains, rows_high + height, LANES), F32),
+            pltpu.VMEM((rows_high, LANES), F32),
+            pltpu.VMEM((domains, height, LANES), F32),
             pltpu.SemaphoreType.DMA((len(arrays),)),
-            pltpu.SemaphoreType.DMA((domains,)),
+            pltpu.SemaphoreType.DMA((2, domains)),
         ],
     )(*[pltpu.with_memory_space_constraint(x, pltpu.HBM) for x in arrays])
     got = lax.all_to_all(sent, "dom", split_axis=0, concat_axis=0, tiled=True)
     outer = swapped(outer, ("dom", "sub"), 1)
     inner = swapped(inner, ("dom", "sub"), 0)
     internal = on_core(
-        internal_kernel, shaped(displacement.shape), 1_500_000_000, 700_000
+        internal_kernel, shaped(displacement.shape), 2_000_000_000_000, 700_000
     )(displacement, inner, outer, modulus, stiffness)
     return on_core(last, shaped(displacement.shape), 900_000_000, 1_500_000)(
-        got, rows, words, turned, mortar, rank, face, face_nodes, internal, node_mass
+        got, rows, words, turned, mortar, rank, face, face_nodes, along_x, internal, node_mass
     )
 
 

time: 27.7 us -> 30.5 us (1.10)
  the two profiles are of different devices: /device:TPU:16 before, /device:TPU:0 now
where the time goes in v5:
time: 30.5 us; the launch traced here: 30.2 us
  waiting for transfers between devices  12.9 us (42%)
  starting transfers between devices  10 us (33%)
  Pallas kernels  7.21 us (24%)
    all_to_all x1, waiting for transfers between devices, shards(): got = lax.all_to_all(sent, 'dom', split_axis=0, concat_axis=0, tiled=True)  12.9 us
    all_to_all x1, starting transfers between devices, shards(): got = lax.all_to_all(sent, 'dom', split_axis=0, concat_axis=0, tiled=True)  8.83 us
    pallas_call x1, Pallas kernels, shards(): on_core(first, [shaped((domains, rows_high + height, LANES)), shaped((12...  3.16 us
    pallas_call x1, Pallas kernels, shards(): on_core(last, shaped(displacement.shape), 900000000, 1500000)  2.91 us
    ppermute x2, starting transfers between devices, swapped(): return lax.ppermute(block, axis, route)  1.18 us
    pallas_call x1, Pallas kernels, shards(): on_core(internal_kernel, shaped(displacement.shape), 2000000000000, 700000)  1.14 us
  transfers between devices with their start and end apart: 3, of which 1 were waited for; matrix products, arithmetic and copies ran while one was open for 0% of the time, Pallas kernels for 4%

profile of v5, /device:TPU:0, one launch (start us, length us, event | category | flops | bytes accessed | tf_op | source)
XLA Modules:
  0.0 30.2 jit_solution(4257702554211159266)
XLA Ops:
  0.0 3.2 %shard_map.127 = (f32[8,120,128]{2,1,0:T(8,128)}, f32[24,256]{1,0:T(8,128)S(1)}, f32[136,256]{1,0:T(8,128)S(1)}, f32[104,256]{1,0:T(8,128)S(1)}, s32[1,256]{1,0:...) custom-call(s32[4,512]{1,0:T(4,128)} %refs_7_.3, ...), custom_call_target="tpu_custom_call" | custom-call | flops 900000000 | bytes 1500000 | tf_op jit(solution)/shard_map/pallas_call | solution.py:442
  3.2 0.5 %collective-permute-start = (f32[4,32,256]{2,1,0:T(8,128)S(1)}, f32[4,32,256]{2,1,0:T(8,128)S(1)}, u32[]{:S(2)}, u32[]{:S(2)}) collective-permute-start(f32[4,32,256]{2,1,0:T(8,128)S(1)} %get-tuple-element.23), channel_id=1, source_target_pairs={{0,1},{1,0},{2,3},{3,2},{4,5},{5,4},{6,7},{7,6},{8,9},{9,8},{10,11... | collective-permute-start | bytes 393224 | tf_op jit(solution)/shard_map/ppermute | solution.py:384
  3.7 0.7 %collective-permute-start.1 = (f32[4,32,256]{2,1,0:T(8,128)S(1)}, f32[4,32,256]{2,1,0:T(8,128)S(1)}, u32[]{:S(2)}, u32[]{:S(2)}) collective-permute-start(f32[4,32,256]{2,1,0:T(8,128)S(1)} %get-tuple-element.24), channel_id=1, source_target_pairs={{1,2},{2,1},{3,4},{4,3},{5,6},{6,5},{7,8},{8,7},{9,10},{10,9},{11,... | collective-permute-start | bytes 393224 | tf_op jit(solution)/shard_map/ppermute | solution.py:384
  4.3 0.0 copy-start
  4.4 0.0 copy-start.1
  4.4 0.0 copy-start.3
  4.4 8.8 %all-to-all-start = ((f32[8,120,128]{2,1,0:T(8,128)}), f32[8,120,128]{2,1,0:T(8,128)}, u32[]{:S(2)}, u32[]{:S(2)}) async-start(f32[8,120,128]{2,1,0:T(8,128)} %get-tuple-element.15), calls=%async_computation | async-start | bytes 983040 | tf_op jit(solution)/shard_map/all_to_all | solution.py:468
  13.2 0.0 collective-permute-done.inner_ref
  13.2 0.0 collective-permute-done.1.outer_ref
  13.2 0.0 copy-done
  13.2 0.0 copy-done.1
  13.3 0.0 copy-done.3
  13.3 0.0 copy-start.2
  13.3 1.1 %shard_map.128.refs_9_ = f32[3,2,32,256]{3,2,1,0:T(8,128)S(1)} custom-call(f32[3,2,32,256]{3,2,1,0:T(8,128)S(1)} %copy-done, f32[4,32,256]{2,1,0:T(8,128)S(1)} %collective-permute-done.inner_ref, f32[4,32,256]{2,1,0:T(8,128)S(1)} %collective-permute-done.1.outer_ref, f32[2,32,256]{2,1,0:T(8,128)S(1)} %copy-done.1, f32[24,24]{1,0:T(8,128)S(1)} %copy-done.3), custom_call_target="tpu_custom_call" | custom-call | flops 1999999991808 | bytes 700000 | tf_op jit(solution)/shard_map/pallas_call | solution.py:471
  14.4 0.0 copy-start.4
  14.4 12.9 %all-to-all-done.refs_0_ = f32[8,120,128]{2,1,0:T(8,128)} async-done(((f32[8,120,128]{2,1,0:T(8,128)}), f32[8,120,128]{2,1,0:T(8,128)}, u32[]{:S(2)}, u32[]{:S(2)}) %all-to-all-start) | async-done | bytes 491552 | tf_op jit(solution)/shard_map/all_to_all | solution.py:468
  27.3 0.0 copy-done.2
  27.3 0.0 copy-done.4
  27.3 2.9 %shard_map.129 = f32[3,2,32,256]{3,2,1,0:T(8,128)} custom-call(f32[8,120,128]{2,1,0:T(8,128)} %all-to-all-done.refs_0_, f32[24,256]{1,0:T(8,128)S(1)} %get-tuple-element.16.refs_1_, f32[136,256]{1,0:T(8,128)S(1)} %get-tuple-element.17.refs_2_, f32[104,256]{1,0:T(8,128)S(1)} %get-tuple-element.18.refs_3_, s32[1,256]{1,0:T(1,128)S(1)} %get-tuple-element.19.refs_4_, ...), custom_call_target="tpu_custom_call" | custom-call | flops 900000000 | bytes 1500000 | tf_op jit(solution)/shard_map/pallas_call | solution.py:474
Async XLA Ops:
  3.2 10.1 %collective-permute-start = (f32[4,32,256]{2,1,0:T(8,128)S(1)}, f32[4,32,256]{2,1,0:T(8,128)S(1)}, u32[]{:S(2)}, u32[]{:S(2)}) collective-permute-start(f32[4,32,256]{2,1,0:T(8,128)S(1)} %get-tuple-element.23), channel_id=1, source_target_pairs={{0,1},{1,0},{2,3},{3,2},{4,5},{5,4},{6,7},{7,6},{8,9},{9,8},{10,11... | collective-permute-start | bytes 393224 | tf_op jit(solution)/shard_map/ppermute | solution.py:384
  3.7 9.5 %collective-permute-start.1 = (f32[4,32,256]{2,1,0:T(8,128)S(1)}, f32[4,32,256]{2,1,0:T(8,128)S(1)}, u32[]{:S(2)}, u32[]{:S(2)}) collective-permute-start(f32[4,32,256]{2,1,0:T(8,128)S(1)} %get-tuple-element.24), channel_id=1, source_target_pairs={{1,2},{2,1},{3,4},{4,3},{5,6},{6,5},{7,8},{8,7},{9,10},{10,9},{11,... | collective-permute-start | bytes 393224 | tf_op jit(solution)/shard_map/ppermute | solution.py:384
  4.3 8.9 %copy-start = (f32[3,2,32,256]{3,2,1,0:T(8,128)S(1)}, f32[3,2,32,256]{3,2,1,0:T(8,128)}, u32[]{:S(2)}) copy-start(f32[3,2,32,256]{3,2,1,0:T(8,128)} %disp_ref.1) | copy-start | bytes 589828
  4.4 8.9 %copy-start.1 = (f32[2,32,256]{2,1,0:T(8,128)S(1)}, f32[2,32,256]{2,1,0:T(8,128)}, u32[]{:S(2)}) copy-start(f32[2,32,256]{2,1,0:T(8,128)} %modulus_ref.1) | copy-start | bytes 196612
  4.4 8.9 %copy-start.3 = (f32[24,24]{1,0:T(8,128)S(1)}, f32[24,24]{1,0:T(8,128)}, u32[]{:S(2)}) copy-start(f32[24,24]{1,0:T(8,128)} %stiffness_ref.1) | copy-start | bytes 6916
  4.4 22.9 %all-to-all-start = ((f32[8,120,128]{2,1,0:T(8,128)}), f32[8,120,128]{2,1,0:T(8,128)}, u32[]{:S(2)}, u32[]{:S(2)}) async-start(f32[8,120,128]{2,1,0:T(8,128)} %get-tuple-element.15), calls=%async_computation | async-start | bytes 983040 | tf_op jit(solution)/shard_map/all_to_all | solution.py:468
  13.3 14.1 %copy-start.2 = (f32[2,32,256]{2,1,0:T(8,128)S(1)}, f32[2,32,256]{2,1,0:T(8,128)}, u32[]{:S(2)}) copy-start(f32[2,32,256]{2,1,0:T(8,128)} %refs_10_.3) | copy-start | bytes 196612
  14.4 12.9 %copy-start.4 = (s32[4,512]{1,0:T(4,128)S(1)}, s32[4,512]{1,0:T(4,128)}, u32[]{:S(2)}) copy-start(s32[4,512]{1,0:T(4,128)} %refs_7_.3) | copy-start | bytes 24580

commit v6 on v5

--- a/solution.py
+++ b/solution.py
@@ -85,12 +85,16 @@
     return jnp.concatenate([normal[k : k + 1] * loads for k in range(3)], axis=0)
 
 
+def place_in_group(domain, domains):
+    inner = domains // 4
+    return {0: inner, inner: 0}.get(domain, domain)
+
+
 def first_kernel(capacity, *refs):
     (
         nodes_hbm, disp_hbm, mortar_hbm, rank_hbm, face_hbm, count_hbm, weight_hbm, normal_hbm,
         gap_hbm, shape_hbm, modulus_hbm,
         sent_ref, rows_ref, words_ref, turned_ref, mortar_ref, rank_ref, face_ref, inner_ref, outer_ref,
-        marks_ref,
         nodes, disp, count, weight, normal_v, gap_v, shape, modulus, halved, blocks, sems, copy_sems,
     ) = refs
     components, layers, rows_y, cols_x = disp.shape
@@ -114,8 +118,7 @@
     strips = layers * rows_y
     brought[0].wait()
     indices = [nodes[corner : corner + 1, :] for corner in range(4)]
-    for corner in range(4):
-        marks_ref[corner] = marks(indices[corner] & (cols_x - 1), cols_x)
+    along_x = [marks(index & (cols_x - 1), cols_x) for index in indices]
 
     for copy in brought[2:5]:
         copy.wait()
@@ -134,7 +137,7 @@
     folds = face_count // cols_x
     for corner in range(4):
         strip = indices[corner] >> halves(cols_x)
-        found = summed(times(parts, marks_ref[corner])).reshape(components, strips, face_count)
+        found = summed(times(parts, along_x[corner])).reshape(components, strips, face_count)
         values = jnp.sum(jnp.where((numbers == strip)[None], found, 0.0), axis=1)
         for fold in range(folds):
             for k in range(components):
@@ -196,7 +199,9 @@
         blocks[domain] = block
         copies.append(
             pltpu.make_async_copy(
-                blocks.at[domain], sent_ref.at[domain, rows_high:], copy_sems.at[1, domain]
+                blocks.at[domain],
+                sent_ref.at[place_in_group(domain, domains), rows_high:],
+                copy_sems.at[1, domain],
             )
         )
         copies[-1].start()
@@ -212,7 +217,7 @@
 
 def last_kernel(
     capacity, got_ref, rows_ref, words_ref, turned_ref, mortar_ref, rank_ref, face_ref, nodes_ref,
-    marks_ref, internal_ref, mass_ref, out_ref,
+    internal_ref, mass_ref, out_ref,
 ):
     domains = got_ref.shape[0]
     components, layers, rows_y, cols_x = out_ref.shape
@@ -227,6 +232,8 @@
     own_rows = rows_ref[...]
 
     rank, face = rank_ref[...], face_ref[...]
+    inner = place_in_group(0, domains)
+    place = jnp.where(rank == 0, inner, jnp.where(rank == inner, 0, rank))
     at = marks(face & (cols_x - 1), cols_x)
     step = min(domains, 8)
 
@@ -242,7 +249,7 @@
         )
         found = summed(times(stacked_terms(block), at)).reshape(step, folded, pair_total)
         for i in range(step):
-            total = total + jnp.where(rank == turn * step + i, found[i], 0.0)
+            total = total + jnp.where(place == turn * step + i, found[i], 0.0)
         return total
 
     both = jnp.zeros((folded, pair_total), F32)
@@ -281,13 +288,14 @@
     numbers = lax.broadcasted_iota(jnp.int32, (strips, face_count), 0)
     for corner in range(4):
         index = nodes_ref[corner : corner + 1, :]
+        along_x = marks(index & (cols_x - 1), cols_x)
         strip = numbers == (index >> halves(cols_x))
         spread = []
         for part in parts:
             for k in range(components):
                 at = k * 4 + corner
                 spread.append(jnp.where(strip, part[at : at + 1], 0.0).astype(BF16))
-        total = total + times_turned(jnp.concatenate(spread, axis=0), marks_ref[corner])
+        total = total + times_turned(jnp.concatenate(spread, axis=0), along_x)
     contact = summed(total).reshape(components, layers, rows_y, cols_x)
     out_ref[...] = (internal_ref[...] + contact) / mass_ref[...][None]
 
@@ -439,7 +447,7 @@
     in_hbm = pl.BlockSpec(memory_space=pltpu.HBM)
     in_vmem = pl.BlockSpec(memory_space=pltpu.VMEM)
     kept = [face_nodes, displacement, *arrays[5:]]
-    sent, rows, words, turned, mortar, rank, face, inner, outer, along_x = on_core(
+    sent, rows, words, turned, mortar, rank, face, inner, outer = on_core(
         first,
         [
             shaped((domains, rows_high + height, LANES)),
@@ -451,12 +459,11 @@
             shaped(line, jnp.int32),
             edge,
             edge,
-            shaped((4, cols_x, face_count), BF16),
         ],
         900_000_000,
         1_500_000,
         in_specs=[in_hbm] * len(arrays),
-        out_specs=[in_hbm] + [in_vmem] * 9,
+        out_specs=[in_hbm] + [in_vmem] * 8,
         scratch_shapes=[pltpu.VMEM(x.shape, x.dtype) for x in kept]
         + [
             pltpu.VMEM((rows_high, LANES), F32),
@@ -465,14 +472,17 @@
             pltpu.SemaphoreType.DMA((2, domains)),
         ],
     )(*[pltpu.with_memory_space_constraint(x, pltpu.HBM) for x in arrays])
-    got = lax.all_to_all(sent, "dom", split_axis=0, concat_axis=0, tiled=True)
+    order = [place_in_group(domain, domains) for domain in range(domains)]
+    got = lax.all_to_all(
+        sent, "dom", split_axis=0, concat_axis=0, axis_index_groups=[order], tiled=True
+    )
     outer = swapped(outer, ("dom", "sub"), 1)
     inner = swapped(inner, ("dom", "sub"), 0)
     internal = on_core(
-        internal_kernel, shaped(displacement.shape), 2_000_000_000_000, 700_000
+        internal_kernel, shaped(displacement.shape), 1_500_000_000, 700_000
     )(displacement, inner, outer, modulus, stiffness)
     return on_core(last, shaped(displacement.shape), 900_000_000, 1_500_000)(
-        got, rows, words, turned, mortar, rank, face, face_nodes, along_x, internal, node_mass
+        got, rows, words, turned, mortar, rank, face, face_nodes, internal, node_mass
     )
 
 

time: 30.5 us -> 26.5 us (0.87)
  the two profiles are of different devices: /device:TPU:0 before, /device:TPU:16 now
where the time goes in v6:
time: 26.5 us; the launch traced here: 26.1 us
  waiting for transfers between devices  10 us (38%)
  starting transfers between devices  8.99 us (34%)
  Pallas kernels  6.26 us (24%)
  local copies, waits for them, and re-layouts  0.69 us (3%)
    ppermute x2, waiting for transfers between devices, swapped(): return lax.ppermute(block, axis, route)  10 us
    all_to_all x1, starting transfers between devices, shards(): lax.all_to_all(sent, 'dom', split_axis=0, concat_axis=0, axis_index_group...  5.38 us
    ppermute x2, starting transfers between devices, swapped(): return lax.ppermute(block, axis, route)  3.6 us
    pallas_call x1, Pallas kernels, shards(): on_core(first, [shaped((domains, rows_high + height, LANES)), shaped((12...  3.23 us
    pallas_call x1, Pallas kernels, shards(): on_core(last, shaped(displacement.shape), 900000000, 1500000)  1.89 us
    pallas_call x1, Pallas kernels, shards(): on_core(internal_kernel, shaped(displacement.shape), 1500000000, 700000)  1.14 us
    unnamed x10, local copies, waits for them, and re-layouts  0.69 us
  transfers between devices with their start and end apart: 3, of which 1 were waited for; matrix products, arithmetic and copies ran while one was open for 0% of the time, Pallas kernels for 4%

profile of v6, /device:TPU:16, one launch (start us, length us, event | category | flops | bytes accessed | tf_op | source)
XLA Modules:
  0.0 26.1 jit_solution(15351587113280243583)
XLA Ops:
  0.0 3.2 %shard_map.127 = (f32[8,120,128]{2,1,0:T(8,128)}, f32[24,256]{1,0:T(8,128)S(1)}, f32[136,256]{1,0:T(8,128)S(1)}, f32[104,256]{1,0:T(8,128)S(1)}, s32[1,256]{1,0:...) custom-call(s32[4,512]{1,0:T(4,128)} %refs_7_.3, ...), custom_call_target="tpu_custom_call" | custom-call | flops 900000000 | bytes 1500000 | tf_op jit(solution)/shard_map/pallas_call | solution.py:450
  3.2 0.0 copy-start
  3.3 0.0 copy-start.1
  3.3 0.0 copy-start.3
  3.3 5.4 %all-to-all-start = ((f32[8,120,128]{2,1,0:T(8,128)}), f32[8,120,128]{2,1,0:T(8,128)S(1)}, u32[]{:S(2)}, u32[]{:S(2)}) async-start(f32[8,120,128]{2,1,0:T(8,128)} %get-tuple-element.14), calls=%async_computation | async-start | bytes 983040 | tf_op jit(solution)/shard_map/all_to_all | solution.py:476
  8.7 0.0 collective-permute-start
  8.7 0.0 copy-start.2
  8.7 3.6 %collective-permute-start.1 = (f32[4,32,256]{2,1,0:T(8,128)S(1)}, f32[4,32,256]{2,1,0:T(8,128)S(1)}, u32[]{:S(2)}, u32[]{:S(2)}) collective-permute-start(f32[4,32,256]{2,1,0:T(8,128)S(1)} %get-tuple-element.22), channel_id=1, source_target_pairs={{1,2},{2,1},{3,4},{4,3},{5,6},{6,5},{7,8},{8,7},{9,10},{10,9},{11,... | collective-permute-start | bytes 393224 | tf_op jit(solution)/shard_map/ppermute | solution.py:392
  12.3 0.0 collective-permute-done.inner_ref
  12.3 10.0 %collective-permute-done.1.outer_ref = f32[4,32,256]{2,1,0:T(8,128)S(1)} collective-permute-done((f32[4,32,256]{2,1,0:T(8,128)S(1)}, f32[4,32,256]{2,1,0:T(8,128)S(1)}, u32[]{:S(2)}, u32[]{:S(2)}) %collective-permute-start.1) | collective-permute-done | bytes 131104 | tf_op jit(solution)/shard_map/ppermute | solution.py:392
  22.3 0.0 copy-done
  22.3 0.0 copy-done.1
  22.3 0.0 copy-done.3
  22.3 1.1 %shard_map.128.refs_8_ = f32[3,2,32,256]{3,2,1,0:T(8,128)S(1)} custom-call(f32[3,2,32,256]{3,2,1,0:T(8,128)S(1)} %copy-done, f32[4,32,256]{2,1,0:T(8,128)S(1)} %collective-permute-done.inner_ref, f32[4,32,256]{2,1,0:T(8,128)S(1)} %collective-permute-done.1.outer_ref, f32[2,32,256]{2,1,0:T(8,128)S(1)} %copy-done.1, f32[24,24]{1,0:T(8,128)S(1)} %copy-done.3), custom_call_target="tpu_custom_call" | custom-call | flops 1500000000 | bytes 700000 | tf_op jit(solution)/shard_map/pallas_call | solution.py:481
  23.5 0.0 copy-start.4
  23.5 0.0 all-to-all-done.refs_0_
  23.5 0.0 copy-done.2
  23.5 0.7 %copy-done.4 = s32[4,512]{1,0:T(4,128)S(1)} copy-done((s32[4,512]{1,0:T(4,128)S(1)}, s32[4,512]{1,0:T(4,128)}, u32[]{:S(2)}) %copy-start.4) | copy-done | bytes 8216
  24.2 1.9 %shard_map.129 = f32[3,2,32,256]{3,2,1,0:T(8,128)} custom-call(f32[8,120,128]{2,1,0:T(8,128)S(1)} %all-to-all-done.refs_0_, f32[24,256]{1,0:T(8,128)S(1)} %get-tuple-element.15.refs_1_, f32[136,256]{1,0:T(8,128)S(1)} %get-tuple-element.16.refs_2_, f32[104,256]{1,0:T(8,128)S(1)} %get-tuple-element.17.refs_3_, s32[1,256]{1,0:T(1,128)S(1)} %get-tuple-element.18.refs_4_, ...), custom_call_target="tpu_custom_call" | custom-call | flops 900000000 | bytes 1500000 | tf_op jit(solution)/shard_map/pallas_call | solution.py:484
Async XLA Ops:
  3.2 19.1 %copy-start = (f32[3,2,32,256]{3,2,1,0:T(8,128)S(1)}, f32[3,2,32,256]{3,2,1,0:T(8,128)}, u32[]{:S(2)}) copy-start(f32[3,2,32,256]{3,2,1,0:T(8,128)} %disp_ref.1) | copy-start | bytes 589828
  3.3 19.1 %copy-start.1 = (f32[2,32,256]{2,1,0:T(8,128)S(1)}, f32[2,32,256]{2,1,0:T(8,128)}, u32[]{:S(2)}) copy-start(f32[2,32,256]{2,1,0:T(8,128)} %modulus_ref.1) | copy-start | bytes 196612
  3.3 19.1 %copy-start.3 = (f32[24,24]{1,0:T(8,128)S(1)}, f32[24,24]{1,0:T(8,128)}, u32[]{:S(2)}) copy-start(f32[24,24]{1,0:T(8,128)} %stiffness_ref.1) | copy-start | bytes 6916
  3.3 20.2 %all-to-all-start = ((f32[8,120,128]{2,1,0:T(8,128)}), f32[8,120,128]{2,1,0:T(8,128)S(1)}, u32[]{:S(2)}, u32[]{:S(2)}) async-start(f32[8,120,128]{2,1,0:T(8,128)} %get-tuple-element.14), calls=%async_computation | async-start | bytes 983040 | tf_op jit(solution)/shard_map/all_to_all | solution.py:476
  8.7 3.6 %collective-permute-start = (f32[4,32,256]{2,1,0:T(8,128)S(1)}, f32[4,32,256]{2,1,0:T(8,128)S(1)}, u32[]{:S(2)}, u32[]{:S(2)}) collective-permute-start(f32[4,32,256]{2,1,0:T(8,128)S(1)} %get-tuple-element.21), channel_id=1, source_target_pairs={{0,1},{1,0},{2,3},{3,2},{4,5},{5,4},{6,7},{7,6},{8,9},{9,8},{10,11... | collective-permute-start | bytes 393224 | tf_op jit(solution)/shard_map/ppermute | solution.py:392
  8.7 14.8 %copy-start.2 = (f32[2,32,256]{2,1,0:T(8,128)S(1)}, f32[2,32,256]{2,1,0:T(8,128)}, u32[]{:S(2)}) copy-start(f32[2,32,256]{2,1,0:T(8,128)} %refs_9_.1) | copy-start | bytes 196612
  8.7 13.6 %collective-permute-start.1 = (f32[4,32,256]{2,1,0:T(8,128)S(1)}, f32[4,32,256]{2,1,0:T(8,128)S(1)}, u32[]{:S(2)}, u32[]{:S(2)}) collective-permute-start(f32[4,32,256]{2,1,0:T(8,128)S(1)} %get-tuple-element.22), channel_id=1, source_target_pairs={{1,2},{2,1},{3,4},{4,3},{5,6},{6,5},{7,8},{8,7},{9,10},{10,9},{11,... | collective-permute-start | bytes 393224 | tf_op jit(solution)/shard_map/ppermute | solution.py:392
  23.5 0.7 %copy-start.4 = (s32[4,512]{1,0:T(4,128)S(1)}, s32[4,512]{1,0:T(4,128)}, u32[]{:S(2)}) copy-start(s32[4,512]{1,0:T(4,128)} %refs_7_.3) | copy-start | bytes 24580

commit v7 on v6

--- a/solution.py
+++ b/solution.py
@@ -86,24 +86,25 @@
 
 
 def place_in_group(domain, domains):
-    inner = domains // 4
-    return {0: inner, inner: 0}.get(domain, domain)
+    return {0: domains - 1, domains - 1: 0}.get(domain, domain)
 
 
 def first_kernel(capacity, *refs):
     (
         nodes_hbm, disp_hbm, mortar_hbm, rank_hbm, face_hbm, count_hbm, weight_hbm, normal_hbm,
-        gap_hbm, shape_hbm, modulus_hbm,
-        sent_ref, rows_ref, words_ref, turned_ref, mortar_ref, rank_ref, face_ref, inner_ref, outer_ref,
-        nodes, disp, count, weight, normal_v, gap_v, shape, modulus, halved, blocks, sems, copy_sems,
+        gap_hbm, shape_hbm, modulus_hbm, mass_hbm,
+        sent_ref, rows_ref, words_ref, turned_ref, mortar_ref, rank_ref, face_ref, nodes, mass_ref,
+        inner_ref, outer_ref,
+        disp, count, weight, normal_v, gap_v, shape, modulus, halved, blocks, sems, copy_sems,
     ) = refs
     components, layers, rows_y, cols_x = disp.shape
     sources = (
-        nodes_hbm, disp_hbm, rank_hbm, face_hbm, mortar_hbm, count_hbm, weight_hbm, normal_hbm,
-        gap_hbm, shape_hbm, modulus_hbm,
+        nodes_hbm, disp_hbm, rank_hbm, face_hbm, mortar_hbm, shape_hbm, count_hbm, weight_hbm,
+        normal_hbm, gap_hbm, modulus_hbm, mass_hbm,
     )
     targets = (
-        nodes, disp, rank_ref, face_ref, mortar_ref, count, weight, normal_v, gap_v, shape, modulus,
+        nodes, disp, rank_ref, face_ref, mortar_ref, shape, count, weight, normal_v, gap_v, modulus,
+        mass_ref,
     )
     brought = [
         pltpu.make_async_copy(source, target, sems.at[i])
@@ -116,12 +117,11 @@
     pair_total = rank_ref.shape[1]
     face_count = nodes.shape[1]
     strips = layers * rows_y
-    brought[0].wait()
+    for copy in brought[:-2]:
+        copy.wait()
     indices = [nodes[corner : corner + 1, :] for corner in range(4)]
     along_x = [marks(index & (cols_x - 1), cols_x) for index in indices]
 
-    for copy in brought[2:5]:
-        copy.wait()
     rank, face, mortar = rank_ref[...], face_ref[...], mortar_ref[...]
     chosen = lax.broadcasted_iota(jnp.int32, (domains, pair_total), 0) == rank
     before = lax.broadcasted_iota(jnp.int32, (pair_total, pair_total), 0) < lax.broadcasted_iota(
@@ -131,7 +131,6 @@
     slot = jnp.sum(jnp.where(chosen, earlier, 0.0), axis=0, keepdims=True).astype(jnp.int32)
     place = marks(rank * capacity + slot, domains * capacity)
 
-    brought[1].wait()
     parts = stacked_terms(disp[...].reshape(components * strips, cols_x))
     numbers = lax.broadcasted_iota(jnp.int32, (strips, face_count), 0)
     folds = face_count // cols_x
@@ -158,8 +157,6 @@
         )
         copies[-1].start()
 
-    for copy in brought[5:]:
-        copy.wait()
     mortar_rows = looked_up(rows, mortar, cols_x)
     normal = normal_v[...]
     gap = gap_v[...]
@@ -206,6 +203,8 @@
         )
         copies[-1].start()
 
+    for copy in brought[-2:]:
+        copy.wait()
     sub = lax.axis_index("sub")
     for target, layer in ((inner_ref, (1 - sub) * (layers - 1)), (outer_ref, sub * (layers - 1))):
         for k in range(components):
@@ -217,7 +216,7 @@
 
 def last_kernel(
     capacity, got_ref, rows_ref, words_ref, turned_ref, mortar_ref, rank_ref, face_ref, nodes_ref,
-    internal_ref, mass_ref, out_ref,
+    mass_ref, internal_ref, blocks_ref, own_ref, halo_ref, out_ref,
 ):
     domains = got_ref.shape[0]
     components, layers, rows_y, cols_x = out_ref.shape
@@ -232,8 +231,8 @@
     own_rows = rows_ref[...]
 
     rank, face = rank_ref[...], face_ref[...]
-    inner = place_in_group(0, domains)
-    place = jnp.where(rank == 0, inner, jnp.where(rank == inner, 0, rank))
+    end = domains - 1
+    place = jnp.where(rank == 0, end, jnp.where(rank == end, 0, rank))
     at = marks(face & (cols_x - 1), cols_x)
     step = min(domains, 8)
 
@@ -297,81 +296,100 @@
                 spread.append(jnp.where(strip, part[at : at + 1], 0.0).astype(BF16))
         total = total + times_turned(jnp.concatenate(spread, axis=0), along_x)
     contact = summed(total).reshape(components, layers, rows_y, cols_x)
-    out_ref[...] = (internal_ref[...] + contact) / mass_ref[...][None]
-
-
-def internal_kernel(
-    disp_ref, inner_ref, outer_ref, modulus_ref, stiffness_ref, out_ref
-):
+    upward = lax.axis_index("sub") == 1
+    edge = edge_part(upward, own_ref, halo_ref, blocks_ref)
+    at = jnp.where(upward, layers - 1, 0)
+    for layer in range(layers):
+        for k in range(components):
+            nodal = internal_ref[k, layer] + jnp.where(at == layer, edge[k], 0.0)
+            out_ref[k, layer] = (nodal + contact[k, layer]) / mass_ref[layer]
+
+
+GROUP = 8
+
+
+def shifted(layer):
+    views = []
+    for part in layer:
+        rows_y, cols_x = part.shape
+        for moved in (part, pltpu.roll(part, rows_y - 1, 0)):
+            views += [moved, pltpu.roll(moved, cols_x - 1, 1)]
+    return views
+
+
+def element_forces(matrices, low, high, modulus):
+    rows_y, cols_x = modulus.shape
+    inside = (lax.broadcasted_iota(jnp.int32, (rows_y, cols_x), 0) < rows_y - 1) & (
+        lax.broadcasted_iota(jnp.int32, (rows_y, cols_x), 1) < cols_x - 1
+    )
+    scale = jnp.where(inside, modulus, 0.0)
+    views = shifted(low) + shifted(high)
+    both = jnp.concatenate(matrices, axis=0)
+    count = both.shape[0] // 2
+    strips = []
+    for y in range(0, rows_y, GROUP):
+        leading, second = terms_of(jnp.concatenate([view[y : y + GROUP] for view in views], axis=0), 2)
+        found = times(both, leading)
+        force = found[:count] + (found[count:] + times(matrices[0], second))
+        strips.append(force.reshape(-1, GROUP, cols_x) * scale[y : y + GROUP][None])
+    return jnp.concatenate(strips, axis=1)
+
+
+def on_nodes(forces):
+    sums = []
+    for k in range(forces.shape[0] // 4):
+        straight, crossed = [
+            forces[k * 4 + c] + pltpu.roll(forces[k * 4 + 2 + c], 1, 0) for c in range(2)
+        ]
+        sums.append(-(straight + pltpu.roll(crossed, 1, 1)))
+    return sums
+
+
+def edge_part(upward, own_ref, halo_ref, blocks_ref):
+    components = own_ref.shape[0] - 1
+    size = blocks_ref.shape[1]
+    rows = size // 2
+    start = jnp.where(upward, 0, rows)
+    matrices = [
+        blocks_ref[pl.ds(pl.multiple_of(term * size + start, 16), rows)] for term in range(2)
+    ]
+    low = [jnp.where(upward, own_ref[k], halo_ref[k]) for k in range(components + 1)]
+    high = [jnp.where(upward, halo_ref[k], own_ref[k]) for k in range(components)]
+    return on_nodes(element_forces(matrices, low[:components], high, low[components]))
+
+
+def internal_kernel(disp_ref, modulus_ref, stiffness_ref, own_ref, halo_ref, out_ref, blocks_ref):
     components, layers, rows_y, cols_x = disp_ref.shape
-    group = 8
     dofs = 8 * components
     half = dofs // 2
-
-    row = lax.broadcasted_iota(jnp.int32, (dofs * group, dofs), 0) >> halves(group)
+    size = dofs * GROUP
+
+    row = lax.broadcasted_iota(jnp.int32, (size, dofs), 0) >> halves(GROUP)
     upper = (row >= half).astype(jnp.int32)
     inner = row - half * upper
     dof = (inner >> 2) * 8 + upper * 4 + (inner & 3)
-    pick = (dof == lax.broadcasted_iota(jnp.int32, (dofs * group, dofs), 1)).astype(F32).astype(BF16)
-    size = dofs * group
-    diagonal = (lax.broadcasted_iota(jnp.int32, (size, size), 0) & (group - 1)) == (
-        lax.broadcasted_iota(jnp.int32, (size, size), 1) & (group - 1)
-    )
-    blocks = []
-    for term in terms_of(stiffness_ref[...], 2):
+    pick = (dof == lax.broadcasted_iota(jnp.int32, (size, dofs), 1)).astype(F32).astype(BF16)
+    diagonal = (lax.broadcasted_iota(jnp.int32, (size, size), 0) & (GROUP - 1)) == (
+        lax.broadcasted_iota(jnp.int32, (size, size), 1) & (GROUP - 1)
+    )
+    for i, term in enumerate(terms_of(stiffness_ref[...], 2)):
         wide = times_turned(times(pick, term).astype(BF16), pick)
-        blocks.append(jnp.where(diagonal, wide, 0.0).astype(BF16))
-
-    sub = lax.axis_index("sub")
-    below_ref = [jnp.where(sub == 0, outer_ref[k], inner_ref[k]) for k in range(components + 1)]
-    above_ref = [jnp.where(sub == 0, inner_ref[k], outer_ref[k]) for k in range(components)]
-
-    def shifted(layer):
-        views = []
+        blocks_ref[i * size : (i + 1) * size] = jnp.where(diagonal, wide, 0.0).astype(BF16)
+
+    blocks = [blocks_ref[i * size : (i + 1) * size] for i in range(2)]
+    sums = [[0.0] * components for _ in range(layers)]
+    for e in range(layers - 1):
+        pair = [[disp_ref[k, e + a] for k in range(components)] for a in range(2)]
+        forces = element_forces(blocks, pair[0], pair[1], modulus_ref[e])
+        for a in range(2):
+            part = on_nodes(forces[a * half : (a + 1) * half])
+            sums[e + a] = [x + y for x, y in zip(sums[e + a], part)]
+    upward = lax.axis_index("sub") == 0
+    edge = edge_part(upward, own_ref, halo_ref, blocks_ref)
+    at = jnp.where(upward, layers - 1, 0)
+    for layer in range(layers):
         for k in range(components):
-            for b in range(2):
-                moved = layer[k] if b == 0 else pltpu.roll(layer[k], rows_y - 1, 0)
-                views.append(moved)
-                views.append(pltpu.roll(moved, cols_x - 1, 1))
-        return views
-
-    views = [shifted(below_ref)]
-    for layer in range(layers):
-        views.append(shifted([disp_ref[k, layer] for k in range(components)]))
-    views.append(shifted(above_ref))
-    inside = (lax.broadcasted_iota(jnp.int32, (rows_y, cols_x), 0) < rows_y - 1) & (
-        lax.broadcasted_iota(jnp.int32, (rows_y, cols_x), 1) < cols_x - 1
-    )
-    scales = [below_ref[components]] + [modulus_ref[layer] for layer in range(layers)]
-    scales = [jnp.where(inside, scale, 0.0) for scale in scales]
-
-    lower, higher = [], []
-    for e in range(layers + 1):
-        kept = slice(half * group, None) if e == 0 else slice(0, half * group if e == layers else None)
-        both = jnp.concatenate([block[kept] for block in blocks], axis=0)
-        count = both.shape[0] // 2
-        strips = []
-        for y in range(0, rows_y, group):
-            stacked = jnp.concatenate(
-                [view[y : y + group] for view in views[e] + views[e + 1]], axis=0
-            )
-            high, low = terms_of(stacked, 2)
-            leading = times(both, high)
-            force = leading[:count] + (leading[count:] + times(both[:count], low))
-            force = force.reshape(-1, group, cols_x) * scales[e][y : y + group][None]
-            strips.append(force)
-        forces = jnp.concatenate(strips, axis=1)
-        if e < layers:
-            higher.append(forces[-half:])
-        if e > 0:
-            lower.append(forces[:half])
-    for layer in range(layers):
-        nodal = lower[layer] + higher[layer]
-        for k in range(components):
-            straight, crossed = [
-                nodal[k * 4 + c] + pltpu.roll(nodal[k * 4 + 2 + c], 1, 0) for c in range(2)
-            ]
-            out_ref[k, layer] = -(straight + pltpu.roll(crossed, 1, 1))
+            out_ref[k, layer] = sums[layer][k] + jnp.where(at == layer, edge[k], 0.0)
 
 
 def on_core(kernel, outs, flops, moved, **more):
@@ -442,12 +460,13 @@
         pair_gap,
         jnp.swapaxes(pair_shape, 0, 1),
         modulus,
+        node_mass,
     ]
     edge = shaped((components + 1, rows_y, cols_x))
     in_hbm = pl.BlockSpec(memory_space=pltpu.HBM)
     in_vmem = pl.BlockSpec(memory_space=pltpu.VMEM)
-    kept = [face_nodes, displacement, *arrays[5:]]
-    sent, rows, words, turned, mortar, rank, face, inner, outer = on_core(
+    kept = [displacement, *arrays[5:-1]]
+    sent, rows, words, turned, mortar, rank, face, nodes, mass, inner, outer = on_core(
         first,
         [
             shaped((domains, rows_high + height, LANES)),
@@ -457,13 +476,15 @@
             shaped(line, jnp.int32),
             shaped(line, jnp.int32),
             shaped(line, jnp.int32),
+            shaped(face_nodes.shape, jnp.int32),
+            shaped(node_mass.shape),
             edge,
             edge,
         ],
         900_000_000,
         1_500_000,
         in_specs=[in_hbm] * len(arrays),
-        out_specs=[in_hbm] + [in_vmem] * 8,
+        out_specs=[in_hbm] + [in_vmem] * 10,
         scratch_shapes=[pltpu.VMEM(x.shape, x.dtype) for x in kept]
         + [
             pltpu.VMEM((rows_high, LANES), F32),
@@ -476,13 +497,17 @@
     got = lax.all_to_all(
         sent, "dom", split_axis=0, concat_axis=0, axis_index_groups=[order], tiled=True
     )
-    outer = swapped(outer, ("dom", "sub"), 1)
-    inner = swapped(inner, ("dom", "sub"), 0)
-    internal = on_core(
-        internal_kernel, shaped(displacement.shape), 1_500_000_000, 700_000
-    )(displacement, inner, outer, modulus, stiffness)
-    return on_core(last, shaped(displacement.shape), 900_000_000, 1_500_000)(
-        got, rows, words, turned, mortar, rank, face, face_nodes, internal, node_mass
+    inner_halo = swapped(inner, ("dom", "sub"), 0)
+    outer_halo = swapped(outer, ("dom", "sub"), 1)
+    size = 8 * components * GROUP
+    internal, blocks = on_core(
+        internal_kernel,
+        [shaped(displacement.shape), shaped((2 * size, size), BF16)],
+        1_000_000_000,
+        700_000,
+    )(displacement, modulus, stiffness, inner, inner_halo)
+    return on_core(last, shaped(displacement.shape), 1_000_000_000, 1_500_000)(
+        got, rows, words, turned, mortar, rank, face, nodes, mass, internal, blocks, outer, outer_halo
     )
 
 

time: 26.5 us -> 25.7 us (0.970)
  local copies, waits for them, and re-layouts: 0.69 us -> 0.02 us
  waiting for transfers between devices: 10 us -> 9.46 us
  starting transfers between devices: 8.99 us -> 9.52 us
    unnamed x10 -> x6, local copies, waits for them, and re-layouts: 0.69 us -> 0.02 us
    all_to_all x1, starting transfers between devices: 5.38 us -> 6.05 us  [shards(): lax.all_to_all(sent, 'dom', split_axis=0, concat_axis=0, axis_index_group...]
    ppermute x2, waiting for transfers between devices: 10 us -> 9.46 us  [swapped(): return lax.ppermute(block, axis, route)]
where the time goes in v7:
time: 25.7 us; the launch traced here: 25.4 us
  starting transfers between devices  9.52 us (37%)
  waiting for transfers between devices  9.46 us (37%)
  Pallas kernels  6.3 us (25%)
    ppermute x2, waiting for transfers between devices, swapped(): return lax.ppermute(block, axis, route)  9.46 us
    all_to_all x1, starting transfers between devices, shards(): lax.all_to_all(sent, 'dom', split_axis=0, concat_axis=0, axis_index_group...  6.05 us
    ppermute x2, starting transfers between devices, swapped(): return lax.ppermute(block, axis, route)  3.47 us
    pallas_call x1, Pallas kernels, shards(): on_core(first, [shaped((domains, rows_high + height, LANES)), shaped((12...  3.14 us
    pallas_call x1, Pallas kernels, shards(): on_core(last, shaped(displacement.shape), 1000000000, 1500000)  2.14 us
    pallas_call x1, Pallas kernels, shards(): on_core(internal_kernel, [shaped(displacement.shape), shaped((2 * size, s...  1.03 us
  transfers between devices with their start and end apart: 3, of which 1 were waited for; matrix products, arithmetic and copies ran while one was open for 0% of the time, Pallas kernels for 4%

profile of v7, /device:TPU:16, one launch (start us, length us, event | category | flops | bytes accessed | tf_op | source)
XLA Modules:
  0.0 25.4 jit_solution(10900874848321925428)
XLA Ops:
  0.0 3.1 %shard_map.127 = (f32[8,120,128]{2,1,0:T(8,128)}, f32[24,256]{1,0:T(8,128)S(1)}, f32[136,256]{1,0:T(8,128)S(1)}, f32[104,256]{1,0:T(8,128)S(1)}, s32[1,256]{1,0:...) custom-call(s32[4,512]{1,0:T(4,128)} %refs_0_.1, ...), custom_call_target="tpu_custom_call" | custom-call | flops 900000000 | bytes 1500000 | tf_op jit(solution)/shard_map/pallas_call | solution.py:469
  3.1 0.0 copy-start
  3.2 0.0 copy-start.1
  3.2 0.0 copy-start.2
  3.2 6.1 %all-to-all-start = ((f32[8,120,128]{2,1,0:T(8,128)}), f32[8,120,128]{2,1,0:T(8,128)S(1)}, u32[]{:S(2)}, u32[]{:S(2)}) async-start(f32[8,120,128]{2,1,0:T(8,128)} %get-tuple-element.18), calls=%async_computation | async-start | bytes 983040 | tf_op jit(solution)/shard_map/all_to_all | solution.py:497
  9.2 0.0 collective-permute-start
  9.2 3.5 %collective-permute-start.1 = (f32[4,32,256]{2,1,0:T(8,128)S(1)}, f32[4,32,256]{2,1,0:T(8,128)S(1)}, u32[]{:S(2)}, u32[]{:S(2)}) collective-permute-start(f32[4,32,256]{2,1,0:T(8,128)S(1)} %get-tuple-element.30.refs_11_), channel_id=1, source_target_pairs={{1,2},{2,1},{3,4},{4,3},{5,6},{6,5},{7,8},{8,7},{9,10},{10,9},{11,... | collective-permute-start | bytes 393224 | tf_op jit(solution)/shard_map/ppermute | solution.py:410
  12.7 0.0 collective-permute-done.halo_ref
  12.7 0.0 copy-done
  12.7 0.0 copy-done.1
  12.7 0.0 copy-done.2
  12.8 1.0 %shard_map.128 = (f32[3,2,32,256]{3,2,1,0:T(8,128)S(1)}, bf16[384,192]{1,0:T(8,128)(2,1)S(1)}) custom-call(f32[3,2,32,256]{3,2,1,0:T(8,128)S(1)} %copy-done, f32[2,32,256]{2,1,0:T(8,128)S(1)} %copy-done.1, f32[24,24]{1,0:T(8,128)S(1)} %copy-done.2, f32[4,32,256]{2,1,0:T(8,128)S(1)} %get-tuple-element.27.own_ref, f32[4,32,256]{2,1,0:T(8,128)S(1)} %collective-permute-done.halo_ref), custom_call_target="tpu_custom_call" | custom-call | flops 1000000000 | bytes 700000 | tf_op jit(solution)/shard_map/pallas_call | solution.py:503
  13.8 9.5 %collective-permute-done.1.refs_12_ = f32[4,32,256]{2,1,0:T(8,128)S(1)} collective-permute-done((f32[4,32,256]{2,1,0:T(8,128)S(1)}, f32[4,32,256]{2,1,0:T(8,128)S(1)}, u32[]{:S(2)}, u32[]{:S(2)}) %collective-permute-start.1) | collective-permute-done | bytes 131104 | tf_op jit(solution)/shard_map/ppermute | solution.py:410
  23.2 0.0 all-to-all-done.refs_0_
  23.2 2.1 %shard_map.129 = f32[3,2,32,256]{3,2,1,0:T(8,128)} custom-call(f32[8,120,128]{2,1,0:T(8,128)S(1)} %all-to-all-done.refs_0_, f32[24,256]{1,0:T(8,128)S(1)} %get-tuple-element.19.refs_1_, f32[136,256]{1,0:T(8,128)S(1)} %get-tuple-element.20.refs_2_, f32[104,256]{1,0:T(8,128)S(1)} %get-tuple-element.21.refs_3_, s32[1,256]{1,0:T(1,128)S(1)} %get-tuple-element.22.refs_4_, ...), custom_call_target="tpu_custom_call" | custom-call | flops 1000000000 | bytes 1500000 | tf_op jit(solution)/shard_map/pallas_call | solution.py:509
Async XLA Ops:
  3.1 9.6 %copy-start = (f32[3,2,32,256]{3,2,1,0:T(8,128)S(1)}, f32[3,2,32,256]{3,2,1,0:T(8,128)}, u32[]{:S(2)}) copy-start(f32[3,2,32,256]{3,2,1,0:T(8,128)} %disp_ref.1) | copy-start | bytes 589828
  3.2 9.6 %copy-start.1 = (f32[2,32,256]{2,1,0:T(8,128)S(1)}, f32[2,32,256]{2,1,0:T(8,128)}, u32[]{:S(2)}) copy-start(f32[2,32,256]{2,1,0:T(8,128)} %modulus_ref.1) | copy-start | bytes 196612
  3.2 9.6 %copy-start.2 = (f32[24,24]{1,0:T(8,128)S(1)}, f32[24,24]{1,0:T(8,128)}, u32[]{:S(2)}) copy-start(f32[24,24]{1,0:T(8,128)} %stiffness_ref.1) | copy-start | bytes 6916
  3.2 20.1 %all-to-all-start = ((f32[8,120,128]{2,1,0:T(8,128)}), f32[8,120,128]{2,1,0:T(8,128)S(1)}, u32[]{:S(2)}, u32[]{:S(2)}) async-start(f32[8,120,128]{2,1,0:T(8,128)} %get-tuple-element.18), calls=%async_computation | async-start | bytes 983040 | tf_op jit(solution)/shard_map/all_to_all | solution.py:497
  9.2 3.5 %collective-permute-start = (f32[4,32,256]{2,1,0:T(8,128)S(1)}, f32[4,32,256]{2,1,0:T(8,128)S(1)}, u32[]{:S(2)}, u32[]{:S(2)}) collective-permute-start(f32[4,32,256]{2,1,0:T(8,128)S(1)} %get-tuple-element.27.own_ref), channel_id=1, source_target_pairs={{0,1},{1,0},{2,3},{3,2},{4,5},{5,4},{6,7},{7,6},{8,9},{9,8},{10,11... | collective-permute-start | bytes 393224 | tf_op jit(solution)/shard_map/ppermute | solution.py:410
  9.2 14.0 %collective-permute-start.1 = (f32[4,32,256]{2,1,0:T(8,128)S(1)}, f32[4,32,256]{2,1,0:T(8,128)S(1)}, u32[]{:S(2)}, u32[]{:S(2)}) collective-permute-start(f32[4,32,256]{2,1,0:T(8,128)S(1)} %get-tuple-element.30.refs_11_), channel_id=1, source_target_pairs={{1,2},{2,1},{3,4},{4,3},{5,6},{6,5},{7,8},{8,7},{9,10},{10,9},{11,... | collective-permute-start | bytes 393224 | tf_op jit(solution)/shard_map/ppermute | solution.py:410

commit v8 on v7

--- a/solution.py
+++ b/solution.py
@@ -89,48 +89,28 @@
     return {0: domains - 1, domains - 1: 0}.get(domain, domain)
 
 
-def first_kernel(capacity, *refs):
-    (
-        nodes_hbm, disp_hbm, mortar_hbm, rank_hbm, face_hbm, count_hbm, weight_hbm, normal_hbm,
-        gap_hbm, shape_hbm, modulus_hbm, mass_hbm,
-        sent_ref, rows_ref, words_ref, turned_ref, mortar_ref, rank_ref, face_ref, nodes, mass_ref,
-        inner_ref, outer_ref,
-        disp, count, weight, normal_v, gap_v, shape, modulus, halved, blocks, sems, copy_sems,
-    ) = refs
+def first_kernel(passed, *refs):
+    nodes_hbm, disp_hbm, modulus_hbm, *refs = refs
+    ins, refs = refs[:passed], refs[passed:]
+    sent_ref, rows_ref, inner_ref, outer_ref, nodes, *refs = refs
+    outs, refs = refs[:passed], refs[passed:]
+    disp, modulus, sems, copy_sems = refs
     components, layers, rows_y, cols_x = disp.shape
-    sources = (
-        nodes_hbm, disp_hbm, rank_hbm, face_hbm, mortar_hbm, shape_hbm, count_hbm, weight_hbm,
-        normal_hbm, gap_hbm, modulus_hbm, mass_hbm,
-    )
-    targets = (
-        nodes, disp, rank_ref, face_ref, mortar_ref, shape, count, weight, normal_v, gap_v, modulus,
-        mass_ref,
-    )
+    sources = [nodes_hbm, disp_hbm, modulus_hbm, *ins]
     brought = [
         pltpu.make_async_copy(source, target, sems.at[i])
-        for i, (source, target) in enumerate(zip(sources, targets))
+        for i, (source, target) in enumerate(zip(sources, [nodes, disp, modulus, *outs]))
     ]
     for copy in brought:
         copy.start()
 
     domains = sent_ref.shape[0]
-    pair_total = rank_ref.shape[1]
     face_count = nodes.shape[1]
     strips = layers * rows_y
-    for copy in brought[:-2]:
-        copy.wait()
+    brought[0].wait()
     indices = [nodes[corner : corner + 1, :] for corner in range(4)]
     along_x = [marks(index & (cols_x - 1), cols_x) for index in indices]
-
-    rank, face, mortar = rank_ref[...], face_ref[...], mortar_ref[...]
-    chosen = lax.broadcasted_iota(jnp.int32, (domains, pair_total), 0) == rank
-    before = lax.broadcasted_iota(jnp.int32, (pair_total, pair_total), 0) < lax.broadcasted_iota(
-        jnp.int32, (pair_total, pair_total), 1
-    )
-    earlier = times(chosen.astype(F32).astype(BF16), before.astype(F32).astype(BF16))
-    slot = jnp.sum(jnp.where(chosen, earlier, 0.0), axis=0, keepdims=True).astype(jnp.int32)
-    place = marks(rank * capacity + slot, domains * capacity)
-
+    brought[1].wait()
     parts = stacked_terms(disp[...].reshape(components * strips, cols_x))
     numbers = lax.broadcasted_iota(jnp.int32, (strips, face_count), 0)
     folds = face_count // cols_x
@@ -142,44 +122,62 @@
             for k in range(components):
                 at = fold * 12 + k * 4 + corner
                 rows_ref[at : at + 1, :] = values[k : k + 1, fold * cols_x : (fold + 1) * cols_x]
-
-    rows = rows_ref[...]
-    high = rows.shape[0]
-    rows_high = high * cols_x // LANES
-    copies = []
-    for i in range(cols_x // LANES):
-        halved[i * high : (i + 1) * high] = rows[:, i * LANES : (i + 1) * LANES]
-    for domain in range(domains):
-        copies.append(
-            pltpu.make_async_copy(
-                halved, sent_ref.at[domain, :rows_high], copy_sems.at[0, domain]
-            )
-        )
-        copies[-1].start()
-
-    mortar_rows = looked_up(rows, mortar, cols_x)
-    normal = normal_v[...]
-    gap = gap_v[...]
+    copies = [
+        pltpu.make_async_copy(rows_ref, sent_ref.at[domain], copy_sems.at[domain])
+        for domain in range(domains)
+    ]
+    for copy in copies:
+        copy.start()
+
+    brought[2].wait()
+    sub = lax.axis_index("sub")
+    for target, layer in ((inner_ref, (1 - sub) * (layers - 1)), (outer_ref, sub * (layers - 1))):
+        for k in range(components):
+            target[k] = disp[k, layer]
+        target[components] = modulus[layer]
+    for copy in brought[3:] + copies:
+        copy.wait()
+
+
+def words_kernel(
+    capacity, rows_ref, mortar_ref, rank_ref, face_ref, count_ref, weight_ref, normal_ref, gap_ref,
+    shape_ref, sent_ref, words_ref, turned_ref,
+):
+    domains, height = sent_ref.shape[:2]
+    pair_total = rank_ref.shape[1]
+    cols_x = rows_ref.shape[1]
+    rank, face = rank_ref[...], face_ref[...]
+
+    chosen = lax.broadcasted_iota(jnp.int32, (domains, pair_total), 0) == rank
+    before = lax.broadcasted_iota(jnp.int32, (pair_total, pair_total), 0) < lax.broadcasted_iota(
+        jnp.int32, (pair_total, pair_total), 1
+    )
+    earlier = times(chosen.astype(F32).astype(BF16), before.astype(F32).astype(BF16))
+    slot = jnp.sum(jnp.where(chosen, earlier, 0.0), axis=0, keepdims=True).astype(jnp.int32)
+    place = marks(rank * capacity + slot, domains * capacity)
+
+    mortar_rows = looked_up(rows_ref[...], mortar_ref[...], cols_x)
+    normal = normal_ref[...]
+    gap = gap_ref[...]
     points = gap.shape[0]
     full = points // 8 * 8
-    live = lax.broadcasted_iota(jnp.int32, (points, pair_total), 0) < count[...]
-    root = jnp.where(live, jnp.sqrt(weight[...]), 0.0)
+    live = lax.broadcasted_iota(jnp.int32, (points, pair_total), 0) < count_ref[...]
+    root = jnp.where(live, jnp.sqrt(weight_ref[...]), 0.0)
     turned = []
     for node in range(4):
-        mortar_shape = shape[:, 4 + node]
+        mortar_shape = shape_ref[:, 4 + node]
         across = sum(
             normal[k : k + 1] * mortar_rows[k * 4 + node : k * 4 + node + 1] for k in range(3)
         )
         gap = gap - mortar_shape * across
         turned.append(root * mortar_shape)
+    words = words_of([root * shape_ref[:, node] for node in range(4)], root * gap, normal, face)
+    words_ref[...] = words
     for node in range(4):
         turned_ref[node * full : (node + 1) * full] = turned[node][:full]
         turned_ref[4 * full + node : 4 * full + node + 1] = turned[node][full:]
-    words = words_of([root * shape[:, node] for node in range(4)], root * gap, normal, face)
-    words_ref[...] = words
 
     group = LANES // capacity
-    height = blocks.shape[1]
     extra = group * height - words.shape[0]
     if extra:
         words = jnp.concatenate([words, jnp.zeros((extra, pair_total), F32)], axis=0)
@@ -193,43 +191,19 @@
             if j != spot:
                 piece = pltpu.roll(piece, (j - spot) * capacity % LANES, 1)
             block = piece if block is None else jnp.where(part == j, piece, block)
-        blocks[domain] = block
-        copies.append(
-            pltpu.make_async_copy(
-                blocks.at[domain],
-                sent_ref.at[place_in_group(domain, domains), rows_high:],
-                copy_sems.at[1, domain],
-            )
-        )
-        copies[-1].start()
-
-    for copy in brought[-2:]:
-        copy.wait()
-    sub = lax.axis_index("sub")
-    for target, layer in ((inner_ref, (1 - sub) * (layers - 1)), (outer_ref, sub * (layers - 1))):
-        for k in range(components):
-            target[k] = disp[k, layer]
-        target[components] = modulus[layer]
-    for copy in copies:
-        copy.wait()
-
-
-def last_kernel(
-    capacity, got_ref, rows_ref, words_ref, turned_ref, mortar_ref, rank_ref, face_ref, nodes_ref,
-    mass_ref, internal_ref, blocks_ref, own_ref, halo_ref, out_ref,
+        sent_ref[domain] = block
+
+
+def summed_on_faces(forces, faces, face_count):
+    return summed(times_turned(stacked_terms(forces), marks(faces, face_count)))
+
+
+def own_pairs_kernel(
+    got_ref, words_ref, turned_ref, mortar_ref, rank_ref, face_ref, faces_ref
 ):
-    domains = got_ref.shape[0]
-    components, layers, rows_y, cols_x = out_ref.shape
-    strips = layers * rows_y
-    face_count = nodes_ref.shape[1]
+    domains, folded, cols_x = got_ref.shape
     pair_total = rank_ref.shape[1]
-    folded = rows_ref.shape[0]
-    rows_high = folded * cols_x // LANES
-    height = got_ref.shape[1] - rows_high
-    group = LANES // capacity
     full = (turned_ref.shape[0] - 8) // 4
-    own_rows = rows_ref[...]
-
     rank, face = rank_ref[...], face_ref[...]
     end = domains - 1
     place = jnp.where(rank == 0, end, jnp.where(rank == end, 0, rank))
@@ -237,15 +211,7 @@
     step = min(domains, 8)
 
     def add_step(turn, total):
-        block = jnp.concatenate(
-            [
-                got_ref[pl.ds(turn * step, step), i * folded : (i + 1) * folded].reshape(
-                    step * folded, LANES
-                )
-                for i in range(cols_x // LANES)
-            ],
-            axis=1,
-        )
+        block = got_ref[pl.ds(turn * step, step)].reshape(step * folded, cols_x)
         found = summed(times(stacked_terms(block), at)).reshape(step, folded, pair_total)
         for i in range(step):
             total = total + jnp.where(place == turn * step + i, found[i], 0.0)
@@ -258,8 +224,19 @@
         both = lax.fori_loop(0, domains // step, add_step, both)
     remote_rows = jnp.where(face < cols_x, both[:12], both[12:])
     pressure, last, normal = weighted_pressure(words_ref[...], full, remote_rows)
-    turned = turned_ref[...]
-    mortar_forces = forces_of(-normal, loads_on(turned, full, 4 * full, pressure, last))
+    forces = forces_of(-normal, loads_on(turned_ref[...], full, 4 * full, pressure, last))
+    faces_ref[...] = summed_on_faces(forces, mortar_ref[...], faces_ref.shape[1])
+
+
+def last_kernel(
+    capacity, full, got_ref, rows_ref, faces_ref, nodes_ref, mass_ref, internal_ref, blocks_ref, own_ref,
+    halo_ref, out_ref,
+):
+    domains, height = got_ref.shape[:2]
+    components, layers, rows_y, cols_x = out_ref.shape
+    strips = layers * rows_y
+    face_count = nodes_ref.shape[1]
+    group = LANES // capacity
 
     part = lax.broadcasted_iota(jnp.int32, (height, LANES), 1) >> halves(capacity)
     pieces = []
@@ -268,7 +245,7 @@
         for tile in range(domains // group):
             block = None
             for spot in range(group):
-                piece = got_ref[tile * group + spot, rows_high:]
+                piece = got_ref[tile * group + spot]
                 if j != spot:
                     piece = pltpu.roll(piece, (spot - j) * capacity % LANES, 1)
                 block = piece if block is None else jnp.where(part == spot, piece, block)
@@ -276,12 +253,10 @@
         pieces.append(jnp.concatenate(tiles, axis=1))
     words = jnp.concatenate(pieces, axis=0)
     asked = words[5 * full + 8 : 5 * full + 9].astype(jnp.int32)
-    pressure, last, normal = weighted_pressure(words, full, looked_up(own_rows, asked, cols_x))
+    pressure, last, normal = weighted_pressure(words, full, looked_up(rows_ref[...], asked, cols_x))
     remote_forces = forces_of(normal, loads_on(words, full, 5 * full, pressure, last))
 
-    forces = jnp.concatenate([mortar_forces, remote_forces], axis=1)
-    at = marks(jnp.concatenate([mortar_ref[...], asked], axis=1), face_count)
-    forces = summed(times_turned(stacked_terms(forces), at))
+    forces = faces_ref[...] + summed_on_faces(remote_forces, asked, face_count)
     total = jnp.zeros((2 * components * strips, cols_x), F32)
     parts = [term.astype(F32) for term in terms_of(forces, 2)]
     numbers = lax.broadcasted_iota(jnp.int32, (strips, face_count), 0)
@@ -436,21 +411,8 @@
     group = LANES // capacity
     word_rows = 5 * full + 16
     height = -(-word_rows // (8 * group)) * 8
-    rows_high = 12 * face_count // LANES
     line = (1, pair_total)
-
-    def first(*refs):
-        first_kernel(capacity, *refs)
-
-    def last(*refs):
-        last_kernel(capacity, *refs)
-
-    def shaped(shape, dtype=F32):
-        return jax.ShapeDtypeStruct(shape, dtype)
-
-    arrays = [
-        face_nodes,
-        displacement,
+    pairs = [
         pair_mortar.reshape(line),
         pair_rank.reshape(line),
         pair_face.reshape(line),
@@ -459,46 +421,67 @@
         pair_normal,
         pair_gap,
         jnp.swapaxes(pair_shape, 0, 1),
-        modulus,
-        node_mass,
     ]
+    passed = [*pairs, node_mass]
+    ins = [face_nodes, displacement, modulus, *passed]
+
+    def first(*refs):
+        first_kernel(len(passed), *refs)
+
+    def routed(*refs):
+        words_kernel(capacity, *refs)
+
+    def last(*refs):
+        last_kernel(capacity, full, *refs)
+
+    def shaped(shape, dtype=F32):
+        return jax.ShapeDtypeStruct(shape, dtype)
+
     edge = shaped((components + 1, rows_y, cols_x))
+    rows_shape = (12 * face_count // cols_x, cols_x)
     in_hbm = pl.BlockSpec(memory_space=pltpu.HBM)
     in_vmem = pl.BlockSpec(memory_space=pltpu.VMEM)
-    kept = [displacement, *arrays[5:-1]]
-    sent, rows, words, turned, mortar, rank, face, nodes, mass, inner, outer = on_core(
+    sent_rows, rows, inner, outer, nodes, *pairs, mass = on_core(
         first,
         [
-            shaped((domains, rows_high + height, LANES)),
-            shaped((12 * face_count // cols_x, cols_x)),
+            shaped((domains,) + rows_shape),
+            shaped(rows_shape),
+            edge,
+            edge,
+            shaped(face_nodes.shape, jnp.int32),
+        ]
+        + [shaped(x.shape, x.dtype) for x in passed],
+        600_000_000,
+        1_500_000,
+        in_specs=[in_hbm] * len(ins),
+        out_specs=[in_hbm] + [in_vmem] * (4 + len(passed)),
+        scratch_shapes=[
+            pltpu.VMEM(displacement.shape, F32),
+            pltpu.VMEM(modulus.shape, F32),
+            pltpu.SemaphoreType.DMA((len(ins),)),
+            pltpu.SemaphoreType.DMA((domains,)),
+        ],
+    )(*[pltpu.with_memory_space_constraint(x, pltpu.HBM) for x in ins])
+    order = [place_in_group(domain, domains) for domain in range(domains)]
+    got_rows = lax.all_to_all(
+        sent_rows, "dom", split_axis=0, concat_axis=0, axis_index_groups=[order], tiled=True
+    )
+    sent_words, words, turned = on_core(
+        routed,
+        [
+            shaped((domains, height, LANES)),
             shaped((word_rows, pair_total)),
             shaped((4 * full + 8, pair_total)),
-            shaped(line, jnp.int32),
-            shaped(line, jnp.int32),
-            shaped(line, jnp.int32),
-            shaped(face_nodes.shape, jnp.int32),
-            shaped(node_mass.shape),
-            edge,
-            edge,
         ],
-        900_000_000,
-        1_500_000,
-        in_specs=[in_hbm] * len(arrays),
-        out_specs=[in_hbm] + [in_vmem] * 10,
-        scratch_shapes=[pltpu.VMEM(x.shape, x.dtype) for x in kept]
-        + [
-            pltpu.VMEM((rows_high, LANES), F32),
-            pltpu.VMEM((domains, height, LANES), F32),
-            pltpu.SemaphoreType.DMA((len(arrays),)),
-            pltpu.SemaphoreType.DMA((2, domains)),
-        ],
-    )(*[pltpu.with_memory_space_constraint(x, pltpu.HBM) for x in arrays])
-    order = [place_in_group(domain, domains) for domain in range(domains)]
-    got = lax.all_to_all(
-        sent, "dom", split_axis=0, concat_axis=0, axis_index_groups=[order], tiled=True
-    )
+        200_000_000,
+        1_000_000,
+    )(rows, *pairs)
+    got_words = lax.all_to_all(sent_words, "dom", split_axis=0, concat_axis=0, tiled=True)
     inner_halo = swapped(inner, ("dom", "sub"), 0)
     outer_halo = swapped(outer, ("dom", "sub"), 1)
+    faces = on_core(own_pairs_kernel, shaped((12, face_count)), 100_000_000, 500_000)(
+        got_rows, words, turned, *pairs[:3]
+    )
     size = 8 * components * GROUP
     internal, blocks = on_core(
         internal_kernel,
@@ -507,7 +490,7 @@
         700_000,
     )(displacement, modulus, stiffness, inner, inner_halo)
     return on_core(last, shaped(displacement.shape), 1_000_000_000, 1_500_000)(
-        got, rows, words, turned, mortar, rank, face, nodes, mass, internal, blocks, outer, outer_halo
+        got_words, rows, faces, nodes, mass, internal, blocks, outer, outer_halo
     )
 
 

time: 25.7 us -> 32.2 us (1.25)
  the two profiles are of different devices: /device:TPU:16 before, /device:TPU:0 now
where the time goes in v8:
time: 32.2 us; the launch traced here: 31.9 us
  starting transfers between devices  14.9 us (46%)
  waiting for transfers between devices  9.84 us (31%)
  Pallas kernels  7.14 us (22%)
    all_to_all x1, starting transfers between devices, shards(): lax.all_to_all(sent_rows, 'dom', split_axis=0, concat_axis=0, axis_index_...  9.32 us
    all_to_all x1, waiting for transfers between devices, shards(): lax.all_to_all(sent_words, 'dom', split_axis=0, concat_axis=0, tiled=True)  5.64 us
    all_to_all x1, starting transfers between devices, shards(): lax.all_to_all(sent_words, 'dom', split_axis=0, concat_axis=0, tiled=True)  4.86 us
    all_to_all x1, waiting for transfers between devices, shards(): lax.all_to_all(sent_rows, 'dom', split_axis=0, concat_axis=0, axis_index_...  3.53 us
    pallas_call x1, Pallas kernels, shards(): on_core(first, [shaped((domains,) + rows_shape), shaped(rows_shape), edge...  2.4 us
    pallas_call x1, Pallas kernels, shards(): on_core(last, shaped(displacement.shape), 1000000000, 1500000)  2.01 us
    pallas_call x1, Pallas kernels, shards(): on_core(routed, [shaped((domains, height, LANES)), shaped((word_rows, pai...  1.31 us
    pallas_call x1, Pallas kernels, shards(): on_core(internal_kernel, [shaped(displacement.shape), shaped((2 * size, s...  1.02 us
  transfers between devices with their start and end apart: 4, of which 3 were waited for; matrix products, arithmetic and copies ran while one was open for 0% of the time, Pallas kernels for 9%

profile of v8, /device:TPU:0, one launch (start us, length us, event | category | flops | bytes accessed | tf_op | source)
XLA Modules:
  0.0 31.9 jit_solution(49886717230351139)
XLA Ops:
  0.0 2.4 %shard_map.127 = (f32[8,24,256]{2,1,0:T(8,128)}, f32[24,256]{1,0:T(8,128)S(1)}, f32[4,32,256]{2,1,0:T(8,128)S(1)}, f32[4,32,256]{2,1,0:T(8,128)S(1)}, s32[4,512]...) custom-call(s32[4,512]{1,0:T(4,128)} %refs_0_.1, ...), custom_call_target="tpu_custom_call" | custom-call | flops 600000000 | bytes 1500000 | tf_op jit(solution)/shard_map/pallas_call | solution.py:444
  2.4 9.3 %all-to-all-start.1 = ((f32[8,24,256]{2,1,0:T(8,128)}), f32[8,24,256]{2,1,0:T(8,128)S(1)}, u32[]{:S(2)}, u32[]{:S(2)}) async-start(f32[8,24,256]{2,1,0:T(8,128)} %get-tuple-element.34), calls=%async_computation.1 | async-start | bytes 393216 | tf_op jit(solution)/shard_map/all_to_all | solution.py:466
  11.7 1.3 %shard_map.128 = (f32[8,72,128]{2,1,0:T(8,128)}, f32[136,256]{1,0:T(8,128)S(1)}, f32[104,256]{1,0:T(8,128)S(1)}) custom-call(f32[24,256]{1,0:T(8,128)S(1)} %get-tuple-element.24.refs_0_.refs_1_, s32[1,256]{1,0:T(1,128)S(1)} %get-tuple-element.25.refs_1_.mortar_ref, s32[1,256]{1,0:T(1,128)S(1)} %get-tuple-element.26.refs_2_.rank_ref, ...), custom_call_target="tpu_custom_call" | custom-call | flops 200000000 | bytes 1000000 | tf_op jit(solution)/shard_map/pallas_call | solution.py:469
  13.0 3.5 %all-to-all-done.1.got_ref = f32[8,24,256]{2,1,0:T(8,128)S(1)} async-done(((f32[8,24,256]{2,1,0:T(8,128)}), f32[8,24,256]{2,1,0:T(8,128)S(1)}, u32[]{:S(2)}, u32[]{:S(2)}) %all-to-all-start.1) | async-done | bytes 196640 | tf_op jit(solution)/shard_map/all_to_all | solution.py:466
  16.6 0.0 copy-start
  16.6 0.0 copy-start.1
  16.6 0.0 copy-start.2
  16.6 4.9 %all-to-all-start = ((f32[8,72,128]{2,1,0:T(8,128)}), f32[8,72,128]{2,1,0:T(8,128)S(1)}, u32[]{:S(2)}, u32[]{:S(2)}) async-start(f32[8,72,128]{2,1,0:T(8,128)} %get-tuple-element.33), calls=%async_computation | async-start | bytes 589824 | tf_op jit(solution)/shard_map/all_to_all | solution.py:479
  21.4 0.0 collective-permute-start
  21.4 0.7 %collective-permute-start.1 = (f32[4,32,256]{2,1,0:T(8,128)S(1)}, f32[4,32,256]{2,1,0:T(8,128)S(1)}, u32[]{:S(2)}, u32[]{:S(2)}) collective-permute-start(f32[4,32,256]{2,1,0:T(8,128)S(1)} %get-tuple-element.42.refs_7_), channel_id=1, source_target_pairs={{1,2},{2,1},{3,4},{4,3},{5,6},{6,5},{7,8},{8,7},{9,10},{10,9},{11,... | collective-permute-start | bytes 393224 | tf_op jit(solution)/shard_map/ppermute | solution.py:385
  22.1 0.7 %collective-permute-done.halo_ref = f32[4,32,256]{2,1,0:T(8,128)S(1)} collective-permute-done((f32[4,32,256]{2,1,0:T(8,128)S(1)}, f32[4,32,256]{2,1,0:T(8,128)S(1)}, u32[]{:S(2)}, u32[]{:S(2)}) %collective-permute-start) | collective-permute-done | bytes 131104 | tf_op jit(solution)/shard_map/ppermute | solution.py:385
  22.8 0.0 copy-done
  22.8 0.0 copy-done.1
  22.8 0.0 copy-done.2
  22.8 1.0 %shard_map.130 = (f32[3,2,32,256]{3,2,1,0:T(8,128)S(1)}, bf16[384,192]{1,0:T(8,128)(2,1)S(1)}) custom-call(f32[3,2,32,256]{3,2,1,0:T(8,128)S(1)} %copy-done, f32[2,32,256]{2,1,0:T(8,128)S(1)} %copy-done.1, f32[24,24]{1,0:T(8,128)S(1)} %copy-done.2, f32[4,32,256]{2,1,0:T(8,128)S(1)} %get-tuple-element.39.own_ref, f32[4,32,256]{2,1,0:T(8,128)S(1)} %collective-permute-done.halo_ref), custom_call_target="tpu_custom_call" | custom-call | flops 1000000000 | bytes 700000 | tf_op jit(solution)/shard_map/pallas_call | solution.py:486
  23.8 0.4 %shard_map.129.refs_2_ = f32[12,512]{1,0:T(8,128)S(1)} custom-call(f32[8,24,256]{2,1,0:T(8,128)S(1)} %all-to-all-done.1.got_ref, f32[136,256]{1,0:T(8,128)S(1)} %get-tuple-element.35.words_ref, f32[104,256]{1,0:T(8,128)S(1)} %get-tuple-element.36.turned_ref, s32[1,256]{1,0:T(1,128)S(1)} %get-tuple-element.25.refs_1_.mortar_ref, ...), custom_call_target="tpu_custom_call" | custom-call | flops 100000000 | bytes 500000 | tf_op jit(solution)/shard_map/pallas_call | solution.py:482
  24.2 0.0 collective-permute-done.1.refs_8_
  24.2 5.6 %all-to-all-done.refs_0_ = f32[8,72,128]{2,1,0:T(8,128)S(1)} async-done(((f32[8,72,128]{2,1,0:T(8,128)}), f32[8,72,128]{2,1,0:T(8,128)S(1)}, u32[]{:S(2)}, u32[]{:S(2)}) %all-to-all-start) | async-done | bytes 294944 | tf_op jit(solution)/shard_map/all_to_all | solution.py:479
  29.9 2.0 %shard_map.131 = f32[3,2,32,256]{3,2,1,0:T(8,128)} custom-call(f32[8,72,128]{2,1,0:T(8,128)S(1)} %all-to-all-done.refs_0_, f32[24,256]{1,0:T(8,128)S(1)} %get-tuple-element.24.refs_0_.refs_1_, f32[12,512]{1,0:T(8,128)S(1)} %shard_map.129.refs_2_, s32[4,512]{1,0:T(4,128)S(1)} %get-tuple-element.37.refs_3_, f32[2,32,256]{2,1,0:T(8,128)S(1)} %get-tuple-element.38.refs_4_, ...), custom_call_target="tpu_custom_call" | custom-call | flops 1000000000 | bytes 1500000 | tf_op jit(solution)/shard_map/pallas_call | solution.py:492
Async XLA Ops:
  2.4 14.2 %all-to-all-start.1 = ((f32[8,24,256]{2,1,0:T(8,128)}), f32[8,24,256]{2,1,0:T(8,128)S(1)}, u32[]{:S(2)}, u32[]{:S(2)}) async-start(f32[8,24,256]{2,1,0:T(8,128)} %get-tuple-element.34), calls=%async_computation.1 | async-start | bytes 393216 | tf_op jit(solution)/shard_map/all_to_all | solution.py:466
  16.6 6.2 %copy-start = (f32[3,2,32,256]{3,2,1,0:T(8,128)S(1)}, f32[3,2,32,256]{3,2,1,0:T(8,128)}, u32[]{:S(2)}) copy-start(f32[3,2,32,256]{3,2,1,0:T(8,128)} %disp_ref.1) | copy-start | bytes 589828
  16.6 6.2 %copy-start.1 = (f32[2,32,256]{2,1,0:T(8,128)S(1)}, f32[2,32,256]{2,1,0:T(8,128)}, u32[]{:S(2)}) copy-start(f32[2,32,256]{2,1,0:T(8,128)} %modulus_ref.1) | copy-start | bytes 196612
  16.6 6.2 %copy-start.2 = (f32[24,24]{1,0:T(8,128)S(1)}, f32[24,24]{1,0:T(8,128)}, u32[]{:S(2)}) copy-start(f32[24,24]{1,0:T(8,128)} %stiffness_ref.1) | copy-start | bytes 6916
  16.6 13.3 %all-to-all-start = ((f32[8,72,128]{2,1,0:T(8,128)}), f32[8,72,128]{2,1,0:T(8,128)S(1)}, u32[]{:S(2)}, u32[]{:S(2)}) async-start(f32[8,72,128]{2,1,0:T(8,128)} %get-tuple-element.33), calls=%async_computation | async-start | bytes 589824 | tf_op jit(solution)/shard_map/all_to_all | solution.py:479
  21.4 1.3 %collective-permute-start = (f32[4,32,256]{2,1,0:T(8,128)S(1)}, f32[4,32,256]{2,1,0:T(8,128)S(1)}, u32[]{:S(2)}, u32[]{:S(2)}) collective-permute-start(f32[4,32,256]{2,1,0:T(8,128)S(1)} %get-tuple-element.39.own_ref), channel_id=1, source_target_pairs={{0,1},{1,0},{2,3},{3,2},{4,5},{5,4},{6,7},{7,6},{8,9},{9,8},{10,11... | collective-permute-start | bytes 393224 | tf_op jit(solution)/shard_map/ppermute | solution.py:385
  21.4 2.8 %collective-permute-start.1 = (f32[4,32,256]{2,1,0:T(8,128)S(1)}, f32[4,32,256]{2,1,0:T(8,128)S(1)}, u32[]{:S(2)}, u32[]{:S(2)}) collective-permute-start(f32[4,32,256]{2,1,0:T(8,128)S(1)} %get-tuple-element.42.refs_7_), channel_id=1, source_target_pairs={{1,2},{2,1},{3,4},{4,3},{5,6},{6,5},{7,8},{8,7},{9,10},{10,9},{11,... | collective-permute-start | bytes 393224 | tf_op jit(solution)/shard_map/ppermute | solution.py:385

commit v9 on v7

--- a/solution.py
+++ b/solution.py
@@ -28,8 +28,14 @@
 
 
 def marks(index, count):
-    rows = lax.broadcasted_iota(jnp.int32, (count, index.shape[1]), 0)
-    return (rows == index).astype(F32).astype(BF16)
+    shape = (16, index.shape[1])
+    rows = lax.broadcasted_iota(jnp.int32, shape, 0).astype(jnp.int16)
+    index = jnp.broadcast_to(index, shape).astype(jnp.int16)
+    tiles = [
+        jnp.where(rows == index - jnp.int16(start), jnp.ones((), BF16), jnp.zeros((), BF16))
+        for start in range(0, count, 16)
+    ]
+    return jnp.concatenate(tiles, axis=0)
 
 
 def times(left, right):
@@ -44,19 +50,47 @@
     return power.bit_length() - 1
 
 
-def looked_up(table, face, width):
-    at = marks(face & (width - 1), width)
+def looked_up(table, face, at):
     both = summed(times(stacked_terms(table), at))
-    return jnp.where(face < width, both[:12], both[12:])
-
-
-def words_of(shapes, gap, normal, face):
-    full = gap.shape[0] // 8 * 8
-    last = [x[full:] for x in shapes + [gap]]
-    blank = jnp.zeros((7, face.shape[1]), F32)
-    return jnp.concatenate(
-        [x[:full] for x in shapes + [gap]] + last + [normal, face.astype(F32), blank], axis=0
-    )
+    return jnp.where(face < table.shape[1], both[:12], both[12:])
+
+
+def folded(placed, height, capacity, domain):
+    group = LANES // capacity
+    tile, spot = domain // group, domain % group
+    part = lax.broadcasted_iota(jnp.int32, (height, LANES), 1) >> halves(capacity)
+    block = None
+    for j in range(group):
+        piece = placed[j * height : (j + 1) * height, tile * LANES : (tile + 1) * LANES]
+        if j != spot:
+            piece = pltpu.roll(piece, (j - spot) * capacity % LANES, 1)
+        block = piece if block is None else jnp.where(part == j, piece, block)
+    return block
+
+
+def unfolded(got_ref, start, height, capacity):
+    group = LANES // capacity
+    part = lax.broadcasted_iota(jnp.int32, (height, LANES), 1) >> halves(capacity)
+    pieces = []
+    for j in range(group):
+        tiles = []
+        for first in range(0, got_ref.shape[0], group):
+            block = None
+            for spot in range(group):
+                piece = got_ref[first + spot, start : start + height]
+                if j != spot:
+                    piece = pltpu.roll(piece, (spot - j) * capacity % LANES, 1)
+                block = piece if block is None else jnp.where(part == spot, piece, block)
+            tiles.append(block)
+        pieces.append(jnp.concatenate(tiles, axis=1))
+    return jnp.concatenate(pieces, axis=0)
+
+
+def routed(words, rows, place):
+    extra = rows - words.shape[0]
+    if extra:
+        words = jnp.concatenate([words, jnp.zeros((extra, words.shape[1]), F32)], axis=0)
+    return summed(times_turned(stacked_terms(words), place))
 
 
 def weighted_pressure(words, full, remote_rows):
@@ -89,13 +123,13 @@
     return {0: domains - 1, domains - 1: 0}.get(domain, domain)
 
 
-def first_kernel(capacity, *refs):
+def first_kernel(capacity, heights, *refs):
     (
         nodes_hbm, disp_hbm, mortar_hbm, rank_hbm, face_hbm, count_hbm, weight_hbm, normal_hbm,
         gap_hbm, shape_hbm, modulus_hbm, mass_hbm,
         sent_ref, rows_ref, words_ref, turned_ref, mortar_ref, rank_ref, face_ref, nodes, mass_ref,
         inner_ref, outer_ref,
-        disp, count, weight, normal_v, gap_v, shape, modulus, halved, blocks, sems, copy_sems,
+        disp, count, weight, normal_v, gap_v, shape, modulus, halved, shapes, gaps, sems, copy_sems,
     ) = refs
     components, layers, rows_y, cols_x = disp.shape
     sources = (
@@ -119,10 +153,10 @@
     strips = layers * rows_y
     for copy in brought[:-2]:
         copy.wait()
-    indices = [nodes[corner : corner + 1, :] for corner in range(4)]
-    along_x = [marks(index & (cols_x - 1), cols_x) for index in indices]
-
     rank, face, mortar = rank_ref[...], face_ref[...], mortar_ref[...]
+    normal = normal_v[...]
+    gap = gap_v[...]
+
     chosen = lax.broadcasted_iota(jnp.int32, (domains, pair_total), 0) == rank
     before = lax.broadcasted_iota(jnp.int32, (pair_total, pair_total), 0) < lax.broadcasted_iota(
         jnp.int32, (pair_total, pair_total), 1
@@ -135,73 +169,76 @@
     numbers = lax.broadcasted_iota(jnp.int32, (strips, face_count), 0)
     folds = face_count // cols_x
     for corner in range(4):
-        strip = indices[corner] >> halves(cols_x)
-        found = summed(times(parts, along_x[corner])).reshape(components, strips, face_count)
+        index = nodes[corner : corner + 1, :]
+        strip = index >> halves(cols_x)
+        found = summed(times(parts, marks(index & (cols_x - 1), cols_x)))
+        found = found.reshape(components, strips, face_count)
         values = jnp.sum(jnp.where((numbers == strip)[None], found, 0.0), axis=1)
         for fold in range(folds):
             for k in range(components):
                 at = fold * 12 + k * 4 + corner
                 rows_ref[at : at + 1, :] = values[k : k + 1, fold * cols_x : (fold + 1) * cols_x]
 
-    rows = rows_ref[...]
-    high = rows.shape[0]
-    rows_high = high * cols_x // LANES
-    copies = []
-    for i in range(cols_x // LANES):
-        halved[i * high : (i + 1) * high] = rows[:, i * LANES : (i + 1) * LANES]
-    for domain in range(domains):
-        copies.append(
-            pltpu.make_async_copy(
-                halved, sent_ref.at[domain, :rows_high], copy_sems.at[0, domain]
-            )
-        )
-        copies[-1].start()
-
-    mortar_rows = looked_up(rows, mortar, cols_x)
-    normal = normal_v[...]
-    gap = gap_v[...]
     points = gap.shape[0]
     full = points // 8 * 8
     live = lax.broadcasted_iota(jnp.int32, (points, pair_total), 0) < count[...]
     root = jnp.where(live, jnp.sqrt(weight[...]), 0.0)
-    turned = []
+    weighted = [root * shape[:, node] for node in range(4)]
+    long_words = jnp.concatenate([x[:full] for x in weighted], axis=0)
+    group = LANES // capacity
+    placed = routed(long_words, group * heights[0], place)
+
+    rows = rows_ref[...]
+    high = rows.shape[0]
+    rows_high = high * cols_x // LANES
+    for i in range(cols_x // LANES):
+        halved[i * high : (i + 1) * high] = rows[:, i * LANES : (i + 1) * LANES]
+    starts = (rows_high, rows_high + heights[0], rows_high + sum(heights))
+    copies = []
+    for domain in range(domains):
+        spot = place_in_group(domain, domains)
+        shapes[domain] = folded(placed, heights[0], capacity, domain)
+        copies += [
+            pltpu.make_async_copy(halved, sent_ref.at[spot, :rows_high], copy_sems.at[0, domain]),
+            pltpu.make_async_copy(
+                shapes.at[domain],
+                sent_ref.at[spot, starts[0] : starts[1]],
+                copy_sems.at[1, domain],
+            ),
+        ]
+        for copy in copies[-2:]:
+            copy.start()
+
+    mortar_rows = looked_up(rows, mortar, marks(mortar & (cols_x - 1), cols_x))
     for node in range(4):
-        mortar_shape = shape[:, 4 + node]
         across = sum(
             normal[k : k + 1] * mortar_rows[k * 4 + node : k * 4 + node + 1] for k in range(3)
         )
-        gap = gap - mortar_shape * across
-        turned.append(root * mortar_shape)
-    for node in range(4):
-        turned_ref[node * full : (node + 1) * full] = turned[node][:full]
-        turned_ref[4 * full + node : 4 * full + node + 1] = turned[node][full:]
-    words = words_of([root * shape[:, node] for node in range(4)], root * gap, normal, face)
-    words_ref[...] = words
-
-    group = LANES // capacity
-    height = blocks.shape[1]
-    extra = group * height - words.shape[0]
-    if extra:
-        words = jnp.concatenate([words, jnp.zeros((extra, pair_total), F32)], axis=0)
-    placed = summed(times_turned(stacked_terms(words), place))
-    part = lax.broadcasted_iota(jnp.int32, (height, LANES), 1) >> halves(capacity)
+        gap = gap - shape[:, 4 + node] * across
+    gap = root * gap
+    short_words = jnp.concatenate(
+        [gap[:full]]
+        + [x[full:] for x in weighted + [gap]]
+        + [normal, face.astype(F32), jnp.zeros((7, pair_total), F32)],
+        axis=0,
+    )
+    placed = routed(short_words, group * heights[1], place)
     for domain in range(domains):
-        tile, spot = domain // group, domain % group
-        block = None
-        for j in range(group):
-            piece = placed[j * height : (j + 1) * height, tile * LANES : (tile + 1) * LANES]
-            if j != spot:
-                piece = pltpu.roll(piece, (j - spot) * capacity % LANES, 1)
-            block = piece if block is None else jnp.where(part == j, piece, block)
-        blocks[domain] = block
+        spot = place_in_group(domain, domains)
+        gaps[domain] = folded(placed, heights[1], capacity, domain)
         copies.append(
             pltpu.make_async_copy(
-                blocks.at[domain],
-                sent_ref.at[place_in_group(domain, domains), rows_high:],
-                copy_sems.at[1, domain],
+                gaps.at[domain], sent_ref.at[spot, starts[1] : starts[2]], copy_sems.at[2, domain]
             )
         )
         copies[-1].start()
+
+    words_ref[: 4 * full] = long_words
+    words_ref[4 * full :] = short_words
+    for node in range(4):
+        turned = root * shape[:, 4 + node]
+        turned_ref[node * full : (node + 1) * full] = turned[:full]
+        turned_ref[4 * full + node : 4 * full + node + 1] = turned[full:]
 
     for copy in brought[-2:]:
         copy.wait()
@@ -215,8 +252,8 @@
 
 
 def last_kernel(
-    capacity, got_ref, rows_ref, words_ref, turned_ref, mortar_ref, rank_ref, face_ref, nodes_ref,
-    mass_ref, internal_ref, blocks_ref, own_ref, halo_ref, out_ref,
+    capacity, heights, got_ref, rows_ref, words_ref, turned_ref, mortar_ref, rank_ref, face_ref, nodes_ref,
+    inverse_ref, internal_ref, blocks_ref, own_ref, halo_ref, out_ref,
 ):
     domains = got_ref.shape[0]
     components, layers, rows_y, cols_x = out_ref.shape
@@ -225,8 +262,6 @@
     pair_total = rank_ref.shape[1]
     folded = rows_ref.shape[0]
     rows_high = folded * cols_x // LANES
-    height = got_ref.shape[1] - rows_high
-    group = LANES // capacity
     full = (turned_ref.shape[0] - 8) // 4
     own_rows = rows_ref[...]
 
@@ -261,39 +296,39 @@
     turned = turned_ref[...]
     mortar_forces = forces_of(-normal, loads_on(turned, full, 4 * full, pressure, last))
 
-    part = lax.broadcasted_iota(jnp.int32, (height, LANES), 1) >> halves(capacity)
-    pieces = []
-    for j in range(group):
-        tiles = []
-        for tile in range(domains // group):
-            block = None
-            for spot in range(group):
-                piece = got_ref[tile * group + spot, rows_high:]
-                if j != spot:
-                    piece = pltpu.roll(piece, (spot - j) * capacity % LANES, 1)
-                block = piece if block is None else jnp.where(part == spot, piece, block)
-            tiles.append(block)
-        pieces.append(jnp.concatenate(tiles, axis=1))
-    words = jnp.concatenate(pieces, axis=0)
+    words = jnp.concatenate(
+        [
+            unfolded(got_ref, rows_high, heights[0], capacity)[: 4 * full],
+            unfolded(got_ref, rows_high + heights[0], heights[1], capacity)[: full + 16],
+        ],
+        axis=0,
+    )
     asked = words[5 * full + 8 : 5 * full + 9].astype(jnp.int32)
-    pressure, last, normal = weighted_pressure(words, full, looked_up(own_rows, asked, cols_x))
+    asked_at = marks(asked & (cols_x - 1), cols_x)
+    remote_rows = looked_up(own_rows, asked, asked_at)
+    pressure, last, normal = weighted_pressure(words, full, remote_rows)
     remote_forces = forces_of(normal, loads_on(words, full, 5 * full, pressure, last))
 
     forces = jnp.concatenate([mortar_forces, remote_forces], axis=1)
-    at = marks(jnp.concatenate([mortar_ref[...], asked], axis=1), face_count)
+    into = jnp.concatenate([mortar_ref[...], asked], axis=1)
+    at = jnp.concatenate([marks(mortar_ref[...] & (cols_x - 1), cols_x), asked_at], axis=1)
+    forces = jnp.concatenate(
+        [jnp.where(into < cols_x, forces, 0.0), jnp.where(into < cols_x, 0.0, forces)], axis=0
+    )
     forces = summed(times_turned(stacked_terms(forces), at))
+    forces = jnp.concatenate([forces[:12], forces[12:]], axis=1)
     total = jnp.zeros((2 * components * strips, cols_x), F32)
     parts = [term.astype(F32) for term in terms_of(forces, 2)]
-    numbers = lax.broadcasted_iota(jnp.int32, (strips, face_count), 0)
     for corner in range(4):
         index = nodes_ref[corner : corner + 1, :]
-        along_x = marks(index & (cols_x - 1), cols_x)
-        strip = numbers == (index >> halves(cols_x))
+        strip = marks(index >> halves(cols_x), strips)
         spread = []
         for part in parts:
             for k in range(components):
                 at = k * 4 + corner
-                spread.append(jnp.where(strip, part[at : at + 1], 0.0).astype(BF16))
+                row = jnp.broadcast_to(part[at : at + 1], (16, face_count)).astype(BF16)
+                spread.append(strip * jnp.concatenate([row] * (strips // 16), axis=0))
+        along_x = marks(index & (cols_x - 1), cols_x)
         total = total + times_turned(jnp.concatenate(spread, axis=0), along_x)
     contact = summed(total).reshape(components, layers, rows_y, cols_x)
     upward = lax.axis_index("sub") == 1
@@ -302,7 +337,7 @@
     for layer in range(layers):
         for k in range(components):
             nodal = internal_ref[k, layer] + jnp.where(at == layer, edge[k], 0.0)
-            out_ref[k, layer] = (nodal + contact[k, layer]) / mass_ref[layer]
+            out_ref[k, layer] = (nodal + contact[k, layer]) * inverse_ref[layer]
 
 
 GROUP = 8
@@ -358,7 +393,10 @@
     return on_nodes(element_forces(matrices, low[:components], high, low[components]))
 
 
-def internal_kernel(disp_ref, modulus_ref, stiffness_ref, own_ref, halo_ref, out_ref, blocks_ref):
+def internal_kernel(
+    disp_ref, modulus_ref, stiffness_ref, mass_ref, own_ref, halo_ref, out_ref, blocks_ref, inverse_ref
+):
+    inverse_ref[...] = 1.0 / mass_ref[...]
     components, layers, rows_y, cols_x = disp_ref.shape
     dofs = 8 * components
     half = dofs // 2
@@ -435,15 +473,15 @@
     full = points // 8 * 8
     group = LANES // capacity
     word_rows = 5 * full + 16
-    height = -(-word_rows // (8 * group)) * 8
+    heights = tuple(-(-rows // (8 * group)) * 8 for rows in (4 * full, full + 16))
     rows_high = 12 * face_count // LANES
     line = (1, pair_total)
 
     def first(*refs):
-        first_kernel(capacity, *refs)
+        first_kernel(capacity, heights, *refs)
 
     def last(*refs):
-        last_kernel(capacity, *refs)
+        last_kernel(capacity, heights, *refs)
 
     def shaped(shape, dtype=F32):
         return jax.ShapeDtypeStruct(shape, dtype)
@@ -469,7 +507,7 @@
     sent, rows, words, turned, mortar, rank, face, nodes, mass, inner, outer = on_core(
         first,
         [
-            shaped((domains, rows_high + height, LANES)),
+            shaped((domains, rows_high + sum(heights), LANES)),
             shaped((12 * face_count // cols_x, cols_x)),
             shaped((word_rows, pair_total)),
             shaped((4 * full + 8, pair_total)),
@@ -488,9 +526,10 @@
         scratch_shapes=[pltpu.VMEM(x.shape, x.dtype) for x in kept]
         + [
             pltpu.VMEM((rows_high, LANES), F32),
-            pltpu.VMEM((domains, height, LANES), F32),
+            pltpu.VMEM((domains, heights[0], LANES), F32),
+            pltpu.VMEM((domains, heights[1], LANES), F32),
             pltpu.SemaphoreType.DMA((len(arrays),)),
-            pltpu.SemaphoreType.DMA((2, domains)),
+            pltpu.SemaphoreType.DMA((3, domains)),
         ],
     )(*[pltpu.with_memory_space_constraint(x, pltpu.HBM) for x in arrays])
     order = [place_in_group(domain, domains) for domain in range(domains)]
@@ -500,14 +539,14 @@
     inner_halo = swapped(inner, ("dom", "sub"), 0)
     outer_halo = swapped(outer, ("dom", "sub"), 1)
     size = 8 * components * GROUP
-    internal, blocks = on_core(
+    internal, blocks, inverse = on_core(
         internal_kernel,
-        [shaped(displacement.shape), shaped((2 * size, size), BF16)],
+        [shaped(displacement.shape), shaped((2 * size, size), BF16), shaped(mass.shape)],
         1_000_000_000,
         700_000,
-    )(displacement, modulus, stiffness, inner, inner_halo)
+    )(displacement, modulus, stiffness, mass, inner, inner_halo)
     return on_core(last, shaped(displacement.shape), 1_000_000_000, 1_500_000)(
-        got, rows, words, turned, mortar, rank, face, nodes, mass, internal, blocks, outer, outer_halo
+        got, rows, words, turned, mortar, rank, face, nodes, inverse, internal, blocks, outer, outer_halo
     )
 
 

time: 25.7 us -> 25.6 us (level)
  no operation moved by 1% of the time
where the time goes in v9:
time: 25.6 us; the launch traced here: 25.3 us
  starting transfers between devices  9.52 us (37%)
  waiting for transfers between devices  9.46 us (37%)
  Pallas kernels  6.25 us (24%)
    ppermute x2, waiting for transfers between devices, swapped(): return lax.ppermute(block, axis, route)  9.46 us
    all_to_all x1, starting transfers between devices, shards(): lax.all_to_all(sent, 'dom', split_axis=0, concat_axis=0, axis_index_group...  6.05 us
    ppermute x2, starting transfers between devices, swapped(): return lax.ppermute(block, axis, route)  3.47 us
    pallas_call x1, Pallas kernels, shards(): on_core(first, [shaped((domains, rows_high + sum(heights), LANES)), shape...  3.09 us
    pallas_call x1, Pallas kernels, shards(): on_core(last, shaped(displacement.shape), 1000000000, 1500000)  2.14 us
    pallas_call x1, Pallas kernels, shards(): on_core(internal_kernel, [shaped(displacement.shape), shaped((2 * size, s...  1.02 us
  transfers between devices with their start and end apart: 3, of which 1 were waited for; matrix products, arithmetic and copies ran while one was open for 0% of the time, Pallas kernels for 4%

profile of v9, /device:TPU:16, one launch (start us, length us, event | category | flops | bytes accessed | tf_op | source)
XLA Modules:
  0.0 25.3 jit_solution(16594079032336224507)
XLA Ops:
  0.0 3.1 %shard_map.127 = (f32[8,120,128]{2,1,0:T(8,128)}, f32[24,256]{1,0:T(8,128)S(1)}, f32[136,256]{1,0:T(8,128)S(1)}, f32[104,256]{1,0:T(8,128)S(1)}, s32[1,256]{1,0:...) custom-call(s32[4,512]{1,0:T(4,128)} %refs_0_.1, ...), custom_call_target="tpu_custom_call" | custom-call | flops 900000000 | bytes 1500000 | tf_op jit(solution)/shard_map/pallas_call | solution.py:507
  3.1 0.0 copy-start
  3.1 0.0 copy-start.1
  3.1 0.0 copy-start.2
  3.1 6.1 %all-to-all-start = ((f32[8,120,128]{2,1,0:T(8,128)}), f32[8,120,128]{2,1,0:T(8,128)S(1)}, u32[]{:S(2)}, u32[]{:S(2)}) async-start(f32[8,120,128]{2,1,0:T(8,128)} %get-tuple-element.19), calls=%async_computation | async-start | bytes 983040 | tf_op jit(solution)/shard_map/all_to_all | solution.py:536
  9.2 0.0 collective-permute-start
  9.2 3.5 %collective-permute-start.1 = (f32[4,32,256]{2,1,0:T(8,128)S(1)}, f32[4,32,256]{2,1,0:T(8,128)S(1)}, u32[]{:S(2)}, u32[]{:S(2)}) collective-permute-start(f32[4,32,256]{2,1,0:T(8,128)S(1)} %get-tuple-element.32.refs_11_), channel_id=1, source_target_pairs={{1,2},{2,1},{3,4},{4,3},{5,6},{6,5},{7,8},{8,7},{9,10},{10,9},{11,... | collective-permute-start | bytes 393224 | tf_op jit(solution)/shard_map/ppermute | solution.py:448
  12.7 0.0 collective-permute-done.halo_ref
  12.7 0.0 copy-done
  12.7 0.0 copy-done.1
  12.7 0.0 copy-done.2
  12.7 1.0 %shard_map.128 = (f32[3,2,32,256]{3,2,1,0:T(8,128)S(1)}, bf16[384,192]{1,0:T(8,128)(2,1)S(1)}, f32[2,32,256]{2,1,0:T(8,128)S(1)}) custom-call(f32[3,2,32,256]{3,2,1,0:T(8,128)S(1)} %copy-done, f32[2,32,256]{2,1,0:T(8,128)S(1)} %copy-done.1, f32[24,24]{1,0:T(8,128)S(1)} %copy-done.2, f32[2,32,256]{2,1,0:T(8,128)S(1)} %get-tuple-element.27.mass_ref, ...), custom_call_target="tpu_custom_call" | custom-call | flops 1000000000 | bytes 700000 | tf_op jit(solution)/shard_map/pallas_call | solution.py:542
  13.7 9.5 %collective-permute-done.1.refs_12_ = f32[4,32,256]{2,1,0:T(8,128)S(1)} collective-permute-done((f32[4,32,256]{2,1,0:T(8,128)S(1)}, f32[4,32,256]{2,1,0:T(8,128)S(1)}, u32[]{:S(2)}, u32[]{:S(2)}) %collective-permute-start.1) | collective-permute-done | bytes 131104 | tf_op jit(solution)/shard_map/ppermute | solution.py:448
  23.2 0.0 all-to-all-done.refs_0_
  23.2 2.1 %shard_map.129 = f32[3,2,32,256]{3,2,1,0:T(8,128)} custom-call(f32[8,120,128]{2,1,0:T(8,128)S(1)} %all-to-all-done.refs_0_, f32[24,256]{1,0:T(8,128)S(1)} %get-tuple-element.20.refs_1_, f32[136,256]{1,0:T(8,128)S(1)} %get-tuple-element.21.refs_2_, f32[104,256]{1,0:T(8,128)S(1)} %get-tuple-element.22.refs_3_, s32[1,256]{1,0:T(1,128)S(1)} %get-tuple-element.23.refs_4_, ...), custom_call_target="tpu_custom_call" | custom-call | flops 1000000000 | bytes 1500000 | tf_op jit(solution)/shard_map/pallas_call | solution.py:548
Async XLA Ops:
  3.1 9.6 %copy-start = (f32[3,2,32,256]{3,2,1,0:T(8,128)S(1)}, f32[3,2,32,256]{3,2,1,0:T(8,128)}, u32[]{:S(2)}) copy-start(f32[3,2,32,256]{3,2,1,0:T(8,128)} %disp_ref.1) | copy-start | bytes 589828
  3.1 9.6 %copy-start.1 = (f32[2,32,256]{2,1,0:T(8,128)S(1)}, f32[2,32,256]{2,1,0:T(8,128)}, u32[]{:S(2)}) copy-start(f32[2,32,256]{2,1,0:T(8,128)} %modulus_ref.1) | copy-start | bytes 196612
  3.1 9.6 %copy-start.2 = (f32[24,24]{1,0:T(8,128)S(1)}, f32[24,24]{1,0:T(8,128)}, u32[]{:S(2)}) copy-start(f32[24,24]{1,0:T(8,128)} %stiffness_ref.1) | copy-start | bytes 6916
  3.1 20.1 %all-to-all-start = ((f32[8,120,128]{2,1,0:T(8,128)}), f32[8,120,128]{2,1,0:T(8,128)S(1)}, u32[]{:S(2)}, u32[]{:S(2)}) async-start(f32[8,120,128]{2,1,0:T(8,128)} %get-tuple-element.19), calls=%async_computation | async-start | bytes 983040 | tf_op jit(solution)/shard_map/all_to_all | solution.py:536
  9.2 3.5 %collective-permute-start = (f32[4,32,256]{2,1,0:T(8,128)S(1)}, f32[4,32,256]{2,1,0:T(8,128)S(1)}, u32[]{:S(2)}, u32[]{:S(2)}) collective-permute-start(f32[4,32,256]{2,1,0:T(8,128)S(1)} %get-tuple-element.28.own_ref), channel_id=1, source_target_pairs={{0,1},{1,0},{2,3},{3,2},{4,5},{5,4},{6,7},{7,6},{8,9},{9,8},{10,11... | collective-permute-start | bytes 393224 | tf_op jit(solution)/shard_map/ppermute | solution.py:448
  9.2 14.0 %collective-permute-start.1 = (f32[4,32,256]{2,1,0:T(8,128)S(1)}, f32[4,32,256]{2,1,0:T(8,128)S(1)}, u32[]{:S(2)}, u32[]{:S(2)}) collective-permute-start(f32[4,32,256]{2,1,0:T(8,128)S(1)} %get-tuple-element.32.refs_11_), channel_id=1, source_target_pairs={{1,2},{2,1},{3,4},{4,3},{5,6},{6,5},{7,8},{8,7},{9,10},{10,9},{11,... | collective-permute-start | bytes 393224 | tf_op jit(solution)/shard_map/ppermute | solution.py:448

commit v10 on v9

--- a/solution.py
+++ b/solution.py
@@ -123,12 +123,28 @@
     return {0: domains - 1, domains - 1: 0}.get(domain, domain)
 
 
+def in_pieces(source, target, sems, first):
+    shape = source.shape
+    if len(shape) == 4:
+        parts = [(i, j) for i in range(shape[0]) for j in range(shape[1])]
+    elif len(shape) == 3 and shape[0] <= 4:
+        parts = [(i,) for i in range(shape[0])]
+    elif len(shape) == 3:
+        parts = [(pl.ds(start, min(5, shape[0] - start)),) for start in range(0, shape[0], 5)]
+    else:
+        return [pltpu.make_async_copy(source, target, sems.at[first])]
+    return [
+        pltpu.make_async_copy(source.at[part], target.at[part], sems.at[first + i])
+        for i, part in enumerate(parts)
+    ]
+
+
 def first_kernel(capacity, heights, *refs):
     (
         nodes_hbm, disp_hbm, mortar_hbm, rank_hbm, face_hbm, count_hbm, weight_hbm, normal_hbm,
         gap_hbm, shape_hbm, modulus_hbm, mass_hbm,
         sent_ref, rows_ref, words_ref, turned_ref, mortar_ref, rank_ref, face_ref, nodes, mass_ref,
-        inner_ref, outer_ref,
+        inner_ref, outer_ref, top_ref,
         disp, count, weight, normal_v, gap_v, shape, modulus, halved, shapes, gaps, sems, copy_sems,
     ) = refs
     components, layers, rows_y, cols_x = disp.shape
@@ -140,10 +156,9 @@
         nodes, disp, rank_ref, face_ref, mortar_ref, shape, count, weight, normal_v, gap_v, modulus,
         mass_ref,
     )
-    brought = [
-        pltpu.make_async_copy(source, target, sems.at[i])
-        for i, (source, target) in enumerate(zip(sources, targets))
-    ]
+    brought = []
+    for source, target in zip(sources, targets):
+        brought += in_pieces(source, target, sems, len(brought))
     for copy in brought:
         copy.start()
 
@@ -151,7 +166,8 @@
     pair_total = rank_ref.shape[1]
     face_count = nodes.shape[1]
     strips = layers * rows_y
-    for copy in brought[:-2]:
+    late = 2 * layers
+    for copy in brought[:-late]:
         copy.wait()
     rank, face, mortar = rank_ref[...], face_ref[...], mortar_ref[...]
     normal = normal_v[...]
@@ -240,20 +256,20 @@
         turned_ref[node * full : (node + 1) * full] = turned[:full]
         turned_ref[4 * full + node : 4 * full + node + 1] = turned[full:]
 
-    for copy in brought[-2:]:
+    for copy in brought[-late:]:
         copy.wait()
     sub = lax.axis_index("sub")
     for target, layer in ((inner_ref, (1 - sub) * (layers - 1)), (outer_ref, sub * (layers - 1))):
         for k in range(components):
             target[k] = disp[k, layer]
-        target[components] = modulus[layer]
+    top_ref[...] = modulus[layers - 1]
     for copy in copies:
         copy.wait()
 
 
 def last_kernel(
     capacity, heights, got_ref, rows_ref, words_ref, turned_ref, mortar_ref, rank_ref, face_ref, nodes_ref,
-    inverse_ref, internal_ref, blocks_ref, own_ref, halo_ref, out_ref,
+    inverse_ref, internal_ref, blocks_ref, own_ref, halo_ref, top_ref, under_ref, out_hbm, out_ref, sems,
 ):
     domains = got_ref.shape[0]
     components, layers, rows_y, cols_x = out_ref.shape
@@ -332,12 +348,21 @@
         total = total + times_turned(jnp.concatenate(spread, axis=0), along_x)
     contact = summed(total).reshape(components, layers, rows_y, cols_x)
     upward = lax.axis_index("sub") == 1
-    edge = edge_part(upward, own_ref, halo_ref, blocks_ref)
+    edge = edge_part(upward, own_ref, halo_ref, top_ref, under_ref, blocks_ref)
     at = jnp.where(upward, layers - 1, 0)
+    copies = []
     for layer in range(layers):
         for k in range(components):
             nodal = internal_ref[k, layer] + jnp.where(at == layer, edge[k], 0.0)
             out_ref[k, layer] = (nodal + contact[k, layer]) * inverse_ref[layer]
+            copies.append(
+                pltpu.make_async_copy(
+                    out_ref.at[k, layer], out_hbm.at[k, layer], sems.at[k, layer]
+                )
+            )
+            copies[-1].start()
+    for copy in copies:
+        copy.wait()
 
 
 GROUP = 8
@@ -380,21 +405,23 @@
     return sums
 
 
-def edge_part(upward, own_ref, halo_ref, blocks_ref):
-    components = own_ref.shape[0] - 1
+def edge_part(upward, own_ref, halo_ref, top_ref, under_ref, blocks_ref):
+    components = own_ref.shape[0]
     size = blocks_ref.shape[1]
     rows = size // 2
     start = jnp.where(upward, 0, rows)
     matrices = [
         blocks_ref[pl.ds(pl.multiple_of(term * size + start, 16), rows)] for term in range(2)
     ]
-    low = [jnp.where(upward, own_ref[k], halo_ref[k]) for k in range(components + 1)]
+    low = [jnp.where(upward, own_ref[k], halo_ref[k]) for k in range(components)]
     high = [jnp.where(upward, halo_ref[k], own_ref[k]) for k in range(components)]
-    return on_nodes(element_forces(matrices, low[:components], high, low[components]))
+    modulus = jnp.where(upward, top_ref[...], under_ref[...])
+    return on_nodes(element_forces(matrices, low, high, modulus))
 
 
 def internal_kernel(
-    disp_ref, modulus_ref, stiffness_ref, mass_ref, own_ref, halo_ref, out_ref, blocks_ref, inverse_ref
+    disp_ref, modulus_ref, stiffness_ref, mass_ref, own_ref, halo_ref, top_ref, under_ref, out_ref,
+    blocks_ref, inverse_ref,
 ):
     inverse_ref[...] = 1.0 / mass_ref[...]
     components, layers, rows_y, cols_x = disp_ref.shape
@@ -423,7 +450,7 @@
             part = on_nodes(forces[a * half : (a + 1) * half])
             sums[e + a] = [x + y for x, y in zip(sums[e + a], part)]
     upward = lax.axis_index("sub") == 0
-    edge = edge_part(upward, own_ref, halo_ref, blocks_ref)
+    edge = edge_part(upward, own_ref, halo_ref, top_ref, under_ref, blocks_ref)
     at = jnp.where(upward, layers - 1, 0)
     for layer in range(layers):
         for k in range(components):
@@ -446,6 +473,10 @@
     for i in range(first, size - 1, 2):
         route += [(i, i + 1), (i + 1, i)]
     return lax.ppermute(block, axis, route)
+
+
+def raised(block, axis):
+    return lax.ppermute(block, axis, [(i, i + 1) for i in range(lax.axis_size(axis) - 1)])
 
 
 def shards(
@@ -500,11 +531,11 @@
         modulus,
         node_mass,
     ]
-    edge = shaped((components + 1, rows_y, cols_x))
+    edge = shaped((components, rows_y, cols_x))
     in_hbm = pl.BlockSpec(memory_space=pltpu.HBM)
     in_vmem = pl.BlockSpec(memory_space=pltpu.VMEM)
     kept = [displacement, *arrays[5:-1]]
-    sent, rows, words, turned, mortar, rank, face, nodes, mass, inner, outer = on_core(
+    sent, rows, words, turned, mortar, rank, face, nodes, mass, inner, outer, top = on_core(
         first,
         [
             shaped((domains, rows_high + sum(heights), LANES)),
@@ -518,17 +549,18 @@
             shaped(node_mass.shape),
             edge,
             edge,
+            shaped((rows_y, cols_x)),
         ],
         900_000_000,
         1_500_000,
         in_specs=[in_hbm] * len(arrays),
-        out_specs=[in_hbm] + [in_vmem] * 10,
+        out_specs=[in_hbm] + [in_vmem] * 11,
         scratch_shapes=[pltpu.VMEM(x.shape, x.dtype) for x in kept]
         + [
             pltpu.VMEM((rows_high, LANES), F32),
             pltpu.VMEM((domains, heights[0], LANES), F32),
             pltpu.VMEM((domains, heights[1], LANES), F32),
-            pltpu.SemaphoreType.DMA((len(arrays),)),
+            pltpu.SemaphoreType.DMA((64,)),
             pltpu.SemaphoreType.DMA((3, domains)),
         ],
     )(*[pltpu.with_memory_space_constraint(x, pltpu.HBM) for x in arrays])
@@ -538,15 +570,27 @@
     )
     inner_halo = swapped(inner, ("dom", "sub"), 0)
     outer_halo = swapped(outer, ("dom", "sub"), 1)
+    under = raised(top, ("dom", "sub"))
     size = 8 * components * GROUP
     internal, blocks, inverse = on_core(
         internal_kernel,
         [shaped(displacement.shape), shaped((2 * size, size), BF16), shaped(mass.shape)],
         1_000_000_000,
         700_000,
-    )(displacement, modulus, stiffness, mass, inner, inner_halo)
-    return on_core(last, shaped(displacement.shape), 1_000_000_000, 1_500_000)(
-        got, rows, words, turned, mortar, rank, face, nodes, inverse, internal, blocks, outer, outer_halo
+    )(displacement, modulus, stiffness, mass, inner, inner_halo, top, under)
+    return on_core(
+        last,
+        shaped(displacement.shape),
+        1_000_000_000,
+        1_500_000,
+        out_specs=in_hbm,
+        scratch_shapes=[
+            pltpu.VMEM(displacement.shape, F32),
+            pltpu.SemaphoreType.DMA((components, layers)),
+        ],
+    )(
+        got, rows, words, turned, mortar, rank, face, nodes, inverse, internal, blocks, outer,
+        outer_halo, top, under,
     )
 
 

time: 25.6 us -> 26 us (1.016)
  starting transfers between devices: 9.52 us -> 12.5 us
  waiting for transfers between devices: 9.46 us -> 6.48 us
  Pallas kernels: 6.25 us -> 6.67 us
    ppermute x2, waiting for transfers between devices: 9.46 us -> 0.65 us  [swapped(): return lax.ppermute(block, axis, route)]
    ppermute x0 -> x1, waiting for transfers between devices: none -> 5.83 us  [raised(): lax.ppermute(block, axis, [(i, i + 1) for i in range(lax.axis_size(axis)...]
    ppermute x0 -> x1, starting transfers between devices: none -> 2.4 us  [raised(): lax.ppermute(block, axis, [(i, i + 1) for i in range(lax.axis_size(axis)...]
    ppermute x2, starting transfers between devices: 3.47 us -> 4.05 us  [swapped(): return lax.ppermute(block, axis, route)]
    pallas_call x1, Pallas kernels: 3.09 us -> 3.49 us  [shards(): on_core(first, [shaped((domains, rows_high + sum(heights), LANES)), shape...]
  transfers between devices with their start and end apart: 3 -> 4, of which waited for: 1 -> 2; matrix products, arithmetic and copies ran while one was open for 0% -> 0% of each run, Pallas kernels for 4% -> 4%
where the time goes in v10:
time: 26 us; the launch traced here: 25.7 us
  starting transfers between devices  12.5 us (48%)
  Pallas kernels  6.67 us (26%)
  waiting for transfers between devices  6.48 us (25%)
    all_to_all x1, starting transfers between devices, shards(): lax.all_to_all(sent, 'dom', split_axis=0, concat_axis=0, axis_index_group...  6.05 us
    ppermute x1, waiting for transfers between devices, raised(): lax.ppermute(block, axis, [(i, i + 1) for i in range(lax.axis_size(axis)...  5.83 us
    ppermute x2, starting transfers between devices, swapped(): return lax.ppermute(block, axis, route)  4.05 us
    pallas_call x1, Pallas kernels, shards(): on_core(first, [shaped((domains, rows_high + sum(heights), LANES)), shape...  3.49 us
    ppermute x1, starting transfers between devices, raised(): lax.ppermute(block, axis, [(i, i + 1) for i in range(lax.axis_size(axis)...  2.4 us
    pallas_call x1, Pallas kernels, shards(): on_core(last, shaped(displacement.shape), 1000000000, 1500000, out_specs=...  2.15 us
    pallas_call x1, Pallas kernels, shards(): on_core(internal_kernel, [shaped(displacement.shape), shaped((2 * size, s...  1.03 us
    ppermute x2, waiting for transfers between devices, swapped(): return lax.ppermute(block, axis, route)  0.65 us
  transfers between devices with their start and end apart: 4, of which 2 were waited for; matrix products, arithmetic and copies ran while one was open for 0% of the time, Pallas kernels for 4%

profile of v10, /device:TPU:16, one launch (start us, length us, event | category | flops | bytes accessed | tf_op | source)
XLA Modules:
  0.0 25.7 jit_solution(11030686882803202706)
XLA Ops:
  0.0 3.5 %shard_map.127 = (f32[8,120,128]{2,1,0:T(8,128)}, f32[24,256]{1,0:T(8,128)S(1)}, f32[136,256]{1,0:T(8,128)S(1)}, f32[104,256]{1,0:T(8,128)S(1)}, s32[1,256]{1,0:...) custom-call(s32[4,512]{1,0:T(4,128)} %refs_0_.1, ...), custom_call_target="tpu_custom_call" | custom-call | flops 900000000 | bytes 1500000 | tf_op jit(solution)/shard_map/pallas_call | solution.py:538
  3.5 0.0 copy-start
  3.5 0.0 copy-start.1
  3.5 0.0 copy-start.2
  3.5 6.1 %all-to-all-start = ((f32[8,120,128]{2,1,0:T(8,128)}), f32[8,120,128]{2,1,0:T(8,128)S(1)}, u32[]{:S(2)}, u32[]{:S(2)}) async-start(f32[8,120,128]{2,1,0:T(8,128)} %get-tuple-element.20), calls=%async_computation | async-start | bytes 983040 | tf_op jit(solution)/shard_map/all_to_all | solution.py:568
  9.6 0.0 collective-permute-start
  9.6 2.4 %collective-permute-start.1 = (f32[32,256]{1,0:T(8,128)S(1)}, f32[32,256]{1,0:T(8,128)S(1)}, u32[]{:S(2)}, u32[]{:S(2)}) collective-permute-start(f32[32,256]{1,0:T(8,128)S(1)} %get-tuple-element.30.top_ref.refs_13_), channel_id=1, source_target_pairs={{0,1},{1,2},{2,3},{3,4},{4,5},{5,6},{6,7},{7,8},{8,9},{9,10},{10,1... | collective-permute-start | bytes 98312 | tf_op jit(solution)/shard_map/ppermute | solution.py:479
  12.0 4.0 %collective-permute-start.2 = (f32[3,32,256]{2,1,0:T(8,128)S(1)}, f32[3,32,256]{2,1,0:T(8,128)S(1)}, u32[]{:S(2)}, u32[]{:S(2)}) collective-permute-start(f32[3,32,256]{2,1,0:T(8,128)S(1)} %get-tuple-element.34.refs_11_), channel_id=1, source_target_pairs={{1,2},{2,1},{3,4},{4,3},{5,6},{6,5},{7,8},{8,7},{9,10},{10,9},{11,... | collective-permute-start | bytes 294920 | tf_op jit(solution)/shard_map/ppermute | solution.py:475
  16.1 5.8 %collective-permute-done.1.under_ref.refs_14_ = f32[32,256]{1,0:T(8,128)S(1)} collective-permute-done((f32[32,256]{1,0:T(8,128)S(1)}, f32[32,256]{1,0:T(8,128)S(1)}, u32[]{:S(2)}, u32[]{:S(2)}) %collective-permute-start.1) | collective-permute-done | bytes 32800 | tf_op jit(solution)/shard_map/ppermute | solution.py:479
  21.9 0.0 collective-permute-done.halo_ref
  21.9 0.0 copy-done
  21.9 0.0 copy-done.1
  21.9 0.0 copy-done.2
  21.9 1.0 %shard_map.128 = (f32[3,2,32,256]{3,2,1,0:T(8,128)S(1)}, bf16[384,192]{1,0:T(8,128)(2,1)S(1)}, f32[2,32,256]{2,1,0:T(8,128)S(1)}) custom-call(f32[3,2,32,256]{3,2,1,0:T(8,128)S(1)} %copy-done, f32[2,32,256]{2,1,0:T(8,128)S(1)} %copy-done.1, f32[24,24]{1,0:T(8,128)S(1)} %copy-done.2, f32[2,32,256]{2,1,0:T(8,128)S(1)} %get-tuple-element.28.mass_ref, ...), custom_call_target="tpu_custom_call" | custom-call | flops 1000000000 | bytes 700000 | tf_op jit(solution)/shard_map/pallas_call | solution.py:575
  22.9 0.6 %collective-permute-done.2.refs_12_ = f32[3,32,256]{2,1,0:T(8,128)S(1)} collective-permute-done((f32[3,32,256]{2,1,0:T(8,128)S(1)}, f32[3,32,256]{2,1,0:T(8,128)S(1)}, u32[]{:S(2)}, u32[]{:S(2)}) %collective-permute-start.2) | collective-permute-done | bytes 98336 | tf_op jit(solution)/shard_map/ppermute | solution.py:475
  23.6 0.0 all-to-all-done.refs_0_
  23.6 2.2 %shard_map.129 = f32[3,2,32,256]{3,2,1,0:T(8,128)} custom-call(f32[8,120,128]{2,1,0:T(8,128)S(1)} %all-to-all-done.refs_0_, f32[24,256]{1,0:T(8,128)S(1)} %get-tuple-element.21.refs_1_, f32[136,256]{1,0:T(8,128)S(1)} %get-tuple-element.22.refs_2_, f32[104,256]{1,0:T(8,128)S(1)} %get-tuple-element.23.refs_3_, s32[1,256]{1,0:T(1,128)S(1)} %get-tuple-element.24.refs_4_, ...), custom_call_target="tpu_custom_call" | custom-call | flops 1000000000 | bytes 1500000 | tf_op jit(solution)/shard_map/pallas_call | solution.py:581
Async XLA Ops:
  3.5 18.4 %copy-start = (f32[3,2,32,256]{3,2,1,0:T(8,128)S(1)}, f32[3,2,32,256]{3,2,1,0:T(8,128)}, u32[]{:S(2)}) copy-start(f32[3,2,32,256]{3,2,1,0:T(8,128)} %disp_ref.1) | copy-start | bytes 589828
  3.5 18.4 %copy-start.1 = (f32[2,32,256]{2,1,0:T(8,128)S(1)}, f32[2,32,256]{2,1,0:T(8,128)}, u32[]{:S(2)}) copy-start(f32[2,32,256]{2,1,0:T(8,128)} %modulus_ref.1) | copy-start | bytes 196612
  3.5 18.4 %copy-start.2 = (f32[24,24]{1,0:T(8,128)S(1)}, f32[24,24]{1,0:T(8,128)}, u32[]{:S(2)}) copy-start(f32[24,24]{1,0:T(8,128)} %stiffness_ref.1) | copy-start | bytes 6916
  3.5 20.1 %all-to-all-start = ((f32[8,120,128]{2,1,0:T(8,128)}), f32[8,120,128]{2,1,0:T(8,128)S(1)}, u32[]{:S(2)}, u32[]{:S(2)}) async-start(f32[8,120,128]{2,1,0:T(8,128)} %get-tuple-element.20), calls=%async_computation | async-start | bytes 983040 | tf_op jit(solution)/shard_map/all_to_all | solution.py:568
  9.6 12.3 %collective-permute-start = (f32[3,32,256]{2,1,0:T(8,128)S(1)}, f32[3,32,256]{2,1,0:T(8,128)S(1)}, u32[]{:S(2)}, u32[]{:S(2)}) collective-permute-start(f32[3,32,256]{2,1,0:T(8,128)S(1)} %get-tuple-element.29.own_ref), channel_id=1, source_target_pairs={{0,1},{1,0},{2,3},{3,2},{4,5},{5,4},{6,7},{7,6},{8,9},{9,8},{10,11... | collective-permute-start | bytes 294920 | tf_op jit(solution)/shard_map/ppermute | solution.py:475
  9.6 12.3 %collective-permute-start.1 = (f32[32,256]{1,0:T(8,128)S(1)}, f32[32,256]{1,0:T(8,128)S(1)}, u32[]{:S(2)}, u32[]{:S(2)}) collective-permute-start(f32[32,256]{1,0:T(8,128)S(1)} %get-tuple-element.30.top_ref.refs_13_), channel_id=1, source_target_pairs={{0,1},{1,2},{2,3},{3,4},{4,5},{5,6},{6,7},{7,8},{8,9},{9,10},{10,1... | collective-permute-start | bytes 98312 | tf_op jit(solution)/shard_map/ppermute | solution.py:479
  12.0 11.6 %collective-permute-start.2 = (f32[3,32,256]{2,1,0:T(8,128)S(1)}, f32[3,32,256]{2,1,0:T(8,128)S(1)}, u32[]{:S(2)}, u32[]{:S(2)}) collective-permute-start(f32[3,32,256]{2,1,0:T(8,128)S(1)} %get-tuple-element.34.refs_11_), channel_id=1, source_target_pairs={{1,2},{2,1},{3,4},{4,3},{5,6},{6,5},{7,8},{8,7},{9,10},{10,9},{11,... | collective-permute-start | bytes 294920 | tf_op jit(solution)/shard_map/ppermute | solution.py:475

commit v11 on v9

--- a/solution.py
+++ b/solution.py
@@ -126,19 +126,18 @@
 def first_kernel(capacity, heights, *refs):
     (
         nodes_hbm, disp_hbm, mortar_hbm, rank_hbm, face_hbm, count_hbm, weight_hbm, normal_hbm,
-        gap_hbm, shape_hbm, modulus_hbm, mass_hbm,
-        sent_ref, rows_ref, words_ref, turned_ref, mortar_ref, rank_ref, face_ref, nodes, mass_ref,
+        gap_hbm, shape_hbm, modulus_hbm,
+        sent_ref, rows_ref, words_ref, turned_ref, mortar_ref, rank_ref, face_ref, nodes,
         inner_ref, outer_ref,
-        disp, count, weight, normal_v, gap_v, shape, modulus, halved, shapes, gaps, sems, copy_sems,
+        disp, count, weight, normal_v, gap_v, shape, modulus, blocks, sems, copy_sems,
     ) = refs
     components, layers, rows_y, cols_x = disp.shape
     sources = (
         nodes_hbm, disp_hbm, rank_hbm, face_hbm, mortar_hbm, shape_hbm, count_hbm, weight_hbm,
-        normal_hbm, gap_hbm, modulus_hbm, mass_hbm,
+        normal_hbm, gap_hbm, modulus_hbm.at[disp.shape[1] - 1],
     )
     targets = (
         nodes, disp, rank_ref, face_ref, mortar_ref, shape, count, weight, normal_v, gap_v, modulus,
-        mass_ref,
     )
     brought = [
         pltpu.make_async_copy(source, target, sems.at[i])
@@ -151,7 +150,7 @@
     pair_total = rank_ref.shape[1]
     face_count = nodes.shape[1]
     strips = layers * rows_y
-    for copy in brought[:-2]:
+    for copy in brought[:-1]:
         copy.wait()
     rank, face, mortar = rank_ref[...], face_ref[...], mortar_ref[...]
     normal = normal_v[...]
@@ -191,23 +190,23 @@
     rows = rows_ref[...]
     high = rows.shape[0]
     rows_high = high * cols_x // LANES
-    for i in range(cols_x // LANES):
-        halved[i * high : (i + 1) * high] = rows[:, i * LANES : (i + 1) * LANES]
-    starts = (rows_high, rows_high + heights[0], rows_high + sum(heights))
-    copies = []
+    halved = jnp.concatenate(
+        [rows[:, i * LANES : (i + 1) * LANES] for i in range(cols_x // LANES)], axis=0
+    )
+    starts = (0, rows_high, rows_high + heights[0], rows_high + sum(heights))
+    copies = [
+        pltpu.make_async_copy(
+            blocks.at[:, start:end], sent_ref.at[:, start:end], copy_sems.at[i]
+        )
+        for i, (start, end) in enumerate(zip(starts, starts[1:]))
+    ]
+    for domain in range(domains):
+        blocks[domain, :rows_high] = halved
+    copies[0].start()
     for domain in range(domains):
         spot = place_in_group(domain, domains)
-        shapes[domain] = folded(placed, heights[0], capacity, domain)
-        copies += [
-            pltpu.make_async_copy(halved, sent_ref.at[spot, :rows_high], copy_sems.at[0, domain]),
-            pltpu.make_async_copy(
-                shapes.at[domain],
-                sent_ref.at[spot, starts[0] : starts[1]],
-                copy_sems.at[1, domain],
-            ),
-        ]
-        for copy in copies[-2:]:
-            copy.start()
+        blocks[spot, starts[1] : starts[2]] = folded(placed, heights[0], capacity, domain)
+    copies[1].start()
 
     mortar_rows = looked_up(rows, mortar, marks(mortar & (cols_x - 1), cols_x))
     for node in range(4):
@@ -225,13 +224,8 @@
     placed = routed(short_words, group * heights[1], place)
     for domain in range(domains):
         spot = place_in_group(domain, domains)
-        gaps[domain] = folded(placed, heights[1], capacity, domain)
-        copies.append(
-            pltpu.make_async_copy(
-                gaps.at[domain], sent_ref.at[spot, starts[1] : starts[2]], copy_sems.at[2, domain]
-            )
-        )
-        copies[-1].start()
+        blocks[spot, starts[2] :] = folded(placed, heights[1], capacity, domain)
+    copies[2].start()
 
     words_ref[: 4 * full] = long_words
     words_ref[4 * full :] = short_words
@@ -240,13 +234,12 @@
         turned_ref[node * full : (node + 1) * full] = turned[:full]
         turned_ref[4 * full + node : 4 * full + node + 1] = turned[full:]
 
-    for copy in brought[-2:]:
-        copy.wait()
+    brought[-1].wait()
     sub = lax.axis_index("sub")
     for target, layer in ((inner_ref, (1 - sub) * (layers - 1)), (outer_ref, sub * (layers - 1))):
         for k in range(components):
             target[k] = disp[k, layer]
-        target[components] = modulus[layer]
+        target[components] = modulus[...]
     for copy in copies:
         copy.wait()
 
@@ -498,13 +491,12 @@
         pair_gap,
         jnp.swapaxes(pair_shape, 0, 1),
         modulus,
-        node_mass,
     ]
     edge = shaped((components + 1, rows_y, cols_x))
     in_hbm = pl.BlockSpec(memory_space=pltpu.HBM)
     in_vmem = pl.BlockSpec(memory_space=pltpu.VMEM)
-    kept = [displacement, *arrays[5:-1]]
-    sent, rows, words, turned, mortar, rank, face, nodes, mass, inner, outer = on_core(
+    kept = [displacement, *arrays[5:-1], modulus[0]]
+    sent, rows, words, turned, mortar, rank, face, nodes, inner, outer = on_core(
         first,
         [
             shaped((domains, rows_high + sum(heights), LANES)),
@@ -515,21 +507,18 @@
             shaped(line, jnp.int32),
             shaped(line, jnp.int32),
             shaped(face_nodes.shape, jnp.int32),
-            shaped(node_mass.shape),
             edge,
             edge,
         ],
         900_000_000,
         1_500_000,
         in_specs=[in_hbm] * len(arrays),
-        out_specs=[in_hbm] + [in_vmem] * 10,
+        out_specs=[in_hbm] + [in_vmem] * 9,
         scratch_shapes=[pltpu.VMEM(x.shape, x.dtype) for x in kept]
         + [
-            pltpu.VMEM((rows_high, LANES), F32),
-            pltpu.VMEM((domains, heights[0], LANES), F32),
-            pltpu.VMEM((domains, heights[1], LANES), F32),
+            pltpu.VMEM((domains, rows_high + sum(heights), LANES), F32),
             pltpu.SemaphoreType.DMA((len(arrays),)),
-            pltpu.SemaphoreType.DMA((3, domains)),
+            pltpu.SemaphoreType.DMA((3,)),
         ],
     )(*[pltpu.with_memory_space_constraint(x, pltpu.HBM) for x in arrays])
     order = [place_in_group(domain, domains) for domain in range(domains)]
@@ -541,10 +530,10 @@
     size = 8 * components * GROUP
     internal, blocks, inverse = on_core(
         internal_kernel,
-        [shaped(displacement.shape), shaped((2 * size, size), BF16), shaped(mass.shape)],
+        [shaped(displacement.shape), shaped((2 * size, size), BF16), shaped(node_mass.shape)],
         1_000_000_000,
         700_000,
-    )(displacement, modulus, stiffness, mass, inner, inner_halo)
+    )(displacement, modulus, stiffness, node_mass, inner, inner_halo)
     return on_core(last, shaped(displacement.shape), 1_000_000_000, 1_500_000)(
         got, rows, words, turned, mortar, rank, face, nodes, inverse, internal, blocks, outer, outer_halo
     )

time: 25.6 us -> 25.5 us (level)
  no operation moved by 1% of the time
where the time goes in v11:
time: 25.5 us; the launch traced here: 25.2 us
  starting transfers between devices  9.52 us (37%)
  waiting for transfers between devices  9.46 us (37%)
  Pallas kernels  6.05 us (24%)
    ppermute x2, waiting for transfers between devices, swapped(): return lax.ppermute(block, axis, route)  9.46 us
    all_to_all x1, starting transfers between devices, shards(): lax.all_to_all(sent, 'dom', split_axis=0, concat_axis=0, axis_index_group...  6.06 us
    ppermute x2, starting transfers between devices, swapped(): return lax.ppermute(block, axis, route)  3.47 us
    pallas_call x1, Pallas kernels, shards(): on_core(first, [shaped((domains, rows_high + sum(heights), LANES)), shape...  2.9 us
    pallas_call x1, Pallas kernels, shards(): on_core(last, shaped(displacement.shape), 1000000000, 1500000)  2.14 us
    pallas_call x1, Pallas kernels, shards(): on_core(internal_kernel, [shaped(displacement.shape), shaped((2 * size, s...  1.01 us
  transfers between devices with their start and end apart: 3, of which 1 were waited for; matrix products, arithmetic and copies ran while one was open for 0% of the time, Pallas kernels for 4%

profile of v11, /device:TPU:16, one launch (start us, length us, event | category | flops | bytes accessed | tf_op | source)
XLA Modules:
  0.0 25.2 jit_solution(1217093198737950496)
XLA Ops:
  0.0 2.9 %shard_map.127 = (f32[8,120,128]{2,1,0:T(8,128)}, f32[24,256]{1,0:T(8,128)S(1)}, f32[136,256]{1,0:T(8,128)S(1)}, f32[104,256]{1,0:T(8,128)S(1)}, s32[1,256]{1,0:...) custom-call(s32[4,512]{1,0:T(4,128)} %refs_0_.1, ...), custom_call_target="tpu_custom_call" | custom-call | flops 900000000 | bytes 1500000 | tf_op jit(solution)/shard_map/pallas_call | solution.py:499
  2.9 0.0 copy-start
  2.9 0.0 copy-start.1
  2.9 0.0 copy-start.2
  2.9 0.0 copy-start.3
  3.0 6.1 %all-to-all-start = ((f32[8,120,128]{2,1,0:T(8,128)}), f32[8,120,128]{2,1,0:T(8,128)S(1)}, u32[]{:S(2)}, u32[]{:S(2)}) async-start(f32[8,120,128]{2,1,0:T(8,128)} %get-tuple-element.18), calls=%async_computation | async-start | bytes 983040 | tf_op jit(solution)/shard_map/all_to_all | solution.py:525
  9.0 0.0 collective-permute-start
  9.0 3.5 %collective-permute-start.1 = (f32[4,32,256]{2,1,0:T(8,128)S(1)}, f32[4,32,256]{2,1,0:T(8,128)S(1)}, u32[]{:S(2)}, u32[]{:S(2)}) collective-permute-start(f32[4,32,256]{2,1,0:T(8,128)S(1)} %get-tuple-element.30.refs_11_), channel_id=1, source_target_pairs={{1,2},{2,1},{3,4},{4,3},{5,6},{6,5},{7,8},{8,7},{9,10},{10,9},{11,... | collective-permute-start | bytes 393224 | tf_op jit(solution)/shard_map/ppermute | solution.py:441
  12.5 0.0 collective-permute-done.halo_ref
  12.5 0.0 copy-done
  12.5 0.0 copy-done.1
  12.5 0.0 copy-done.2
  12.5 0.0 copy-done.3
  12.5 1.0 %shard_map.128 = (f32[3,2,32,256]{3,2,1,0:T(8,128)S(1)}, bf16[384,192]{1,0:T(8,128)(2,1)S(1)}, f32[2,32,256]{2,1,0:T(8,128)S(1)}) custom-call(f32[3,2,32,256]{3,2,1,0:T(8,128)S(1)} %copy-done, f32[2,32,256]{2,1,0:T(8,128)S(1)} %copy-done.1, f32[24,24]{1,0:T(8,128)S(1)} %copy-done.3, f32[2,32,256]{2,1,0:T(8,128)S(1)} %copy-done.2, ...), custom_call_target="tpu_custom_call" | custom-call | flops 1000000000 | bytes 700000 | tf_op jit(solution)/shard_map/pallas_call | solution.py:531
  13.6 9.5 %collective-permute-done.1.refs_12_ = f32[4,32,256]{2,1,0:T(8,128)S(1)} collective-permute-done((f32[4,32,256]{2,1,0:T(8,128)S(1)}, f32[4,32,256]{2,1,0:T(8,128)S(1)}, u32[]{:S(2)}, u32[]{:S(2)}) %collective-permute-start.1) | collective-permute-done | bytes 131104 | tf_op jit(solution)/shard_map/ppermute | solution.py:441
  23.0 0.0 all-to-all-done.refs_0_
  23.0 2.1 %shard_map.129 = f32[3,2,32,256]{3,2,1,0:T(8,128)} custom-call(f32[8,120,128]{2,1,0:T(8,128)S(1)} %all-to-all-done.refs_0_, f32[24,256]{1,0:T(8,128)S(1)} %get-tuple-element.19.refs_1_, f32[136,256]{1,0:T(8,128)S(1)} %get-tuple-element.20.refs_2_, f32[104,256]{1,0:T(8,128)S(1)} %get-tuple-element.21.refs_3_, s32[1,256]{1,0:T(1,128)S(1)} %get-tuple-element.22.refs_4_, ...), custom_call_target="tpu_custom_call" | custom-call | flops 1000000000 | bytes 1500000 | tf_op jit(solution)/shard_map/pallas_call | solution.py:537
Async XLA Ops:
  2.9 9.6 %copy-start = (f32[3,2,32,256]{3,2,1,0:T(8,128)S(1)}, f32[3,2,32,256]{3,2,1,0:T(8,128)}, u32[]{:S(2)}) copy-start(f32[3,2,32,256]{3,2,1,0:T(8,128)} %disp_ref.1) | copy-start | bytes 589828
  2.9 9.6 %copy-start.1 = (f32[2,32,256]{2,1,0:T(8,128)S(1)}, f32[2,32,256]{2,1,0:T(8,128)}, u32[]{:S(2)}) copy-start(f32[2,32,256]{2,1,0:T(8,128)} %modulus_ref.1) | copy-start | bytes 196612
  2.9 9.6 %copy-start.2 = (f32[2,32,256]{2,1,0:T(8,128)S(1)}, f32[2,32,256]{2,1,0:T(8,128)}, u32[]{:S(2)}) copy-start(f32[2,32,256]{2,1,0:T(8,128)} %mass_ref.1) | copy-start | bytes 196612
  2.9 9.6 %copy-start.3 = (f32[24,24]{1,0:T(8,128)S(1)}, f32[24,24]{1,0:T(8,128)}, u32[]{:S(2)}) copy-start(f32[24,24]{1,0:T(8,128)} %stiffness_ref.1) | copy-start | bytes 6916
  3.0 20.1 %all-to-all-start = ((f32[8,120,128]{2,1,0:T(8,128)}), f32[8,120,128]{2,1,0:T(8,128)S(1)}, u32[]{:S(2)}, u32[]{:S(2)}) async-start(f32[8,120,128]{2,1,0:T(8,128)} %get-tuple-element.18), calls=%async_computation | async-start | bytes 983040 | tf_op jit(solution)/shard_map/all_to_all | solution.py:525
  9.0 3.5 %collective-permute-start = (f32[4,32,256]{2,1,0:T(8,128)S(1)}, f32[4,32,256]{2,1,0:T(8,128)S(1)}, u32[]{:S(2)}, u32[]{:S(2)}) collective-permute-start(f32[4,32,256]{2,1,0:T(8,128)S(1)} %get-tuple-element.26.own_ref), channel_id=1, source_target_pairs={{0,1},{1,0},{2,3},{3,2},{4,5},{5,4},{6,7},{7,6},{8,9},{9,8},{10,11... | collective-permute-start | bytes 393224 | tf_op jit(solution)/shard_map/ppermute | solution.py:441
  9.0 14.0 %collective-permute-start.1 = (f32[4,32,256]{2,1,0:T(8,128)S(1)}, f32[4,32,256]{2,1,0:T(8,128)S(1)}, u32[]{:S(2)}, u32[]{:S(2)}) collective-permute-start(f32[4,32,256]{2,1,0:T(8,128)S(1)} %get-tuple-element.30.refs_11_), channel_id=1, source_target_pairs={{1,2},{2,1},{3,4},{4,3},{5,6},{6,5},{7,8},{8,7},{9,10},{10,9},{11,... | collective-permute-start | bytes 393224 | tf_op jit(solution)/shard_map/ppermute | solution.py:441

commit v12 on v11

--- a/solution.py
+++ b/solution.py
@@ -120,7 +120,10 @@
 
 
 def place_in_group(domain, domains):
-    return {0: domains - 1, domains - 1: 0}.get(domain, domain)
+    half = domains // 2
+    if isinstance(domain, int):
+        return 2 * (domains - 1 - domain) if domain >= half else 2 * (half - 1 - domain) + 1
+    return jnp.where(domain >= half, 2 * (domains - 1 - domain), 2 * (half - 1 - domain) + 1)
 
 
 def first_kernel(capacity, heights, *refs):
@@ -259,8 +262,7 @@
     own_rows = rows_ref[...]
 
     rank, face = rank_ref[...], face_ref[...]
-    end = domains - 1
-    place = jnp.where(rank == 0, end, jnp.where(rank == end, 0, rank))
+    place = place_in_group(rank, domains)
     at = marks(face & (cols_x - 1), cols_x)
     step = min(domains, 8)
 
@@ -521,7 +523,7 @@
             pltpu.SemaphoreType.DMA((3,)),
         ],
     )(*[pltpu.with_memory_space_constraint(x, pltpu.HBM) for x in arrays])
-    order = [place_in_group(domain, domains) for domain in range(domains)]
+    order = sorted(range(domains), key=lambda domain: place_in_group(domain, domains))
     got = lax.all_to_all(
         sent, "dom", split_axis=0, concat_axis=0, axis_index_groups=[order], tiled=True
     )

time: 25.5 us -> 26.5 us (1.039)
  the two profiles are of different devices: /device:TPU:16 before, /device:TPU:0 now
where the time goes in v12:
time: 26.5 us; the launch traced here: 26.3 us
  starting transfers between devices  10.2 us (38%)
  waiting for transfers between devices  9.93 us (37%)
  Pallas kernels  6.07 us (23%)
    all_to_all x1, starting transfers between devices, shards(): lax.all_to_all(sent, 'dom', split_axis=0, concat_axis=0, axis_index_group...  9.54 us
    all_to_all x1, waiting for transfers between devices, shards(): lax.all_to_all(sent, 'dom', split_axis=0, concat_axis=0, axis_index_group...  9.25 us
    pallas_call x1, Pallas kernels, shards(): on_core(first, [shaped((domains, rows_high + sum(heights), LANES)), shape...  2.9 us
    pallas_call x1, Pallas kernels, shards(): on_core(last, shaped(displacement.shape), 1000000000, 1500000)  2.14 us
    pallas_call x1, Pallas kernels, shards(): on_core(internal_kernel, [shaped(displacement.shape), shaped((2 * size, s...  1.03 us
    ppermute x2, waiting for transfers between devices, swapped(): return lax.ppermute(block, axis, route)  0.68 us
    ppermute x2, starting transfers between devices, swapped(): return lax.ppermute(block, axis, route)  0.66 us
  transfers between devices with their start and end apart: 3, of which 2 were waited for; matrix products, arithmetic and copies ran while one was open for 0% of the time, Pallas kernels for 4%

profile of v12, /device:TPU:0, one launch (start us, length us, event | category | flops | bytes accessed | tf_op | source)
XLA Modules:
  0.0 26.3 jit_solution(2930799064292625680)
XLA Ops:
  0.0 2.9 %shard_map.127 = (f32[8,120,128]{2,1,0:T(8,128)}, f32[24,256]{1,0:T(8,128)S(1)}, f32[136,256]{1,0:T(8,128)S(1)}, f32[104,256]{1,0:T(8,128)S(1)}, s32[1,256]{1,0:...) custom-call(s32[4,512]{1,0:T(4,128)} %refs_0_.1, ...), custom_call_target="tpu_custom_call" | custom-call | flops 900000000 | bytes 1500000 | tf_op jit(solution)/shard_map/pallas_call | solution.py:501
  2.9 0.0 copy-start
  2.9 0.0 copy-start.1
  2.9 0.0 copy-start.2
  2.9 0.0 copy-start.3
  3.0 9.5 %all-to-all-start = ((f32[8,120,128]{2,1,0:T(8,128)}), f32[8,120,128]{2,1,0:T(8,128)S(1)}, u32[]{:S(2)}, u32[]{:S(2)}) async-start(f32[8,120,128]{2,1,0:T(8,128)} %get-tuple-element.18), calls=%async_computation | async-start | bytes 983040 | tf_op jit(solution)/shard_map/all_to_all | solution.py:527
  12.5 0.0 collective-permute-start
  12.5 0.7 %collective-permute-start.1 = (f32[4,32,256]{2,1,0:T(8,128)S(1)}, f32[4,32,256]{2,1,0:T(8,128)S(1)}, u32[]{:S(2)}, u32[]{:S(2)}) collective-permute-start(f32[4,32,256]{2,1,0:T(8,128)S(1)} %get-tuple-element.30.refs_11_), channel_id=1, source_target_pairs={{1,2},{2,1},{3,4},{4,3},{5,6},{6,5},{7,8},{8,7},{9,10},{10,9},{11,... | collective-permute-start | bytes 393224 | tf_op jit(solution)/shard_map/ppermute | solution.py:443
  13.2 0.7 %collective-permute-done.halo_ref = f32[4,32,256]{2,1,0:T(8,128)S(1)} collective-permute-done((f32[4,32,256]{2,1,0:T(8,128)S(1)}, f32[4,32,256]{2,1,0:T(8,128)S(1)}, u32[]{:S(2)}, u32[]{:S(2)}) %collective-permute-start) | collective-permute-done | bytes 131104 | tf_op jit(solution)/shard_map/ppermute | solution.py:443
  13.9 0.0 copy-done
  13.9 0.0 copy-done.1
  13.9 0.0 copy-done.2
  13.9 0.0 copy-done.3
  13.9 1.0 %shard_map.128 = (f32[3,2,32,256]{3,2,1,0:T(8,128)S(1)}, bf16[384,192]{1,0:T(8,128)(2,1)S(1)}, f32[2,32,256]{2,1,0:T(8,128)S(1)}) custom-call(f32[3,2,32,256]{3,2,1,0:T(8,128)S(1)} %copy-done, f32[2,32,256]{2,1,0:T(8,128)S(1)} %copy-done.1, f32[24,24]{1,0:T(8,128)S(1)} %copy-done.3, f32[2,32,256]{2,1,0:T(8,128)S(1)} %copy-done.2, ...), custom_call_target="tpu_custom_call" | custom-call | flops 1000000000 | bytes 700000 | tf_op jit(solution)/shard_map/pallas_call | solution.py:533
  14.9 0.0 collective-permute-done.1.refs_12_
  14.9 9.2 %all-to-all-done.refs_0_ = f32[8,120,128]{2,1,0:T(8,128)S(1)} async-done(((f32[8,120,128]{2,1,0:T(8,128)}), f32[8,120,128]{2,1,0:T(8,128)S(1)}, u32[]{:S(2)}, u32[]{:S(2)}) %all-to-all-start) | async-done | bytes 491552 | tf_op jit(solution)/shard_map/all_to_all | solution.py:527
  24.2 2.1 %shard_map.129 = f32[3,2,32,256]{3,2,1,0:T(8,128)} custom-call(f32[8,120,128]{2,1,0:T(8,128)S(1)} %all-to-all-done.refs_0_, f32[24,256]{1,0:T(8,128)S(1)} %get-tuple-element.19.refs_1_, f32[136,256]{1,0:T(8,128)S(1)} %get-tuple-element.20.refs_2_, f32[104,256]{1,0:T(8,128)S(1)} %get-tuple-element.21.refs_3_, s32[1,256]{1,0:T(1,128)S(1)} %get-tuple-element.22.refs_4_, ...), custom_call_target="tpu_custom_call" | custom-call | flops 1000000000 | bytes 1500000 | tf_op jit(solution)/shard_map/pallas_call | solution.py:539
Async XLA Ops:
  2.9 10.9 %copy-start = (f32[3,2,32,256]{3,2,1,0:T(8,128)S(1)}, f32[3,2,32,256]{3,2,1,0:T(8,128)}, u32[]{:S(2)}) copy-start(f32[3,2,32,256]{3,2,1,0:T(8,128)} %disp_ref.1) | copy-start | bytes 589828
  2.9 10.9 %copy-start.1 = (f32[2,32,256]{2,1,0:T(8,128)S(1)}, f32[2,32,256]{2,1,0:T(8,128)}, u32[]{:S(2)}) copy-start(f32[2,32,256]{2,1,0:T(8,128)} %modulus_ref.1) | copy-start | bytes 196612
  2.9 10.9 %copy-start.2 = (f32[2,32,256]{2,1,0:T(8,128)S(1)}, f32[2,32,256]{2,1,0:T(8,128)}, u32[]{:S(2)}) copy-start(f32[2,32,256]{2,1,0:T(8,128)} %mass_ref.1) | copy-start | bytes 196612
  2.9 10.9 %copy-start.3 = (f32[24,24]{1,0:T(8,128)S(1)}, f32[24,24]{1,0:T(8,128)}, u32[]{:S(2)}) copy-start(f32[24,24]{1,0:T(8,128)} %stiffness_ref.1) | copy-start | bytes 6916
  3.0 21.2 %all-to-all-start = ((f32[8,120,128]{2,1,0:T(8,128)}), f32[8,120,128]{2,1,0:T(8,128)S(1)}, u32[]{:S(2)}, u32[]{:S(2)}) async-start(f32[8,120,128]{2,1,0:T(8,128)} %get-tuple-element.18), calls=%async_computation | async-start | bytes 983040 | tf_op jit(solution)/shard_map/all_to_all | solution.py:527
  12.5 1.3 %collective-permute-start = (f32[4,32,256]{2,1,0:T(8,128)S(1)}, f32[4,32,256]{2,1,0:T(8,128)S(1)}, u32[]{:S(2)}, u32[]{:S(2)}) collective-permute-start(f32[4,32,256]{2,1,0:T(8,128)S(1)} %get-tuple-element.26.own_ref), channel_id=1, source_target_pairs={{0,1},{1,0},{2,3},{3,2},{4,5},{5,4},{6,7},{7,6},{8,9},{9,8},{10,11... | collective-permute-start | bytes 393224 | tf_op jit(solution)/shard_map/ppermute | solution.py:443
  12.5 2.4 %collective-permute-start.1 = (f32[4,32,256]{2,1,0:T(8,128)S(1)}, f32[4,32,256]{2,1,0:T(8,128)S(1)}, u32[]{:S(2)}, u32[]{:S(2)}) collective-permute-start(f32[4,32,256]{2,1,0:T(8,128)S(1)} %get-tuple-element.30.refs_11_), channel_id=1, source_target_pairs={{1,2},{2,1},{3,4},{4,3},{5,6},{6,5},{7,8},{8,7},{9,10},{10,9},{11,... | collective-permute-start | bytes 393224 | tf_op jit(solution)/shard_map/ppermute | solution.py:443

commit v13 on v11

--- a/solution.py
+++ b/solution.py
@@ -120,7 +120,7 @@
 
 
 def place_in_group(domain, domains):
-    return {0: domains - 1, domains - 1: 0}.get(domain, domain)
+    return domains - 1 - domain
 
 
 def first_kernel(capacity, heights, *refs):
@@ -259,8 +259,7 @@
     own_rows = rows_ref[...]
 
     rank, face = rank_ref[...], face_ref[...]
-    end = domains - 1
-    place = jnp.where(rank == 0, end, jnp.where(rank == end, 0, rank))
+    place = place_in_group(rank, domains)
     at = marks(face & (cols_x - 1), cols_x)
     step = min(domains, 8)
 
@@ -310,19 +309,20 @@
     )
     forces = summed(times_turned(stacked_terms(forces), at))
     forces = jnp.concatenate([forces[:12], forces[12:]], axis=1)
-    total = jnp.zeros((2 * components * strips, cols_x), F32)
     parts = [term.astype(F32) for term in terms_of(forces, 2)]
+    spread, along_x = [], []
     for corner in range(4):
         index = nodes_ref[corner : corner + 1, :]
         strip = marks(index >> halves(cols_x), strips)
-        spread = []
+        rows = []
         for part in parts:
             for k in range(components):
                 at = k * 4 + corner
                 row = jnp.broadcast_to(part[at : at + 1], (16, face_count)).astype(BF16)
-                spread.append(strip * jnp.concatenate([row] * (strips // 16), axis=0))
-        along_x = marks(index & (cols_x - 1), cols_x)
-        total = total + times_turned(jnp.concatenate(spread, axis=0), along_x)
+                rows.append(strip * jnp.concatenate([row] * (strips // 16), axis=0))
+        spread.append(jnp.concatenate(rows, axis=0))
+        along_x.append(marks(index & (cols_x - 1), cols_x))
+    total = times_turned(jnp.concatenate(spread, axis=1), jnp.concatenate(along_x, axis=1))
     contact = summed(total).reshape(components, layers, rows_y, cols_x)
     upward = lax.axis_index("sub") == 1
     edge = edge_part(upward, own_ref, halo_ref, blocks_ref)

time: 25.5 us -> 26.5 us (1.039)
  the two profiles are of different devices: /device:TPU:16 before, /device:TPU:0 now
where the time goes in v13:
time: 26.5 us; the launch traced here: 26.3 us
  starting transfers between devices  10.2 us (38%)
  waiting for transfers between devices  9.92 us (37%)
  Pallas kernels  6.07 us (23%)
    all_to_all x1, starting transfers between devices, shards(): lax.all_to_all(sent, 'dom', split_axis=0, concat_axis=0, axis_index_group...  9.54 us
    all_to_all x1, waiting for transfers between devices, shards(): lax.all_to_all(sent, 'dom', split_axis=0, concat_axis=0, axis_index_group...  9.24 us
    pallas_call x1, Pallas kernels, shards(): on_core(first, [shaped((domains, rows_high + sum(heights), LANES)), shape...  2.9 us
    pallas_call x1, Pallas kernels, shards(): on_core(last, shaped(displacement.shape), 1000000000, 1500000)  2.14 us
    pallas_call x1, Pallas kernels, shards(): on_core(internal_kernel, [shaped(displacement.shape), shaped((2 * size, s...  1.03 us
    ppermute x2, waiting for transfers between devices, swapped(): return lax.ppermute(block, axis, route)  0.68 us
    ppermute x2, starting transfers between devices, swapped(): return lax.ppermute(block, axis, route)  0.66 us
  transfers between devices with their start and end apart: 3, of which 2 were waited for; matrix products, arithmetic and copies ran while one was open for 0% of the time, Pallas kernels for 4%

profile of v13, /device:TPU:0, one launch (start us, length us, event | category | flops | bytes accessed | tf_op | source)
XLA Modules:
  0.0 26.3 jit_solution(1960587444198802065)
XLA Ops:
  0.0 2.9 %shard_map.127 = (f32[8,120,128]{2,1,0:T(8,128)}, f32[24,256]{1,0:T(8,128)S(1)}, f32[136,256]{1,0:T(8,128)S(1)}, f32[104,256]{1,0:T(8,128)S(1)}, s32[1,256]{1,0:...) custom-call(s32[4,512]{1,0:T(4,128)} %refs_0_.1, ...), custom_call_target="tpu_custom_call" | custom-call | flops 900000000 | bytes 1500000 | tf_op jit(solution)/shard_map/pallas_call | solution.py:499
  2.9 0.0 copy-start
  2.9 0.0 copy-start.1
  2.9 0.0 copy-start.2
  2.9 0.0 copy-start.3
  3.0 9.5 %all-to-all-start = ((f32[8,120,128]{2,1,0:T(8,128)}), f32[8,120,128]{2,1,0:T(8,128)S(1)}, u32[]{:S(2)}, u32[]{:S(2)}) async-start(f32[8,120,128]{2,1,0:T(8,128)} %get-tuple-element.18), calls=%async_computation | async-start | bytes 983040 | tf_op jit(solution)/shard_map/all_to_all | solution.py:525
  12.5 0.0 collective-permute-start
  12.5 0.7 %collective-permute-start.1 = (f32[4,32,256]{2,1,0:T(8,128)S(1)}, f32[4,32,256]{2,1,0:T(8,128)S(1)}, u32[]{:S(2)}, u32[]{:S(2)}) collective-permute-start(f32[4,32,256]{2,1,0:T(8,128)S(1)} %get-tuple-element.30.refs_11_), channel_id=1, source_target_pairs={{1,2},{2,1},{3,4},{4,3},{5,6},{6,5},{7,8},{8,7},{9,10},{10,9},{11,... | collective-permute-start | bytes 393224 | tf_op jit(solution)/shard_map/ppermute | solution.py:441
  13.2 0.7 %collective-permute-done.halo_ref = f32[4,32,256]{2,1,0:T(8,128)S(1)} collective-permute-done((f32[4,32,256]{2,1,0:T(8,128)S(1)}, f32[4,32,256]{2,1,0:T(8,128)S(1)}, u32[]{:S(2)}, u32[]{:S(2)}) %collective-permute-start) | collective-permute-done | bytes 131104 | tf_op jit(solution)/shard_map/ppermute | solution.py:441
  13.9 0.0 copy-done
  13.9 0.0 copy-done.1
  13.9 0.0 copy-done.2
  13.9 0.0 copy-done.3
  13.9 1.0 %shard_map.128 = (f32[3,2,32,256]{3,2,1,0:T(8,128)S(1)}, bf16[384,192]{1,0:T(8,128)(2,1)S(1)}, f32[2,32,256]{2,1,0:T(8,128)S(1)}) custom-call(f32[3,2,32,256]{3,2,1,0:T(8,128)S(1)} %copy-done, f32[2,32,256]{2,1,0:T(8,128)S(1)} %copy-done.1, f32[24,24]{1,0:T(8,128)S(1)} %copy-done.3, f32[2,32,256]{2,1,0:T(8,128)S(1)} %copy-done.2, ...), custom_call_target="tpu_custom_call" | custom-call | flops 1000000000 | bytes 700000 | tf_op jit(solution)/shard_map/pallas_call | solution.py:531
  14.9 0.0 collective-permute-done.1.refs_12_
  14.9 9.2 %all-to-all-done.refs_0_ = f32[8,120,128]{2,1,0:T(8,128)S(1)} async-done(((f32[8,120,128]{2,1,0:T(8,128)}), f32[8,120,128]{2,1,0:T(8,128)S(1)}, u32[]{:S(2)}, u32[]{:S(2)}) %all-to-all-start) | async-done | bytes 491552 | tf_op jit(solution)/shard_map/all_to_all | solution.py:525
  24.2 2.1 %shard_map.129 = f32[3,2,32,256]{3,2,1,0:T(8,128)} custom-call(f32[8,120,128]{2,1,0:T(8,128)S(1)} %all-to-all-done.refs_0_, f32[24,256]{1,0:T(8,128)S(1)} %get-tuple-element.19.refs_1_, f32[136,256]{1,0:T(8,128)S(1)} %get-tuple-element.20.refs_2_, f32[104,256]{1,0:T(8,128)S(1)} %get-tuple-element.21.refs_3_, s32[1,256]{1,0:T(1,128)S(1)} %get-tuple-element.22.refs_4_, ...), custom_call_target="tpu_custom_call" | custom-call | flops 1000000000 | bytes 1500000 | tf_op jit(solution)/shard_map/pallas_call | solution.py:537
Async XLA Ops:
  2.9 10.9 %copy-start = (f32[3,2,32,256]{3,2,1,0:T(8,128)S(1)}, f32[3,2,32,256]{3,2,1,0:T(8,128)}, u32[]{:S(2)}) copy-start(f32[3,2,32,256]{3,2,1,0:T(8,128)} %disp_ref.1) | copy-start | bytes 589828
  2.9 10.9 %copy-start.1 = (f32[2,32,256]{2,1,0:T(8,128)S(1)}, f32[2,32,256]{2,1,0:T(8,128)}, u32[]{:S(2)}) copy-start(f32[2,32,256]{2,1,0:T(8,128)} %modulus_ref.1) | copy-start | bytes 196612
  2.9 10.9 %copy-start.2 = (f32[2,32,256]{2,1,0:T(8,128)S(1)}, f32[2,32,256]{2,1,0:T(8,128)}, u32[]{:S(2)}) copy-start(f32[2,32,256]{2,1,0:T(8,128)} %mass_ref.1) | copy-start | bytes 196612
  2.9 10.9 %copy-start.3 = (f32[24,24]{1,0:T(8,128)S(1)}, f32[24,24]{1,0:T(8,128)}, u32[]{:S(2)}) copy-start(f32[24,24]{1,0:T(8,128)} %stiffness_ref.1) | copy-start | bytes 6916
  3.0 21.2 %all-to-all-start = ((f32[8,120,128]{2,1,0:T(8,128)}), f32[8,120,128]{2,1,0:T(8,128)S(1)}, u32[]{:S(2)}, u32[]{:S(2)}) async-start(f32[8,120,128]{2,1,0:T(8,128)} %get-tuple-element.18), calls=%async_computation | async-start | bytes 983040 | tf_op jit(solution)/shard_map/all_to_all | solution.py:525
  12.5 1.3 %collective-permute-start = (f32[4,32,256]{2,1,0:T(8,128)S(1)}, f32[4,32,256]{2,1,0:T(8,128)S(1)}, u32[]{:S(2)}, u32[]{:S(2)}) collective-permute-start(f32[4,32,256]{2,1,0:T(8,128)S(1)} %get-tuple-element.26.own_ref), channel_id=1, source_target_pairs={{0,1},{1,0},{2,3},{3,2},{4,5},{5,4},{6,7},{7,6},{8,9},{9,8},{10,11... | collective-permute-start | bytes 393224 | tf_op jit(solution)/shard_map/ppermute | solution.py:441
  12.5 2.4 %collective-permute-start.1 = (f32[4,32,256]{2,1,0:T(8,128)S(1)}, f32[4,32,256]{2,1,0:T(8,128)S(1)}, u32[]{:S(2)}, u32[]{:S(2)}) collective-permute-start(f32[4,32,256]{2,1,0:T(8,128)S(1)} %get-tuple-element.30.refs_11_), channel_id=1, source_target_pairs={{1,2},{2,1},{3,4},{4,3},{5,6},{6,5},{7,8},{8,7},{9,10},{10,9},{11,... | collective-permute-start | bytes 393224 | tf_op jit(solution)/shard_map/ppermute | solution.py:441

commit v14 on v13

--- a/solution.py
+++ b/solution.py
@@ -120,7 +120,7 @@
 
 
 def place_in_group(domain, domains):
-    return domains - 1 - domain
+    return (domain + 1) % domains
 
 
 def first_kernel(capacity, heights, *refs):
@@ -521,7 +521,7 @@
             pltpu.SemaphoreType.DMA((3,)),
         ],
     )(*[pltpu.with_memory_space_constraint(x, pltpu.HBM) for x in arrays])
-    order = [place_in_group(domain, domains) for domain in range(domains)]
+    order = sorted(range(domains), key=lambda domain: place_in_group(domain, domains))
     got = lax.all_to_all(
         sent, "dom", split_axis=0, concat_axis=0, axis_index_groups=[order], tiled=True
     )

time: 26.5 us -> 26.6 us (level)
  no operation moved by 1% of the time
where the time goes in v14:
time: 26.6 us; the launch traced here: 26.3 us
  starting transfers between devices  10.2 us (38%)
  waiting for transfers between devices  9.99 us (38%)
  Pallas kernels  6.08 us (23%)
    all_to_all x1, starting transfers between devices, shards(): lax.all_to_all(sent, 'dom', split_axis=0, concat_axis=0, axis_index_group...  9.5 us
    all_to_all x1, waiting for transfers between devices, shards(): lax.all_to_all(sent, 'dom', split_axis=0, concat_axis=0, axis_index_group...  9.31 us
    pallas_call x1, Pallas kernels, shards(): on_core(first, [shaped((domains, rows_high + sum(heights), LANES)), shape...  2.9 us
    pallas_call x1, Pallas kernels, shards(): on_core(last, shaped(displacement.shape), 1000000000, 1500000)  2.14 us
    pallas_call x1, Pallas kernels, shards(): on_core(internal_kernel, [shaped(displacement.shape), shaped((2 * size, s...  1.04 us
    ppermute x2, waiting for transfers between devices, swapped(): return lax.ppermute(block, axis, route)  0.68 us
    ppermute x2, starting transfers between devices, swapped(): return lax.ppermute(block, axis, route)  0.66 us
  transfers between devices with their start and end apart: 3, of which 2 were waited for; matrix products, arithmetic and copies ran while one was open for 0% of the time, Pallas kernels for 4%

profile of v14, /device:TPU:0, one launch (start us, length us, event | category | flops | bytes accessed | tf_op | source)
XLA Modules:
  0.0 26.3 jit_solution(7464958379189893385)
XLA Ops:
  0.0 2.9 %shard_map.127 = (f32[8,120,128]{2,1,0:T(8,128)}, f32[24,256]{1,0:T(8,128)S(1)}, f32[136,256]{1,0:T(8,128)S(1)}, f32[104,256]{1,0:T(8,128)S(1)}, s32[1,256]{1,0:...) custom-call(s32[4,512]{1,0:T(4,128)} %refs_0_.1, ...), custom_call_target="tpu_custom_call" | custom-call | flops 900000000 | bytes 1500000 | tf_op jit(solution)/shard_map/pallas_call | solution.py:499
  2.9 0.0 copy-start
  2.9 0.0 copy-start.1
  2.9 0.0 copy-start.2
  2.9 0.0 copy-start.3
  3.0 9.5 %all-to-all-start = ((f32[8,120,128]{2,1,0:T(8,128)}), f32[8,120,128]{2,1,0:T(8,128)S(1)}, u32[]{:S(2)}, u32[]{:S(2)}) async-start(f32[8,120,128]{2,1,0:T(8,128)} %get-tuple-element.18), calls=%async_computation | async-start | bytes 983040 | tf_op jit(solution)/shard_map/all_to_all | solution.py:525
  12.5 0.0 collective-permute-start
  12.5 0.7 %collective-permute-start.1 = (f32[4,32,256]{2,1,0:T(8,128)S(1)}, f32[4,32,256]{2,1,0:T(8,128)S(1)}, u32[]{:S(2)}, u32[]{:S(2)}) collective-permute-start(f32[4,32,256]{2,1,0:T(8,128)S(1)} %get-tuple-element.30.refs_11_), channel_id=1, source_target_pairs={{1,2},{2,1},{3,4},{4,3},{5,6},{6,5},{7,8},{8,7},{9,10},{10,9},{11,... | collective-permute-start | bytes 393224 | tf_op jit(solution)/shard_map/ppermute | solution.py:441
  13.1 0.7 %collective-permute-done.halo_ref = f32[4,32,256]{2,1,0:T(8,128)S(1)} collective-permute-done((f32[4,32,256]{2,1,0:T(8,128)S(1)}, f32[4,32,256]{2,1,0:T(8,128)S(1)}, u32[]{:S(2)}, u32[]{:S(2)}) %collective-permute-start) | collective-permute-done | bytes 131104 | tf_op jit(solution)/shard_map/ppermute | solution.py:441
  13.8 0.0 copy-done
  13.8 0.0 copy-done.1
  13.8 0.0 copy-done.2
  13.8 0.0 copy-done.3
  13.8 1.0 %shard_map.128 = (f32[3,2,32,256]{3,2,1,0:T(8,128)S(1)}, bf16[384,192]{1,0:T(8,128)(2,1)S(1)}, f32[2,32,256]{2,1,0:T(8,128)S(1)}) custom-call(f32[3,2,32,256]{3,2,1,0:T(8,128)S(1)} %copy-done, f32[2,32,256]{2,1,0:T(8,128)S(1)} %copy-done.1, f32[24,24]{1,0:T(8,128)S(1)} %copy-done.3, f32[2,32,256]{2,1,0:T(8,128)S(1)} %copy-done.2, ...), custom_call_target="tpu_custom_call" | custom-call | flops 1000000000 | bytes 700000 | tf_op jit(solution)/shard_map/pallas_call | solution.py:531
  14.9 0.0 collective-permute-done.1.refs_12_
  14.9 9.3 %all-to-all-done.refs_0_ = f32[8,120,128]{2,1,0:T(8,128)S(1)} async-done(((f32[8,120,128]{2,1,0:T(8,128)}), f32[8,120,128]{2,1,0:T(8,128)S(1)}, u32[]{:S(2)}, u32[]{:S(2)}) %all-to-all-start) | async-done | bytes 491552 | tf_op jit(solution)/shard_map/all_to_all | solution.py:525
  24.2 2.1 %shard_map.129 = f32[3,2,32,256]{3,2,1,0:T(8,128)} custom-call(f32[8,120,128]{2,1,0:T(8,128)S(1)} %all-to-all-done.refs_0_, f32[24,256]{1,0:T(8,128)S(1)} %get-tuple-element.19.refs_1_, f32[136,256]{1,0:T(8,128)S(1)} %get-tuple-element.20.refs_2_, f32[104,256]{1,0:T(8,128)S(1)} %get-tuple-element.21.refs_3_, s32[1,256]{1,0:T(1,128)S(1)} %get-tuple-element.22.refs_4_, ...), custom_call_target="tpu_custom_call" | custom-call | flops 1000000000 | bytes 1500000 | tf_op jit(solution)/shard_map/pallas_call | solution.py:537
Async XLA Ops:
  2.9 10.9 %copy-start = (f32[3,2,32,256]{3,2,1,0:T(8,128)S(1)}, f32[3,2,32,256]{3,2,1,0:T(8,128)}, u32[]{:S(2)}) copy-start(f32[3,2,32,256]{3,2,1,0:T(8,128)} %disp_ref.1) | copy-start | bytes 589828
  2.9 10.9 %copy-start.1 = (f32[2,32,256]{2,1,0:T(8,128)S(1)}, f32[2,32,256]{2,1,0:T(8,128)}, u32[]{:S(2)}) copy-start(f32[2,32,256]{2,1,0:T(8,128)} %modulus_ref.1) | copy-start | bytes 196612
  2.9 10.9 %copy-start.2 = (f32[2,32,256]{2,1,0:T(8,128)S(1)}, f32[2,32,256]{2,1,0:T(8,128)}, u32[]{:S(2)}) copy-start(f32[2,32,256]{2,1,0:T(8,128)} %mass_ref.1) | copy-start | bytes 196612
  2.9 10.9 %copy-start.3 = (f32[24,24]{1,0:T(8,128)S(1)}, f32[24,24]{1,0:T(8,128)}, u32[]{:S(2)}) copy-start(f32[24,24]{1,0:T(8,128)} %stiffness_ref.1) | copy-start | bytes 6916
  3.0 21.2 %all-to-all-start = ((f32[8,120,128]{2,1,0:T(8,128)}), f32[8,120,128]{2,1,0:T(8,128)S(1)}, u32[]{:S(2)}, u32[]{:S(2)}) async-start(f32[8,120,128]{2,1,0:T(8,128)} %get-tuple-element.18), calls=%async_computation | async-start | bytes 983040 | tf_op jit(solution)/shard_map/all_to_all | solution.py:525
  12.5 1.3 %collective-permute-start = (f32[4,32,256]{2,1,0:T(8,128)S(1)}, f32[4,32,256]{2,1,0:T(8,128)S(1)}, u32[]{:S(2)}, u32[]{:S(2)}) collective-permute-start(f32[4,32,256]{2,1,0:T(8,128)S(1)} %get-tuple-element.26.own_ref), channel_id=1, source_target_pairs={{0,1},{1,0},{2,3},{3,2},{4,5},{5,4},{6,7},{7,6},{8,9},{9,8},{10,11... | collective-permute-start | bytes 393224 | tf_op jit(solution)/shard_map/ppermute | solution.py:441
  12.5 2.4 %collective-permute-start.1 = (f32[4,32,256]{2,1,0:T(8,128)S(1)}, f32[4,32,256]{2,1,0:T(8,128)S(1)}, u32[]{:S(2)}, u32[]{:S(2)}) collective-permute-start(f32[4,32,256]{2,1,0:T(8,128)S(1)} %get-tuple-element.30.refs_11_), channel_id=1, source_target_pairs={{1,2},{2,1},{3,4},{4,3},{5,6},{6,5},{7,8},{8,7},{9,10},{10,9},{11,... | collective-permute-start | bytes 393224 | tf_op jit(solution)/shard_map/ppermute | solution.py:441

commit v15 on v11

--- a/solution.py
+++ b/solution.py
@@ -68,16 +68,17 @@
     return block
 
 
-def unfolded(got_ref, start, height, capacity):
+def unfolded(got_ref, block_rows, start, height, capacity):
     group = LANES // capacity
     part = lax.broadcasted_iota(jnp.int32, (height, LANES), 1) >> halves(capacity)
     pieces = []
     for j in range(group):
         tiles = []
-        for first in range(0, got_ref.shape[0], group):
+        for first in range(0, got_ref.shape[0] // block_rows, group):
             block = None
             for spot in range(group):
-                piece = got_ref[first + spot, start : start + height]
+                at = (first + spot) * block_rows + start
+                piece = got_ref[at : at + height]
                 if j != spot:
                     piece = pltpu.roll(piece, (spot - j) * capacity % LANES, 1)
                 block = piece if block is None else jnp.where(part == spot, piece, block)
@@ -87,7 +88,7 @@
 
 
 def routed(words, rows, place):
-    extra = rows - words.shape[0]
+    extra = -(-rows // 16) * 16 - words.shape[0]
     if extra:
         words = jnp.concatenate([words, jnp.zeros((extra, words.shape[1]), F32)], axis=0)
     return summed(times_turned(stacked_terms(words), place))
@@ -129,9 +130,10 @@
         gap_hbm, shape_hbm, modulus_hbm,
         sent_ref, rows_ref, words_ref, turned_ref, mortar_ref, rank_ref, face_ref, nodes,
         inner_ref, outer_ref,
-        disp, count, weight, normal_v, gap_v, shape, modulus, blocks, sems, copy_sems,
+        disp, count, weight, normal_v, gap_v, shape, modulus, blocks, sems, copy_sem,
     ) = refs
     components, layers, rows_y, cols_x = disp.shape
+    block_rows = 12 * nodes.shape[1] // LANES + sum(heights)
     sources = (
         nodes_hbm, disp_hbm, rank_hbm, face_hbm, mortar_hbm, shape_hbm, count_hbm, weight_hbm,
         normal_hbm, gap_hbm, modulus_hbm.at[disp.shape[1] - 1],
@@ -146,7 +148,7 @@
     for copy in brought:
         copy.start()
 
-    domains = sent_ref.shape[0]
+    domains = sent_ref.shape[0] // block_rows
     pair_total = rank_ref.shape[1]
     face_count = nodes.shape[1]
     strips = layers * rows_y
@@ -193,20 +195,11 @@
     halved = jnp.concatenate(
         [rows[:, i * LANES : (i + 1) * LANES] for i in range(cols_x // LANES)], axis=0
     )
-    starts = (0, rows_high, rows_high + heights[0], rows_high + sum(heights))
-    copies = [
-        pltpu.make_async_copy(
-            blocks.at[:, start:end], sent_ref.at[:, start:end], copy_sems.at[i]
-        )
-        for i, (start, end) in enumerate(zip(starts, starts[1:]))
-    ]
     for domain in range(domains):
-        blocks[domain, :rows_high] = halved
-    copies[0].start()
-    for domain in range(domains):
-        spot = place_in_group(domain, domains)
-        blocks[spot, starts[1] : starts[2]] = folded(placed, heights[0], capacity, domain)
-    copies[1].start()
+        at = place_in_group(domain, domains) * block_rows
+        blocks[at : at + rows_high] = halved
+        at += rows_high
+        blocks[at : at + heights[0]] = folded(placed, heights[0], capacity, domain)
 
     mortar_rows = looked_up(rows, mortar, marks(mortar & (cols_x - 1), cols_x))
     for node in range(4):
@@ -218,14 +211,15 @@
     short_words = jnp.concatenate(
         [gap[:full]]
         + [x[full:] for x in weighted + [gap]]
-        + [normal, face.astype(F32), jnp.zeros((7, pair_total), F32)],
+        + [normal, face.astype(F32)],
         axis=0,
     )
     placed = routed(short_words, group * heights[1], place)
     for domain in range(domains):
-        spot = place_in_group(domain, domains)
-        blocks[spot, starts[2] :] = folded(placed, heights[1], capacity, domain)
-    copies[2].start()
+        at = place_in_group(domain, domains) * block_rows + rows_high + heights[0]
+        blocks[at : at + heights[1]] = folded(placed, heights[1], capacity, domain)
+    sending = pltpu.make_async_copy(blocks, sent_ref, copy_sem)
+    sending.start()
 
     words_ref[: 4 * full] = long_words
     words_ref[4 * full :] = short_words
@@ -240,21 +234,21 @@
         for k in range(components):
             target[k] = disp[k, layer]
         target[components] = modulus[...]
-    for copy in copies:
-        copy.wait()
+    sending.wait()
 
 
 def last_kernel(
     capacity, heights, got_ref, rows_ref, words_ref, turned_ref, mortar_ref, rank_ref, face_ref, nodes_ref,
     inverse_ref, internal_ref, blocks_ref, own_ref, halo_ref, out_ref,
 ):
-    domains = got_ref.shape[0]
+    block_rows = 12 * nodes_ref.shape[1] // LANES + sum(heights)
+    domains = got_ref.shape[0] // block_rows
     components, layers, rows_y, cols_x = out_ref.shape
     strips = layers * rows_y
     face_count = nodes_ref.shape[1]
     pair_total = rank_ref.shape[1]
-    folded = rows_ref.shape[0]
-    rows_high = folded * cols_x // LANES
+    high = rows_ref.shape[0]
+    rows_high = high * cols_x // LANES
     full = (turned_ref.shape[0] - 8) // 4
     own_rows = rows_ref[...]
 
@@ -265,21 +259,23 @@
     step = min(domains, 8)
 
     def add_step(turn, total):
-        block = jnp.concatenate(
-            [
-                got_ref[pl.ds(turn * step, step), i * folded : (i + 1) * folded].reshape(
-                    step * folded, LANES
-                )
-                for i in range(cols_x // LANES)
-            ],
-            axis=1,
-        )
-        found = summed(times(stacked_terms(block), at)).reshape(step, folded, pair_total)
+        halves_of = [
+            jnp.concatenate(
+                [
+                    got_ref[pl.ds((turn * step + i) * block_rows + j * high, high)]
+                    for j in range(cols_x // LANES)
+                ],
+                axis=1,
+            )
+            for i in range(step)
+        ]
+        block = jnp.concatenate(halves_of, axis=0)
+        found = summed(times(stacked_terms(block), at)).reshape(step, high, pair_total)
         for i in range(step):
             total = total + jnp.where(place == turn * step + i, found[i], 0.0)
         return total
 
-    both = jnp.zeros((folded, pair_total), F32)
+    both = jnp.zeros((high, pair_total), F32)
     if domains == step:
         both = add_step(0, both)
     else:
@@ -291,8 +287,8 @@
 
     words = jnp.concatenate(
         [
-            unfolded(got_ref, rows_high, heights[0], capacity)[: 4 * full],
-            unfolded(got_ref, rows_high + heights[0], heights[1], capacity)[: full + 16],
+            unfolded(got_ref, block_rows, rows_high, heights[0], capacity)[: 4 * full],
+            unfolded(got_ref, block_rows, rows_high + heights[0], heights[1], capacity)[: full + 9],
         ],
         axis=0,
     )
@@ -465,8 +461,8 @@
     points = pair_weight.shape[0]
     full = points // 8 * 8
     group = LANES // capacity
-    word_rows = 5 * full + 16
-    heights = tuple(-(-rows // (8 * group)) * 8 for rows in (4 * full, full + 16))
+    word_rows = 5 * full + 9
+    heights = tuple(-(-rows // group) for rows in (4 * full, full + 9))
     rows_high = 12 * face_count // LANES
     line = (1, pair_total)
 
@@ -499,7 +495,7 @@
     sent, rows, words, turned, mortar, rank, face, nodes, inner, outer = on_core(
         first,
         [
-            shaped((domains, rows_high + sum(heights), LANES)),
+            shaped((domains * (rows_high + sum(heights)), LANES)),
             shaped((12 * face_count // cols_x, cols_x)),
             shaped((word_rows, pair_total)),
             shaped((4 * full + 8, pair_total)),
@@ -516,15 +512,20 @@
         out_specs=[in_hbm] + [in_vmem] * 9,
         scratch_shapes=[pltpu.VMEM(x.shape, x.dtype) for x in kept]
         + [
-            pltpu.VMEM((domains, rows_high + sum(heights), LANES), F32),
+            pltpu.VMEM((domains * (rows_high + sum(heights)), LANES), F32),
             pltpu.SemaphoreType.DMA((len(arrays),)),
-            pltpu.SemaphoreType.DMA((3,)),
+            pltpu.SemaphoreType.DMA(()),
         ],
     )(*[pltpu.with_memory_space_constraint(x, pltpu.HBM) for x in arrays])
     order = [place_in_group(domain, domains) for domain in range(domains)]
     got = lax.all_to_all(
-        sent, "dom", split_axis=0, concat_axis=0, axis_index_groups=[order], tiled=True
-    )
+        sent.reshape(domains, 1, -1),
+        "dom",
+        split_axis=0,
+        concat_axis=0,
+        axis_index_groups=[order],
+        tiled=True,
+    ).reshape(sent.shape)
     inner_halo = swapped(inner, ("dom", "sub"), 0)
     outer_halo = swapped(outer, ("dom", "sub"), 1)
     size = 8 * components * GROUP

time: 25.5 us -> 24.9 us (0.976)
  waiting for transfers between devices: 9.46 us -> 8.85 us
    ppermute x2, waiting for transfers between devices: 9.46 us -> 8.85 us  [swapped(): return lax.ppermute(block, axis, route)]
where the time goes in v15:
time: 24.9 us; the launch traced here: 24.6 us
  starting transfers between devices  9.51 us (38%)
  waiting for transfers between devices  8.85 us (36%)
  Pallas kernels  6.13 us (25%)
    ppermute x2, waiting for transfers between devices, swapped(): return lax.ppermute(block, axis, route)  8.85 us
    all_to_all x1, starting transfers between devices, shards(): lax.all_to_all(sent.reshape(domains, 1, -1), 'dom', split_axis=0, concat_...  6.04 us
    ppermute x2, starting transfers between devices, swapped(): return lax.ppermute(block, axis, route)  3.47 us
    pallas_call x1, Pallas kernels, shards(): on_core(first, [shaped((domains * (rows_high + sum(heights)), LANES)), sh...  2.99 us
    pallas_call x1, Pallas kernels, shards(): on_core(last, shaped(displacement.shape), 1000000000, 1500000)  2.13 us
    pallas_call x1, Pallas kernels, shards(): on_core(internal_kernel, [shaped(displacement.shape), shaped((2 * size, s...  1.01 us
  transfers between devices with their start and end apart: 3, of which 1 were waited for; matrix products, arithmetic and copies ran while one was open for 0% of the time, Pallas kernels for 4%

profile of v15, /device:TPU:16, one launch (start us, length us, event | category | flops | bytes accessed | tf_op | source)
XLA Modules:
  0.0 24.6 jit_solution(18328973663053263724)
XLA Ops:
  0.0 3.0 %shard_map.127 = (f32[904,128]{1,0:T(8,128)}, f32[24,256]{1,0:T(8,128)S(1)}, f32[129,256]{1,0:T(8,128)S(1)}, f32[104,256]{1,0:T(8,128)S(1)}, s32[1,256]{1,0:T(1,...) custom-call(s32[4,512]{1,0:T(4,128)} %refs_0_.1, ...), custom_call_target="tpu_custom_call" | custom-call | flops 900000000 | bytes 1500000 | tf_op jit(solution)/shard_map/pallas_call | solution.py:495
  3.0 0.0 copy-start
  3.0 0.0 copy-start.1
  3.0 0.0 copy-start.2
  3.0 0.0 copy-start.3
  3.1 6.0 %all-to-all-start = ((f32[8,1,14464]{2,1,0:T(1,128)}), f32[8,1,14464]{2,1,0:T(1,128)S(1)}, u32[]{:S(2)}, u32[]{:S(2)}) async-start(f32[8,1,14464]{2,1,0:T(1,128)} %bitcast.5), calls=%async_computation | async-start | bytes 925696 | tf_op jit(solution)/shard_map/all_to_all | solution.py:521
  9.1 0.0 collective-permute-start
  9.1 3.5 %collective-permute-start.1 = (f32[4,32,256]{2,1,0:T(8,128)S(1)}, f32[4,32,256]{2,1,0:T(8,128)S(1)}, u32[]{:S(2)}, u32[]{:S(2)}) collective-permute-start(f32[4,32,256]{2,1,0:T(8,128)S(1)} %get-tuple-element.30.refs_11_), channel_id=1, source_target_pairs={{1,2},{2,1},{3,4},{4,3},{5,6},{6,5},{7,8},{8,7},{9,10},{10,9},{11,... | collective-permute-start | bytes 393224 | tf_op jit(solution)/shard_map/ppermute | solution.py:437
  12.6 0.0 collective-permute-done.halo_ref
  12.6 0.0 copy-done
  12.6 0.0 copy-done.1
  12.6 0.0 copy-done.2
  12.6 0.0 copy-done.3
  12.6 1.0 %shard_map.128 = (f32[3,2,32,256]{3,2,1,0:T(8,128)S(1)}, bf16[384,192]{1,0:T(8,128)(2,1)S(1)}, f32[2,32,256]{2,1,0:T(8,128)S(1)}) custom-call(f32[3,2,32,256]{3,2,1,0:T(8,128)S(1)} %copy-done, f32[2,32,256]{2,1,0:T(8,128)S(1)} %copy-done.1, f32[24,24]{1,0:T(8,128)S(1)} %copy-done.3, f32[2,32,256]{2,1,0:T(8,128)S(1)} %copy-done.2, ...), custom_call_target="tpu_custom_call" | custom-call | flops 1000000000 | bytes 700000 | tf_op jit(solution)/shard_map/pallas_call | solution.py:532
  13.6 8.8 %collective-permute-done.1.refs_12_ = f32[4,32,256]{2,1,0:T(8,128)S(1)} collective-permute-done((f32[4,32,256]{2,1,0:T(8,128)S(1)}, f32[4,32,256]{2,1,0:T(8,128)S(1)}, u32[]{:S(2)}, u32[]{:S(2)}) %collective-permute-start.1) | collective-permute-done | bytes 131104 | tf_op jit(solution)/shard_map/ppermute | solution.py:437
  22.5 0.0 all-to-all-done
  22.5 2.1 %shard_map.129 = f32[3,2,32,256]{3,2,1,0:T(8,128)} custom-call(f32[904,128]{1,0:T(8,128)S(1)} %bitcast.7, f32[24,256]{1,0:T(8,128)S(1)} %get-tuple-element.19.refs_1_, f32[129,256]{1,0:T(8,128)S(1)} %get-tuple-element.20.refs_2_, f32[104,256]{1,0:T(8,128)S(1)} %get-tuple-element.21.refs_3_, s32[1,256]{1,0:T(1,128)S(1)} %get-tuple-element.22.refs_4_, ...), custom_call_target="tpu_custom_call" | custom-call | flops 1000000000 | bytes 1500000 | tf_op jit(solution)/shard_map/pallas_call | solution.py:538
Async XLA Ops:
  3.0 9.6 %copy-start = (f32[3,2,32,256]{3,2,1,0:T(8,128)S(1)}, f32[3,2,32,256]{3,2,1,0:T(8,128)}, u32[]{:S(2)}) copy-start(f32[3,2,32,256]{3,2,1,0:T(8,128)} %disp_ref.1) | copy-start | bytes 589828
  3.0 9.6 %copy-start.1 = (f32[2,32,256]{2,1,0:T(8,128)S(1)}, f32[2,32,256]{2,1,0:T(8,128)}, u32[]{:S(2)}) copy-start(f32[2,32,256]{2,1,0:T(8,128)} %modulus_ref.1) | copy-start | bytes 196612
  3.0 9.6 %copy-start.2 = (f32[2,32,256]{2,1,0:T(8,128)S(1)}, f32[2,32,256]{2,1,0:T(8,128)}, u32[]{:S(2)}) copy-start(f32[2,32,256]{2,1,0:T(8,128)} %mass_ref.1) | copy-start | bytes 196612
  3.0 9.6 %copy-start.3 = (f32[24,24]{1,0:T(8,128)S(1)}, f32[24,24]{1,0:T(8,128)}, u32[]{:S(2)}) copy-start(f32[24,24]{1,0:T(8,128)} %stiffness_ref.1) | copy-start | bytes 6916
  3.1 19.4 %all-to-all-start = ((f32[8,1,14464]{2,1,0:T(1,128)}), f32[8,1,14464]{2,1,0:T(1,128)S(1)}, u32[]{:S(2)}, u32[]{:S(2)}) async-start(f32[8,1,14464]{2,1,0:T(1,128)} %bitcast.5), calls=%async_computation | async-start | bytes 925696 | tf_op jit(solution)/shard_map/all_to_all | solution.py:521
  9.1 3.5 %collective-permute-start = (f32[4,32,256]{2,1,0:T(8,128)S(1)}, f32[4,32,256]{2,1,0:T(8,128)S(1)}, u32[]{:S(2)}, u32[]{:S(2)}) collective-permute-start(f32[4,32,256]{2,1,0:T(8,128)S(1)} %get-tuple-element.26.own_ref), channel_id=1, source_target_pairs={{0,1},{1,0},{2,3},{3,2},{4,5},{5,4},{6,7},{7,6},{8,9},{9,8},{10,11... | collective-permute-start | bytes 393224 | tf_op jit(solution)/shard_map/ppermute | solution.py:437
  9.1 13.4 %collective-permute-start.1 = (f32[4,32,256]{2,1,0:T(8,128)S(1)}, f32[4,32,256]{2,1,0:T(8,128)S(1)}, u32[]{:S(2)}, u32[]{:S(2)}) collective-permute-start(f32[4,32,256]{2,1,0:T(8,128)S(1)} %get-tuple-element.30.refs_11_), channel_id=1, source_target_pairs={{1,2},{2,1},{3,4},{4,3},{5,6},{6,5},{7,8},{8,7},{9,10},{10,9},{11,... | collective-permute-start | bytes 393224 | tf_op jit(solution)/shard_map/ppermute | solution.py:437

commit v16 on v15

--- a/solution.py
+++ b/solution.py
@@ -152,20 +152,8 @@
     pair_total = rank_ref.shape[1]
     face_count = nodes.shape[1]
     strips = layers * rows_y
-    for copy in brought[:-1]:
+    for copy in brought[:2]:
         copy.wait()
-    rank, face, mortar = rank_ref[...], face_ref[...], mortar_ref[...]
-    normal = normal_v[...]
-    gap = gap_v[...]
-
-    chosen = lax.broadcasted_iota(jnp.int32, (domains, pair_total), 0) == rank
-    before = lax.broadcasted_iota(jnp.int32, (pair_total, pair_total), 0) < lax.broadcasted_iota(
-        jnp.int32, (pair_total, pair_total), 1
-    )
-    earlier = times(chosen.astype(F32).astype(BF16), before.astype(F32).astype(BF16))
-    slot = jnp.sum(jnp.where(chosen, earlier, 0.0), axis=0, keepdims=True).astype(jnp.int32)
-    place = marks(rank * capacity + slot, domains * capacity)
-
     parts = stacked_terms(disp[...].reshape(components * strips, cols_x))
     numbers = lax.broadcasted_iota(jnp.int32, (strips, face_count), 0)
     folds = face_count // cols_x
@@ -180,6 +168,20 @@
                 at = fold * 12 + k * 4 + corner
                 rows_ref[at : at + 1, :] = values[k : k + 1, fold * cols_x : (fold + 1) * cols_x]
 
+    for copy in brought[2:-1]:
+        copy.wait()
+    rank, face, mortar = rank_ref[...], face_ref[...], mortar_ref[...]
+    normal = normal_v[...]
+    gap = gap_v[...]
+
+    chosen = lax.broadcasted_iota(jnp.int32, (domains, pair_total), 0) == rank
+    before = lax.broadcasted_iota(jnp.int32, (pair_total, pair_total), 0) < lax.broadcasted_iota(
+        jnp.int32, (pair_total, pair_total), 1
+    )
+    earlier = times(chosen.astype(F32).astype(BF16), before.astype(F32).astype(BF16))
+    slot = jnp.sum(jnp.where(chosen, earlier, 0.0), axis=0, keepdims=True).astype(jnp.int32)
+    place = marks(rank * capacity + slot, domains * capacity)
+
     points = gap.shape[0]
     full = points // 8 * 8
     live = lax.broadcasted_iota(jnp.int32, (points, pair_total), 0) < count[...]
@@ -239,7 +241,7 @@
 
 def last_kernel(
     capacity, heights, got_ref, rows_ref, words_ref, turned_ref, mortar_ref, rank_ref, face_ref, nodes_ref,
-    inverse_ref, internal_ref, blocks_ref, own_ref, halo_ref, out_ref,
+    marks_ref, inverse_ref, internal_ref, blocks_ref, own_ref, halo_ref, out_ref,
 ):
     block_rows = 12 * nodes_ref.shape[1] // LANES + sum(heights)
     domains = got_ref.shape[0] // block_rows
@@ -317,8 +319,7 @@
                 at = k * 4 + corner
                 row = jnp.broadcast_to(part[at : at + 1], (16, face_count)).astype(BF16)
                 spread.append(strip * jnp.concatenate([row] * (strips // 16), axis=0))
-        along_x = marks(index & (cols_x - 1), cols_x)
-        total = total + times_turned(jnp.concatenate(spread, axis=0), along_x)
+        total = total + times_turned(jnp.concatenate(spread, axis=0), marks_ref[corner])
     contact = summed(total).reshape(components, layers, rows_y, cols_x)
     upward = lax.axis_index("sub") == 1
     edge = edge_part(upward, own_ref, halo_ref, blocks_ref)
@@ -383,9 +384,13 @@
 
 
 def internal_kernel(
-    disp_ref, modulus_ref, stiffness_ref, mass_ref, own_ref, halo_ref, out_ref, blocks_ref, inverse_ref
+    disp_ref, modulus_ref, stiffness_ref, mass_ref, nodes_ref, own_ref, halo_ref, out_ref, blocks_ref,
+    inverse_ref, marks_ref,
 ):
     inverse_ref[...] = 1.0 / mass_ref[...]
+    for corner in range(4):
+        width = disp_ref.shape[3]
+        marks_ref[corner] = marks(nodes_ref[corner : corner + 1, :] & (width - 1), width)
     components, layers, rows_y, cols_x = disp_ref.shape
     dofs = 8 * components
     half = dofs // 2
@@ -529,14 +534,16 @@
     inner_halo = swapped(inner, ("dom", "sub"), 0)
     outer_halo = swapped(outer, ("dom", "sub"), 1)
     size = 8 * components * GROUP
-    internal, blocks, inverse = on_core(
+    internal, blocks, inverse, along_x = on_core(
         internal_kernel,
-        [shaped(displacement.shape), shaped((2 * size, size), BF16), shaped(node_mass.shape)],
+        [shaped(displacement.shape), shaped((2 * size, size), BF16), shaped(node_mass.shape),
+            shaped((4, cols_x, face_count), BF16),
+        ],
         1_000_000_000,
         700_000,
-    )(displacement, modulus, stiffness, node_mass, inner, inner_halo)
+    )(displacement, modulus, stiffness, node_mass, nodes, inner, inner_halo)
     return on_core(last, shaped(displacement.shape), 1_000_000_000, 1_500_000)(
-        got, rows, words, turned, mortar, rank, face, nodes, inverse, internal, blocks, outer, outer_halo
+        got, rows, words, turned, mortar, rank, face, nodes, along_x, inverse, internal, blocks, outer, outer_halo
     )
 
 

time: 24.9 us -> 25.1 us (level)
  Pallas kernels: 6.13 us -> 6.44 us
  transfers between devices with their start and end apart: 3 -> 3, of which waited for: 1 -> 1; matrix products, arithmetic and copies ran while one was open for 0% -> 0% of each run, Pallas kernels for 4% -> 5%
where the time goes in v16:
time: 25.1 us; the launch traced here: 24.8 us
  starting transfers between devices  9.51 us (38%)
  waiting for transfers between devices  8.69 us (35%)
  Pallas kernels  6.44 us (26%)
    ppermute x2, waiting for transfers between devices, swapped(): return lax.ppermute(block, axis, route)  8.69 us
    all_to_all x1, starting transfers between devices, shards(): lax.all_to_all(sent.reshape(domains, 1, -1), 'dom', split_axis=0, concat_...  6.04 us
    ppermute x2, starting transfers between devices, swapped(): return lax.ppermute(block, axis, route)  3.47 us
    pallas_call x1, Pallas kernels, shards(): on_core(first, [shaped((domains * (rows_high + sum(heights)), LANES)), sh...  3.13 us
    pallas_call x1, Pallas kernels, shards(): on_core(last, shaped(displacement.shape), 1000000000, 1500000)  2.14 us
    pallas_call x1, Pallas kernels, shards(): on_core(internal_kernel, [shaped(displacement.shape), shaped((2 * size, s...  1.17 us
  transfers between devices with their start and end apart: 3, of which 1 were waited for; matrix products, arithmetic and copies ran while one was open for 0% of the time, Pallas kernels for 5%

profile of v16, /device:TPU:16, one launch (start us, length us, event | category | flops | bytes accessed | tf_op | source)
XLA Modules:
  0.0 24.8 jit_solution(5680594418797913162)
XLA Ops:
  0.0 3.1 %shard_map.127 = (f32[904,128]{1,0:T(8,128)}, f32[24,256]{1,0:T(8,128)S(1)}, f32[129,256]{1,0:T(8,128)S(1)}, f32[104,256]{1,0:T(8,128)S(1)}, s32[1,256]{1,0:T(1,...) custom-call(s32[4,512]{1,0:T(4,128)} %refs_0_.1, ...), custom_call_target="tpu_custom_call" | custom-call | flops 900000000 | bytes 1500000 | tf_op jit(solution)/shard_map/pallas_call | solution.py:500
  3.1 0.0 copy-start
  3.2 0.0 copy-start.1
  3.2 0.0 copy-start.2
  3.2 0.0 copy-start.3
  3.2 6.0 %all-to-all-start = ((f32[8,1,14464]{2,1,0:T(1,128)}), f32[8,1,14464]{2,1,0:T(1,128)S(1)}, u32[]{:S(2)}, u32[]{:S(2)}) async-start(f32[8,1,14464]{2,1,0:T(1,128)} %bitcast.5), calls=%async_computation | async-start | bytes 925696 | tf_op jit(solution)/shard_map/all_to_all | solution.py:526
  9.2 0.0 collective-permute-start
  9.2 3.5 %collective-permute-start.1 = (f32[4,32,256]{2,1,0:T(8,128)S(1)}, f32[4,32,256]{2,1,0:T(8,128)S(1)}, u32[]{:S(2)}, u32[]{:S(2)}) collective-permute-start(f32[4,32,256]{2,1,0:T(8,128)S(1)} %get-tuple-element.32.refs_12_), channel_id=1, source_target_pairs={{1,2},{2,1},{3,4},{4,3},{5,6},{6,5},{7,8},{8,7},{9,10},{10,9},{11,... | collective-permute-start | bytes 393224 | tf_op jit(solution)/shard_map/ppermute | solution.py:442
  12.7 0.0 collective-permute-done.halo_ref
  12.7 0.0 copy-done
  12.7 0.0 copy-done.1
  12.7 0.0 copy-done.2
  12.7 0.0 copy-done.3
  12.8 1.2 %shard_map.128 = (f32[3,2,32,256]{3,2,1,0:T(8,128)S(1)}, bf16[384,192]{1,0:T(8,128)(2,1)S(1)}, f32[2,32,256]{2,1,0:T(8,128)S(1)}, bf16[4,256,512]{2,1,0:T(8,128)(2,1)S(1)}) custom-call(f32[3,2,32,256]{3,2,1,0:T(8,128)S(1)} %copy-done, f32[2,32,256]{2,1,0:T(8,128)S(1)} %copy-done.1, f32[24,24]{1,0:T(8,128)S(1)} %copy-done.3, f32[2,32,256]{2,1,0:T(8,128)S(1)} %copy-done.2, ...), custom_call_target="tpu_custom_call" | custom-call | flops 1000000000 | bytes 700000 | tf_op jit(solution)/shard_map/pallas_call | solution.py:537
  13.9 8.7 %collective-permute-done.1.refs_13_ = f32[4,32,256]{2,1,0:T(8,128)S(1)} collective-permute-done((f32[4,32,256]{2,1,0:T(8,128)S(1)}, f32[4,32,256]{2,1,0:T(8,128)S(1)}, u32[]{:S(2)}, u32[]{:S(2)}) %collective-permute-start.1) | collective-permute-done | bytes 131104 | tf_op jit(solution)/shard_map/ppermute | solution.py:442
  22.6 0.0 all-to-all-done
  22.6 2.1 %shard_map.129 = f32[3,2,32,256]{3,2,1,0:T(8,128)} custom-call(f32[904,128]{1,0:T(8,128)S(1)} %bitcast.7, f32[24,256]{1,0:T(8,128)S(1)} %get-tuple-element.20.refs_1_, f32[129,256]{1,0:T(8,128)S(1)} %get-tuple-element.21.refs_2_, f32[104,256]{1,0:T(8,128)S(1)} %get-tuple-element.22.refs_3_, s32[1,256]{1,0:T(1,128)S(1)} %get-tuple-element.23.refs_4_, ...), custom_call_target="tpu_custom_call" | custom-call | flops 1000000000 | bytes 1500000 | tf_op jit(solution)/shard_map/pallas_call | solution.py:545
Async XLA Ops:
  3.1 9.6 %copy-start = (f32[3,2,32,256]{3,2,1,0:T(8,128)S(1)}, f32[3,2,32,256]{3,2,1,0:T(8,128)}, u32[]{:S(2)}) copy-start(f32[3,2,32,256]{3,2,1,0:T(8,128)} %disp_ref.1) | copy-start | bytes 589828
  3.2 9.6 %copy-start.1 = (f32[2,32,256]{2,1,0:T(8,128)S(1)}, f32[2,32,256]{2,1,0:T(8,128)}, u32[]{:S(2)}) copy-start(f32[2,32,256]{2,1,0:T(8,128)} %modulus_ref.1) | copy-start | bytes 196612
  3.2 9.6 %copy-start.2 = (f32[2,32,256]{2,1,0:T(8,128)S(1)}, f32[2,32,256]{2,1,0:T(8,128)}, u32[]{:S(2)}) copy-start(f32[2,32,256]{2,1,0:T(8,128)} %mass_ref.1) | copy-start | bytes 196612
  3.2 9.6 %copy-start.3 = (f32[24,24]{1,0:T(8,128)S(1)}, f32[24,24]{1,0:T(8,128)}, u32[]{:S(2)}) copy-start(f32[24,24]{1,0:T(8,128)} %stiffness_ref.1) | copy-start | bytes 6916
  3.2 19.4 %all-to-all-start = ((f32[8,1,14464]{2,1,0:T(1,128)}), f32[8,1,14464]{2,1,0:T(1,128)S(1)}, u32[]{:S(2)}, u32[]{:S(2)}) async-start(f32[8,1,14464]{2,1,0:T(1,128)} %bitcast.5), calls=%async_computation | async-start | bytes 925696 | tf_op jit(solution)/shard_map/all_to_all | solution.py:526
  9.2 3.5 %collective-permute-start = (f32[4,32,256]{2,1,0:T(8,128)S(1)}, f32[4,32,256]{2,1,0:T(8,128)S(1)}, u32[]{:S(2)}, u32[]{:S(2)}) collective-permute-start(f32[4,32,256]{2,1,0:T(8,128)S(1)} %get-tuple-element.27.own_ref), channel_id=1, source_target_pairs={{0,1},{1,0},{2,3},{3,2},{4,5},{5,4},{6,7},{7,6},{8,9},{9,8},{10,11... | collective-permute-start | bytes 393224 | tf_op jit(solution)/shard_map/ppermute | solution.py:442
  9.2 13.4 %collective-permute-start.1 = (f32[4,32,256]{2,1,0:T(8,128)S(1)}, f32[4,32,256]{2,1,0:T(8,128)S(1)}, u32[]{:S(2)}, u32[]{:S(2)}) collective-permute-start(f32[4,32,256]{2,1,0:T(8,128)S(1)} %get-tuple-element.32.refs_12_), channel_id=1, source_target_pairs={{1,2},{2,1},{3,4},{4,3},{5,6},{6,5},{7,8},{8,7},{9,10},{10,9},{11,... | collective-permute-start | bytes 393224 | tf_op jit(solution)/shard_map/ppermute | solution.py:442

commit v17 on v15

--- a/solution.py
+++ b/solution.py
@@ -36,6 +36,12 @@
         for start in range(0, count, 16)
     ]
     return jnp.concatenate(tiles, axis=0)
+
+
+def marks_turned(index, count):
+    column = jnp.broadcast_to(index.astype(F32), (8, index.shape[1])).T[:, :1]
+    columns = lax.broadcasted_iota(jnp.int32, (index.shape[1], count), 1).astype(F32)
+    return jnp.where(columns == column, 1.0, 0.0).astype(BF16)
 
 
 def times(left, right):
@@ -91,7 +97,7 @@
     extra = -(-rows // 16) * 16 - words.shape[0]
     if extra:
         words = jnp.concatenate([words, jnp.zeros((extra, words.shape[1]), F32)], axis=0)
-    return summed(times_turned(stacked_terms(words), place))
+    return summed(times(stacked_terms(words), place))
 
 
 def weighted_pressure(words, full, remote_rows):
@@ -164,7 +170,7 @@
     )
     earlier = times(chosen.astype(F32).astype(BF16), before.astype(F32).astype(BF16))
     slot = jnp.sum(jnp.where(chosen, earlier, 0.0), axis=0, keepdims=True).astype(jnp.int32)
-    place = marks(rank * capacity + slot, domains * capacity)
+    place = marks_turned(rank * capacity + slot, domains * capacity)
 
     parts = stacked_terms(disp[...].reshape(components * strips, cols_x))
     numbers = lax.broadcasted_iota(jnp.int32, (strips, face_count), 0)
@@ -239,7 +245,7 @@
 
 def last_kernel(
     capacity, heights, got_ref, rows_ref, words_ref, turned_ref, mortar_ref, rank_ref, face_ref, nodes_ref,
-    inverse_ref, internal_ref, blocks_ref, own_ref, halo_ref, out_ref,
+    marks_ref, inverse_ref, internal_ref, blocks_ref, own_ref, halo_ref, out_ref,
 ):
     block_rows = 12 * nodes_ref.shape[1] // LANES + sum(heights)
     domains = got_ref.shape[0] // block_rows
@@ -317,8 +323,7 @@
                 at = k * 4 + corner
                 row = jnp.broadcast_to(part[at : at + 1], (16, face_count)).astype(BF16)
                 spread.append(strip * jnp.concatenate([row] * (strips // 16), axis=0))
-        along_x = marks(index & (cols_x - 1), cols_x)
-        total = total + times_turned(jnp.concatenate(spread, axis=0), along_x)
+        total = total + times(jnp.concatenate(spread, axis=0), marks_ref[corner])
     contact = summed(total).reshape(components, layers, rows_y, cols_x)
     upward = lax.axis_index("sub") == 1
     edge = edge_part(upward, own_ref, halo_ref, blocks_ref)
@@ -383,9 +388,13 @@
 
 
 def internal_kernel(
-    disp_ref, modulus_ref, stiffness_ref, mass_ref, own_ref, halo_ref, out_ref, blocks_ref, inverse_ref
+    disp_ref, modulus_ref, stiffness_ref, mass_ref, nodes_ref, own_ref, halo_ref, out_ref, blocks_ref,
+    inverse_ref, marks_ref,
 ):
     inverse_ref[...] = 1.0 / mass_ref[...]
+    for corner in range(4):
+        width = disp_ref.shape[3]
+        marks_ref[corner] = marks_turned(nodes_ref[corner : corner + 1, :] & (width - 1), width)
     components, layers, rows_y, cols_x = disp_ref.shape
     dofs = 8 * components
     half = dofs // 2
@@ -529,14 +538,16 @@
     inner_halo = swapped(inner, ("dom", "sub"), 0)
     outer_halo = swapped(outer, ("dom", "sub"), 1)
     size = 8 * components * GROUP
-    internal, blocks, inverse = on_core(
+    internal, blocks, inverse, along_x = on_core(
         internal_kernel,
-        [shaped(displacement.shape), shaped((2 * size, size), BF16), shaped(node_mass.shape)],
+        [shaped(displacement.shape), shaped((2 * size, size), BF16), shaped(node_mass.shape),
+            shaped((4, face_count, cols_x), BF16),
+        ],
         1_000_000_000,
         700_000,
-    )(displacement, modulus, stiffness, node_mass, inner, inner_halo)
+    )(displacement, modulus, stiffness, node_mass, nodes, inner, inner_halo)
     return on_core(last, shaped(displacement.shape), 1_000_000_000, 1_500_000)(
-        got, rows, words, turned, mortar, rank, face, nodes, inverse, internal, blocks, outer, outer_halo
+        got, rows, words, turned, mortar, rank, face, nodes, along_x, inverse, internal, blocks, outer, outer_halo
     )
 
 

time: 24.9 us -> 25 us (level)
  Pallas kernels: 6.13 us -> 6.49 us
  waiting for transfers between devices: 8.85 us -> 8.59 us
    pallas_call x1, Pallas kernels: 1.01 us -> 1.27 us  [shards(): on_core(internal_kernel, [shaped(displacement.shape), shaped((2 * size, s...]
    ppermute x2, waiting for transfers between devices: 8.85 us -> 8.59 us  [swapped(): return lax.ppermute(block, axis, route)]
  transfers between devices with their start and end apart: 3 -> 3, of which waited for: 1 -> 1; matrix products, arithmetic and copies ran while one was open for 0% -> 0% of each run, Pallas kernels for 4% -> 5%
where the time goes in v17:
time: 25 us; the launch traced here: 24.7 us
  starting transfers between devices  9.5 us (38%)
  waiting for transfers between devices  8.59 us (34%)
  Pallas kernels  6.49 us (26%)
    ppermute x2, waiting for transfers between devices, swapped(): return lax.ppermute(block, axis, route)  8.59 us
    all_to_all x1, starting transfers between devices, shards(): lax.all_to_all(sent.reshape(domains, 1, -1), 'dom', split_axis=0, concat_...  6.03 us
    ppermute x2, starting transfers between devices, swapped(): return lax.ppermute(block, axis, route)  3.47 us
    pallas_call x1, Pallas kernels, shards(): on_core(first, [shaped((domains * (rows_high + sum(heights)), LANES)), sh...  3.07 us
    pallas_call x1, Pallas kernels, shards(): on_core(last, shaped(displacement.shape), 1000000000, 1500000)  2.14 us
    pallas_call x1, Pallas kernels, shards(): on_core(internal_kernel, [shaped(displacement.shape), shaped((2 * size, s...  1.27 us
  transfers between devices with their start and end apart: 3, of which 1 were waited for; matrix products, arithmetic and copies ran while one was open for 0% of the time, Pallas kernels for 5%

profile of v17, /device:TPU:16, one launch (start us, length us, event | category | flops | bytes accessed | tf_op | source)
XLA Modules:
  0.0 24.7 jit_solution(4047182970125842338)
XLA Ops:
  0.0 3.1 %shard_map.127 = (f32[904,128]{1,0:T(8,128)}, f32[24,256]{1,0:T(8,128)S(1)}, f32[129,256]{1,0:T(8,128)S(1)}, f32[104,256]{1,0:T(8,128)S(1)}, s32[1,256]{1,0:T(1,...) custom-call(s32[4,512]{1,0:T(4,128)} %refs_0_.1, ...), custom_call_target="tpu_custom_call" | custom-call | flops 900000000 | bytes 1500000 | tf_op jit(solution)/shard_map/pallas_call | solution.py:504
  3.1 0.0 copy-start
  3.1 0.0 copy-start.1
  3.1 0.0 copy-start.2
  3.1 0.0 copy-start.3
  3.1 6.0 %all-to-all-start = ((f32[8,1,14464]{2,1,0:T(1,128)}), f32[8,1,14464]{2,1,0:T(1,128)S(1)}, u32[]{:S(2)}, u32[]{:S(2)}) async-start(f32[8,1,14464]{2,1,0:T(1,128)} %bitcast.5), calls=%async_computation | async-start | bytes 925696 | tf_op jit(solution)/shard_map/all_to_all | solution.py:530
  9.2 0.0 collective-permute-start
  9.2 3.5 %collective-permute-start.1 = (f32[4,32,256]{2,1,0:T(8,128)S(1)}, f32[4,32,256]{2,1,0:T(8,128)S(1)}, u32[]{:S(2)}, u32[]{:S(2)}) collective-permute-start(f32[4,32,256]{2,1,0:T(8,128)S(1)} %get-tuple-element.32.refs_12_), channel_id=1, source_target_pairs={{1,2},{2,1},{3,4},{4,3},{5,6},{6,5},{7,8},{8,7},{9,10},{10,9},{11,... | collective-permute-start | bytes 393224 | tf_op jit(solution)/shard_map/ppermute | solution.py:446
  12.6 0.0 collective-permute-done.halo_ref
  12.7 0.0 copy-done
  12.7 0.0 copy-done.1
  12.7 0.0 copy-done.2
  12.7 0.0 copy-done.3
  12.7 1.3 %shard_map.128 = (f32[3,2,32,256]{3,2,1,0:T(8,128)S(1)}, bf16[384,192]{1,0:T(8,128)(2,1)S(1)}, f32[2,32,256]{2,1,0:T(8,128)S(1)}, bf16[4,512,256]{2,1,0:T(8,128)(2,1)S(1)}) custom-call(f32[3,2,32,256]{3,2,1,0:T(8,128)S(1)} %copy-done, f32[2,32,256]{2,1,0:T(8,128)S(1)} %copy-done.1, f32[24,24]{1,0:T(8,128)S(1)} %copy-done.3, f32[2,32,256]{2,1,0:T(8,128)S(1)} %copy-done.2, ...), custom_call_target="tpu_custom_call" | custom-call | flops 1000000000 | bytes 700000 | tf_op jit(solution)/shard_map/pallas_call | solution.py:541
  14.0 8.6 %collective-permute-done.1.refs_13_ = f32[4,32,256]{2,1,0:T(8,128)S(1)} collective-permute-done((f32[4,32,256]{2,1,0:T(8,128)S(1)}, f32[4,32,256]{2,1,0:T(8,128)S(1)}, u32[]{:S(2)}, u32[]{:S(2)}) %collective-permute-start.1) | collective-permute-done | bytes 131104 | tf_op jit(solution)/shard_map/ppermute | solution.py:446
  22.6 0.0 all-to-all-done
  22.6 2.1 %shard_map.129 = f32[3,2,32,256]{3,2,1,0:T(8,128)} custom-call(f32[904,128]{1,0:T(8,128)S(1)} %bitcast.7, f32[24,256]{1,0:T(8,128)S(1)} %get-tuple-element.20.refs_1_, f32[129,256]{1,0:T(8,128)S(1)} %get-tuple-element.21.refs_2_, f32[104,256]{1,0:T(8,128)S(1)} %get-tuple-element.22.refs_3_, s32[1,256]{1,0:T(1,128)S(1)} %get-tuple-element.23.refs_4_, ...), custom_call_target="tpu_custom_call" | custom-call | flops 1000000000 | bytes 1500000 | tf_op jit(solution)/shard_map/pallas_call | solution.py:549
Async XLA Ops:
  3.1 9.6 %copy-start = (f32[3,2,32,256]{3,2,1,0:T(8,128)S(1)}, f32[3,2,32,256]{3,2,1,0:T(8,128)}, u32[]{:S(2)}) copy-start(f32[3,2,32,256]{3,2,1,0:T(8,128)} %disp_ref.1) | copy-start | bytes 589828
  3.1 9.6 %copy-start.1 = (f32[2,32,256]{2,1,0:T(8,128)S(1)}, f32[2,32,256]{2,1,0:T(8,128)}, u32[]{:S(2)}) copy-start(f32[2,32,256]{2,1,0:T(8,128)} %modulus_ref.1) | copy-start | bytes 196612
  3.1 9.6 %copy-start.2 = (f32[2,32,256]{2,1,0:T(8,128)S(1)}, f32[2,32,256]{2,1,0:T(8,128)}, u32[]{:S(2)}) copy-start(f32[2,32,256]{2,1,0:T(8,128)} %mass_ref.1) | copy-start | bytes 196612
  3.1 9.6 %copy-start.3 = (f32[24,24]{1,0:T(8,128)S(1)}, f32[24,24]{1,0:T(8,128)}, u32[]{:S(2)}) copy-start(f32[24,24]{1,0:T(8,128)} %stiffness_ref.1) | copy-start | bytes 6916
  3.1 19.4 %all-to-all-start = ((f32[8,1,14464]{2,1,0:T(1,128)}), f32[8,1,14464]{2,1,0:T(1,128)S(1)}, u32[]{:S(2)}, u32[]{:S(2)}) async-start(f32[8,1,14464]{2,1,0:T(1,128)} %bitcast.5), calls=%async_computation | async-start | bytes 925696 | tf_op jit(solution)/shard_map/all_to_all | solution.py:530
  9.2 3.5 %collective-permute-start = (f32[4,32,256]{2,1,0:T(8,128)S(1)}, f32[4,32,256]{2,1,0:T(8,128)S(1)}, u32[]{:S(2)}, u32[]{:S(2)}) collective-permute-start(f32[4,32,256]{2,1,0:T(8,128)S(1)} %get-tuple-element.27.own_ref), channel_id=1, source_target_pairs={{0,1},{1,0},{2,3},{3,2},{4,5},{5,4},{6,7},{7,6},{8,9},{9,8},{10,11... | collective-permute-start | bytes 393224 | tf_op jit(solution)/shard_map/ppermute | solution.py:446
  9.2 13.4 %collective-permute-start.1 = (f32[4,32,256]{2,1,0:T(8,128)S(1)}, f32[4,32,256]{2,1,0:T(8,128)S(1)}, u32[]{:S(2)}, u32[]{:S(2)}) collective-permute-start(f32[4,32,256]{2,1,0:T(8,128)S(1)} %get-tuple-element.32.refs_12_), channel_id=1, source_target_pairs={{1,2},{2,1},{3,4},{4,3},{5,6},{6,5},{7,8},{8,7},{9,10},{10,9},{11,... | collective-permute-start | bytes 393224 | tf_op jit(solution)/shard_map/ppermute | solution.py:446

commit v18 on v15

--- a/solution.py
+++ b/solution.py
@@ -239,7 +239,7 @@
 
 def last_kernel(
     capacity, heights, got_ref, rows_ref, words_ref, turned_ref, mortar_ref, rank_ref, face_ref, nodes_ref,
-    inverse_ref, internal_ref, blocks_ref, own_ref, halo_ref, out_ref,
+    inverse_ref, internal_ref, blocks_ref, own_ref, halo_ref, out_hbm, out_ref, sems,
 ):
     block_rows = 12 * nodes_ref.shape[1] // LANES + sum(heights)
     domains = got_ref.shape[0] // block_rows
@@ -306,27 +306,35 @@
     )
     forces = summed(times_turned(stacked_terms(forces), at))
     forces = jnp.concatenate([forces[:12], forces[12:]], axis=1)
-    total = jnp.zeros((2 * components * strips, cols_x), F32)
     parts = [term.astype(F32) for term in terms_of(forces, 2)]
-    for corner in range(4):
-        index = nodes_ref[corner : corner + 1, :]
-        strip = marks(index >> halves(cols_x), strips)
-        spread = []
-        for part in parts:
-            for k in range(components):
-                at = k * 4 + corner
-                row = jnp.broadcast_to(part[at : at + 1], (16, face_count)).astype(BF16)
-                spread.append(strip * jnp.concatenate([row] * (strips // 16), axis=0))
-        along_x = marks(index & (cols_x - 1), cols_x)
-        total = total + times_turned(jnp.concatenate(spread, axis=0), along_x)
-    contact = summed(total).reshape(components, layers, rows_y, cols_x)
+    indices = [nodes_ref[corner : corner + 1, :] for corner in range(4)]
+    along_x = [marks(index & (cols_x - 1), cols_x) for index in indices]
+    strip = [marks(index >> halves(cols_x), strips) for index in indices]
     upward = lax.axis_index("sub") == 1
     edge = edge_part(upward, own_ref, halo_ref, blocks_ref)
-    at = jnp.where(upward, layers - 1, 0)
+    at_edge = jnp.where(upward, layers - 1, 0)
+    copies = []
     for layer in range(layers):
+        total = jnp.zeros((2 * components * rows_y, cols_x), F32)
+        for corner in range(4):
+            here = strip[corner][layer * rows_y : (layer + 1) * rows_y]
+            spread = []
+            for part in parts:
+                for k in range(components):
+                    at = k * 4 + corner
+                    row = jnp.broadcast_to(part[at : at + 1], (16, face_count)).astype(BF16)
+                    spread.append(here * jnp.concatenate([row] * (rows_y // 16), axis=0))
+            total = total + times_turned(jnp.concatenate(spread, axis=0), along_x[corner])
+        contact = summed(total).reshape(components, rows_y, cols_x)
         for k in range(components):
-            nodal = internal_ref[k, layer] + jnp.where(at == layer, edge[k], 0.0)
-            out_ref[k, layer] = (nodal + contact[k, layer]) * inverse_ref[layer]
+            nodal = internal_ref[k, layer] + jnp.where(at_edge == layer, edge[k], 0.0)
+            out_ref[k, layer] = (nodal + contact[k]) * inverse_ref[layer]
+        copies.append(
+            pltpu.make_async_copy(out_ref.at[:, layer], out_hbm.at[:, layer], sems.at[layer])
+        )
+        copies[-1].start()
+    for copy in copies:
+        copy.wait()
 
 
 GROUP = 8
@@ -535,8 +543,19 @@
         1_000_000_000,
         700_000,
     )(displacement, modulus, stiffness, node_mass, inner, inner_halo)
-    return on_core(last, shaped(displacement.shape), 1_000_000_000, 1_500_000)(
-        got, rows, words, turned, mortar, rank, face, nodes, inverse, internal, blocks, outer, outer_halo
+    return on_core(
+        last,
+        shaped(displacement.shape),
+        1_000_000_000,
+        1_500_000,
+        out_specs=in_hbm,
+        scratch_shapes=[
+            pltpu.VMEM(displacement.shape, F32),
+            pltpu.SemaphoreType.DMA((layers,)),
+        ],
+    )(
+        got, rows, words, turned, mortar, rank, face, nodes, inverse, internal, blocks, outer,
+        outer_halo,
     )
 
 

time: 24.9 us -> 24.9 us (level)
  no operation moved by 1% of the time
where the time goes in v18:
time: 24.9 us; the launch traced here: 24.6 us
  starting transfers between devices  9.51 us (38%)
  waiting for transfers between devices  8.85 us (36%)
  Pallas kernels  6.16 us (25%)
    ppermute x2, waiting for transfers between devices, swapped(): return lax.ppermute(block, axis, route)  8.85 us
    all_to_all x1, starting transfers between devices, shards(): lax.all_to_all(sent.reshape(domains, 1, -1), 'dom', split_axis=0, concat_...  6.04 us
    ppermute x2, starting transfers between devices, swapped(): return lax.ppermute(block, axis, route)  3.47 us
    pallas_call x1, Pallas kernels, shards(): on_core(first, [shaped((domains * (rows_high + sum(heights)), LANES)), sh...  2.99 us
    pallas_call x1, Pallas kernels, shards(): on_core(last, shaped(displacement.shape), 1000000000, 1500000, out_specs=...  2.15 us
    pallas_call x1, Pallas kernels, shards(): on_core(internal_kernel, [shaped(displacement.shape), shaped((2 * size, s...  1.01 us
  transfers between devices with their start and end apart: 3, of which 1 were waited for; matrix products, arithmetic and copies ran while one was open for 0% of the time, Pallas kernels for 4%

profile of v18, /device:TPU:16, one launch (start us, length us, event | category | flops | bytes accessed | tf_op | source)
XLA Modules:
  0.0 24.6 jit_solution(788804320815150755)
XLA Ops:
  0.0 3.0 %shard_map.127 = (f32[904,128]{1,0:T(8,128)}, f32[24,256]{1,0:T(8,128)S(1)}, f32[129,256]{1,0:T(8,128)S(1)}, f32[104,256]{1,0:T(8,128)S(1)}, s32[1,256]{1,0:T(1,...) custom-call(s32[4,512]{1,0:T(4,128)} %refs_0_.1, ...), custom_call_target="tpu_custom_call" | custom-call | flops 900000000 | bytes 1500000 | tf_op jit(solution)/shard_map/pallas_call | solution.py:503
  3.0 0.0 copy-start
  3.0 0.0 copy-start.1
  3.0 0.0 copy-start.2
  3.0 0.0 copy-start.3
  3.1 6.0 %all-to-all-start = ((f32[8,1,14464]{2,1,0:T(1,128)}), f32[8,1,14464]{2,1,0:T(1,128)S(1)}, u32[]{:S(2)}, u32[]{:S(2)}) async-start(f32[8,1,14464]{2,1,0:T(1,128)} %bitcast.5), calls=%async_computation | async-start | bytes 925696 | tf_op jit(solution)/shard_map/all_to_all | solution.py:529
  9.1 0.0 collective-permute-start
  9.1 3.5 %collective-permute-start.1 = (f32[4,32,256]{2,1,0:T(8,128)S(1)}, f32[4,32,256]{2,1,0:T(8,128)S(1)}, u32[]{:S(2)}, u32[]{:S(2)}) collective-permute-start(f32[4,32,256]{2,1,0:T(8,128)S(1)} %get-tuple-element.30.refs_11_), channel_id=1, source_target_pairs={{1,2},{2,1},{3,4},{4,3},{5,6},{6,5},{7,8},{8,7},{9,10},{10,9},{11,... | collective-permute-start | bytes 393224 | tf_op jit(solution)/shard_map/ppermute | solution.py:445
  12.6 0.0 collective-permute-done.halo_ref
  12.6 0.0 copy-done
  12.6 0.0 copy-done.1
  12.6 0.0 copy-done.2
  12.6 0.0 copy-done.3
  12.6 1.0 %shard_map.128 = (f32[3,2,32,256]{3,2,1,0:T(8,128)S(1)}, bf16[384,192]{1,0:T(8,128)(2,1)S(1)}, f32[2,32,256]{2,1,0:T(8,128)S(1)}) custom-call(f32[3,2,32,256]{3,2,1,0:T(8,128)S(1)} %copy-done, f32[2,32,256]{2,1,0:T(8,128)S(1)} %copy-done.1, f32[24,24]{1,0:T(8,128)S(1)} %copy-done.3, f32[2,32,256]{2,1,0:T(8,128)S(1)} %copy-done.2, ...), custom_call_target="tpu_custom_call" | custom-call | flops 1000000000 | bytes 700000 | tf_op jit(solution)/shard_map/pallas_call | solution.py:540
  13.6 8.8 %collective-permute-done.1.refs_12_ = f32[4,32,256]{2,1,0:T(8,128)S(1)} collective-permute-done((f32[4,32,256]{2,1,0:T(8,128)S(1)}, f32[4,32,256]{2,1,0:T(8,128)S(1)}, u32[]{:S(2)}, u32[]{:S(2)}) %collective-permute-start.1) | collective-permute-done | bytes 131104 | tf_op jit(solution)/shard_map/ppermute | solution.py:445
  22.5 0.0 all-to-all-done
  22.5 2.2 %shard_map.129 = f32[3,2,32,256]{3,2,1,0:T(8,128)} custom-call(f32[904,128]{1,0:T(8,128)S(1)} %bitcast.7, f32[24,256]{1,0:T(8,128)S(1)} %get-tuple-element.19.refs_1_, f32[129,256]{1,0:T(8,128)S(1)} %get-tuple-element.20.refs_2_, f32[104,256]{1,0:T(8,128)S(1)} %get-tuple-element.21.refs_3_, s32[1,256]{1,0:T(1,128)S(1)} %get-tuple-element.22.refs_4_, ...), custom_call_target="tpu_custom_call" | custom-call | flops 1000000000 | bytes 1500000 | tf_op jit(solution)/shard_map/pallas_call | solution.py:546
Async XLA Ops:
  3.0 9.6 %copy-start = (f32[3,2,32,256]{3,2,1,0:T(8,128)S(1)}, f32[3,2,32,256]{3,2,1,0:T(8,128)}, u32[]{:S(2)}) copy-start(f32[3,2,32,256]{3,2,1,0:T(8,128)} %disp_ref.1) | copy-start | bytes 589828
  3.0 9.6 %copy-start.1 = (f32[2,32,256]{2,1,0:T(8,128)S(1)}, f32[2,32,256]{2,1,0:T(8,128)}, u32[]{:S(2)}) copy-start(f32[2,32,256]{2,1,0:T(8,128)} %modulus_ref.1) | copy-start | bytes 196612
  3.0 9.6 %copy-start.2 = (f32[2,32,256]{2,1,0:T(8,128)S(1)}, f32[2,32,256]{2,1,0:T(8,128)}, u32[]{:S(2)}) copy-start(f32[2,32,256]{2,1,0:T(8,128)} %mass_ref.1) | copy-start | bytes 196612
  3.0 9.6 %copy-start.3 = (f32[24,24]{1,0:T(8,128)S(1)}, f32[24,24]{1,0:T(8,128)}, u32[]{:S(2)}) copy-start(f32[24,24]{1,0:T(8,128)} %stiffness_ref.1) | copy-start | bytes 6916
  3.1 19.4 %all-to-all-start = ((f32[8,1,14464]{2,1,0:T(1,128)}), f32[8,1,14464]{2,1,0:T(1,128)S(1)}, u32[]{:S(2)}, u32[]{:S(2)}) async-start(f32[8,1,14464]{2,1,0:T(1,128)} %bitcast.5), calls=%async_computation | async-start | bytes 925696 | tf_op jit(solution)/shard_map/all_to_all | solution.py:529
  9.1 3.5 %collective-permute-start = (f32[4,32,256]{2,1,0:T(8,128)S(1)}, f32[4,32,256]{2,1,0:T(8,128)S(1)}, u32[]{:S(2)}, u32[]{:S(2)}) collective-permute-start(f32[4,32,256]{2,1,0:T(8,128)S(1)} %get-tuple-element.26.own_ref), channel_id=1, source_target_pairs={{0,1},{1,0},{2,3},{3,2},{4,5},{5,4},{6,7},{7,6},{8,9},{9,8},{10,11... | collective-permute-start | bytes 393224 | tf_op jit(solution)/shard_map/ppermute | solution.py:445
  9.1 13.4 %collective-permute-start.1 = (f32[4,32,256]{2,1,0:T(8,128)S(1)}, f32[4,32,256]{2,1,0:T(8,128)S(1)}, u32[]{:S(2)}, u32[]{:S(2)}) collective-permute-start(f32[4,32,256]{2,1,0:T(8,128)S(1)} %get-tuple-element.30.refs_11_), channel_id=1, source_target_pairs={{1,2},{2,1},{3,4},{4,3},{5,6},{6,5},{7,8},{8,7},{9,10},{10,9},{11,... | collective-permute-start | bytes 393224 | tf_op jit(solution)/shard_map/ppermute | solution.py:445

commit v19 on v18

--- a/solution.py
+++ b/solution.py
@@ -130,7 +130,7 @@
         gap_hbm, shape_hbm, modulus_hbm,
         sent_ref, rows_ref, words_ref, turned_ref, mortar_ref, rank_ref, face_ref, nodes,
         inner_ref, outer_ref,
-        disp, count, weight, normal_v, gap_v, shape, modulus, blocks, sems, copy_sem,
+        disp, count, weight, normal_v, gap_v, shape, modulus, blocks, sems, copy_sems,
     ) = refs
     components, layers, rows_y, cols_x = disp.shape
     block_rows = 12 * nodes.shape[1] // LANES + sum(heights)
@@ -215,11 +215,20 @@
         axis=0,
     )
     placed = routed(short_words, group * heights[1], place)
-    for domain in range(domains):
-        at = place_in_group(domain, domains) * block_rows + rows_high + heights[0]
+    members = sorted(range(domains), key=lambda domain: place_in_group(domain, domains))
+    chunk = sent_ref.shape[0] // copy_sems.shape[0]
+    copies = []
+    for spot, domain in enumerate(members):
+        at = spot * block_rows + rows_high + heights[0]
         blocks[at : at + heights[1]] = folded(placed, heights[1], capacity, domain)
-    sending = pltpu.make_async_copy(blocks, sent_ref, copy_sem)
-    sending.start()
+        if (spot + 1) * block_rows % chunk == 0:
+            part = pl.ds((spot + 1) * block_rows - chunk, chunk)
+            copies.append(
+                pltpu.make_async_copy(
+                    blocks.at[part], sent_ref.at[part], copy_sems.at[len(copies)]
+                )
+            )
+            copies[-1].start()
 
     words_ref[: 4 * full] = long_words
     words_ref[4 * full :] = short_words
@@ -234,7 +243,8 @@
         for k in range(components):
             target[k] = disp[k, layer]
         target[components] = modulus[...]
-    sending.wait()
+    for copy in copies:
+        copy.wait()
 
 
 def last_kernel(
@@ -522,7 +532,7 @@
         + [
             pltpu.VMEM((domains * (rows_high + sum(heights)), LANES), F32),
             pltpu.SemaphoreType.DMA((len(arrays),)),
-            pltpu.SemaphoreType.DMA(()),
+            pltpu.SemaphoreType.DMA((4,)),
         ],
     )(*[pltpu.with_memory_space_constraint(x, pltpu.HBM) for x in arrays])
     order = [place_in_group(domain, domains) for domain in range(domains)]

time: 24.9 us -> 25 us (level)
  no operation moved by 1% of the time
where the time goes in v19:
time: 25 us; the launch traced here: 24.7 us
  starting transfers between devices  9.51 us (38%)
  waiting for transfers between devices  8.85 us (35%)
  Pallas kernels  6.17 us (25%)
    ppermute x2, waiting for transfers between devices, swapped(): return lax.ppermute(block, axis, route)  8.84 us
    all_to_all x1, starting transfers between devices, shards(): lax.all_to_all(sent.reshape(domains, 1, -1), 'dom', split_axis=0, concat_...  6.04 us
    ppermute x2, starting transfers between devices, swapped(): return lax.ppermute(block, axis, route)  3.47 us
    pallas_call x1, Pallas kernels, shards(): on_core(first, [shaped((domains * (rows_high + sum(heights)), LANES)), sh...  3.01 us
    pallas_call x1, Pallas kernels, shards(): on_core(last, shaped(displacement.shape), 1000000000, 1500000, out_specs=...  2.15 us
    pallas_call x1, Pallas kernels, shards(): on_core(internal_kernel, [shaped(displacement.shape), shaped((2 * size, s...  1.02 us
  transfers between devices with their start and end apart: 3, of which 1 were waited for; matrix products, arithmetic and copies ran while one was open for 0% of the time, Pallas kernels for 4%

profile of v19, /device:TPU:16, one launch (start us, length us, event | category | flops | bytes accessed | tf_op | source)
XLA Modules:
  0.0 24.7 jit_solution(2397300539361650203)
XLA Ops:
  0.0 3.0 %shard_map.127 = (f32[904,128]{1,0:T(8,128)}, f32[24,256]{1,0:T(8,128)S(1)}, f32[129,256]{1,0:T(8,128)S(1)}, f32[104,256]{1,0:T(8,128)S(1)}, s32[1,256]{1,0:T(1,...) custom-call(s32[4,512]{1,0:T(4,128)} %refs_0_.1, ...), custom_call_target="tpu_custom_call" | custom-call | flops 900000000 | bytes 1500000 | tf_op jit(solution)/shard_map/pallas_call | solution.py:513
  3.0 0.0 copy-start
  3.0 0.0 copy-start.1
  3.0 0.0 copy-start.2
  3.1 0.0 copy-start.3
  3.1 6.0 %all-to-all-start = ((f32[8,1,14464]{2,1,0:T(1,128)}), f32[8,1,14464]{2,1,0:T(1,128)S(1)}, u32[]{:S(2)}, u32[]{:S(2)}) async-start(f32[8,1,14464]{2,1,0:T(1,128)} %bitcast.5), calls=%async_computation | async-start | bytes 925696 | tf_op jit(solution)/shard_map/all_to_all | solution.py:539
  9.1 0.0 collective-permute-start
  9.1 3.5 %collective-permute-start.1 = (f32[4,32,256]{2,1,0:T(8,128)S(1)}, f32[4,32,256]{2,1,0:T(8,128)S(1)}, u32[]{:S(2)}, u32[]{:S(2)}) collective-permute-start(f32[4,32,256]{2,1,0:T(8,128)S(1)} %get-tuple-element.30.refs_11_), channel_id=1, source_target_pairs={{1,2},{2,1},{3,4},{4,3},{5,6},{6,5},{7,8},{8,7},{9,10},{10,9},{11,... | collective-permute-start | bytes 393224 | tf_op jit(solution)/shard_map/ppermute | solution.py:455
  12.6 0.0 collective-permute-done.halo_ref
  12.6 0.0 copy-done
  12.6 0.0 copy-done.1
  12.6 0.0 copy-done.2
  12.6 0.0 copy-done.3
  12.6 1.0 %shard_map.128 = (f32[3,2,32,256]{3,2,1,0:T(8,128)S(1)}, bf16[384,192]{1,0:T(8,128)(2,1)S(1)}, f32[2,32,256]{2,1,0:T(8,128)S(1)}) custom-call(f32[3,2,32,256]{3,2,1,0:T(8,128)S(1)} %copy-done, f32[2,32,256]{2,1,0:T(8,128)S(1)} %copy-done.1, f32[24,24]{1,0:T(8,128)S(1)} %copy-done.3, f32[2,32,256]{2,1,0:T(8,128)S(1)} %copy-done.2, ...), custom_call_target="tpu_custom_call" | custom-call | flops 1000000000 | bytes 700000 | tf_op jit(solution)/shard_map/pallas_call | solution.py:550
  13.7 8.8 %collective-permute-done.1.refs_12_ = f32[4,32,256]{2,1,0:T(8,128)S(1)} collective-permute-done((f32[4,32,256]{2,1,0:T(8,128)S(1)}, f32[4,32,256]{2,1,0:T(8,128)S(1)}, u32[]{:S(2)}, u32[]{:S(2)}) %collective-permute-start.1) | collective-permute-done | bytes 131104 | tf_op jit(solution)/shard_map/ppermute | solution.py:455
  22.5 0.0 all-to-all-done
  22.5 2.2 %shard_map.129 = f32[3,2,32,256]{3,2,1,0:T(8,128)} custom-call(f32[904,128]{1,0:T(8,128)S(1)} %bitcast.7, f32[24,256]{1,0:T(8,128)S(1)} %get-tuple-element.19.refs_1_, f32[129,256]{1,0:T(8,128)S(1)} %get-tuple-element.20.refs_2_, f32[104,256]{1,0:T(8,128)S(1)} %get-tuple-element.21.refs_3_, s32[1,256]{1,0:T(1,128)S(1)} %get-tuple-element.22.refs_4_, ...), custom_call_target="tpu_custom_call" | custom-call | flops 1000000000 | bytes 1500000 | tf_op jit(solution)/shard_map/pallas_call | solution.py:556
Async XLA Ops:
  3.0 9.6 %copy-start = (f32[3,2,32,256]{3,2,1,0:T(8,128)S(1)}, f32[3,2,32,256]{3,2,1,0:T(8,128)}, u32[]{:S(2)}) copy-start(f32[3,2,32,256]{3,2,1,0:T(8,128)} %disp_ref.1) | copy-start | bytes 589828
  3.0 9.6 %copy-start.1 = (f32[2,32,256]{2,1,0:T(8,128)S(1)}, f32[2,32,256]{2,1,0:T(8,128)}, u32[]{:S(2)}) copy-start(f32[2,32,256]{2,1,0:T(8,128)} %modulus_ref.1) | copy-start | bytes 196612
  3.0 9.6 %copy-start.2 = (f32[2,32,256]{2,1,0:T(8,128)S(1)}, f32[2,32,256]{2,1,0:T(8,128)}, u32[]{:S(2)}) copy-start(f32[2,32,256]{2,1,0:T(8,128)} %mass_ref.1) | copy-start | bytes 196612
  3.1 9.6 %copy-start.3 = (f32[24,24]{1,0:T(8,128)S(1)}, f32[24,24]{1,0:T(8,128)}, u32[]{:S(2)}) copy-start(f32[24,24]{1,0:T(8,128)} %stiffness_ref.1) | copy-start | bytes 6916
  3.1 19.4 %all-to-all-start = ((f32[8,1,14464]{2,1,0:T(1,128)}), f32[8,1,14464]{2,1,0:T(1,128)S(1)}, u32[]{:S(2)}, u32[]{:S(2)}) async-start(f32[8,1,14464]{2,1,0:T(1,128)} %bitcast.5), calls=%async_computation | async-start | bytes 925696 | tf_op jit(solution)/shard_map/all_to_all | solution.py:539
  9.1 3.5 %collective-permute-start = (f32[4,32,256]{2,1,0:T(8,128)S(1)}, f32[4,32,256]{2,1,0:T(8,128)S(1)}, u32[]{:S(2)}, u32[]{:S(2)}) collective-permute-start(f32[4,32,256]{2,1,0:T(8,128)S(1)} %get-tuple-element.26.own_ref), channel_id=1, source_target_pairs={{0,1},{1,0},{2,3},{3,2},{4,5},{5,4},{6,7},{7,6},{8,9},{9,8},{10,11... | collective-permute-start | bytes 393224 | tf_op jit(solution)/shard_map/ppermute | solution.py:455
  9.1 13.4 %collective-permute-start.1 = (f32[4,32,256]{2,1,0:T(8,128)S(1)}, f32[4,32,256]{2,1,0:T(8,128)S(1)}, u32[]{:S(2)}, u32[]{:S(2)}) collective-permute-start(f32[4,32,256]{2,1,0:T(8,128)S(1)} %get-tuple-element.30.refs_11_), channel_id=1, source_target_pairs={{1,2},{2,1},{3,4},{4,3},{5,6},{6,5},{7,8},{8,7},{9,10},{10,9},{11,... | collective-permute-start | bytes 393224 | tf_op jit(solution)/shard_map/ppermute | solution.py:455

commit v20 on v18

--- a/solution.py
+++ b/solution.py
@@ -134,12 +134,15 @@
     ) = refs
     components, layers, rows_y, cols_x = disp.shape
     block_rows = 12 * nodes.shape[1] // LANES + sum(heights)
+    pieces = [pl.ds(start, LANES) for start in range(0, shape_hbm.shape[1], LANES)]
     sources = (
-        nodes_hbm, disp_hbm, rank_hbm, face_hbm, mortar_hbm, shape_hbm, count_hbm, weight_hbm,
-        normal_hbm, gap_hbm, modulus_hbm.at[disp.shape[1] - 1],
+        nodes_hbm, disp_hbm, rank_hbm, face_hbm, mortar_hbm,
+        *[shape_hbm.at[:, piece] for piece in pieces],
+        count_hbm, weight_hbm, normal_hbm, gap_hbm, modulus_hbm.at[disp.shape[1] - 1],
     )
     targets = (
-        nodes, disp, rank_ref, face_ref, mortar_ref, shape, count, weight, normal_v, gap_v, modulus,
+        nodes, disp, rank_ref, face_ref, mortar_ref, *[shape.at[i, : shape_hbm.shape[0]] for i in range(len(pieces))],
+        count, weight, normal_v, gap_v, modulus,
     )
     brought = [
         pltpu.make_async_copy(source, target, sems.at[i])
@@ -181,10 +184,16 @@
                 rows_ref[at : at + 1, :] = values[k : k + 1, fold * cols_x : (fold + 1) * cols_x]
 
     points = gap.shape[0]
+
+    def shape_of(node):
+        return jnp.concatenate(
+            [shape[i, pl.ds(node, points, 8)] for i in range(pair_total // LANES)], axis=1
+        )
+
     full = points // 8 * 8
     live = lax.broadcasted_iota(jnp.int32, (points, pair_total), 0) < count[...]
     root = jnp.where(live, jnp.sqrt(weight[...]), 0.0)
-    weighted = [root * shape[:, node] for node in range(4)]
+    weighted = [root * shape_of(node) for node in range(4)]
     long_words = jnp.concatenate([x[:full] for x in weighted], axis=0)
     group = LANES // capacity
     placed = routed(long_words, group * heights[0], place)
@@ -206,7 +215,7 @@
         across = sum(
             normal[k : k + 1] * mortar_rows[k * 4 + node : k * 4 + node + 1] for k in range(3)
         )
-        gap = gap - shape[:, 4 + node] * across
+        gap = gap - shape_of(4 + node) * across
     gap = root * gap
     short_words = jnp.concatenate(
         [gap[:full]]
@@ -224,7 +233,7 @@
     words_ref[: 4 * full] = long_words
     words_ref[4 * full :] = short_words
     for node in range(4):
-        turned = root * shape[:, 4 + node]
+        turned = root * shape_of(4 + node)
         turned_ref[node * full : (node + 1) * full] = turned[:full]
         turned_ref[4 * full + node : 4 * full + node + 1] = turned[full:]
 
@@ -493,13 +502,14 @@
         pair_weight,
         pair_normal,
         pair_gap,
-        jnp.swapaxes(pair_shape, 0, 1),
+        jnp.swapaxes(pair_shape, 0, 1).reshape(-1, pair_total),
         modulus,
     ]
     edge = shaped((components + 1, rows_y, cols_x))
     in_hbm = pl.BlockSpec(memory_space=pltpu.HBM)
     in_vmem = pl.BlockSpec(memory_space=pltpu.VMEM)
-    kept = [displacement, *arrays[5:-1], modulus[0]]
+    shapes = shaped((pair_total // LANES, 8 * (full + 8), LANES))
+    kept = [displacement, *arrays[5:-2], shapes, shaped((rows_y, cols_x))]
     sent, rows, words, turned, mortar, rank, face, nodes, inner, outer = on_core(
         first,
         [
@@ -521,7 +531,7 @@
         scratch_shapes=[pltpu.VMEM(x.shape, x.dtype) for x in kept]
         + [
             pltpu.VMEM((domains * (rows_high + sum(heights)), LANES), F32),
-            pltpu.SemaphoreType.DMA((len(arrays),)),
+            pltpu.SemaphoreType.DMA((len(arrays) + pair_total // LANES,)),
             pltpu.SemaphoreType.DMA(()),
         ],
     )(*[pltpu.with_memory_space_constraint(x, pltpu.HBM) for x in arrays])

time: 24.9 us -> 25 us (level)
  no operation moved by 1% of the time
where the time goes in v20:
time: 25 us; the launch traced here: 24.7 us
  starting transfers between devices  9.51 us (38%)
  waiting for transfers between devices  8.83 us (35%)
  Pallas kernels  6.2 us (25%)
    ppermute x2, waiting for transfers between devices, swapped(): return lax.ppermute(block, axis, route)  8.83 us
    all_to_all x1, starting transfers between devices, shards(): lax.all_to_all(sent.reshape(domains, 1, -1), 'dom', split_axis=0, concat_...  6.04 us
    ppermute x2, starting transfers between devices, swapped(): return lax.ppermute(block, axis, route)  3.47 us
    pallas_call x1, Pallas kernels, shards(): on_core(first, [shaped((domains * (rows_high + sum(heights)), LANES)), sh...  3.01 us
    pallas_call x1, Pallas kernels, shards(): on_core(last, shaped(displacement.shape), 1000000000, 1500000, out_specs=...  2.15 us
    pallas_call x1, Pallas kernels, shards(): on_core(internal_kernel, [shaped(displacement.shape), shaped((2 * size, s...  1.03 us
  transfers between devices with their start and end apart: 3, of which 1 were waited for; matrix products, arithmetic and copies ran while one was open for 0% of the time, Pallas kernels for 4%

profile of v20, /device:TPU:16, one launch (start us, length us, event | category | flops | bytes accessed | tf_op | source)
XLA Modules:
  0.0 24.7 jit_solution(17692154542860611400)
XLA Ops:
  0.0 3.0 %shard_map.127 = (f32[904,128]{1,0:T(8,128)}, f32[24,256]{1,0:T(8,128)S(1)}, f32[129,256]{1,0:T(8,128)S(1)}, f32[104,256]{1,0:T(8,128)S(1)}, s32[1,256]{1,0:T(1,...) custom-call(s32[4,512]{1,0:T(4,128)} %refs_0_.1, ...), custom_call_target="tpu_custom_call" | custom-call | flops 900000000 | bytes 1500000 | tf_op jit(solution)/shard_map/pallas_call | solution.py:513
  3.0 0.0 copy-start
  3.0 0.0 copy-start.1
  3.0 0.0 copy-start.2
  3.1 0.0 copy-start.3
  3.1 6.0 %all-to-all-start = ((f32[8,1,14464]{2,1,0:T(1,128)}), f32[8,1,14464]{2,1,0:T(1,128)S(1)}, u32[]{:S(2)}, u32[]{:S(2)}) async-start(f32[8,1,14464]{2,1,0:T(1,128)} %bitcast.6), calls=%async_computation | async-start | bytes 925696 | tf_op jit(solution)/shard_map/all_to_all | solution.py:539
  9.1 0.0 collective-permute-start
  9.1 3.5 %collective-permute-start.1 = (f32[4,32,256]{2,1,0:T(8,128)S(1)}, f32[4,32,256]{2,1,0:T(8,128)S(1)}, u32[]{:S(2)}, u32[]{:S(2)}) collective-permute-start(f32[4,32,256]{2,1,0:T(8,128)S(1)} %get-tuple-element.30.refs_11_), channel_id=1, source_target_pairs={{1,2},{2,1},{3,4},{4,3},{5,6},{6,5},{7,8},{8,7},{9,10},{10,9},{11,... | collective-permute-start | bytes 393224 | tf_op jit(solution)/shard_map/ppermute | solution.py:454
  12.6 0.0 collective-permute-done.halo_ref
  12.6 0.0 copy-done
  12.6 0.0 copy-done.1
  12.6 0.0 copy-done.2
  12.6 0.0 copy-done.3
  12.6 1.0 %shard_map.128 = (f32[3,2,32,256]{3,2,1,0:T(8,128)S(1)}, bf16[384,192]{1,0:T(8,128)(2,1)S(1)}, f32[2,32,256]{2,1,0:T(8,128)S(1)}) custom-call(f32[3,2,32,256]{3,2,1,0:T(8,128)S(1)} %copy-done, f32[2,32,256]{2,1,0:T(8,128)S(1)} %copy-done.1, f32[24,24]{1,0:T(8,128)S(1)} %copy-done.3, f32[2,32,256]{2,1,0:T(8,128)S(1)} %copy-done.2, ...), custom_call_target="tpu_custom_call" | custom-call | flops 1000000000 | bytes 700000 | tf_op jit(solution)/shard_map/pallas_call | solution.py:550
  13.7 8.8 %collective-permute-done.1.refs_12_ = f32[4,32,256]{2,1,0:T(8,128)S(1)} collective-permute-done((f32[4,32,256]{2,1,0:T(8,128)S(1)}, f32[4,32,256]{2,1,0:T(8,128)S(1)}, u32[]{:S(2)}, u32[]{:S(2)}) %collective-permute-start.1) | collective-permute-done | bytes 131104 | tf_op jit(solution)/shard_map/ppermute | solution.py:454
  22.5 0.0 all-to-all-done
  22.5 2.2 %shard_map.129 = f32[3,2,32,256]{3,2,1,0:T(8,128)} custom-call(f32[904,128]{1,0:T(8,128)S(1)} %bitcast.9, f32[24,256]{1,0:T(8,128)S(1)} %get-tuple-element.19.refs_1_, f32[129,256]{1,0:T(8,128)S(1)} %get-tuple-element.20.refs_2_, f32[104,256]{1,0:T(8,128)S(1)} %get-tuple-element.21.refs_3_, s32[1,256]{1,0:T(1,128)S(1)} %get-tuple-element.22.refs_4_, ...), custom_call_target="tpu_custom_call" | custom-call | flops 1000000000 | bytes 1500000 | tf_op jit(solution)/shard_map/pallas_call | solution.py:556
Async XLA Ops:
  3.0 9.6 %copy-start = (f32[3,2,32,256]{3,2,1,0:T(8,128)S(1)}, f32[3,2,32,256]{3,2,1,0:T(8,128)}, u32[]{:S(2)}) copy-start(f32[3,2,32,256]{3,2,1,0:T(8,128)} %disp_ref.1) | copy-start | bytes 589828
  3.0 9.6 %copy-start.1 = (f32[2,32,256]{2,1,0:T(8,128)S(1)}, f32[2,32,256]{2,1,0:T(8,128)}, u32[]{:S(2)}) copy-start(f32[2,32,256]{2,1,0:T(8,128)} %modulus_ref.1) | copy-start | bytes 196612
  3.0 9.6 %copy-start.2 = (f32[2,32,256]{2,1,0:T(8,128)S(1)}, f32[2,32,256]{2,1,0:T(8,128)}, u32[]{:S(2)}) copy-start(f32[2,32,256]{2,1,0:T(8,128)} %mass_ref.1) | copy-start | bytes 196612
  3.1 9.6 %copy-start.3 = (f32[24,24]{1,0:T(8,128)S(1)}, f32[24,24]{1,0:T(8,128)}, u32[]{:S(2)}) copy-start(f32[24,24]{1,0:T(8,128)} %stiffness_ref.1) | copy-start | bytes 6916
  3.1 19.4 %all-to-all-start = ((f32[8,1,14464]{2,1,0:T(1,128)}), f32[8,1,14464]{2,1,0:T(1,128)S(1)}, u32[]{:S(2)}, u32[]{:S(2)}) async-start(f32[8,1,14464]{2,1,0:T(1,128)} %bitcast.6), calls=%async_computation | async-start | bytes 925696 | tf_op jit(solution)/shard_map/all_to_all | solution.py:539
  9.1 3.5 %collective-permute-start = (f32[4,32,256]{2,1,0:T(8,128)S(1)}, f32[4,32,256]{2,1,0:T(8,128)S(1)}, u32[]{:S(2)}, u32[]{:S(2)}) collective-permute-start(f32[4,32,256]{2,1,0:T(8,128)S(1)} %get-tuple-element.26.own_ref), channel_id=1, source_target_pairs={{0,1},{1,0},{2,3},{3,2},{4,5},{5,4},{6,7},{7,6},{8,9},{9,8},{10,11... | collective-permute-start | bytes 393224 | tf_op jit(solution)/shard_map/ppermute | solution.py:454
  9.1 13.4 %collective-permute-start.1 = (f32[4,32,256]{2,1,0:T(8,128)S(1)}, f32[4,32,256]{2,1,0:T(8,128)S(1)}, u32[]{:S(2)}, u32[]{:S(2)}) collective-permute-start(f32[4,32,256]{2,1,0:T(8,128)S(1)} %get-tuple-element.30.refs_11_), channel_id=1, source_target_pairs={{1,2},{2,1},{3,4},{4,3},{5,6},{6,5},{7,8},{8,7},{9,10},{10,9},{11,... | collective-permute-start | bytes 393224 | tf_op jit(solution)/shard_map/ppermute | solution.py:454

commit v21 on v18

--- a/solution.py
+++ b/solution.py
@@ -68,6 +68,13 @@
     return block
 
 
+def rows_of(ref, start, count):
+    if not isinstance(start, int):
+        return ref[pl.ds(start, count)]
+    first, end = start // 8 * 8, -(-(start + count) // 8) * 8
+    return ref[first:end][start - first : start - first + count]
+
+
 def unfolded(got_ref, block_rows, start, height, capacity):
     group = LANES // capacity
     part = lax.broadcasted_iota(jnp.int32, (height, LANES), 1) >> halves(capacity)
@@ -78,7 +85,7 @@
             block = None
             for spot in range(group):
                 at = (first + spot) * block_rows + start
-                piece = got_ref[at : at + height]
+                piece = rows_of(got_ref, at, height)
                 if j != spot:
                     piece = pltpu.roll(piece, (spot - j) * capacity % LANES, 1)
                 block = piece if block is None else jnp.where(part == spot, piece, block)
@@ -218,7 +225,7 @@
     for domain in range(domains):
         at = place_in_group(domain, domains) * block_rows + rows_high + heights[0]
         blocks[at : at + heights[1]] = folded(placed, heights[1], capacity, domain)
-    sending = pltpu.make_async_copy(blocks, sent_ref, copy_sem)
+    sending = pltpu.make_async_copy(blocks.at[: sent_ref.shape[0]], sent_ref, copy_sem)
     sending.start()
 
     words_ref[: 4 * full] = long_words
@@ -262,7 +269,7 @@
         halves_of = [
             jnp.concatenate(
                 [
-                    got_ref[pl.ds((turn * step + i) * block_rows + j * high, high)]
+                    rows_of(got_ref, (turn * step + i) * block_rows + j * high, high)
                     for j in range(cols_x // LANES)
                 ],
                 axis=1,
@@ -499,7 +506,7 @@
     edge = shaped((components + 1, rows_y, cols_x))
     in_hbm = pl.BlockSpec(memory_space=pltpu.HBM)
     in_vmem = pl.BlockSpec(memory_space=pltpu.VMEM)
-    kept = [displacement, *arrays[5:-1], modulus[0]]
+    kept = [displacement, *arrays[5:-1], shaped((rows_y, cols_x))]
     sent, rows, words, turned, mortar, rank, face, nodes, inner, outer = on_core(
         first,
         [
@@ -520,7 +527,7 @@
         out_specs=[in_hbm] + [in_vmem] * 9,
         scratch_shapes=[pltpu.VMEM(x.shape, x.dtype) for x in kept]
         + [
-            pltpu.VMEM((domains * (rows_high + sum(heights)), LANES), F32),
+            pltpu.VMEM((domains * (rows_high + sum(heights)) + 8, LANES), F32),
             pltpu.SemaphoreType.DMA((len(arrays),)),
             pltpu.SemaphoreType.DMA(()),
         ],

time: 24.9 us -> 25 us (level)
  no operation moved by 1% of the time
where the time goes in v21:
time: 25 us; the launch traced here: 24.7 us
  starting transfers between devices  9.51 us (38%)
  waiting for transfers between devices  8.84 us (35%)
  Pallas kernels  6.17 us (25%)
    ppermute x2, waiting for transfers between devices, swapped(): return lax.ppermute(block, axis, route)  8.84 us
    all_to_all x1, starting transfers between devices, shards(): lax.all_to_all(sent.reshape(domains, 1, -1), 'dom', split_axis=0, concat_...  6.05 us
    ppermute x2, starting transfers between devices, swapped(): return lax.ppermute(block, axis, route)  3.47 us
    pallas_call x1, Pallas kernels, shards(): on_core(first, [shaped((domains * (rows_high + sum(heights)), LANES)), sh...  3 us
    pallas_call x1, Pallas kernels, shards(): on_core(last, shaped(displacement.shape), 1000000000, 1500000, out_specs=...  2.16 us
    pallas_call x1, Pallas kernels, shards(): on_core(internal_kernel, [shaped(displacement.shape), shaped((2 * size, s...  1.01 us
  transfers between devices with their start and end apart: 3, of which 1 were waited for; matrix products, arithmetic and copies ran while one was open for 0% of the time, Pallas kernels for 4%

profile of v21, /device:TPU:16, one launch (start us, length us, event | category | flops | bytes accessed | tf_op | source)
XLA Modules:
  0.0 24.7 jit_solution(14781838561012953683)
XLA Ops:
  0.0 3.0 %shard_map.127 = (f32[904,128]{1,0:T(8,128)}, f32[24,256]{1,0:T(8,128)S(1)}, f32[129,256]{1,0:T(8,128)S(1)}, f32[104,256]{1,0:T(8,128)S(1)}, s32[1,256]{1,0:T(1,...) custom-call(s32[4,512]{1,0:T(4,128)} %refs_0_.1, ...), custom_call_target="tpu_custom_call" | custom-call | flops 900000000 | bytes 1500000 | tf_op jit(solution)/shard_map/pallas_call | solution.py:510
  3.0 0.0 copy-start
  3.0 0.0 copy-start.1
  3.0 0.0 copy-start.2
  3.0 0.0 copy-start.3
  3.1 6.0 %all-to-all-start = ((f32[8,1,14464]{2,1,0:T(1,128)}), f32[8,1,14464]{2,1,0:T(1,128)S(1)}, u32[]{:S(2)}, u32[]{:S(2)}) async-start(f32[8,1,14464]{2,1,0:T(1,128)} %bitcast.5), calls=%async_computation | async-start | bytes 925696 | tf_op jit(solution)/shard_map/all_to_all | solution.py:536
  9.1 0.0 collective-permute-start
  9.1 3.5 %collective-permute-start.1 = (f32[4,32,256]{2,1,0:T(8,128)S(1)}, f32[4,32,256]{2,1,0:T(8,128)S(1)}, u32[]{:S(2)}, u32[]{:S(2)}) collective-permute-start(f32[4,32,256]{2,1,0:T(8,128)S(1)} %get-tuple-element.30.refs_11_), channel_id=1, source_target_pairs={{1,2},{2,1},{3,4},{4,3},{5,6},{6,5},{7,8},{8,7},{9,10},{10,9},{11,... | collective-permute-start | bytes 393224 | tf_op jit(solution)/shard_map/ppermute | solution.py:452
  12.6 0.0 collective-permute-done.halo_ref
  12.6 0.0 copy-done
  12.6 0.0 copy-done.1
  12.6 0.0 copy-done.2
  12.6 0.0 copy-done.3
  12.6 1.0 %shard_map.128 = (f32[3,2,32,256]{3,2,1,0:T(8,128)S(1)}, bf16[384,192]{1,0:T(8,128)(2,1)S(1)}, f32[2,32,256]{2,1,0:T(8,128)S(1)}) custom-call(f32[3,2,32,256]{3,2,1,0:T(8,128)S(1)} %copy-done, f32[2,32,256]{2,1,0:T(8,128)S(1)} %copy-done.1, f32[24,24]{1,0:T(8,128)S(1)} %copy-done.3, f32[2,32,256]{2,1,0:T(8,128)S(1)} %copy-done.2, ...), custom_call_target="tpu_custom_call" | custom-call | flops 1000000000 | bytes 700000 | tf_op jit(solution)/shard_map/pallas_call | solution.py:547
  13.6 8.8 %collective-permute-done.1.refs_12_ = f32[4,32,256]{2,1,0:T(8,128)S(1)} collective-permute-done((f32[4,32,256]{2,1,0:T(8,128)S(1)}, f32[4,32,256]{2,1,0:T(8,128)S(1)}, u32[]{:S(2)}, u32[]{:S(2)}) %collective-permute-start.1) | collective-permute-done | bytes 131104 | tf_op jit(solution)/shard_map/ppermute | solution.py:452
  22.5 0.0 all-to-all-done
  22.5 2.2 %shard_map.129 = f32[3,2,32,256]{3,2,1,0:T(8,128)} custom-call(f32[904,128]{1,0:T(8,128)S(1)} %bitcast.7, f32[24,256]{1,0:T(8,128)S(1)} %get-tuple-element.19.refs_1_, f32[129,256]{1,0:T(8,128)S(1)} %get-tuple-element.20.refs_2_, f32[104,256]{1,0:T(8,128)S(1)} %get-tuple-element.21.refs_3_, s32[1,256]{1,0:T(1,128)S(1)} %get-tuple-element.22.refs_4_, ...), custom_call_target="tpu_custom_call" | custom-call | flops 1000000000 | bytes 1500000 | tf_op jit(solution)/shard_map/pallas_call | solution.py:553
Async XLA Ops:
  3.0 9.6 %copy-start = (f32[3,2,32,256]{3,2,1,0:T(8,128)S(1)}, f32[3,2,32,256]{3,2,1,0:T(8,128)}, u32[]{:S(2)}) copy-start(f32[3,2,32,256]{3,2,1,0:T(8,128)} %disp_ref.1) | copy-start | bytes 589828
  3.0 9.6 %copy-start.1 = (f32[2,32,256]{2,1,0:T(8,128)S(1)}, f32[2,32,256]{2,1,0:T(8,128)}, u32[]{:S(2)}) copy-start(f32[2,32,256]{2,1,0:T(8,128)} %modulus_ref.1) | copy-start | bytes 196612
  3.0 9.6 %copy-start.2 = (f32[2,32,256]{2,1,0:T(8,128)S(1)}, f32[2,32,256]{2,1,0:T(8,128)}, u32[]{:S(2)}) copy-start(f32[2,32,256]{2,1,0:T(8,128)} %mass_ref.1) | copy-start | bytes 196612
  3.0 9.6 %copy-start.3 = (f32[24,24]{1,0:T(8,128)S(1)}, f32[24,24]{1,0:T(8,128)}, u32[]{:S(2)}) copy-start(f32[24,24]{1,0:T(8,128)} %stiffness_ref.1) | copy-start | bytes 6916
  3.1 19.4 %all-to-all-start = ((f32[8,1,14464]{2,1,0:T(1,128)}), f32[8,1,14464]{2,1,0:T(1,128)S(1)}, u32[]{:S(2)}, u32[]{:S(2)}) async-start(f32[8,1,14464]{2,1,0:T(1,128)} %bitcast.5), calls=%async_computation | async-start | bytes 925696 | tf_op jit(solution)/shard_map/all_to_all | solution.py:536
  9.1 3.5 %collective-permute-start = (f32[4,32,256]{2,1,0:T(8,128)S(1)}, f32[4,32,256]{2,1,0:T(8,128)S(1)}, u32[]{:S(2)}, u32[]{:S(2)}) collective-permute-start(f32[4,32,256]{2,1,0:T(8,128)S(1)} %get-tuple-element.26.own_ref), channel_id=1, source_target_pairs={{0,1},{1,0},{2,3},{3,2},{4,5},{5,4},{6,7},{7,6},{8,9},{9,8},{10,11... | collective-permute-start | bytes 393224 | tf_op jit(solution)/shard_map/ppermute | solution.py:452
  9.1 13.4 %collective-permute-start.1 = (f32[4,32,256]{2,1,0:T(8,128)S(1)}, f32[4,32,256]{2,1,0:T(8,128)S(1)}, u32[]{:S(2)}, u32[]{:S(2)}) collective-permute-start(f32[4,32,256]{2,1,0:T(8,128)S(1)} %get-tuple-element.30.refs_11_), channel_id=1, source_target_pairs={{1,2},{2,1},{3,4},{4,3},{5,6},{6,5},{7,8},{8,7},{9,10},{10,9},{11,... | collective-permute-start | bytes 393224 | tf_op jit(solution)/shard_map/ppermute | solution.py:452

commit v22 on v21

--- a/solution.py
+++ b/solution.py
@@ -246,7 +246,7 @@
 
 def last_kernel(
     capacity, heights, got_ref, rows_ref, words_ref, turned_ref, mortar_ref, rank_ref, face_ref, nodes_ref,
-    inverse_ref, internal_ref, blocks_ref, own_ref, halo_ref, out_hbm, out_ref, sems,
+    inverse_ref, internal_ref, out_ref,
 ):
     block_rows = 12 * nodes_ref.shape[1] // LANES + sum(heights)
     domains = got_ref.shape[0] // block_rows
@@ -317,10 +317,6 @@
     indices = [nodes_ref[corner : corner + 1, :] for corner in range(4)]
     along_x = [marks(index & (cols_x - 1), cols_x) for index in indices]
     strip = [marks(index >> halves(cols_x), strips) for index in indices]
-    upward = lax.axis_index("sub") == 1
-    edge = edge_part(upward, own_ref, halo_ref, blocks_ref)
-    at_edge = jnp.where(upward, layers - 1, 0)
-    copies = []
     for layer in range(layers):
         total = jnp.zeros((2 * components * rows_y, cols_x), F32)
         for corner in range(4):
@@ -334,14 +330,18 @@
             total = total + times_turned(jnp.concatenate(spread, axis=0), along_x[corner])
         contact = summed(total).reshape(components, rows_y, cols_x)
         for k in range(components):
-            nodal = internal_ref[k, layer] + jnp.where(at_edge == layer, edge[k], 0.0)
-            out_ref[k, layer] = (nodal + contact[k]) * inverse_ref[layer]
-        copies.append(
-            pltpu.make_async_copy(out_ref.at[:, layer], out_hbm.at[:, layer], sems.at[layer])
-        )
-        copies[-1].start()
-    for copy in copies:
-        copy.wait()
+            out_ref[k, layer] = (internal_ref[k, layer] + contact[k]) * inverse_ref[layer]
+
+
+def edge_kernel(partial_ref, inverse_ref, blocks_ref, own_ref, halo_ref, out_ref):
+    components, layers = out_ref.shape[:2]
+    upward = lax.axis_index("sub") == 1
+    edge = edge_part(upward, own_ref, halo_ref, blocks_ref)
+    at_edge = jnp.where(upward, layers - 1, 0)
+    for layer in range(layers):
+        for k in range(components):
+            added = jnp.where(at_edge == layer, edge[k], 0.0) * inverse_ref[layer]
+            out_ref[k, layer] = partial_ref[k, layer] + added
 
 
 GROUP = 8
@@ -550,19 +550,11 @@
         1_000_000_000,
         700_000,
     )(displacement, modulus, stiffness, node_mass, inner, inner_halo)
-    return on_core(
-        last,
-        shaped(displacement.shape),
-        1_000_000_000,
-        1_500_000,
-        out_specs=in_hbm,
-        scratch_shapes=[
-            pltpu.VMEM(displacement.shape, F32),
-            pltpu.SemaphoreType.DMA((layers,)),
-        ],
-    )(
-        got, rows, words, turned, mortar, rank, face, nodes, inverse, internal, blocks, outer,
-        outer_halo,
+    partial = on_core(last, shaped(displacement.shape), 1_000_000_000, 1_500_000)(
+        got, rows, words, turned, mortar, rank, face, nodes, inverse, internal
+    )
+    return on_core(edge_kernel, shaped(displacement.shape), 200_000_000, 600_000)(
+        partial, inverse, blocks, outer, outer_halo
     )
 
 

time: 25 us -> 25.1 us (level)
  Pallas kernels: 6.17 us -> 6.64 us
  waiting for transfers between devices: 8.84 us -> 8.43 us
    ppermute x2, waiting for transfers between devices: 8.84 us -> 0.01 us  [swapped(): return lax.ppermute(block, axis, route)]
    all_to_all x1, waiting for transfers between devices: 0.01 us -> 8.43 us  [shards(): lax.all_to_all(sent.reshape(domains, 1, -1), 'dom', split_axis=0, concat_...]
    pallas_call x1 -> x2, Pallas kernels: 2.16 us -> 2.63 us  [the longest x1 1.42 us: shards(): on_core(last, shaped(displacement.shape), 1000000000, 1500000)]
  transfers between devices with their start and end apart: 3 -> 3, of which waited for: 1 -> 1; matrix products, arithmetic and copies ran while one was open for 0% -> 0% of each run, Pallas kernels for 4% -> 10%
where the time goes in v22:
time: 25.1 us; the launch traced here: 24.7 us
  starting transfers between devices  9.51 us (38%)
  waiting for transfers between devices  8.43 us (34%)
  Pallas kernels  6.64 us (26%)
    all_to_all x1, waiting for transfers between devices, shards(): lax.all_to_all(sent.reshape(domains, 1, -1), 'dom', split_axis=0, concat_...  8.43 us
    all_to_all x1, starting transfers between devices, shards(): lax.all_to_all(sent.reshape(domains, 1, -1), 'dom', split_axis=0, concat_...  6.05 us
    ppermute x2, starting transfers between devices, swapped(): return lax.ppermute(block, axis, route)  3.47 us
    pallas_call x1, Pallas kernels, shards(): on_core(first, [shaped((domains * (rows_high + sum(heights)), LANES)), sh...  3 us
    pallas_call x1, Pallas kernels, shards(): on_core(last, shaped(displacement.shape), 1000000000, 1500000)  1.42 us
    pallas_call x1, Pallas kernels, shards(): on_core(edge_kernel, shaped(displacement.shape), 200000000, 600000)  1.2 us
    pallas_call x1, Pallas kernels, shards(): on_core(internal_kernel, [shaped(displacement.shape), shaped((2 * size, s...  1.02 us
  transfers between devices with their start and end apart: 3, of which 1 were waited for; matrix products, arithmetic and copies ran while one was open for 0% of the time, Pallas kernels for 10%

profile of v22, /device:TPU:16, one launch (start us, length us, event | category | flops | bytes accessed | tf_op | source)
XLA Modules:
  0.0 24.7 jit_solution(16711344181259355617)
XLA Ops:
  0.0 3.0 %shard_map.127 = (f32[904,128]{1,0:T(8,128)}, f32[24,256]{1,0:T(8,128)S(1)}, f32[129,256]{1,0:T(8,128)S(1)}, f32[104,256]{1,0:T(8,128)S(1)}, s32[1,256]{1,0:T(1,...) custom-call(s32[4,512]{1,0:T(4,128)} %refs_0_.1, ...), custom_call_target="tpu_custom_call" | custom-call | flops 900000000 | bytes 1500000 | tf_op jit(solution)/shard_map/pallas_call | solution.py:510
  3.0 0.0 copy-start
  3.0 0.0 copy-start.1
  3.0 0.0 copy-start.2
  3.0 0.0 copy-start.3
  3.1 6.0 %all-to-all-start = ((f32[8,1,14464]{2,1,0:T(1,128)}), f32[8,1,14464]{2,1,0:T(1,128)S(1)}, u32[]{:S(2)}, u32[]{:S(2)}) async-start(f32[8,1,14464]{2,1,0:T(1,128)} %bitcast.5), calls=%async_computation | async-start | bytes 925696 | tf_op jit(solution)/shard_map/all_to_all | solution.py:536
  9.1 0.0 collective-permute-start
  9.1 3.5 %collective-permute-start.1 = (f32[4,32,256]{2,1,0:T(8,128)S(1)}, f32[4,32,256]{2,1,0:T(8,128)S(1)}, u32[]{:S(2)}, u32[]{:S(2)}) collective-permute-start(f32[4,32,256]{2,1,0:T(8,128)S(1)} %get-tuple-element.30.own_ref), channel_id=1, source_target_pairs={{1,2},{2,1},{3,4},{4,3},{5,6},{6,5},{7,8},{8,7},{9,10},{10,9},{11,... | collective-permute-start | bytes 393224 | tf_op jit(solution)/shard_map/ppermute | solution.py:452
  12.6 0.0 collective-permute-done.halo_ref
  12.6 0.0 copy-done
  12.6 0.0 copy-done.1
  12.6 0.0 copy-done.2
  12.6 0.0 copy-done.3
  12.6 1.0 %shard_map.128 = (f32[3,2,32,256]{3,2,1,0:T(8,128)S(1)}, bf16[384,192]{1,0:T(8,128)(2,1)S(1)}, f32[2,32,256]{2,1,0:T(8,128)S(1)}) custom-call(f32[3,2,32,256]{3,2,1,0:T(8,128)S(1)} %copy-done, f32[2,32,256]{2,1,0:T(8,128)S(1)} %copy-done.1, f32[24,24]{1,0:T(8,128)S(1)} %copy-done.3, f32[2,32,256]{2,1,0:T(8,128)S(1)} %copy-done.2, ...), custom_call_target="tpu_custom_call" | custom-call | flops 1000000000 | bytes 700000 | tf_op jit(solution)/shard_map/pallas_call | solution.py:547
  13.7 8.4 %all-to-all-done = f32[8,1,14464]{2,1,0:T(1,128)S(1)} async-done(((f32[8,1,14464]{2,1,0:T(1,128)}), f32[8,1,14464]{2,1,0:T(1,128)S(1)}, u32[]{:S(2)}, u32[]{:S(2)}) %all-to-all-start) | async-done | bytes 462880 | tf_op jit(solution)/shard_map/all_to_all | solution.py:536
  22.1 1.4 %shard_map.129.partial_ref = f32[3,2,32,256]{3,2,1,0:T(8,128)S(1)} custom-call(f32[904,128]{1,0:T(8,128)S(1)} %bitcast.7, f32[24,256]{1,0:T(8,128)S(1)} %get-tuple-element.19.refs_1_, f32[129,256]{1,0:T(8,128)S(1)} %get-tuple-element.20.refs_2_, f32[104,256]{1,0:T(8,128)S(1)} %get-tuple-element.21.refs_3_, s32[1,256]{1,0:T(1,128)S(1)} %get-tuple-element.22.refs_4_, ...), custom_call_target="tpu_custom_call" | custom-call | flops 1000000000 | bytes 1500000 | tf_op jit(solution)/shard_map/pallas_call | solution.py:553
  23.5 0.0 collective-permute-done.1.halo_ref
  23.5 1.2 %shard_map.130 = f32[3,2,32,256]{3,2,1,0:T(8,128)} custom-call(f32[3,2,32,256]{3,2,1,0:T(8,128)S(1)} %shard_map.129.partial_ref, f32[2,32,256]{2,1,0:T(8,128)S(1)} %get-tuple-element.27.refs_8_.inverse_ref, bf16[384,192]{1,0:T(8,128)(2,1)S(1)} %get-tuple-element.29.blocks_ref, f32[4,32,256]{2,1,0:T(8,128)S(1)} %get-tuple-element.30.own_ref, ...), custom_call_target="tpu_custom_call" | custom-call | flops 200000000 | bytes 600000 | tf_op jit(solution)/shard_map/pallas_call | solution.py:556
Async XLA Ops:
  3.0 9.6 %copy-start = (f32[3,2,32,256]{3,2,1,0:T(8,128)S(1)}, f32[3,2,32,256]{3,2,1,0:T(8,128)}, u32[]{:S(2)}) copy-start(f32[3,2,32,256]{3,2,1,0:T(8,128)} %disp_ref.1) | copy-start | bytes 589828
  3.0 9.6 %copy-start.1 = (f32[2,32,256]{2,1,0:T(8,128)S(1)}, f32[2,32,256]{2,1,0:T(8,128)}, u32[]{:S(2)}) copy-start(f32[2,32,256]{2,1,0:T(8,128)} %modulus_ref.1) | copy-start | bytes 196612
  3.0 9.6 %copy-start.2 = (f32[2,32,256]{2,1,0:T(8,128)S(1)}, f32[2,32,256]{2,1,0:T(8,128)}, u32[]{:S(2)}) copy-start(f32[2,32,256]{2,1,0:T(8,128)} %mass_ref.1) | copy-start | bytes 196612
  3.0 9.6 %copy-start.3 = (f32[24,24]{1,0:T(8,128)S(1)}, f32[24,24]{1,0:T(8,128)}, u32[]{:S(2)}) copy-start(f32[24,24]{1,0:T(8,128)} %stiffness_ref.1) | copy-start | bytes 6916
  3.1 19.0 %all-to-all-start = ((f32[8,1,14464]{2,1,0:T(1,128)}), f32[8,1,14464]{2,1,0:T(1,128)S(1)}, u32[]{:S(2)}, u32[]{:S(2)}) async-start(f32[8,1,14464]{2,1,0:T(1,128)} %bitcast.5), calls=%async_computation | async-start | bytes 925696 | tf_op jit(solution)/shard_map/all_to_all | solution.py:536
  9.1 3.5 %collective-permute-start = (f32[4,32,256]{2,1,0:T(8,128)S(1)}, f32[4,32,256]{2,1,0:T(8,128)S(1)}, u32[]{:S(2)}, u32[]{:S(2)}) collective-permute-start(f32[4,32,256]{2,1,0:T(8,128)S(1)} %get-tuple-element.26.own_ref), channel_id=1, source_target_pairs={{0,1},{1,0},{2,3},{3,2},{4,5},{5,4},{6,7},{7,6},{8,9},{9,8},{10,11... | collective-permute-start | bytes 393224 | tf_op jit(solution)/shard_map/ppermute | solution.py:452
  9.1 14.4 %collective-permute-start.1 = (f32[4,32,256]{2,1,0:T(8,128)S(1)}, f32[4,32,256]{2,1,0:T(8,128)S(1)}, u32[]{:S(2)}, u32[]{:S(2)}) collective-permute-start(f32[4,32,256]{2,1,0:T(8,128)S(1)} %get-tuple-element.30.own_ref), channel_id=1, source_target_pairs={{1,2},{2,1},{3,4},{4,3},{5,6},{6,5},{7,8},{8,7},{9,10},{10,9},{11,... | collective-permute-start | bytes 393224 | tf_op jit(solution)/shard_map/ppermute | solution.py:452

commit v23 on v21

--- a/solution.py
+++ b/solution.py
@@ -246,7 +246,7 @@
 
 def last_kernel(
     capacity, heights, got_ref, rows_ref, words_ref, turned_ref, mortar_ref, rank_ref, face_ref, nodes_ref,
-    inverse_ref, internal_ref, blocks_ref, own_ref, halo_ref, out_hbm, out_ref, sems,
+    inverse_ref, internal_ref, blocks_ref, part_ref, own_ref, halo_ref, out_hbm, out_ref, sems,
 ):
     block_rows = 12 * nodes_ref.shape[1] // LANES + sum(heights)
     domains = got_ref.shape[0] // block_rows
@@ -318,7 +318,12 @@
     along_x = [marks(index & (cols_x - 1), cols_x) for index in indices]
     strip = [marks(index >> halves(cols_x), strips) for index in indices]
     upward = lax.axis_index("sub") == 1
-    edge = edge_part(upward, own_ref, halo_ref, blocks_ref)
+    components_all = halo_ref.shape[0] - 1
+    half_rows = blocks_ref.shape[0] // 2
+    matrices = [blocks_ref[i * half_rows : (i + 1) * half_rows] for i in range(2)]
+    halo = products(matrices, shifted([halo_ref[k] for k in range(components_all)]))
+    modulus = jnp.where(upward, own_ref[components_all], halo_ref[components_all])
+    edge = on_nodes(scaled(part_ref[...] + halo, modulus))
     at_edge = jnp.where(upward, layers - 1, 0)
     copies = []
     for layer in range(layers):
@@ -356,13 +361,8 @@
     return views
 
 
-def element_forces(matrices, low, high, modulus):
-    rows_y, cols_x = modulus.shape
-    inside = (lax.broadcasted_iota(jnp.int32, (rows_y, cols_x), 0) < rows_y - 1) & (
-        lax.broadcasted_iota(jnp.int32, (rows_y, cols_x), 1) < cols_x - 1
-    )
-    scale = jnp.where(inside, modulus, 0.0)
-    views = shifted(low) + shifted(high)
+def products(matrices, views):
+    rows_y, cols_x = views[0].shape
     both = jnp.concatenate(matrices, axis=0)
     count = both.shape[0] // 2
     strips = []
@@ -370,8 +370,20 @@
         leading, second = terms_of(jnp.concatenate([view[y : y + GROUP] for view in views], axis=0), 2)
         found = times(both, leading)
         force = found[:count] + (found[count:] + times(matrices[0], second))
-        strips.append(force.reshape(-1, GROUP, cols_x) * scale[y : y + GROUP][None])
+        strips.append(force.reshape(-1, GROUP, cols_x))
     return jnp.concatenate(strips, axis=1)
+
+
+def scaled(forces, modulus):
+    rows_y, cols_x = modulus.shape
+    inside = (lax.broadcasted_iota(jnp.int32, (rows_y, cols_x), 0) < rows_y - 1) & (
+        lax.broadcasted_iota(jnp.int32, (rows_y, cols_x), 1) < cols_x - 1
+    )
+    return forces * jnp.where(inside, modulus, 0.0)[None]
+
+
+def element_forces(matrices, low, high, modulus):
+    return scaled(products(matrices, shifted(low) + shifted(high)), modulus)
 
 
 def on_nodes(forces):
@@ -398,7 +410,8 @@
 
 
 def internal_kernel(
-    disp_ref, modulus_ref, stiffness_ref, mass_ref, own_ref, halo_ref, out_ref, blocks_ref, inverse_ref
+    disp_ref, modulus_ref, stiffness_ref, mass_ref, own_ref, halo_ref, outer_ref, out_ref, inverse_ref,
+    far_ref, part_ref, blocks_ref,
 ):
     inverse_ref[...] = 1.0 / mass_ref[...]
     components, layers, rows_y, cols_x = disp_ref.shape
@@ -410,13 +423,24 @@
     upper = (row >= half).astype(jnp.int32)
     inner = row - half * upper
     dof = (inner >> 2) * 8 + upper * 4 + (inner & 3)
-    pick = (dof == lax.broadcasted_iota(jnp.int32, (size, dofs), 1)).astype(F32).astype(BF16)
+    pick = (dof == lax.broadcasted_iota(jnp.int32, (size, dofs), 1)).astype(F32)
+    rows = size // 2
+    outward = lax.axis_index("sub") == 1
+    near = jnp.where(outward, pick[:rows], pick[rows:]).astype(BF16)
+    far = jnp.where(outward, pick[rows:], pick[:rows]).astype(BF16)
+    pick = pick.astype(BF16)
+    near_blocks = []
     diagonal = (lax.broadcasted_iota(jnp.int32, (size, size), 0) & (GROUP - 1)) == (
         lax.broadcasted_iota(jnp.int32, (size, size), 1) & (GROUP - 1)
     )
     for i, term in enumerate(terms_of(stiffness_ref[...], 2)):
         wide = times_turned(times(pick, term).astype(BF16), pick)
         blocks_ref[i * size : (i + 1) * size] = jnp.where(diagonal, wide, 0.0).astype(BF16)
+        tall = times(near, term).astype(BF16)
+        same = diagonal[:rows, :rows]
+        near_blocks.append(jnp.where(same, times_turned(tall, near), 0.0).astype(BF16))
+        far_ref[i * rows : (i + 1) * rows] = jnp.where(same, times_turned(tall, far), 0.0).astype(BF16)
+    part_ref[...] = products(near_blocks, shifted([outer_ref[k] for k in range(components)]))
 
     blocks = [blocks_ref[i * size : (i + 1) * size] for i in range(2)]
     sums = [[0.0] * components for _ in range(layers)]
@@ -544,12 +568,18 @@
     inner_halo = swapped(inner, ("dom", "sub"), 0)
     outer_halo = swapped(outer, ("dom", "sub"), 1)
     size = 8 * components * GROUP
-    internal, blocks, inverse = on_core(
+    internal, inverse, far, part = on_core(
         internal_kernel,
-        [shaped(displacement.shape), shaped((2 * size, size), BF16), shaped(node_mass.shape)],
+        [
+            shaped(displacement.shape),
+            shaped(node_mass.shape),
+            shaped((size, size // 2), BF16),
+            shaped((size // 2 // GROUP, rows_y, cols_x)),
+        ],
         1_000_000_000,
         700_000,
-    )(displacement, modulus, stiffness, node_mass, inner, inner_halo)
+        scratch_shapes=[pltpu.VMEM((2 * size, size), BF16)],
+    )(displacement, modulus, stiffness, node_mass, inner, inner_halo, outer)
     return on_core(
         last,
         shaped(displacement.shape),
@@ -561,7 +591,7 @@
             pltpu.SemaphoreType.DMA((layers,)),
         ],
     )(
-        got, rows, words, turned, mortar, rank, face, nodes, inverse, internal, blocks, outer,
+        got, rows, words, turned, mortar, rank, face, nodes, inverse, internal, far, part, outer,
         outer_halo,
     )
 

time: 25 us -> 25 us (level)
  Pallas kernels: 6.17 us -> 6.52 us
  waiting for transfers between devices: 8.84 us -> 8.49 us
    ppermute x2, waiting for transfers between devices: 8.84 us -> 8.49 us  [swapped(): return lax.ppermute(block, axis, route)]
    pallas_call x1, Pallas kernels: 1.01 us -> 1.36 us  [shards(): on_core(internal_kernel, [shaped(displacement.shape), shaped(node_mass.sh...]
  transfers between devices with their start and end apart: 3 -> 3, of which waited for: 1 -> 1; matrix products, arithmetic and copies ran while one was open for 0% -> 0% of each run, Pallas kernels for 4% -> 6%
where the time goes in v23:
time: 25 us; the launch traced here: 24.7 us
  starting transfers between devices  9.51 us (38%)
  waiting for transfers between devices  8.49 us (34%)
  Pallas kernels  6.52 us (26%)
    ppermute x2, waiting for transfers between devices, swapped(): return lax.ppermute(block, axis, route)  8.49 us
    all_to_all x1, starting transfers between devices, shards(): lax.all_to_all(sent.reshape(domains, 1, -1), 'dom', split_axis=0, concat_...  6.05 us
    ppermute x2, starting transfers between devices, swapped(): return lax.ppermute(block, axis, route)  3.47 us
    pallas_call x1, Pallas kernels, shards(): on_core(first, [shaped((domains * (rows_high + sum(heights)), LANES)), sh...  3 us
    pallas_call x1, Pallas kernels, shards(): on_core(last, shaped(displacement.shape), 1000000000, 1500000, out_specs=...  2.16 us
    pallas_call x1, Pallas kernels, shards(): on_core(internal_kernel, [shaped(displacement.shape), shaped(node_mass.sh...  1.36 us
  transfers between devices with their start and end apart: 3, of which 1 were waited for; matrix products, arithmetic and copies ran while one was open for 0% of the time, Pallas kernels for 6%

profile of v23, /device:TPU:16, one launch (start us, length us, event | category | flops | bytes accessed | tf_op | source)
XLA Modules:
  0.0 24.7 jit_solution(137514473609933397)
XLA Ops:
  0.0 3.0 %shard_map.127 = (f32[904,128]{1,0:T(8,128)}, f32[24,256]{1,0:T(8,128)S(1)}, f32[129,256]{1,0:T(8,128)S(1)}, f32[104,256]{1,0:T(8,128)S(1)}, s32[1,256]{1,0:T(1,...) custom-call(s32[4,512]{1,0:T(4,128)} %refs_0_.1, ...), custom_call_target="tpu_custom_call" | custom-call | flops 900000000 | bytes 1500000 | tf_op jit(solution)/shard_map/pallas_call | solution.py:534
  3.0 0.0 copy-start
  3.0 0.0 copy-start.1
  3.0 0.0 copy-start.2
  3.0 0.0 copy-start.3
  3.1 6.0 %all-to-all-start = ((f32[8,1,14464]{2,1,0:T(1,128)}), f32[8,1,14464]{2,1,0:T(1,128)S(1)}, u32[]{:S(2)}, u32[]{:S(2)}) async-start(f32[8,1,14464]{2,1,0:T(1,128)} %bitcast.5), calls=%async_computation | async-start | bytes 925696 | tf_op jit(solution)/shard_map/all_to_all | solution.py:560
  9.1 0.0 collective-permute-start
  9.1 3.5 %collective-permute-start.1 = (f32[4,32,256]{2,1,0:T(8,128)S(1)}, f32[4,32,256]{2,1,0:T(8,128)S(1)}, u32[]{:S(2)}, u32[]{:S(2)}) collective-permute-start(f32[4,32,256]{2,1,0:T(8,128)S(1)} %get-tuple-element.28.outer_ref.refs_12_), channel_id=1, source_target_pairs={{1,2},{2,1},{3,4},{4,3},{5,6},{6,5},{7,8},{8,7},{9,10},{10,9},{11,... | collective-permute-start | bytes 393224 | tf_op jit(solution)/shard_map/ppermute | solution.py:476
  12.6 0.0 collective-permute-done.halo_ref
  12.6 0.0 copy-done
  12.6 0.0 copy-done.1
  12.6 0.0 copy-done.2
  12.6 0.0 copy-done.3
  12.6 1.4 %shard_map.128 = (f32[3,2,32,256]{3,2,1,0:T(8,128)S(1)}, f32[2,32,256]{2,1,0:T(8,128)S(1)}, bf16[192,96]{1,0:T(8,128)(2,1)S(1)}, f32[12,32,256]{2,1,0:T(8,128)S(1)}) custom-call(f32[3,2,32,256]{3,2,1,0:T(8,128)S(1)} %copy-done, f32[2,32,256]{2,1,0:T(8,128)S(1)} %copy-done.1, f32[24,24]{1,0:T(8,128)S(1)} %copy-done.3, f32[2,32,256]{2,1,0:T(8,128)S(1)} %copy-done.2, ...), custom_call_target="tpu_custom_call" | custom-call | flops 1000000000 | bytes 700000 | tf_op jit(solution)/shard_map/pallas_call | solution.py:571
  14.0 8.5 %collective-permute-done.1.refs_13_ = f32[4,32,256]{2,1,0:T(8,128)S(1)} collective-permute-done((f32[4,32,256]{2,1,0:T(8,128)S(1)}, f32[4,32,256]{2,1,0:T(8,128)S(1)}, u32[]{:S(2)}, u32[]{:S(2)}) %collective-permute-start.1) | collective-permute-done | bytes 131104 | tf_op jit(solution)/shard_map/ppermute | solution.py:476
  22.5 0.0 all-to-all-done
  22.5 2.2 %shard_map.129 = f32[3,2,32,256]{3,2,1,0:T(8,128)} custom-call(f32[904,128]{1,0:T(8,128)S(1)} %bitcast.7, f32[24,256]{1,0:T(8,128)S(1)} %get-tuple-element.20.refs_1_, f32[129,256]{1,0:T(8,128)S(1)} %get-tuple-element.21.refs_2_, f32[104,256]{1,0:T(8,128)S(1)} %get-tuple-element.22.refs_3_, s32[1,256]{1,0:T(1,128)S(1)} %get-tuple-element.23.refs_4_, ...), custom_call_target="tpu_custom_call" | custom-call | flops 1000000000 | bytes 1500000 | tf_op jit(solution)/shard_map/pallas_call | solution.py:583
Async XLA Ops:
  3.0 9.6 %copy-start = (f32[3,2,32,256]{3,2,1,0:T(8,128)S(1)}, f32[3,2,32,256]{3,2,1,0:T(8,128)}, u32[]{:S(2)}) copy-start(f32[3,2,32,256]{3,2,1,0:T(8,128)} %disp_ref.1) | copy-start | bytes 589828
  3.0 9.6 %copy-start.1 = (f32[2,32,256]{2,1,0:T(8,128)S(1)}, f32[2,32,256]{2,1,0:T(8,128)}, u32[]{:S(2)}) copy-start(f32[2,32,256]{2,1,0:T(8,128)} %modulus_ref.1) | copy-start | bytes 196612
  3.0 9.6 %copy-start.2 = (f32[2,32,256]{2,1,0:T(8,128)S(1)}, f32[2,32,256]{2,1,0:T(8,128)}, u32[]{:S(2)}) copy-start(f32[2,32,256]{2,1,0:T(8,128)} %mass_ref.1) | copy-start | bytes 196612
  3.0 9.6 %copy-start.3 = (f32[24,24]{1,0:T(8,128)S(1)}, f32[24,24]{1,0:T(8,128)}, u32[]{:S(2)}) copy-start(f32[24,24]{1,0:T(8,128)} %stiffness_ref.1) | copy-start | bytes 6916
  3.1 19.4 %all-to-all-start = ((f32[8,1,14464]{2,1,0:T(1,128)}), f32[8,1,14464]{2,1,0:T(1,128)S(1)}, u32[]{:S(2)}, u32[]{:S(2)}) async-start(f32[8,1,14464]{2,1,0:T(1,128)} %bitcast.5), calls=%async_computation | async-start | bytes 925696 | tf_op jit(solution)/shard_map/all_to_all | solution.py:560
  9.1 3.5 %collective-permute-start = (f32[4,32,256]{2,1,0:T(8,128)S(1)}, f32[4,32,256]{2,1,0:T(8,128)S(1)}, u32[]{:S(2)}, u32[]{:S(2)}) collective-permute-start(f32[4,32,256]{2,1,0:T(8,128)S(1)} %get-tuple-element.27.own_ref), channel_id=1, source_target_pairs={{0,1},{1,0},{2,3},{3,2},{4,5},{5,4},{6,7},{7,6},{8,9},{9,8},{10,11... | collective-permute-start | bytes 393224 | tf_op jit(solution)/shard_map/ppermute | solution.py:476
  9.1 13.4 %collective-permute-start.1 = (f32[4,32,256]{2,1,0:T(8,128)S(1)}, f32[4,32,256]{2,1,0:T(8,128)S(1)}, u32[]{:S(2)}, u32[]{:S(2)}) collective-permute-start(f32[4,32,256]{2,1,0:T(8,128)S(1)} %get-tuple-element.28.outer_ref.refs_12_), channel_id=1, source_target_pairs={{1,2},{2,1},{3,4},{4,3},{5,6},{6,5},{7,8},{8,7},{9,10},{10,9},{11,... | collective-permute-start | bytes 393224 | tf_op jit(solution)/shard_map/ppermute | solution.py:476

commit v24 on v21

--- a/solution.py
+++ b/solution.py
@@ -142,11 +142,11 @@
     components, layers, rows_y, cols_x = disp.shape
     block_rows = 12 * nodes.shape[1] // LANES + sum(heights)
     sources = (
-        nodes_hbm, disp_hbm, rank_hbm, face_hbm, mortar_hbm, shape_hbm, count_hbm, weight_hbm,
-        normal_hbm, gap_hbm, modulus_hbm.at[disp.shape[1] - 1],
+        disp_hbm, shape_hbm, nodes_hbm, gap_hbm, weight_hbm, normal_hbm, rank_hbm, face_hbm,
+        mortar_hbm, count_hbm, modulus_hbm.at[disp.shape[1] - 1],
     )
     targets = (
-        nodes, disp, rank_ref, face_ref, mortar_ref, shape, count, weight, normal_v, gap_v, modulus,
+        disp, shape, nodes, gap_v, weight, normal_v, rank_ref, face_ref, mortar_ref, count, modulus,
     )
     brought = [
         pltpu.make_async_copy(source, target, sems.at[i])

time: 25 us -> 24.9 us (level)
  no operation moved by 1% of the time
where the time goes in v24:
time: 24.9 us; the launch traced here: 24.6 us
  starting transfers between devices  9.51 us (38%)
  waiting for transfers between devices  8.86 us (36%)
  Pallas kernels  6.11 us (25%)
    ppermute x2, waiting for transfers between devices, swapped(): return lax.ppermute(block, axis, route)  8.86 us
    all_to_all x1, starting transfers between devices, shards(): lax.all_to_all(sent.reshape(domains, 1, -1), 'dom', split_axis=0, concat_...  6.04 us
    ppermute x2, starting transfers between devices, swapped(): return lax.ppermute(block, axis, route)  3.47 us
    pallas_call x1, Pallas kernels, shards(): on_core(first, [shaped((domains * (rows_high + sum(heights)), LANES)), sh...  2.94 us
    pallas_call x1, Pallas kernels, shards(): on_core(last, shaped(displacement.shape), 1000000000, 1500000, out_specs=...  2.17 us
    pallas_call x1, Pallas kernels, shards(): on_core(internal_kernel, [shaped(displacement.shape), shaped((2 * size, s...  1 us
  transfers between devices with their start and end apart: 3, of which 1 were waited for; matrix products, arithmetic and copies ran while one was open for 0% of the time, Pallas kernels for 4%

profile of v24, /device:TPU:16, one launch (start us, length us, event | category | flops | bytes accessed | tf_op | source)
XLA Modules:
  0.0 24.6 jit_solution(6683545411220355589)
XLA Ops:
  0.0 2.9 %shard_map.127 = (f32[904,128]{1,0:T(8,128)}, f32[24,256]{1,0:T(8,128)S(1)}, f32[129,256]{1,0:T(8,128)S(1)}, f32[104,256]{1,0:T(8,128)S(1)}, s32[1,256]{1,0:T(1,...) custom-call(s32[4,512]{1,0:T(4,128)} %refs_0_.1, ...), custom_call_target="tpu_custom_call" | custom-call | flops 900000000 | bytes 1500000 | tf_op jit(solution)/shard_map/pallas_call | solution.py:510
  2.9 0.0 copy-start
  3.0 0.0 copy-start.1
  3.0 0.0 copy-start.2
  3.0 0.0 copy-start.3
  3.0 6.0 %all-to-all-start = ((f32[8,1,14464]{2,1,0:T(1,128)}), f32[8,1,14464]{2,1,0:T(1,128)S(1)}, u32[]{:S(2)}, u32[]{:S(2)}) async-start(f32[8,1,14464]{2,1,0:T(1,128)} %bitcast.5), calls=%async_computation | async-start | bytes 925696 | tf_op jit(solution)/shard_map/all_to_all | solution.py:536
  9.0 0.0 collective-permute-start
  9.0 3.5 %collective-permute-start.1 = (f32[4,32,256]{2,1,0:T(8,128)S(1)}, f32[4,32,256]{2,1,0:T(8,128)S(1)}, u32[]{:S(2)}, u32[]{:S(2)}) collective-permute-start(f32[4,32,256]{2,1,0:T(8,128)S(1)} %get-tuple-element.30.refs_11_), channel_id=1, source_target_pairs={{1,2},{2,1},{3,4},{4,3},{5,6},{6,5},{7,8},{8,7},{9,10},{10,9},{11,... | collective-permute-start | bytes 393224 | tf_op jit(solution)/shard_map/ppermute | solution.py:452
  12.5 0.0 collective-permute-done.halo_ref
  12.5 0.0 copy-done
  12.5 0.0 copy-done.1
  12.5 0.0 copy-done.2
  12.6 0.0 copy-done.3
  12.6 1.0 %shard_map.128 = (f32[3,2,32,256]{3,2,1,0:T(8,128)S(1)}, bf16[384,192]{1,0:T(8,128)(2,1)S(1)}, f32[2,32,256]{2,1,0:T(8,128)S(1)}) custom-call(f32[3,2,32,256]{3,2,1,0:T(8,128)S(1)} %copy-done, f32[2,32,256]{2,1,0:T(8,128)S(1)} %copy-done.1, f32[24,24]{1,0:T(8,128)S(1)} %copy-done.3, f32[2,32,256]{2,1,0:T(8,128)S(1)} %copy-done.2, ...), custom_call_target="tpu_custom_call" | custom-call | flops 1000000000 | bytes 700000 | tf_op jit(solution)/shard_map/pallas_call | solution.py:547
  13.6 8.9 %collective-permute-done.1.refs_12_ = f32[4,32,256]{2,1,0:T(8,128)S(1)} collective-permute-done((f32[4,32,256]{2,1,0:T(8,128)S(1)}, f32[4,32,256]{2,1,0:T(8,128)S(1)}, u32[]{:S(2)}, u32[]{:S(2)}) %collective-permute-start.1) | collective-permute-done | bytes 131104 | tf_op jit(solution)/shard_map/ppermute | solution.py:452
  22.4 0.0 all-to-all-done
  22.4 2.2 %shard_map.129 = f32[3,2,32,256]{3,2,1,0:T(8,128)} custom-call(f32[904,128]{1,0:T(8,128)S(1)} %bitcast.7, f32[24,256]{1,0:T(8,128)S(1)} %get-tuple-element.19.refs_1_, f32[129,256]{1,0:T(8,128)S(1)} %get-tuple-element.20.refs_2_, f32[104,256]{1,0:T(8,128)S(1)} %get-tuple-element.21.refs_3_, s32[1,256]{1,0:T(1,128)S(1)} %get-tuple-element.22.refs_4_, ...), custom_call_target="tpu_custom_call" | custom-call | flops 1000000000 | bytes 1500000 | tf_op jit(solution)/shard_map/pallas_call | solution.py:553
Async XLA Ops:
  2.9 9.6 %copy-start = (f32[3,2,32,256]{3,2,1,0:T(8,128)S(1)}, f32[3,2,32,256]{3,2,1,0:T(8,128)}, u32[]{:S(2)}) copy-start(f32[3,2,32,256]{3,2,1,0:T(8,128)} %disp_ref.1) | copy-start | bytes 589828
  3.0 9.6 %copy-start.1 = (f32[2,32,256]{2,1,0:T(8,128)S(1)}, f32[2,32,256]{2,1,0:T(8,128)}, u32[]{:S(2)}) copy-start(f32[2,32,256]{2,1,0:T(8,128)} %modulus_ref.1) | copy-start | bytes 196612
  3.0 9.6 %copy-start.2 = (f32[2,32,256]{2,1,0:T(8,128)S(1)}, f32[2,32,256]{2,1,0:T(8,128)}, u32[]{:S(2)}) copy-start(f32[2,32,256]{2,1,0:T(8,128)} %mass_ref.1) | copy-start | bytes 196612
  3.0 9.6 %copy-start.3 = (f32[24,24]{1,0:T(8,128)S(1)}, f32[24,24]{1,0:T(8,128)}, u32[]{:S(2)}) copy-start(f32[24,24]{1,0:T(8,128)} %stiffness_ref.1) | copy-start | bytes 6916
  3.0 19.4 %all-to-all-start = ((f32[8,1,14464]{2,1,0:T(1,128)}), f32[8,1,14464]{2,1,0:T(1,128)S(1)}, u32[]{:S(2)}, u32[]{:S(2)}) async-start(f32[8,1,14464]{2,1,0:T(1,128)} %bitcast.5), calls=%async_computation | async-start | bytes 925696 | tf_op jit(solution)/shard_map/all_to_all | solution.py:536
  9.0 3.5 %collective-permute-start = (f32[4,32,256]{2,1,0:T(8,128)S(1)}, f32[4,32,256]{2,1,0:T(8,128)S(1)}, u32[]{:S(2)}, u32[]{:S(2)}) collective-permute-start(f32[4,32,256]{2,1,0:T(8,128)S(1)} %get-tuple-element.26.own_ref), channel_id=1, source_target_pairs={{0,1},{1,0},{2,3},{3,2},{4,5},{5,4},{6,7},{7,6},{8,9},{9,8},{10,11... | collective-permute-start | bytes 393224 | tf_op jit(solution)/shard_map/ppermute | solution.py:452
  9.0 13.4 %collective-permute-start.1 = (f32[4,32,256]{2,1,0:T(8,128)S(1)}, f32[4,32,256]{2,1,0:T(8,128)S(1)}, u32[]{:S(2)}, u32[]{:S(2)}) collective-permute-start(f32[4,32,256]{2,1,0:T(8,128)S(1)} %get-tuple-element.30.refs_11_), channel_id=1, source_target_pairs={{1,2},{2,1},{3,4},{4,3},{5,6},{6,5},{7,8},{8,7},{9,10},{10,9},{11,... | collective-permute-start | bytes 393224 | tf_op jit(solution)/shard_map/ppermute | solution.py:452
